TPU v7x, 32 devices: a whole 2x2x4 slice. The times are simulated.
32 devices in a mesh: dp: 4 (over y, x), seq: 8 (over z, core).
Axes of the slice: x: 2, y: 2, z: 4, core: 2. Of those that a mesh axis runs over, the one named last changes fastest.
Arguments:
- tokens: bfloat16 [4096, 1600], P(('dp', 'seq')), may hold values from -6 to 6
- w_qkv: bfloat16 [1600, 4800], P('dp', 'seq'), may hold values from -0.15625 to 0.15625
- w_out: bfloat16 [1600, 1600], P('dp', 'seq'), may hold values from -0.625 to 0.625
- vectors: bfloat16 [8, 1600], P('dp', 'seq'), may hold values from -1.2 to 1.4, as said below
- w_fc: bfloat16 [1600, 6400], P('dp', 'seq'), may hold values from -0.15625 to 0.15625
- b_fc: bfloat16 [6400], P(('dp', 'seq')), may hold values from -2 to 2
- w_proj: bfloat16 [6400, 1600], P('dp', 'seq'), may hold values from -0.078125 to 0.078125
- cotangent: bfloat16 [4096, 1600], P(('dp', 'seq')), may hold values from -6 to 6
Outputs:
- activations: bfloat16 [4096, 1600], P(('dp', 'seq'))
- input_grad: bfloat16 [4096, 1600], P(('dp', 'seq'))
- grad_w_qkv: float32 [1600, 4800], P('dp', 'seq')
- grad_w_out: float32 [1600, 1600], P('dp', 'seq')
- grad_vectors: float32 [8, 1600], P('dp', 'seq')
- grad_w_fc: float32 [1600, 6400], P('dp', 'seq')
- grad_b_fc: float32 [6400], P(('dp', 'seq'))
- grad_w_proj: float32 [6400, 1600], P('dp', 'seq')
Inputs may be any that keep to these rules, and one draw needn't show every extreme that they name: `vectors`: rows 0 and 5 (the gains) lie in 0.6 to 1.4; the other rows in -1.2 to 1.2.
All inputs are finite; a program needn't handle non-finite values.
Results may differ from a plain program's by a relative error of at most 0.013.
Values may be sent and summed in bfloat16 or wider, within the bound.
No kernel may reach another device: no remote copies, remote signals or barrier semaphores. Data moves between devices by JAX's collectives and lax.ppermute only.
A program may use at most 512 MiB of HBM per device.

v0:
```python
import math

import jax
import jax.numpy as jnp
from jax import lax
from jax.sharding import PartitionSpec as P

HD = 64


EPSILON = 1e-05
GELU_C = 0.7978845608028654
NEG_FILL = -1e30


def layer_norm(features, scale_row, shift_row):
    row_mean = jnp.mean(features, axis=-1, keepdims=True)
    centred = features - row_mean
    variance = jnp.mean(centred * centred, axis=-1, keepdims=True)
    return centred * lax.rsqrt(variance + EPSILON) * scale_row + shift_row


def gelu_tanh(pre_act):
    return (
        0.5
        * pre_act
        * (1.0 + jnp.tanh(GELU_C * (pre_act + 0.044715 * pre_act * pre_act * pre_act)))
    )


def block_view(gathered, dp_count, seq_count, shard_shape):
    return gathered.reshape(dp_count, seq_count, shard_shape[0], shard_shape[1])


def vector_table(gathered, dp_count, seq_count, shard_shape):
    stacked = gathered.reshape(dp_count, seq_count, shard_shape[0], shard_shape[1])
    joined = stacked.transpose(0, 2, 1, 3).reshape(
        dp_count * shard_shape[0], seq_count * shard_shape[1]
    )
    return joined.astype(jnp.float32)


def vector_term(grads, dp_count, seq_count, shard_shape):
    parted = grads.reshape(dp_count, shard_shape[0], seq_count, shard_shape[1])
    return parted.transpose(0, 2, 1, 3).reshape(
        dp_count * seq_count * shard_shape[0], shard_shape[1]
    )


def apply_right(operand, blocks):
    dp_count, seq_count, rows_in, cols_in = blocks.shape
    split_rows = operand.reshape(operand.shape[0], dp_count, rows_in)
    result = jnp.einsum("tpa,pnab->tnb", split_rows, blocks, preferred_element_type=jnp.float32)
    return result.reshape(operand.shape[0], seq_count * cols_in)


def apply_left(grads, blocks):
    dp_count, seq_count, rows_in, cols_in = blocks.shape
    split_rows = grads.reshape(grads.shape[0], seq_count, cols_in)
    result = jnp.einsum("tnb,pnab->tpa", split_rows, blocks, preferred_element_type=jnp.float32)
    return result.reshape(grads.shape[0], dp_count * rows_in)


def weight_term(operand, grads, blocks_shape):
    dp_count, seq_count, rows_in, cols_in = blocks_shape
    left_split = operand.reshape(operand.shape[0], dp_count, rows_in)
    right_split = grads.reshape(grads.shape[0], seq_count, cols_in)
    term = jnp.einsum("tpa,tnb->pnab", left_split, right_split, preferred_element_type=jnp.float32)
    return term.reshape(dp_count * seq_count * rows_in, cols_in)


def group_split(matrix, group_count):
    return matrix.reshape(matrix.shape[0], group_count, -1).transpose(1, 0, 2)


def group_join(stacked):
    return stacked.transpose(1, 0, 2).reshape(stacked.shape[1], -1)


def heads_per_group(head_count, tok_rows):
    best_size = 1
    for trial in range(1, head_count + 1):
        if head_count % trial == 0 and trial * tok_rows <= 2048:
            best_size = trial
    return best_size


def body(tokens, w_qkv, w_out, vectors, w_fc, b_fc, w_proj, cotangent):
    dp_count = lax.axis_size("dp")
    seq_count = lax.axis_size("seq")
    tok_rows, model_width = tokens.shape
    seq_length = tok_rows * seq_count
    head_count = model_width // HD
    group_size = heads_per_group(head_count, tok_rows)
    group_count = head_count // group_size
    score_scale = 1.0 / math.sqrt(HD)
    query_pos = lax.axis_index("seq") * tok_rows + jnp.arange(tok_rows, dtype=jnp.int32)
    key_pos = jnp.arange(seq_length, dtype=jnp.int32)
    allowed = key_pos[None, :] <= query_pos[:, None]
    inputs = tokens.astype(jnp.float32)
    attn_set = (
        lax.all_gather(w_qkv, ("dp", "seq"), axis=0, tiled=True),
        lax.all_gather(w_out, ("dp", "seq"), axis=0, tiled=True),
        lax.all_gather(vectors, ("dp", "seq"), axis=0, tiled=True),
    )
    qkv_blocks = block_view(attn_set[0], dp_count, seq_count, w_qkv.shape)
    out_blocks = block_view(attn_set[1], dp_count, seq_count, w_out.shape)
    vec_table = vector_table(attn_set[2], dp_count, seq_count, vectors.shape)
    normed = layer_norm(inputs, vec_table[0], vec_table[1]).astype(jnp.bfloat16)
    projected = apply_right(normed, qkv_blocks)
    queries = (projected[:, :model_width] + vec_table[2]).astype(jnp.bfloat16)
    key_rows = projected[:, model_width : 2 * model_width].astype(jnp.bfloat16)
    value_rows = (projected[:, 2 * model_width :] + vec_table[3]).astype(jnp.bfloat16)
    query_groups = group_split(queries, group_count)
    local_keys = group_split(key_rows, group_count)
    local_values = group_split(value_rows, group_count)
    key_groups, value_groups = (
        lax.all_gather(local_keys, "seq", axis=1, tiled=True),
        lax.all_gather(local_values, "seq", axis=1, tiled=True),
    )

    def forward_group(operands):
        query_block, key_block, value_block = operands
        query_heads = query_block.reshape(tok_rows, group_size, HD)
        key_heads = key_block.reshape(seq_length, group_size, HD)
        value_heads = value_block.reshape(seq_length, group_size, HD)
        raw_scores = (
            jnp.einsum("tgd,kgd->gtk", query_heads, key_heads, preferred_element_type=jnp.float32)
            * score_scale
        )
        scores = jnp.where(allowed[None], raw_scores, NEG_FILL)
        row_max = jnp.max(scores, axis=-1, keepdims=True)
        unnormed = jnp.exp(scores - row_max)
        row_sum = jnp.sum(unnormed, axis=-1, keepdims=True)
        weights = (unnormed / row_sum).astype(jnp.bfloat16)
        mixed_heads = jnp.einsum(
            "gtk,kgd->tgd", weights, value_heads, preferred_element_type=jnp.float32
        )
        return (mixed_heads.reshape(tok_rows, group_size * HD), row_max + jnp.log(row_sum))

    attn_groups, log_sums = lax.map(forward_group, (query_groups, key_groups, value_groups))
    attended = group_join(attn_groups).astype(jnp.bfloat16)
    middle = inputs + (apply_right(attended, out_blocks) + vec_table[4])
    mlp_set = (
        lax.all_gather(w_fc, ("dp", "seq"), axis=0, tiled=True),
        lax.all_gather(w_proj, ("dp", "seq"), axis=0, tiled=True),
        lax.all_gather(b_fc, ("dp", "seq"), axis=0, tiled=True),
    )
    fc_blocks = block_view(mlp_set[0], dp_count, seq_count, w_fc.shape)
    proj_blocks = block_view(mlp_set[1], dp_count, seq_count, w_proj.shape)
    fc_bias = mlp_set[2].astype(jnp.float32)
    normed_two = layer_norm(middle, vec_table[5], vec_table[6]).astype(jnp.bfloat16)
    pre_act = apply_right(normed_two, fc_blocks) + fc_bias
    hidden = gelu_tanh(pre_act).astype(jnp.bfloat16)
    outcome = middle + (apply_right(hidden, proj_blocks) + vec_table[7])
    activations = outcome.astype(jnp.bfloat16)
    grad_out = cotangent.astype(jnp.float32)
    mlp_again = (
        lax.all_gather(w_fc, ("dp", "seq"), axis=0, tiled=True),
        lax.all_gather(w_proj, ("dp", "seq"), axis=0, tiled=True),
        lax.all_gather(vectors, ("dp", "seq"), axis=0, tiled=True),
    )
    fc_back = block_view(mlp_again[0], dp_count, seq_count, w_fc.shape)
    proj_back = block_view(mlp_again[1], dp_count, seq_count, w_proj.shape)
    vec_back = vector_table(mlp_again[2], dp_count, seq_count, vectors.shape)
    grad_mlp = grad_out.astype(jnp.bfloat16)
    proj_term = weight_term(hidden, grad_mlp, proj_back.shape)
    bias_proj = jnp.sum(grad_mlp.astype(jnp.float32), axis=0)
    grad_hidden = apply_left(grad_mlp, proj_back)
    gelu_out, gelu_pull = jax.vjp(gelu_tanh, pre_act)
    grad_pre = gelu_pull(grad_hidden)[0].astype(jnp.bfloat16)
    fc_term = weight_term(normed_two, grad_pre, fc_back.shape)
    bias_fc = jnp.sum(grad_pre.astype(jnp.float32), axis=0)
    grad_normed_two = apply_left(grad_pre, fc_back)
    norm_out_two, norm_pull_two = jax.vjp(layer_norm, middle, vec_back[5], vec_back[6])
    grad_middle_norm, grad_scale_two, grad_shift_two = norm_pull_two(grad_normed_two)
    fc_grad, proj_grad, fc_bias_grad = (
        lax.psum_scatter(fc_term, ("dp", "seq"), scatter_dimension=0, tiled=True),
        lax.psum_scatter(proj_term, ("dp", "seq"), scatter_dimension=0, tiled=True),
        lax.psum_scatter(bias_fc, ("dp", "seq"), scatter_dimension=0, tiled=True),
    )
    grad_middle = grad_out + grad_middle_norm
    grad_branch = grad_middle.astype(jnp.bfloat16)
    attn_again = (
        lax.all_gather(w_qkv, ("dp", "seq"), axis=0, tiled=True),
        lax.all_gather(w_out, ("dp", "seq"), axis=0, tiled=True),
    )
    qkv_back = block_view(attn_again[0], dp_count, seq_count, w_qkv.shape)
    out_back = block_view(attn_again[1], dp_count, seq_count, w_out.shape)
    out_term = weight_term(attended, grad_branch, out_back.shape)
    bias_out = jnp.sum(grad_branch.astype(jnp.float32), axis=0)
    grad_attended = apply_left(grad_branch, out_back).astype(jnp.bfloat16)
    grad_groups = group_split(grad_attended, group_count)
    key_back, value_back = (
        lax.all_gather(local_keys, "seq", axis=1, tiled=True),
        lax.all_gather(local_values, "seq", axis=1, tiled=True),
    )

    def backward_group(operands):
        query_block, key_block, value_block, grad_block, log_sum = operands
        query_heads = query_block.reshape(tok_rows, group_size, HD)
        key_heads = key_block.reshape(seq_length, group_size, HD)
        value_heads = value_block.reshape(seq_length, group_size, HD)
        grad_heads = grad_block.reshape(tok_rows, group_size, HD)
        raw_scores = (
            jnp.einsum("tgd,kgd->gtk", query_heads, key_heads, preferred_element_type=jnp.float32)
            * score_scale
        )
        soft_rows = jnp.where(
            allowed[None], jnp.exp(jnp.where(allowed[None], raw_scores, NEG_FILL) - log_sum), 0.0
        )
        soft_low = soft_rows.astype(jnp.bfloat16)
        grad_values = jnp.einsum(
            "gtk,tgd->kgd", soft_low, grad_heads, preferred_element_type=jnp.float32
        )
        grad_soft = jnp.einsum(
            "tgd,kgd->gtk", grad_heads, value_heads, preferred_element_type=jnp.float32
        )
        centre = jnp.sum(soft_rows * grad_soft, axis=-1, keepdims=True)
        grad_scores = (soft_rows * (grad_soft - centre)).astype(jnp.bfloat16)
        grad_queries = (
            jnp.einsum("gtk,kgd->tgd", grad_scores, key_heads, preferred_element_type=jnp.float32)
            * score_scale
        )
        grad_keys = (
            jnp.einsum("gtk,tgd->kgd", grad_scores, query_heads, preferred_element_type=jnp.float32)
            * score_scale
        )
        return (
            grad_queries.reshape(tok_rows, group_size * HD),
            grad_keys.reshape(seq_length, group_size * HD),
            grad_values.reshape(seq_length, group_size * HD),
        )

    query_grads, key_grads, value_grads = lax.map(
        backward_group, (query_groups, key_back, value_back, grad_groups, log_sums)
    )
    key_own, value_own = (
        lax.psum_scatter(
            key_grads.astype(jnp.bfloat16), "seq", scatter_dimension=1, tiled=True
        ).astype(jnp.float32),
        lax.psum_scatter(
            value_grads.astype(jnp.bfloat16), "seq", scatter_dimension=1, tiled=True
        ).astype(jnp.float32),
    )
    grad_projected = jnp.concatenate(
        [
            group_join(query_grads).astype(jnp.bfloat16),
            group_join(key_own).astype(jnp.bfloat16),
            group_join(value_own).astype(jnp.bfloat16),
        ],
        axis=1,
    )
    qkv_term = weight_term(normed, grad_projected, qkv_back.shape)
    bias_query = jnp.sum(grad_projected[:, :model_width].astype(jnp.float32), axis=0)
    bias_value = jnp.sum(grad_projected[:, 2 * model_width :].astype(jnp.float32), axis=0)
    grad_normed = apply_left(grad_projected, qkv_back)
    norm_out_one, norm_pull_one = jax.vjp(layer_norm, inputs, vec_back[0], vec_back[1])
    grad_inputs_norm, grad_scale_one, grad_shift_one = norm_pull_one(grad_normed)
    input_grad = (grad_middle + grad_inputs_norm).astype(jnp.bfloat16)
    vector_grads = jnp.stack(
        [
            grad_scale_one,
            grad_shift_one,
            bias_query,
            bias_value,
            bias_out,
            grad_scale_two,
            grad_shift_two,
            bias_proj,
        ]
    )
    vec_term = vector_term(vector_grads, dp_count, seq_count, vectors.shape)
    qkv_grad, out_grad, vec_grad = (
        lax.psum_scatter(qkv_term, ("dp", "seq"), scatter_dimension=0, tiled=True),
        lax.psum_scatter(out_term, ("dp", "seq"), scatter_dimension=0, tiled=True),
        lax.psum_scatter(vec_term, ("dp", "seq"), scatter_dimension=0, tiled=True),
    )
    return (activations, input_grad, qkv_grad, out_grad, vec_grad, fc_grad, fc_bias_grad, proj_grad)


def solution(mesh):
    placed = (
        P(("dp", "seq"), None),
        P("dp", "seq"),
        P("dp", "seq"),
        P("dp", "seq"),
        P("dp", "seq"),
        P(("dp", "seq")),
        P("dp", "seq"),
        P(("dp", "seq"), None),
    )
    return jax.shard_map(
        body,
        mesh=mesh,
        in_specs=placed,
        out_specs=(
            P(("dp", "seq"), None),
            P(("dp", "seq"), None),
            P("dp", "seq"),
            P("dp", "seq"),
            P("dp", "seq"),
            P("dp", "seq"),
            P(("dp", "seq")),
            P("dp", "seq"),
        ),
        check_vma=False,
    )
```

profile of v0, /device:TPU:0, one launch (start us, length us, event | category | flops | bytes accessed | tf_op | source)
XLA Modules:
  0.0 2546.6 jit_solution(648543727720467439)
XLA Ops:
  8.7 43.8 %all-gather = bf16[32,2,200]{2,1,0:T(2,128)(2,1)S(1)} all-gather(bf16[1,2,200]{2,1,0:T(2,128)(2,1)} %bitcast.325), channel_id=1, replica_groups=mesh['dp'=4,'seq'=8] {'dp','seq'}, dimensions={0}, use_global_device_ids=true | all-gather | bytes 26400 | tf_op jit(solution)/shard_map/all_gather | solution.py:104
  57.3 69.5 %all-gather.9.cloned.1.call-done = bf16[12800,600]{1,0:T(8,128)(2,1)} async-done(((bf16[400,600]{1,0:T(8,128)(2,1)}), bf16[12800,600]{1,0:T(8,128)(2,1)}) %all-gather.9.cloned.1.call-update) | async-done | bytes 15360016 | tf_op jit(solution)/shard_map/all_gather | solution.py:102
  126.8 21.7 copy.117
  148.5 27.1 %dot_general.90 = bf16[4800,400,4]{0,1,2:T(8,128)(2,1)} reshape(bf16[8,600,400,4]{1,0,2,3:T(8,128)(2,1)} %bitcast.270) | data formatting | bytes 30720000 | tf_op jit(solution)/shard_map/tpa,pnab->tnb/dot_general | solution.py:53
  188.9 41.2 %all-reduce = bf16[6400]{0:T(1024)(128)(2,1)S(1)} all-reduce(bf16[6400]{0:T(1024)(128)(2,1)S(1)} %dynamic-update-slice), channel_id=1, replica_groups=mesh['dp'=4,'seq'=8] {'dp','seq'}, use_global_device_ids=true, to_apply=%add | all-reduce | flops 6400 | bytes 25600
  230.1 13.1 copy.71
  263.2 12.7 dot_general.108
  280.7 20.0 while.28
  306.6 118.9 %all-gather.17.cloned.1.call-done = bf16[12800,800]{1,0:T(8,128)(2,1)} async-done(((bf16[400,800]{1,0:T(8,128)(2,1)}), bf16[12800,800]{1,0:T(8,128)(2,1)}) %all-gather.17.cloned.1.call-update) | async-done | bytes 20480016 | tf_op jit(solution)/shard_map/all_gather | solution.py:145
  425.5 32.6 %copy.116 = bf16[4,8,400,800]{3,1,2,0:T(8,128)(2,1)} copy(bf16[4,8,400,800]{3,2,1,0:T(8,128)(2,1)} %bitcast.284) | data formatting | bytes 40960000 | tf_op jit(solution)/shard_map/reshape | solution.py:32
  458.2 36.9 %dot_general.96 = bf16[6400,400,4]{0,1,2:T(8,128)(2,1)} reshape(bf16[8,800,400,4]{1,0,2,3:T(8,128)(2,1)} %bitcast.267) | data formatting | bytes 40960000 | tf_op jit(solution)/shard_map/tpa,pnab->tnb/dot_general | solution.py:53
  495.1 67.6 %all-gather.19.cloned.1.call-done = bf16[32,1600,200]{1,2,0:T(8,128)(2,1)} async-done(((bf16[1,1600,200]{1,2,0:T(8,128)(2,1)}), bf16[32,1600,200]{1,2,0:T(8,128)(2,1)}) %all-gather.19.cloned.1.call-update) | async-done | bytes 20480016 | tf_op jit(solution)/shard_map/all_gather | solution.py:146
  562.7 37.5 %copy.67 = bf16[4,1600,200,8]{1,0,2,3:T(4,128)(2,1)} copy(bf16[4,1600,200,8]{1,2,3,0:T(8,128)(2,1)} %bitcast.285) | data formatting | bytes 40960000 | tf_op jit(solution)/shard_map/tnb,pnab->tpa/dot_general | solution.py:60
  600.3 35.1 %dot_general.102 = bf16[6400,200,8]{0,1,2:T(8,128)(2,1)} reshape(bf16[4,1600,200,8]{1,0,2,3:T(4,128)(2,1)} %copy.67) | data formatting | bytes 40960000 | tf_op jit(solution)/shard_map/tnb,pnab->tpa/dot_general | solution.py:60
  635.3 13.5 multiply_convert_fusion.1
  661.5 17.9 multiply_reduce_fusion.1
  684.9 39.5 %while.29 = (s32[]{:T(128)}, bf16[5,128,320]{1,2,0:T(8,128)(2,1)S(1)}, bf16[5,1024,320]{1,2,0:T(8,128)(2,1)}, bf16[5,1024,320]{1,2,0:T(8,128)(2,1)}, bf16[5,1024...) while((s32[]{:T(128)}, ...), condition=%wide.region_12.13_spmd.clone, body=%wide.region_10.12_spmd.clone.sunk | while | flops 426851712 | bytes 29357200 | solution.py:235
  763.7 19.1 reduce-scatter.21.cloned.1.call-done
  788.6 37.7 %reduce-scatter.19.cloned.1.call-done = bf16[128,1600]{1,0:T(8,128)(2,1)} async-done(((bf16[1024,1600]{1,0:T(8,128)(2,1)}), bf16[128,1600]{1,0:T(8,128)(2,1)}) %reduce-scatter.19.cloned.1.call-update) | async-done | bytes 409616
  833.3 13.8 fusion.51
  852.2 17.9 convolution_bitcast_fusion
  870.1 46.0 %copy.93 = f32[4,8,1600,200]{3,2,1,0:T(8,128)} copy(f32[4,8,1600,200]{2,3,1,0:T(8,128)} %convolution_bitcast_fusion) | data formatting | bytes 81920000
  923.7 14.5 copy.92
  939.6 13.0 convolution_bitcast_fusion.2
  952.6 22.3 copy.74
  975.9 20.1 convolution_bitcast_fusion.1
  996.0 31.8 %copy.77 = f32[4,8,400,800]{3,2,1,0:T(8,128)} copy(f32[4,8,400,800]{3,2,0,1:T(8,128)} %convolution_bitcast_fusion.1) | data formatting | bytes 81920000 | tf_op jit(solution)/shard_map/tpa,tnb->pnab/transpose | solution.py:68
  1029.0 13.5 fusion.32
  1045.1 487.3 %reduce-scatter.25.cloned.1.call-done = f32[1600,200]{1,0:T(8,128)} async-done(((f32[51200,200]{1,0:T(8,128)}), f32[1600,200]{1,0:T(8,128)}) %reduce-scatter.25.cloned.1.call-update) | async-done | bytes 1280016
  1535.3 161.5 %reduce-scatter.23.cloned.1.call-done = f32[400,200]{1,0:T(8,128)} async-done(((f32[12800,200]{1,0:T(8,128)}), f32[400,200]{1,0:T(8,128)}) %reduce-scatter.23.cloned.1.call-update) | async-done | bytes 320016
  1696.8 354.2 %reduce-scatter.15.cloned.1.call-done = f32[400,600]{1,0:T(8,128)} async-done(((f32[12800,600]{1,0:T(8,128)}), f32[400,600]{1,0:T(8,128)}) %reduce-scatter.15.cloned.1.call-update) | async-done | bytes 960016 | tf_op jit(solution)/shard_map/reduce_scatter | solution.py:275
  2051.0 488.7 %reduce-scatter.17.cloned.1.call-done = f32[400,800]{1,0:T(8,128)} async-done(((f32[12800,800]{1,0:T(8,128)}), f32[400,800]{1,0:T(8,128)}) %reduce-scatter.17.cloned.1.call-update) | async-done | bytes 1280016 | tf_op jit(solution)/shard_map/reduce_scatter | solution.py:178
  (258 shorter events, 200.8 us)
Async XLA Ops:
  7.2 119.6 %all-gather.9.cloned.1.call-start = ((), (), s32[]{:S(2)}) async-start(), calls=%async_computation.6 | async-start | bytes 16896000 | tf_op jit(solution)/shard_map/all_gather | solution.py:102
  7.9 222.2 %all-gather.15.cloned.1.call-start = ((), (), s32[]{:S(2)}) async-start(), calls=%async_computation.9 | async-start | bytes 6758400 | tf_op jit(solution)/shard_map/all_gather | solution.py:103
  8.7 267.2 %all-gather.13.cloned.1.call-start = ((), (), s32[]{:S(2)}) async-start(), calls=%async_computation.8 | async-start | bytes 3686400 | tf_op jit(solution)/shard_map/all_gather | solution.py:118
  53.2 95.2 %copy-start.16 = (f32[1600]{0:T(1024)}, f32[1600]{0:T(1024)S(1)}, u32[]{:S(2)}) copy-start(f32[1600]{0:T(1024)S(1)} %get-tuple-element.183) | copy-start | bytes 19204
  54.5 94.0 %copy-start.19 = (f32[128]{0:T(128)}, f32[128]{0:T(128)S(1)}, u32[]{:S(2)}) copy-start(f32[128]{0:T(128)S(1)} %broadcast_multiply_fusion.1) | copy-start | bytes 1540
  55.7 92.7 %copy-start.23 = (f32[128]{0:T(128)}, f32[128]{0:T(128)S(1)}, u32[]{:S(2)}) copy-start(f32[128]{0:T(128)S(1)} %fusion.43) | copy-start | bytes 1540
  55.7 92.7 %copy-start.21 = (f32[128]{0:T(128)}, f32[128]{0:T(128)S(1)}, u32[]{:S(2)}) copy-start(f32[128]{0:T(128)S(1)} %fusion.49) | copy-start | bytes 1540
  57.3 118.4 %copy-start.8 = (bf16[128,1600]{0,1:T(8,128)(2,1)}, bf16[128,1600]{0,1:T(8,128)(2,1)S(1)}, u32[]{:S(2)}) copy-start(bf16[128,1600]{0,1:T(8,128)(2,1)S(1)} %fusion.41) | copy-start | bytes 1228804
  186.1 94.6 %all-gather.11.cloned.1.call-start = ((), (), s32[]{:S(2)}) async-start(), calls=%async_computation.7 | async-start | bytes 3686400 | tf_op jit(solution)/shard_map/all_gather | solution.py:119
  187.4 238.2 %all-gather.17.cloned.1.call-start = ((), (), s32[]{:S(2)}) async-start(), calls=%async_computation.10 | async-start | bytes 23654400 | tf_op jit(solution)/shard_map/all_gather | solution.py:145
  188.0 374.8 %all-gather.19.cloned.1.call-start = ((), (), s32[]{:S(2)}) async-start(), calls=%async_computation.13 | async-start | bytes 21964800 | tf_op jit(solution)/shard_map/all_gather | solution.py:146
  188.5 594.2 %reduce-scatter.21.cloned.1.call-start = ((), (), s32[]{:S(2)}) async-start(), calls=%async_computation.15 | async-start | bytes 3833856
  280.7 20.1 copy-start.1
  300.7 5.1 copy-start.10
  300.8 5.1 copy-start.12
  305.9 373.7 %copy-start.2 = (f32[128,1600]{0,1:T(8,128)}, f32[128,1600]{0,1:T(8,128)S(1)}, u32[]{:S(2)}) copy-start(f32[128,1600]{0,1:T(8,128)S(1)} %get-tuple-element.241) | copy-start | bytes 2457604
  306.6 328.7 %copy-start.5 = (bf16[128,1600]{0,1:T(8,128)(2,1)}, bf16[128,1600]{0,1:T(8,128)(2,1)S(1)}, u32[]{:S(2)}) copy-start(bf16[128,1600]{0,1:T(8,128)(2,1)S(1)} %add_convert_fusion.1) | copy-start | bytes 1228804
  635.3 14.0 copy-start
  635.3 14.2 copy-start.14
  661.5 18.0 copy-start.4
  661.5 18.3 copy-start.15
  724.5 8.4 copy-start.13
  741.9 84.5 %reduce-scatter.19.cloned.1.call-start = ((), (), s32[]{:S(2)}) async-start(), calls=%async_computation.14 | async-start | bytes 3833856
  759.2 283.2 %all-reduce.6.cloned.1.call-start = ((), (), s32[]{:S(2)}) async-start(), calls=%async_computation.18 | async-start | bytes 188416
  785.1 48.1 %copy-start.17 = (f32[1600]{0:T(1024)S(1)}, f32[1600]{0:T(1024)}, u32[]{:S(2)}) copy-start(f32[1600]{0:T(1024)} %copy-done.16) | copy-start | bytes 19204
  785.1 48.1 %copy-start.20 = (f32[128]{0:T(128)S(1)}, f32[128]{0:T(128)}, u32[]{:S(2)}) copy-start(f32[128]{0:T(128)} %copy-done.19) | copy-start | bytes 1540
  833.3 13.8 copy-start.24
  833.3 13.8 copy-start.22
  852.2 680.1 %reduce-scatter.25.cloned.1.call-start = ((), (), s32[]{:S(2)}) async-start(), calls=%async_computation.17 | async-start | bytes 54067200
  916.2 780.7 %reduce-scatter.23.cloned.1.call-start = ((), (), s32[]{:S(2)}) async-start(), calls=%async_computation.16 | async-start | bytes 13516800
  938.3 1112.7 %reduce-scatter.15.cloned.1.call-start = ((), (), s32[]{:S(2)}) async-start(), calls=%async_computation.11 | async-start | bytes 33792000 | tf_op jit(solution)/shard_map/reduce_scatter | solution.py:275
  975.0 1564.7 %reduce-scatter.17.cloned.1.call-start = ((), (), s32[]{:S(2)}) async-start(), calls=%async_computation.12 | async-start | bytes 47308800 | tf_op jit(solution)/shard_map/reduce_scatter | solution.py:178
  (7 other events, 10.4 us)
Sparse Core Ops, SparseCore 0:
  10.9 115.8 all-gather.8
  129.7 68.9 all-gather.14
  200.8 40.9 all-gather.12
  243.9 36.6 all-gather.10
  283.3 142.1 all-gather.16
  428.3 134.3 all-gather.18
  742.0 40.7 reduce-scatter.20
  785.1 41.2 reduce-scatter.18
  852.3 119.6 all-reduce.5
  974.2 558.0 reduce-scatter.24
  1535.2 161.5 reduce-scatter.22
  1699.7 351.2 reduce-scatter.14
  2053.9 485.7 reduce-scatter.16
where the time goes:
time: 2560 us; the launch traced here: 2550 us
  waiting for transfers between devices  1810 us (71%)
  local copies, waits for them, and re-layouts  444 us (17%)
  matrix products  168 us (7%)
  blocking collectives  85 us (3%)
    unnamed x18, waiting for transfers between devices  708 us
    reduce_scatter x1, waiting for transfers between devices, body(): lax.psum_scatter(fc_term, ('dp', 'seq'), scatter_dimension=0, tiled=True)  489 us
    reduce_scatter x1, waiting for transfers between devices, body(): lax.psum_scatter(qkv_term, ('dp', 'seq'), scatter_dimension=0, tiled=True)  354 us
    all_gather x1, waiting for transfers between devices, body(): lax.all_gather(w_fc, ('dp', 'seq'), axis=0, tiled=True)  119 us
    unnamed x67, local copies, waits for them, and re-layouts  115 us
    dot_general x3, local copies, waits for them, and re-layouts, apply_left(): jnp.einsum('tnb,pnab->tpa', split_rows, blocks, preferred_element_type=jn...  85.3 us
    dot_general x3, local copies, waits for them, and re-layouts, apply_right(): jnp.einsum('tpa,pnab->tnb', split_rows, blocks, preferred_element_type=jn...  75.8 us
    reshape x4, local copies, waits for them, and re-layouts, block_view(): return gathered.reshape(dp_count, seq_count, shard_shape[0], shard_shape[1])  75.5 us
  transfers between devices with their start and end apart: 13, of which 10 were waited for; matrix products, arithmetic and copies ran while one was open for 17% of the time, Pallas kernels for 0%

commit v1 on v0

v1 whole, which is shorter than its diff:
```python
import functools
import math

import jax
import jax.numpy as jnp
import numpy as np
from jax import lax
from jax.experimental import pallas as pl
from jax.experimental.pallas import tpu as pltpu
from jax.sharding import PartitionSpec as P

HD = 64
PAIR = 2 * HD
EPSILON = 1e-05
GELU_C = 0.7978845608028654
NEG_FILL = -1e30
BF = jnp.bfloat16
F32 = jnp.float32


def head_plan(head_count, seq_count, width):
    slots = -(-head_count // seq_count)
    slots += slots % 2
    model = head_count * HD

    def tables(turn):
        owner = np.full((seq_count, slots), -1, np.int32)
        for head in range(head_count):
            row = head // seq_count
            owner[(head + turn * row) % seq_count, row] = head
        place = {}
        for dev in range(seq_count):
            for slot in range(slots):
                if owner[dev, slot] >= 0:
                    place[int(owner[dev, slot])] = (dev, slot)
        lists = [[[] for _ in range(seq_count)] for _ in range(seq_count)]
        for col in range(3 * model):
            kind, rest = divmod(col, model)
            head, lane = divmod(rest, HD)
            dev, slot = place[head]
            src, local = divmod(col, width)
            lists[src][dev].append((local, (kind * slots + slot) * HD + lane))
        most = max(len(cell) for row in lists for cell in row)
        return most, owner, lists

    best = min((tables(turn) for turn in range(seq_count)), key=lambda t: t[0])
    most, owner, lists = best
    wide = -(-most // 128) * 128
    send = np.full((seq_count, seq_count, wide), -1, np.int32)
    recv = np.full((seq_count, seq_count, wide), -1, np.int32)
    for src in range(seq_count):
        for dev in range(seq_count):
            for i, (local, target) in enumerate(lists[src][dev]):
                send[src, dev, i] = local
                recv[src, dev, i] = target
    return slots, owner, wide, send, recv


def xor_perm(count, k):
    return [(i, i ^ k) for i in range(count)]


def gather_rel(block, axis):
    count = lax.axis_size(axis)
    return [block] + [lax.ppermute(block, axis, xor_perm(count, k)) for k in range(1, count)]


def scatter_rel(chunks, axis):
    count = lax.axis_size(axis)
    total = chunks[0].astype(F32)
    for k in range(1, count):
        total = total + lax.ppermute(chunks[k], axis, xor_perm(count, k)).astype(F32)
    return total


def gather_small(block, axis):
    count = lax.axis_size(axis)
    me = lax.axis_index(axis)
    stack = block[None]
    step = 1
    while step < count:
        other = lax.ppermute(stack, axis, xor_perm(count, step))
        low = (me & step) == 0
        stack = jnp.where(
            low, jnp.concatenate([stack, other]), jnp.concatenate([other, stack])
        )
        step *= 2
    return stack


def swap_blocks(matrix, count, me):
    size = matrix.shape[1] // count
    return jnp.concatenate(
        [lax.dynamic_slice_in_dim(matrix, (me ^ k) * size, size, axis=1) for k in range(count)],
        axis=1,
    )


def normalise(rows):
    mean = jnp.mean(rows, axis=-1, keepdims=True)
    centred = rows - mean
    inverse = lax.rsqrt(jnp.mean(centred * centred, axis=-1, keepdims=True) + EPSILON)
    return centred * inverse, inverse


def norm_back(grad, unit, inverse, gain):
    scaled = grad * gain
    return (
        scaled
        - jnp.mean(scaled, axis=-1, keepdims=True)
        - unit * jnp.mean(scaled * unit, axis=-1, keepdims=True)
    ) * inverse


def gelu_parts(u):
    cube = u * u * u
    t = jnp.tanh(GELU_C * (u + 0.044715 * cube))
    value = 0.5 * u * (1.0 + t)
    slope = 0.5 * (1.0 + t) + 0.5 * u * (1.0 - t * t) * GELU_C * (1.0 + 3 * 0.044715 * u * u)
    return value, slope


def mm(a, b):
    return jnp.dot(a, b, preferred_element_type=F32)


def mm_nt(a, b):
    return lax.dot_general(a, b, (((1,), (1,)), ((), ())), preferred_element_type=F32)


def mm_tn(a, b):
    return lax.dot_general(a, b, (((0,), (0,)), ((), ())), preferred_element_type=F32)


def block_rows(length):
    return math.gcd(length, 256)


def attend_kernel(q_ref, k_ref, v_ref, o_ref, lse_ref):
    length = q_ref.shape[0]
    rows = block_rows(length)
    first = lax.broadcasted_iota(jnp.int32, (rows, PAIR), 1) < HD
    causal = lax.broadcasted_iota(jnp.int32, (rows, rows), 0) >= lax.broadcasted_iota(
        jnp.int32, (rows, rows), 1
    )
    for i in range(length // rows):
        here = pl.ds(i * rows, rows)
        seen = (i + 1) * rows
        q = q_ref[here, :] * BF(1.0 / math.sqrt(HD))
        keys = k_ref[0:seen, :]
        values = v_ref[0:seen, :]
        outs, logs = [], []
        for mine in (first, ~first):
            s = mm_nt(jnp.where(mine, q, BF(0)), keys)
            tail = jnp.where(causal, s[:, seen - rows :], NEG_FILL)
            s = tail if i == 0 else jnp.concatenate([s[:, : seen - rows], tail], axis=1)
            top = jnp.max(s, axis=-1, keepdims=True)
            e = jnp.exp(s - top)
            total = jnp.sum(e, axis=-1, keepdims=True)
            outs.append(mm(e.astype(BF), values) / total)
            logs.append(top + jnp.log(total))
        o_ref[here, :] = jnp.where(first, outs[0], outs[1]).astype(BF)
        lse_ref[here, :] = jnp.where(first, logs[0], logs[1])


def attend(qkv, slots):
    length = qkv.shape[0]
    pairs = slots * HD // PAIR
    spec = lambda shift: pl.BlockSpec((length, PAIR), lambda g: (0, g + shift))
    return pl.pallas_call(
        attend_kernel,
        grid=(pairs,),
        in_specs=[spec(0), spec(pairs), spec(2 * pairs)],
        out_specs=[spec(0), spec(0)],
        out_shape=[
            jax.ShapeDtypeStruct((length, slots * HD), BF),
            jax.ShapeDtypeStruct((length, slots * HD), F32),
        ],
        compiler_params=pltpu.CompilerParams(vmem_limit_bytes=48 * 1024 * 1024),
    )(qkv, qkv, qkv)


def attend_back_kernel(q_ref, k_ref, v_ref, ga_ref, lse_ref, gq_ref, gk_ref, gv_ref, ak, av):
    length = q_ref.shape[0]
    rows = block_rows(length)
    first = lax.broadcasted_iota(jnp.int32, (rows, PAIR), 1) < HD
    causal = lax.broadcasted_iota(jnp.int32, (rows, rows), 0) >= lax.broadcasted_iota(
        jnp.int32, (rows, rows), 1
    )
    ak[...] = jnp.zeros_like(ak)
    av[...] = jnp.zeros_like(av)
    for i in range(length // rows):
        here = pl.ds(i * rows, rows)
        seen = (i + 1) * rows
        q = q_ref[here, :] * BF(1.0 / math.sqrt(HD))
        ga = ga_ref[here, :]
        keys = k_ref[0:seen, :]
        values = v_ref[0:seen, :]
        grads = []
        for h, mine in enumerate((first, ~first)):
            q_h = jnp.where(mine, q, BF(0))
            ga_h = jnp.where(mine, ga, BF(0))
            s = mm_nt(q_h, keys)
            tail = jnp.where(causal, s[:, seen - rows :], NEG_FILL)
            s = tail if i == 0 else jnp.concatenate([s[:, : seen - rows], tail], axis=1)
            p = jnp.exp(s - lse_ref[here, h * HD : h * HD + 1])
            gp = mm_nt(ga_h, values)
            centre = jnp.sum(p * gp, axis=-1, keepdims=True)
            gs = (p * (gp - centre)).astype(BF)
            av[0:seen, :] += mm_tn(p.astype(BF), ga_h)
            ak[0:seen, :] += mm_tn(gs, q_h)
            grads.append(mm(gs, keys))
        gq_ref[here, :] = (jnp.where(first, grads[0], grads[1]) * (1.0 / math.sqrt(HD))).astype(BF)
    gk_ref[...] = ak[...].astype(BF)
    gv_ref[...] = av[...].astype(BF)


def attend_back(qkv, grad, lse, slots):
    length = qkv.shape[0]
    pairs = slots * HD // PAIR
    spec = lambda shift: pl.BlockSpec((length, PAIR), lambda g: (0, g + shift))
    shape = jax.ShapeDtypeStruct((length, slots * HD), BF)
    return pl.pallas_call(
        attend_back_kernel,
        grid=(pairs,),
        in_specs=[spec(0), spec(pairs), spec(2 * pairs), spec(0), spec(0)],
        out_specs=[spec(0), spec(0), spec(0)],
        out_shape=[shape, shape, shape],
        scratch_shapes=[pltpu.VMEM((length, PAIR), F32), pltpu.VMEM((length, PAIR), F32)],
        compiler_params=pltpu.CompilerParams(vmem_limit_bytes=48 * 1024 * 1024),
    )(qkv, qkv, qkv, grad, lse)


def body(tokens, w_qkv, w_out, vectors, w_fc, b_fc, w_proj, cotangent):
    dps = lax.axis_size("dp")
    seqs = lax.axis_size("seq")
    dp = lax.axis_index("dp")
    sq = lax.axis_index("seq")
    rows, model = tokens.shape
    head_count = model // HD
    slots, owner, wide, send, recv = head_plan(head_count, seqs, w_qkv.shape[1])
    mine = slots * HD
    ff_mine = w_fc.shape[1]
    ff_part = ff_mine // dps
    ratio = seqs // dps
    col = w_proj.shape[1]
    order = np.concatenate([owner[d] for d in range(seqs)])

    per, wide_vec = vectors.shape
    small = gather_small(jnp.concatenate([vectors.reshape(-1), b_fc])[None], "dp")
    small = gather_small(small, "seq").astype(F32)[:, :, 0]
    table = small[:, :, : per * wide_vec].reshape(seqs, dps, per, wide_vec)
    table = table.transpose(1, 2, 0, 3).reshape(dps * per, model)
    gain1, shift1, bias_q, bias_v, bias_o, gain2, shift2, bias_p = [table[i] for i in range(8)]
    bias_fc = small[:, :, per * wide_vec :].transpose(1, 0, 2).reshape(-1)
    bias_fc = lax.dynamic_slice_in_dim(bias_fc, sq * ff_mine, ff_mine)
    own_heads = jnp.asarray(owner)[sq]
    pick = (own_heads[:, None] == jnp.arange(head_count)[None, :]).astype(F32)

    def head_rows(vector):
        return jnp.sum(pick[:, :, None] * vector.reshape(1, head_count, HD), axis=1).reshape(-1)

    def head_spread(vector):
        return jnp.sum(pick[:, :, None] * vector.reshape(slots, 1, HD), axis=0).reshape(-1)

    bias_qkv = jnp.concatenate([head_rows(bias_q), jnp.zeros((mine,), F32), head_rows(bias_v)])

    to_send = (jnp.arange(w_qkv.shape[1])[:, None, None] == jnp.asarray(send)[sq][None]).astype(BF)
    to_recv = (
        lax.dynamic_index_in_dim(jnp.asarray(recv), sq, 1, keepdims=False)[:, :, None]
        == jnp.arange(3 * mine)[None, None]
    ).astype(BF)
    parts = jnp.einsum("ac,cnw->naw", w_qkv, to_send, preferred_element_type=F32).astype(BF)
    parts = lax.all_to_all(parts, "seq", 0, 0, tiled=True)
    own_qkv = jnp.einsum("naw,nwd->ad", parts, to_recv, preferred_element_type=F32).astype(BF)
    wq = jnp.concatenate(gather_rel(own_qkv, "dp"), axis=0)
    wf = jnp.concatenate(gather_rel(w_fc, "dp"), axis=0)

    pieces = w_proj.reshape(ratio, dps, ff_part, col)
    pieces = lax.all_to_all(pieces.transpose(1, 0, 2, 3), "dp", 0, 0, tiled=True)
    pieces = lax.all_to_all(pieces.reshape(seqs, ff_part, col), "seq", 0, 0, tiled=True)
    own_proj = pieces.transpose(1, 0, 2).reshape(ff_part, model)
    wp_rel = jnp.stack(gather_rel(own_proj, "dp"))
    wp = jnp.concatenate(
        [lax.dynamic_index_in_dim(wp_rel, dp ^ k, 0, keepdims=False) for k in range(dps)], axis=0
    )

    wo = lax.all_gather(w_out, ("dp", "seq"), axis=0, tiled=True)
    wo = wo.reshape(dps, seqs, w_out.shape[0], w_out.shape[1]).transpose(0, 2, 1, 3)
    wo = wo.reshape(head_count, HD, model)
    empty = jnp.zeros((HD, model), BF)
    wo = jnp.concatenate([wo[h] if h >= 0 else empty for h in order], axis=0)

    x = tokens.astype(F32)
    z1, inv1 = normalise(x)
    n1 = swap_blocks((z1 * gain1 + shift1).astype(BF), dps, dp)
    n1_all = lax.all_gather(n1, "seq", axis=0, tiled=True)
    gm_all = lax.all_gather(cotangent, "seq", axis=0, tiled=True)
    qkv = (mm(n1_all, wq) + bias_qkv).astype(BF)
    att, lse = attend(qkv, slots)
    att = lax.all_to_all(att.reshape(seqs, rows, mine), "seq", 0, 0, tiled=True)
    att = att.transpose(1, 0, 2).reshape(rows, seqs * mine)
    r = x + (mm(att, wo) + bias_o)
    z2, inv2 = normalise(r)
    n2 = swap_blocks((z2 * gain2 + shift2).astype(BF), dps, dp)
    n2_all = lax.all_gather(n2, "seq", axis=0, tiled=True)
    u = mm(n2_all, wf) + bias_fc
    value, slope = gelu_parts(u)
    e = value.astype(BF)
    mlp = lax.psum_scatter(mm(e, wp).astype(BF), "seq", scatter_dimension=0, tiled=True)
    activations = (r + (mlp.astype(F32) + bias_p)).astype(BF)

    g = cotangent.astype(F32)
    gu = (mm_nt(gm_all, wp) * slope).astype(BF)
    gn2_part = mm_nt(gu, wf).astype(BF)
    gn2 = lax.psum_scatter(gn2_part, "seq", scatter_dimension=0, tiled=True)
    gn2 = swap_blocks(gn2, dps, dp).astype(F32)
    d_proj = mm_tn(e, gm_all)
    d_fc = mm_tn(n2_all, gu)
    sum_fc = jnp.sum(gu.astype(F32), axis=0)
    gr = g + norm_back(gn2, z2, inv2, gain2)
    go = gr.astype(BF)

    ga = mm_nt(go, wo).astype(BF)
    ga = lax.all_to_all(ga.reshape(rows, seqs, mine).transpose(1, 0, 2), "seq", 0, 0, tiled=True)
    ga = ga.reshape(seqs * rows, mine)
    d_out = mm_tn(att, go)
    gq, gk, gv = attend_back(qkv, ga, lse, slots)
    gqkv = jnp.concatenate([gq, gk, gv], axis=1)
    gn1_part = mm_nt(gqkv, wq).astype(BF)
    gn1 = lax.psum_scatter(gn1_part, "seq", scatter_dimension=0, tiled=True)
    gn1 = swap_blocks(gn1, dps, dp).astype(F32)
    d_qkv = mm_tn(n1_all, gqkv)
    input_grad = (gr + norm_back(gn1, z1, inv1, gain1)).astype(BF)

    def row_chunks(matrix):
        size = matrix.shape[0] // dps
        return [matrix[k * size : (k + 1) * size].astype(BF) for k in range(dps)]

    g_fc = scatter_rel(row_chunks(d_fc), "dp")
    g_qkv = scatter_rel(row_chunks(d_qkv), "dp").astype(BF)
    parts = jnp.einsum("ad,nwd->naw", g_qkv, to_recv, preferred_element_type=F32).astype(BF)
    parts = lax.all_to_all(parts, "seq", 0, 0, tiled=True)
    g_qkv = jnp.einsum("naw,cnw->ac", parts, to_send, preferred_element_type=F32)

    chunks = [
        lax.dynamic_slice_in_dim(d_proj, (dp ^ k) * ff_part, ff_part, axis=0).astype(BF)
        for k in range(dps)
    ]
    g_proj = scatter_rel(chunks, "dp").astype(BF)
    g_proj = g_proj.reshape(ff_part, seqs, col).transpose(1, 0, 2)
    g_proj = lax.all_to_all(g_proj, "seq", 0, 0, tiled=True)
    g_proj = g_proj.reshape(dps, ratio, ff_part, col)
    g_proj = lax.all_to_all(g_proj, "dp", 0, 0, tiled=True)
    g_proj = g_proj.transpose(1, 0, 2, 3).reshape(w_proj.shape).astype(F32)

    d_out = d_out.reshape(seqs * slots, HD, model)
    places = [int(np.where(order == h)[0][0]) for h in range(head_count)]
    d_out = jnp.concatenate([d_out[i] for i in places], axis=0).astype(BF)
    d_out = d_out.reshape(dps, w_out.shape[0], seqs, w_out.shape[1]).transpose(0, 2, 1, 3)
    d_out = d_out.reshape(-1, w_out.shape[1])
    g_out = lax.psum_scatter(d_out, ("dp", "seq"), scatter_dimension=0, tiled=True).astype(F32)

    gqkv_sums = jnp.sum(gqkv.astype(F32), axis=0)
    vector_grads = jnp.stack(
        [
            jnp.sum(gn1 * z1, axis=0),
            jnp.sum(gn1, axis=0),
            head_spread(gqkv_sums[:mine]),
            head_spread(gqkv_sums[2 * mine :]),
            jnp.sum(go.astype(F32), axis=0),
            jnp.sum(gn2 * z2, axis=0),
            jnp.sum(gn2, axis=0),
            jnp.sum(g, axis=0),
        ]
    )
    vector_grads = vector_grads.reshape(dps, per, seqs, wide_vec).transpose(0, 2, 1, 3)
    vector_grads = vector_grads.reshape(dps * seqs, per * wide_vec)
    fc_sums = lax.dynamic_update_slice_in_dim(
        jnp.zeros((dps * seqs * b_fc.shape[0],), F32), sum_fc, sq * ff_mine, axis=0
    ).reshape(dps * seqs, -1)
    sums = jnp.concatenate([vector_grads, fc_sums], axis=1)
    sums = lax.psum_scatter(sums, ("dp", "seq"), scatter_dimension=0, tiled=True)[0]
    return (
        activations,
        input_grad,
        g_qkv,
        g_out,
        sums[: per * wide_vec].reshape(per, wide_vec),
        g_fc,
        sums[per * wide_vec :],
        g_proj,
    )


def solution(mesh):
    rows = P(("dp", "seq"), None)
    grid = P("dp", "seq")
    line = P(("dp", "seq"))
    return jax.shard_map(
        body,
        mesh=mesh,
        in_specs=(rows, grid, grid, grid, grid, line, grid, rows),
        out_specs=(rows, rows, grid, grid, grid, grid, line, grid),
        check_vma=False,
    )
```

time: 2560 us -> 857 us (0.33)
  waiting for transfers between devices: 1810 us -> 386 us
  local copies, waits for them, and re-layouts: 444 us -> 212 us
  matrix products: 168 us -> 75.3 us
  starting transfers between devices: 0.53 us -> 53.2 us
    reduce_scatter x2 -> x1, waiting for transfers between devices: 843 us -> 32.5 us  [body(): lax.psum_scatter(d_out, ('dp', 'seq'), scatter_dimension=0, tiled=True)]
    unnamed x18 -> x13, waiting for transfers between devices: 708 us -> 93.5 us
    all_gather x6 -> x4, waiting for transfers between devices: 261 us -> 42.8 us  [the longest x1 42.8 us: body(): wo = lax.all_gather(w_out, ('dp', 'seq'), axis=0, tiled=True)]
    dot_general x6 -> x0, local copies, waits for them, and re-layouts: 161 us -> none  [the longest x3 85.3 us: apply_left(): jnp.einsum('tnb,pnab->tpa', split_rows, blocks, preferred_element_type=jn...]
    ppermute x0 -> x23, waiting for transfers between devices: none -> 154 us  [the longest x9 101 us: scatter_rel(): lax.ppermute(chunks[k], axis, xor_perm(count, k)).astype(F32)]
    dot_general x47 -> x16, matrix products: 168 us -> 75.3 us  [the longest x4 26.9 us: mm(): return jnp.dot(a, b, preferred_element_type=F32)]
    all_to_all x0 -> x5, waiting for transfers between devices: none -> 62.7 us  [the longest x2 42.1 us: body(): parts = lax.all_to_all(parts, 'seq', 0, 0, tiled=True)]
    all_to_all x0 -> x3, blocking collectives: none -> 60.8 us  [the longest x1 27.1 us: body(): g_proj = lax.all_to_all(g_proj, 'seq', 0, 0, tiled=True)]
  transfers between devices with their start and end apart: 13 -> 37, of which waited for: 10 -> 22; matrix products, arithmetic and copies ran while one was open for 17% -> 29% of each run, Pallas kernels for 0% -> 1%
where the time goes in v1:
time: 857 us; the launch traced here: 845 us
  waiting for transfers between devices  386 us (45%)
  local copies, waits for them, and re-layouts  212 us (25%)
  matrix products  75.3 us (9%)
  blocking collectives  60.8 us (7%)
  starting transfers between devices  53.2 us (6%)
  other arithmetic  23.9 us (3%)
  Pallas kernels  19.1 us (2%)
  between operations  14.9 us (2%)
    ppermute x9, waiting for transfers between devices, scatter_rel(): lax.ppermute(chunks[k], axis, xor_perm(count, k)).astype(F32)  101 us
    unnamed x13, waiting for transfers between devices  93.5 us
    unnamed x143, local copies, waits for them, and re-layouts  87.9 us
    ppermute x9, waiting for transfers between devices, gather_rel(): lax.ppermute(block, axis, xor_perm(count, k))  45.8 us
    all_gather x1, waiting for transfers between devices, body(): wo = lax.all_gather(w_out, ('dp', 'seq'), axis=0, tiled=True)  42.8 us
    all_to_all x2, waiting for transfers between devices, body(): parts = lax.all_to_all(parts, 'seq', 0, 0, tiled=True)  42.1 us
    reduce_scatter x1, waiting for transfers between devices, body(): lax.psum_scatter(d_out, ('dp', 'seq'), scatter_dimension=0, tiled=True)  32.5 us
    all_to_all x1, blocking collectives, body(): g_proj = lax.all_to_all(g_proj, 'seq', 0, 0, tiled=True)  27.1 us
  transfers between devices with their start and end apart: 37, of which 22 were waited for; matrix products, arithmetic and copies ran while one was open for 29% of the time, Pallas kernels for 1%

profile of v1, /device:TPU:0, one launch (start us, length us, event | category | flops | bytes accessed | tf_op | source)
XLA Modules:
  0.0 844.7 jit_solution(741806774635828638)
XLA Ops:
  40.0 42.1 %all-to-all-done = bf16[8,400,128]{2,1,0:T(8,128)(2,1)S(1)} async-done(((bf16[8,400,128]{2,1,0:T(8,128)(2,1)}), bf16[8,400,128]{2,1,0:T(8,128)(2,1)S(1)}, u32[]{:S(2)}, u32[]{:S(2)}) %all-to-all-start) | async-done | bytes 819232 | tf_op jit(solution)/shard_map/all_to_all | solution.py:274
  87.8 12.1 %collective-permute-done.5 = bf16[400,768]{1,0:T(8,128)(2,1)S(1)} collective-permute-done((bf16[400,768]{1,0:T(8,128)(2,1)S(1)}, bf16[400,768]{1,0:T(8,128)(2,1)S(1)}, u32[]{:S(2)}, u32[]{:S(2)}) %collective-permute-start.5) | collective-permute-done | bytes 614432 | tf_op jit(solution)/shard_map/ppermute | solution.py:65
  100.0 14.4 %collective-permute-done.7 = bf16[400,768]{1,0:T(8,128)(2,1)S(1)} collective-permute-done((bf16[400,768]{1,0:T(8,128)(2,1)S(1)}, bf16[400,768]{1,0:T(8,128)(2,1)S(1)}, u32[]{:S(2)}, u32[]{:S(2)}) %collective-permute-start.7) | collective-permute-done | bytes 614432 | tf_op jit(solution)/shard_map/ppermute | solution.py:65
  120.4 7.0 shard_map.170
  132.4 42.8 %all-gather.7.cloned.1.call-done = bf16[12800,200]{1,0:T(8,128)(2,1)} async-done(((bf16[400,200]{1,0:T(8,128)(2,1)}), bf16[12800,200]{1,0:T(8,128)(2,1)}) %all-gather.7.cloned.1.call-update) | async-done | bytes 5120016 | tf_op jit(solution)/shard_map/all_gather | solution.py:288
  175.2 8.2 copy.144
  183.4 11.8 %reshape.834 = bf16[25,64,1600]{2,1,0:T(8,128)(2,1)} reshape(bf16[4,400,8,200]{3,2,1,0:T(8,128)(2,1)} %bitcast.224) | data formatting | bytes 10240000 | tf_op jit(solution)/shard_map/reshape | solution.py:290
  255.6 15.8 %all_to_all.40 = bf16[4,2,200,200]{2,1,3,0:T(2,128)(2,1)} all-to-all(bf16[4,2,200,200]{2,1,3,0:T(2,128)(2,1)S(1)} %copy.108), channel_id=1, replica_groups=mesh['dp'=4,'seq'=8] {'dp'}, dimensions={0} | all-to-all | bytes 1280000 | tf_op jit(solution)/shard_map/all_to_all | solution.py:280
  283.0 20.6 %all-to-all-done.3 = bf16[8,200,200]{2,1,0:T(8,128)(2,1)} async-done(((bf16[8,200,200]{2,1,0:T(8,128)(2,1)}), bf16[8,200,200]{2,1,0:T(8,128)(2,1)}, u32[]{:S(2)}, u32[]{:S(2)}) %all-to-all-start.3) | async-done | bytes 640032 | tf_op jit(solution)/shard_map/all_to_all | solution.py:281
  328.3 14.1 %collective-permute-done.12 = bf16[200,1600]{1,0:T(8,128)(2,1)} collective-permute-done((bf16[200,1600]{1,0:T(8,128)(2,1)}, bf16[200,1600]{1,0:T(8,128)(2,1)}, u32[]{:S(2)}, u32[]{:S(2)}) %collective-permute-start.12) | collective-permute-done | bytes 640032 | tf_op jit(solution)/shard_map/ppermute | solution.py:65
  346.1 7.7 fusion.96
  353.8 8.8 %convert_reduce_fusion = (f32[800]{0:T(1024)}, bf16[1024,800]{0,1:T(8,128)(2,1)S(1)}) fusion(f32[1024,800]{0,1:T(8,128)} %fusion.96, f32[800]{0:T(1024)S(1)} %dynamic_slice.97, bf16[1024,1600]{0,1:T(8,128)(2,1)} %all-gather.11.cloned.1.call-done, bf16[200,1600]{1,0:T(8,128)(2,1)} %get-tuple-element.118, bf16[200,1600]{1,0:T(8,128)(2,1)} %get-tuple-element.119, ...), kind=kOutput, calls=%fused_computation.18 | convolution fusion | flops 2649701632 | bytes 10758400 | tf_op jit(solution)/shard_map/dot_general | solution.py:128
  368.8 5.5 copy.127
  374.7 8.7 %convolution_convert_fusion.3 = bf16[1024,1600]{0,1:T(8,128)(2,1)} fusion(bf16[200,1600]{1,0:T(8,128)(2,1)} %get-tuple-element.118, bf16[200,1600]{1,0:T(8,128)(2,1)} %get-tuple-element.119, bf16[200,1600]{1,0:T(8,128)(2,1)} %get-tuple-element.120, bf16[200,1600]{1,0:T(8,128)(2,1)} %get-tuple-element.117, f32[1024,800]{0,1:T(8,128)} %fusion.96, ...), kind=kOutput, calls=%fused_computation.6 | convolution fusion | flops 2641510400 | bytes 9116800 | tf_op jit(solution)/shard_map/dot_general | solution.py:124
  388.9 28.2 %reduce-scatter.15.cloned.1.call-done = bf16[128,1600]{1,0:T(8,128)(2,1)} async-done(((bf16[1024,1600]{1,0:T(8,128)(2,1)}), bf16[128,1600]{1,0:T(8,128)(2,1)}) %reduce-scatter.15.cloned.1.call-update) | async-done | bytes 409616
  428.0 32.6 %reduce-scatter.13.cloned.1.call-done = bf16[128,1600]{1,0:T(8,128)(2,1)} async-done(((bf16[1024,1600]{1,0:T(8,128)(2,1)}), bf16[128,1600]{1,0:T(8,128)(2,1)}) %reduce-scatter.13.cloned.1.call-update) | async-done | bytes 409616
  465.9 5.6 convolution_convert_fusion.6
  471.5 17.9 %all_to_all.41 = bf16[8,128,256]{2,1,0:T(8,128)(2,1)S(1)} all-to-all(bf16[8,128,256]{2,1,0:T(8,128)(2,1)S(1)} %bitcast.234), channel_id=1, replica_groups=mesh['dp'=4,'seq'=8] {'seq'}, dimensions={0} | all-to-all | bytes 1048576 | tf_op jit(solution)/shard_map/all_to_all | solution.py:325
  489.5 12.0 %shard_map.171 = (bf16[1024,256]{1,0:T(8,128)(2,1)S(1)}, bf16[1024,256]{1,0:T(8,128)(2,1)S(1)}, bf16[1024,256]{1,0:T(8,128)(2,1)S(1)}) custom-call(bf16[1024,768]{1,0:T(8,128)(2,1)S(1)} %add_convert_fusion.q_ref.k_ref.v_ref, bf16[1024,768]{1,0:T(8,128)(2,1)S(1)} %add_convert_fusion.q_ref.k_ref.v_ref, ...), custom_call_target="tpu_custom_call" | custom-call | tf_op jit(solution)/shard_map/pallas_call | solution.py:223
  522.1 31.3 %reduce-scatter.17.cloned.1.call-done = bf16[128,1600]{1,0:T(8,128)(2,1)} async-done(((bf16[1024,1600]{1,0:T(8,128)(2,1)}), bf16[128,1600]{1,0:T(8,128)(2,1)}) %reduce-scatter.17.cloned.1.call-update) | async-done | bytes 409616
  560.4 12.2 %concatenate.320 = bf16[1600,1600]{0,1:T(8,128)(2,1)} concatenate(bf16[64,1600]{0,1:T(8,128)(2,1)S(1)} %get-tuple-element.110, bf16[64,1600]{0,1:T(8,128)(2,1)S(1)} %get-tuple-element.109, bf16[64,1600]{0,1:T(8,128)(2,1)S(1)} %get-tuple-element.108, bf16[64,1600]{0,1:T(8,128)(2,1)S(1)} %get-tuple-element.107, bf16[64,1600]{0,1:T(8,128)(2,1)S(1)} %get-tuple-element.106, ...), dimensions={0} | concatenate | bytes 10240000 | tf_op jit(solution)/shard_map/concatenate | solution.py:359
  572.6 19.0 %convert_element_type.198 = bf16[4,400,8,200]{1,0,3,2:T(4,128)(2,1)} reshape(bf16[1600,1600]{0,1:T(8,128)(2,1)} %concatenate.320) | data formatting | bytes 10240000 | tf_op jit(solution)/shard_map/convert_element_type | solution.py:359
  591.6 13.1 %copy.113 = bf16[4,8,400,200]{3,2,1,0:T(8,128)(2,1)} copy(bf16[4,8,400,200]{2,0,3,1:T(4,128)(2,1)} %bitcast.225) | data formatting | bytes 10240000 | tf_op jit(solution)/shard_map/transpose | solution.py:360
  606.7 5.9 fusion.89
  618.6 14.7 %collective-permute-done.20 = bf16[200,1600]{1,0:T(8,128)(2,1)S(1)} collective-permute-done((bf16[200,1600]{1,0:T(8,128)(2,1)}, bf16[200,1600]{1,0:T(8,128)(2,1)S(1)}, u32[]{:S(2)}, u32[]{:S(2)}) %collective-permute-start.20) | collective-permute-done | bytes 640032 | tf_op jit(solution)/shard_map/ppermute | solution.py:72
  633.3 11.2 %collective-permute-done.21 = bf16[200,1600]{1,0:T(8,128)(2,1)S(1)} collective-permute-done((bf16[200,1600]{1,0:T(8,128)(2,1)S(1)}, bf16[200,1600]{1,0:T(8,128)(2,1)S(1)}, u32[]{:S(2)}, u32[]{:S(2)}) %collective-permute-start.21) | collective-permute-done | bytes 640032 | tf_op jit(solution)/shard_map/ppermute | solution.py:72
  648.1 27.1 %all_to_all.42 = bf16[8,200,200]{2,1,0:T(8,128)(2,1)S(1)} all-to-all(bf16[8,200,200]{2,1,0:T(8,128)(2,1)S(1)} %bitcast.230), channel_id=1, replica_groups=mesh['dp'=4,'seq'=8] {'seq'}, dimensions={0} | all-to-all | bytes 1280000 | tf_op jit(solution)/shard_map/all_to_all | solution.py:352
  692.9 18.1 %collective-permute-done.14 = bf16[400,768]{1,0:T(8,128)(2,1)S(1)} collective-permute-done((bf16[400,768]{1,0:T(8,128)(2,1)S(1)}, bf16[400,768]{1,0:T(8,128)(2,1)S(1)}, u32[]{:S(2)}, u32[]{:S(2)}) %collective-permute-start.14) | collective-permute-done | bytes 614432 | tf_op jit(solution)/shard_map/ppermute | solution.py:72
  711.0 17.5 %collective-permute-done.16 = bf16[400,768]{1,0:T(8,128)(2,1)S(1)} collective-permute-done((bf16[400,768]{1,0:T(8,128)(2,1)S(1)}, bf16[400,768]{1,0:T(8,128)(2,1)S(1)}, u32[]{:S(2)}, u32[]{:S(2)}) %collective-permute-start.16) | collective-permute-done | bytes 614432 | tf_op jit(solution)/shard_map/ppermute | solution.py:72
  747.3 16.0 %collective-permute-done.17 = bf16[400,800]{1,0:T(8,128)(2,1)S(1)} collective-permute-done((bf16[400,800]{1,0:T(8,128)(2,1)S(1)}, bf16[400,800]{1,0:T(8,128)(2,1)S(1)}, u32[]{:S(2)}, u32[]{:S(2)}) %collective-permute-start.17) | collective-permute-done | bytes 640032 | tf_op jit(solution)/shard_map/ppermute | solution.py:72
  763.6 23.0 %collective-permute-done.18 = bf16[400,800]{1,0:T(8,128)(2,1)} collective-permute-done((bf16[400,800]{1,0:T(8,128)(2,1)}, bf16[400,800]{1,0:T(8,128)(2,1)}, u32[]{:S(2)}, u32[]{:S(2)}) %collective-permute-start.18) | collective-permute-done | bytes 640032 | tf_op jit(solution)/shard_map/ppermute | solution.py:72
  803.9 32.5 %reduce-scatter.11.cloned.1.call-done = bf16[400,200]{1,0:T(8,128)(2,1)} async-done(((bf16[12800,200]{1,0:T(8,128)(2,1)}), bf16[400,200]{1,0:T(8,128)(2,1)}) %reduce-scatter.11.cloned.1.call-update) | async-done | bytes 160016 | tf_op jit(solution)/shard_map/reduce_scatter | solution.py:362
  (335 shorter events, 272.6 us)
Async XLA Ops:
  7.2 108.0 %all-gather.5.cloned.1.call-start = ((), (), s32[]{:S(2)}) async-start(), calls=%async_computation.12 | async-start | bytes 3686400 | tf_op jit(solution)/shard_map/all_gather | solution.py:297
  31.1 144.1 %all-gather.7.cloned.1.call-start = ((), (), s32[]{:S(2)}) async-start(), calls=%async_computation.13 | async-start | bytes 6758400 | tf_op jit(solution)/shard_map/all_gather | solution.py:288
  34.4 47.8 %all-to-all-start = ((bf16[8,400,128]{2,1,0:T(8,128)(2,1)}), bf16[8,400,128]{2,1,0:T(8,128)(2,1)S(1)}, u32[]{:S(2)}, u32[]{:S(2)}) async-start(bf16[8,400,128]{2,1,0:T(8,128)(2,1)} %fusion.21), calls=%async_computation | async-start | bytes 1638400 | tf_op jit(solution)/shard_map/all_to_all | solution.py:274
  83.1 16.8 %collective-permute-start.5 = (bf16[400,768]{1,0:T(8,128)(2,1)S(1)}, bf16[400,768]{1,0:T(8,128)(2,1)S(1)}, u32[]{:S(2)}, u32[]{:S(2)}) collective-permute-start(bf16[400,768]{1,0:T(8,128)(2,1)S(1)} %fusion.20), channel_id=1, source_target_pairs={{0,8},{8,0},{16,24},{24,16},{1,9},{9,1},{17,25},{25,17},{2,10},{10... | collective-permute-start | bytes 1843208 | tf_op jit(solution)/shard_map/ppermute | solution.py:65
  84.4 15.5 %collective-permute-start.6 = (bf16[400,768]{1,0:T(8,128)(2,1)S(1)}, bf16[400,768]{1,0:T(8,128)(2,1)S(1)}, u32[]{:S(2)}, u32[]{:S(2)}) collective-permute-start(bf16[400,768]{1,0:T(8,128)(2,1)S(1)} %fusion.20), channel_id=1, source_target_pairs={{0,16},{8,24},{16,0},{24,8},{1,17},{9,25},{17,1},{25,9},{2,18},{10... | collective-permute-start | bytes 1843208 | tf_op jit(solution)/shard_map/ppermute | solution.py:65
  85.9 28.4 %collective-permute-start.7 = (bf16[400,768]{1,0:T(8,128)(2,1)S(1)}, bf16[400,768]{1,0:T(8,128)(2,1)S(1)}, u32[]{:S(2)}, u32[]{:S(2)}) collective-permute-start(bf16[400,768]{1,0:T(8,128)(2,1)S(1)} %fusion.20), channel_id=1, source_target_pairs={{0,24},{8,16},{16,8},{24,0},{1,25},{9,17},{17,9},{25,1},{2,26},{10... | collective-permute-start | bytes 1843208 | tf_op jit(solution)/shard_map/ppermute | solution.py:65
  128.5 112.5 %all-to-all-start.1 = ((bf16[8,128,256]{1,2,0:T(8,128)(2,1)}), bf16[8,128,256]{1,2,0:T(8,128)(2,1)S(1)}, u32[]{:S(2)}, u32[]{:S(2)}) async-start(bf16[8,128,256]{1,2,0:T(8,128)(2,1)} %copy.105), calls=%async_computation.1 | async-start | bytes 1048576 | tf_op jit(solution)/shard_map/all_to_all | solution.py:301
  132.2 213.9 %all-gather.9.cloned.1.call-start = ((), (), s32[]{:S(2)}) async-start(), calls=%async_computation.14 | async-start | bytes 3686400 | tf_op jit(solution)/shard_map/all_gather | solution.py:306
  248.8 105.1 %all-gather.11.cloned.1.call-start = ((), (), s32[]{:S(2)}) async-start(), calls=%async_computation.15 | async-start | bytes 3686400 | tf_op jit(solution)/shard_map/all_gather | solution.py:298
  275.0 28.6 %all-to-all-start.3 = ((bf16[8,200,200]{2,1,0:T(8,128)(2,1)}), bf16[8,200,200]{2,1,0:T(8,128)(2,1)}, u32[]{:S(2)}, u32[]{:S(2)}) async-start(bf16[8,200,200]{2,1,0:T(8,128)(2,1)} %bitcast.229), calls=%async_computation.3 | async-start | bytes 1638400 | tf_op jit(solution)/shard_map/all_to_all | solution.py:281
  279.2 138.0 %reduce-scatter.15.cloned.1.call-start = ((), (), s32[]{:S(2)}) async-start(), calls=%async_computation.18 | async-start | bytes 3833856
  279.5 32.0 %collective-permute-start.8 = (bf16[400,800]{1,0:T(8,128)(2,1)}, bf16[400,800]{1,0:T(8,128)(2,1)}, u32[]{:S(2)}, u32[]{:S(2)}) collective-permute-start(bf16[400,800]{1,0:T(8,128)(2,1)} %param.15), channel_id=1, source_target_pairs={{0,8},{8,0},{16,24},{24,16},{1,9},{9,1},{17,25},{25,17},{2,10},{10... | collective-permute-start | bytes 1920008 | tf_op jit(solution)/shard_map/ppermute | solution.py:65
  280.2 36.2 %collective-permute-start.9 = (bf16[400,800]{1,0:T(8,128)(2,1)}, bf16[400,800]{1,0:T(8,128)(2,1)}, u32[]{:S(2)}, u32[]{:S(2)}) collective-permute-start(bf16[400,800]{1,0:T(8,128)(2,1)} %param.15), channel_id=1, source_target_pairs={{0,16},{8,24},{16,0},{24,8},{1,17},{9,25},{17,1},{25,9},{2,18},{10... | collective-permute-start | bytes 1920008 | tf_op jit(solution)/shard_map/ppermute | solution.py:65
  280.7 37.7 %collective-permute-start.10 = (bf16[400,800]{1,0:T(8,128)(2,1)}, bf16[400,800]{1,0:T(8,128)(2,1)}, u32[]{:S(2)}, u32[]{:S(2)}) collective-permute-start(bf16[400,800]{1,0:T(8,128)(2,1)} %param.15), channel_id=1, source_target_pairs={{0,24},{8,16},{16,8},{24,0},{1,25},{9,17},{17,9},{25,1},{2,26},{10... | collective-permute-start | bytes 1920008 | tf_op jit(solution)/shard_map/ppermute | solution.py:65
  308.4 19.9 %collective-permute-start.11 = (bf16[200,1600]{1,0:T(8,128)(2,1)}, bf16[200,1600]{1,0:T(8,128)(2,1)}, u32[]{:S(2)}, u32[]{:S(2)}) collective-permute-start(bf16[200,1600]{1,0:T(8,128)(2,1)} %reshape.838), channel_id=1, source_target_pairs={{0,8},{8,0},{16,24},{24,16},{1,9},{9,1},{17,25},{25,17},{2,10},{10... | collective-permute-start | bytes 1920008 | tf_op jit(solution)/shard_map/ppermute | solution.py:65
  310.0 32.4 %collective-permute-start.12 = (bf16[200,1600]{1,0:T(8,128)(2,1)}, bf16[200,1600]{1,0:T(8,128)(2,1)}, u32[]{:S(2)}, u32[]{:S(2)}) collective-permute-start(bf16[200,1600]{1,0:T(8,128)(2,1)} %reshape.838), channel_id=1, source_target_pairs={{0,16},{8,24},{16,0},{24,8},{1,17},{9,25},{17,1},{25,9},{2,18},{10... | collective-permute-start | bytes 1920008 | tf_op jit(solution)/shard_map/ppermute | solution.py:65
  311.5 30.9 %collective-permute-start.13 = (bf16[200,1600]{1,0:T(8,128)(2,1)}, bf16[200,1600]{1,0:T(8,128)(2,1)}, u32[]{:S(2)}, u32[]{:S(2)}) collective-permute-start(bf16[200,1600]{1,0:T(8,128)(2,1)} %reshape.838), channel_id=1, source_target_pairs={{0,24},{8,16},{16,8},{24,0},{1,25},{9,17},{17,9},{25,1},{2,26},{10... | collective-permute-start | bytes 1920008 | tf_op jit(solution)/shard_map/ppermute | solution.py:65
  374.3 86.3 %reduce-scatter.13.cloned.1.call-start = ((), (), s32[]{:S(2)}) async-start(), calls=%async_computation.17 | async-start | bytes 3833856
  388.9 164.6 %reduce-scatter.17.cloned.1.call-start = ((), (), s32[]{:S(2)}) async-start(), calls=%async_computation.19 | async-start | bytes 3833856
  511.9 289.2 %all-reduce.3.cloned.1.call-start = ((), (), s32[]{:S(2)}) async-start(), calls=%async_computation.20 | async-start | bytes 163840
  558.3 278.1 %reduce-scatter.11.cloned.1.call-start = ((), (), s32[]{:S(2)}) async-start(), calls=%async_computation.16 | async-start | bytes 6758400 | tf_op jit(solution)/shard_map/reduce_scatter | solution.py:362
  615.1 18.2 %collective-permute-start.20 = (bf16[200,1600]{1,0:T(8,128)(2,1)}, bf16[200,1600]{1,0:T(8,128)(2,1)S(1)}, u32[]{:S(2)}, u32[]{:S(2)}) collective-permute-start(bf16[200,1600]{1,0:T(8,128)(2,1)} %get-tuple-element.111), channel_id=1, source_target_pairs={{0,8},{8,0},{16,24},{24,16},{1,9},{9,1},{17,25},{25,17},{2,10},{10... | collective-permute-start | bytes 1920008 | tf_op jit(solution)/shard_map/ppermute | solution.py:72
  616.6 27.9 %collective-permute-start.21 = (bf16[200,1600]{1,0:T(8,128)(2,1)S(1)}, bf16[200,1600]{1,0:T(8,128)(2,1)S(1)}, u32[]{:S(2)}, u32[]{:S(2)}) collective-permute-start(bf16[200,1600]{1,0:T(8,128)(2,1)S(1)} %get-tuple-element.113), channel_id=1, source_target_pairs={{0,16},{8,24},{16,0},{24,8},{1,17},{9,25},{17,1},{25,9},{2,18},{10... | collective-permute-start | bytes 1920008 | tf_op jit(solution)/shard_map/ppermute | solution.py:72
  618.1 27.2 %collective-permute-start.22 = (bf16[200,1600]{1,0:T(8,128)(2,1)S(1)}, bf16[200,1600]{1,0:T(8,128)(2,1)S(1)}, u32[]{:S(2)}, u32[]{:S(2)}) collective-permute-start(bf16[200,1600]{1,0:T(8,128)(2,1)S(1)} %get-tuple-element.112), channel_id=1, source_target_pairs={{0,24},{8,16},{16,8},{24,0},{1,25},{9,17},{17,9},{25,1},{2,26},{10... | collective-permute-start | bytes 1920008 | tf_op jit(solution)/shard_map/ppermute | solution.py:72
  677.1 53.5 %all-to-all-start.7 = ((bf16[4,2,200,200]{2,1,3,0:T(2,128)(2,1)}), bf16[4,2,200,200]{2,1,3,0:T(2,128)(2,1)S(1)}, u32[]{:S(2)}, u32[]{:S(2)}) async-start(bf16[4,2,200,200]{2,1,3,0:T(2,128)(2,1)} %copy.122), calls=%async_computation.8 | async-start | bytes 1638400 | tf_op jit(solution)/shard_map/all_to_all | solution.py:354
  685.8 25.1 %collective-permute-start.14 = (bf16[400,768]{1,0:T(8,128)(2,1)S(1)}, bf16[400,768]{1,0:T(8,128)(2,1)S(1)}, u32[]{:S(2)}, u32[]{:S(2)}) collective-permute-start(bf16[400,768]{1,0:T(8,128)(2,1)S(1)} %get-tuple-element.121), channel_id=1, source_target_pairs={{0,8},{8,0},{16,24},{24,16},{1,9},{9,1},{17,25},{25,17},{2,10},{10... | collective-permute-start | bytes 1843208 | tf_op jit(solution)/shard_map/ppermute | solution.py:72
  687.9 23.1 %collective-permute-start.15 = (bf16[400,768]{1,0:T(8,128)(2,1)S(1)}, bf16[400,768]{1,0:T(8,128)(2,1)S(1)}, u32[]{:S(2)}, u32[]{:S(2)}) collective-permute-start(bf16[400,768]{1,0:T(8,128)(2,1)S(1)} %get-tuple-element.123), channel_id=1, source_target_pairs={{0,16},{8,24},{16,0},{24,8},{1,17},{9,25},{17,1},{25,9},{2,18},{10... | collective-permute-start | bytes 1843208 | tf_op jit(solution)/shard_map/ppermute | solution.py:72
  689.4 39.1 %collective-permute-start.16 = (bf16[400,768]{1,0:T(8,128)(2,1)S(1)}, bf16[400,768]{1,0:T(8,128)(2,1)S(1)}, u32[]{:S(2)}, u32[]{:S(2)}) collective-permute-start(bf16[400,768]{1,0:T(8,128)(2,1)S(1)} %get-tuple-element.122), channel_id=1, source_target_pairs={{0,24},{8,16},{16,8},{24,0},{1,25},{9,17},{17,9},{25,1},{2,26},{10... | collective-permute-start | bytes 1843208 | tf_op jit(solution)/shard_map/ppermute | solution.py:72
  731.5 66.7 %all-to-all-start.5 = ((bf16[8,400,128]{2,1,0:T(8,128)(2,1)}), bf16[8,400,128]{2,1,0:T(8,128)(2,1)}, u32[]{:S(2)}, u32[]{:S(2)}) async-start(bf16[8,400,128]{2,1,0:T(8,128)(2,1)} %fusion.22), calls=%async_computation.5 | async-start | bytes 1638400 | tf_op jit(solution)/shard_map/all_to_all | solution.py:343
  740.2 23.0 %collective-permute-start.17 = (bf16[400,800]{1,0:T(8,128)(2,1)S(1)}, bf16[400,800]{1,0:T(8,128)(2,1)S(1)}, u32[]{:S(2)}, u32[]{:S(2)}) collective-permute-start(bf16[400,800]{1,0:T(8,128)(2,1)S(1)} %copy.115), channel_id=1, source_target_pairs={{0,8},{8,0},{16,24},{24,16},{1,9},{9,1},{17,25},{25,17},{2,10},{10... | collective-permute-start | bytes 1920008 | tf_op jit(solution)/shard_map/ppermute | solution.py:72
  743.5 43.1 %collective-permute-start.18 = (bf16[400,800]{1,0:T(8,128)(2,1)}, bf16[400,800]{1,0:T(8,128)(2,1)}, u32[]{:S(2)}, u32[]{:S(2)}) collective-permute-start(bf16[400,800]{1,0:T(8,128)(2,1)} %copy.117), channel_id=1, source_target_pairs={{0,16},{8,24},{16,0},{24,8},{1,17},{9,25},{17,1},{25,9},{2,18},{10... | collective-permute-start | bytes 1920008 | tf_op jit(solution)/shard_map/ppermute | solution.py:72
  744.9 43.0 %collective-permute-start.19 = (bf16[400,800]{1,0:T(8,128)(2,1)}, bf16[400,800]{1,0:T(8,128)(2,1)}, u32[]{:S(2)}, u32[]{:S(2)}) collective-permute-start(bf16[400,800]{1,0:T(8,128)(2,1)} %copy.119), channel_id=1, source_target_pairs={{0,24},{8,16},{16,8},{24,0},{1,25},{9,17},{17,9},{25,1},{2,26},{10... | collective-permute-start | bytes 1920008 | tf_op jit(solution)/shard_map/ppermute | solution.py:72
  (52 other events, 886.9 us)
Sparse Core Ops, SparseCore 0:
  31.2 57.8 all-gather.4
  92.0 83.1 all-gather.6
  248.9 46.2 all-gather.8
  296.6 39.9 all-gather.10
  374.4 42.7 reduce-scatter.14
  419.3 41.2 reduce-scatter.12
  512.0 41.3 reduce-scatter.16
  559.0 120.4 all-reduce.2
  681.8 154.4 reduce-scatter.10

commit v2 on v1

--- a/solution.py
+++ b/solution.py
@@ -231,6 +231,203 @@
     )(qkv, qkv, qkv, grad, lse)
 
 
+ANY = pl.BlockSpec(memory_space=pl.ANY)
+WHOLE = pl.BlockSpec(memory_space=pltpu.VMEM)
+SCALAR = pl.BlockSpec(memory_space=pltpu.SMEM)
+ROOM = pltpu.CompilerParams(vmem_limit_bytes=48 * 1024 * 1024)
+
+
+def out_blocks(w_out):
+    seqs = lax.axis_size("seq")
+    line = [w_out] + [
+        lax.ppermute(w_out, "seq", xor_perm(seqs, 2 * dz)) for dz in range(1, seqs // 2)
+    ]
+    near = gather_rel(jnp.stack(line), "dp")
+    return [[b, lax.ppermute(b, "seq", xor_perm(seqs, 1))] for b in near]
+
+
+def block_copies(where, blocks, store, sems, outward):
+    copies = []
+    for dk, pair in enumerate(blocks):
+        for dc, ref in enumerate(pair):
+            for dz in range(ref.shape[0]):
+                near, far = ref.at[dz], store.at[where[0] ^ dk, where[1] ^ (2 * dz + dc)]
+                src, dst = (far, near) if outward else (near, far)
+                copies.append(pltpu.make_async_copy(src, dst, sems.at[len(copies)]))
+    return copies
+
+
+def head_columns(att_ref, owner):
+    count = int(owner.max()) + 1
+    parts = []
+    for h in range(count):
+        dev, slot = [int(i[0]) for i in np.where(owner == h)]
+        parts.append(att_ref[dev, :, slot * HD : (slot + 1) * HD])
+    return jnp.concatenate(parts, axis=1)
+
+
+def out_kernel(dps, seqs, owner, where, att_ref, x_ref, vec_ref, *rest):
+    flat = rest[: 2 * dps]
+    r_ref, n2_ref, store, sems = rest[2 * dps :]
+    blocks = [flat[2 * k : 2 * k + 2] for k in range(dps)]
+    copies = block_copies(where, blocks, store, sems, False)
+    for c in copies:
+        c.start()
+    att = head_columns(att_ref, owner)
+    depth, width = store.shape[2:]
+    for c in copies:
+        c.wait()
+    for n in range(seqs):
+        here = slice(n * width, (n + 1) * width)
+        total = x_ref[:, here].astype(F32) + vec_ref[4:5, here]
+        for p in range(dps):
+            total = total + mm(att[:, p * depth : (p + 1) * depth], store[p, n])
+        r_ref[:, here] = total
+    unit, _ = normalise(r_ref[...])
+    n2 = (unit * vec_ref[5:6, :] + vec_ref[6:7, :]).astype(BF)
+    me = where[0]
+    for k in range(dps):
+        piece = n2[:, k * depth : (k + 1) * depth]
+        for i in range(1, dps):
+            piece = jnp.where(me == i, n2[:, (i ^ k) * depth : ((i ^ k) + 1) * depth], piece)
+        n2_ref[:, k * depth : (k + 1) * depth] = piece
+
+
+def out_project(where, att, x, table, blocks, owner):
+    flat = [b for pair in blocks for b in pair]
+    dps, seqs = len(blocks), att.shape[0]
+    depth, width = flat[0].shape[1:]
+    return pl.pallas_call(
+        functools.partial(out_kernel, dps, seqs, owner),
+        in_specs=[SCALAR, WHOLE, WHOLE, WHOLE] + [ANY] * len(flat),
+        out_specs=[WHOLE, WHOLE],
+        out_shape=[jax.ShapeDtypeStruct(x.shape, F32), jax.ShapeDtypeStruct(x.shape, BF)],
+        scratch_shapes=[
+            pltpu.VMEM((dps, seqs, depth, width), BF),
+            pltpu.SemaphoreType.DMA((dps * seqs,)),
+        ],
+        compiler_params=ROOM,
+    )(where, att, x, table, *flat)
+
+
+def back_kernel(dps, seqs, owner, where, gn2_ref, r_ref, g_ref, vec_ref, *rest):
+    flat = rest[: 2 * dps]
+    gr_ref, go_ref, ga_ref, sums_ref, store, sems = rest[2 * dps :]
+    blocks = [flat[2 * k : 2 * k + 2] for k in range(dps)]
+    copies = block_copies(where, blocks, store, sems, False)
+    for c in copies:
+        c.start()
+    depth, width = store.shape[2:]
+    me = where[0]
+    for k in range(dps):
+        piece = gn2_ref[:, k * depth : (k + 1) * depth]
+        for i in range(1, dps):
+            piece = jnp.where(me == i, gn2_ref[:, (i ^ k) * depth : ((i ^ k) + 1) * depth], piece)
+        gr_ref[:, k * depth : (k + 1) * depth] = piece.astype(F32)
+    gn2 = gr_ref[...]
+    unit, inverse = normalise(r_ref[...])
+    gr = g_ref[...].astype(F32) + norm_back(gn2, unit, inverse, vec_ref[5:6, :])
+    go = gr.astype(BF)
+    gr_ref[...] = gr
+    go_ref[...] = go
+    sums_ref[0:1, :] = jnp.sum(go.astype(F32), axis=0, keepdims=True)
+    sums_ref[1:2, :] = jnp.sum(gn2 * unit, axis=0, keepdims=True)
+    sums_ref[2:3, :] = jnp.sum(gn2, axis=0, keepdims=True)
+    sums_ref[3:4, :] = jnp.sum(g_ref[...].astype(F32), axis=0, keepdims=True)
+    for c in copies:
+        c.wait()
+    parts = []
+    for p in range(dps):
+        total = mm_nt(go[:, 0:width], store[p, 0])
+        for n in range(1, seqs):
+            total = total + mm_nt(go[:, n * width : (n + 1) * width], store[p, n])
+        parts.append(total)
+    ga = jnp.concatenate(parts, axis=1).astype(BF)
+    ga_ref[...] = jnp.zeros_like(ga_ref)
+    for h in range(int(owner.max()) + 1):
+        dev, slot = [int(i[0]) for i in np.where(owner == h)]
+        ga_ref[dev, :, slot * HD : (slot + 1) * HD] = ga[:, h * HD : (h + 1) * HD]
+
+
+def out_back(where, gn2, r, g, table, blocks, owner):
+    flat = [b for pair in blocks for b in pair]
+    dps, seqs = len(blocks), owner.shape[0]
+    depth, width = flat[0].shape[1:]
+    return pl.pallas_call(
+        functools.partial(back_kernel, dps, seqs, owner),
+        in_specs=[SCALAR, WHOLE, WHOLE, WHOLE, WHOLE] + [ANY] * len(flat),
+        out_specs=[WHOLE] * 4,
+        out_shape=[
+            jax.ShapeDtypeStruct(r.shape, F32),
+            jax.ShapeDtypeStruct(r.shape, BF),
+            jax.ShapeDtypeStruct((seqs, r.shape[0], owner.shape[1] * HD), BF),
+            jax.ShapeDtypeStruct((4, r.shape[1]), F32),
+        ],
+        scratch_shapes=[
+            pltpu.VMEM((dps, seqs, depth, width), BF),
+            pltpu.SemaphoreType.DMA((dps * seqs,)),
+        ],
+        compiler_params=ROOM,
+    )(where, gn2, r, g, table, *flat)
+
+
+def grad_out_kernel(dps, seqs, owner, where, att_ref, go_ref, *rest):
+    flat = rest[: 2 * dps]
+    store, sems = rest[2 * dps :]
+    blocks = [flat[2 * k : 2 * k + 2] for k in range(dps)]
+    att = head_columns(att_ref, owner)
+    depth, width = store.shape[2:]
+    for p in range(dps):
+        rows = att[:, p * depth : (p + 1) * depth]
+        for n in range(seqs):
+            store[p, n] = mm_tn(rows, go_ref[:, n * width : (n + 1) * width]).astype(BF)
+    copies = block_copies(where, blocks, store, sems, True)
+    for c in copies:
+        c.start()
+    for c in copies:
+        c.wait()
+
+
+def grad_out(where, att, go, dps, owner):
+    seqs = att.shape[0]
+    depth, width = go.shape[1] // dps, go.shape[1] // seqs
+    shape = jax.ShapeDtypeStruct((seqs // 2, depth, width), BF)
+    flat = pl.pallas_call(
+        functools.partial(grad_out_kernel, dps, seqs, owner),
+        in_specs=[SCALAR, WHOLE, WHOLE],
+        out_specs=[ANY] * (2 * dps),
+        out_shape=[shape] * (2 * dps),
+        scratch_shapes=[
+            pltpu.VMEM((dps, seqs, depth, width), BF),
+            pltpu.SemaphoreType.DMA((dps * seqs,)),
+        ],
+        compiler_params=ROOM,
+    )(where, att, go)
+    return [flat[2 * k : 2 * k + 2] for k in range(dps)]
+
+
+def sum_out_blocks(blocks):
+    seqs = lax.axis_size("seq")
+    chip = [
+        (mine.astype(F32) + lax.ppermute(other, "seq", xor_perm(seqs, 1)).astype(F32)).astype(BF)
+        for mine, other in blocks
+    ]
+    line = scatter_rel(chip, "dp").astype(BF)
+    total = line[0].astype(F32)
+    for dz in range(1, seqs // 2):
+        total = total + lax.ppermute(line[dz], "seq", xor_perm(seqs, 2 * dz)).astype(F32)
+    return total
+
+
+def sum_all(block):
+    for axis in ("dp", "seq"):
+        step = 1
+        while step < lax.axis_size(axis):
+            block = block + lax.ppermute(block, axis, xor_perm(lax.axis_size(axis), step))
+            step *= 2
+    return block
+
+
 def body(tokens, w_qkv, w_out, vectors, w_fc, b_fc, w_proj, cotangent):
     dps = lax.axis_size("dp")
     seqs = lax.axis_size("seq")
@@ -244,7 +441,6 @@
     ff_part = ff_mine // dps
     ratio = seqs // dps
     col = w_proj.shape[1]
-    order = np.concatenate([owner[d] for d in range(seqs)])
 
     per, wide_vec = vectors.shape
     small = gather_small(jnp.concatenate([vectors.reshape(-1), b_fc])[None], "dp")
@@ -273,7 +469,6 @@
     parts = jnp.einsum("ac,cnw->naw", w_qkv, to_send, preferred_element_type=F32).astype(BF)
     parts = lax.all_to_all(parts, "seq", 0, 0, tiled=True)
     own_qkv = jnp.einsum("naw,nwd->ad", parts, to_recv, preferred_element_type=F32).astype(BF)
-    wq = jnp.concatenate(gather_rel(own_qkv, "dp"), axis=0)
     wf = jnp.concatenate(gather_rel(w_fc, "dp"), axis=0)
 
     pieces = w_proj.reshape(ratio, dps, ff_part, col)
@@ -285,50 +480,44 @@
         [lax.dynamic_index_in_dim(wp_rel, dp ^ k, 0, keepdims=False) for k in range(dps)], axis=0
     )
 
-    wo = lax.all_gather(w_out, ("dp", "seq"), axis=0, tiled=True)
-    wo = wo.reshape(dps, seqs, w_out.shape[0], w_out.shape[1]).transpose(0, 2, 1, 3)
-    wo = wo.reshape(head_count, HD, model)
-    empty = jnp.zeros((HD, model), BF)
-    wo = jnp.concatenate([wo[h] if h >= 0 else empty for h in order], axis=0)
+    where = jnp.stack([dp, sq]).astype(jnp.int32)
+    wo = out_blocks(w_out)
 
     x = tokens.astype(F32)
     z1, inv1 = normalise(x)
     n1 = swap_blocks((z1 * gain1 + shift1).astype(BF), dps, dp)
+    n1, own_qkv = lax.optimization_barrier((n1, own_qkv))
     n1_all = lax.all_gather(n1, "seq", axis=0, tiled=True)
-    gm_all = lax.all_gather(cotangent, "seq", axis=0, tiled=True)
+    wq = jnp.concatenate(gather_rel(own_qkv, "dp"), axis=0)
+    cot, n1_all = lax.optimization_barrier((cotangent, n1_all))
+    gm_all = lax.all_gather(cot, "seq", axis=0, tiled=True)
     qkv = (mm(n1_all, wq) + bias_qkv).astype(BF)
     att, lse = attend(qkv, slots)
     att = lax.all_to_all(att.reshape(seqs, rows, mine), "seq", 0, 0, tiled=True)
-    att = att.transpose(1, 0, 2).reshape(rows, seqs * mine)
-    r = x + (mm(att, wo) + bias_o)
-    z2, inv2 = normalise(r)
-    n2 = swap_blocks((z2 * gain2 + shift2).astype(BF), dps, dp)
+    r, n2 = out_project(where, att, tokens, table, wo, owner)
     n2_all = lax.all_gather(n2, "seq", axis=0, tiled=True)
     u = mm(n2_all, wf) + bias_fc
     value, slope = gelu_parts(u)
     e = value.astype(BF)
-    mlp = lax.psum_scatter(mm(e, wp).astype(BF), "seq", scatter_dimension=0, tiled=True)
-    activations = (r + (mlp.astype(F32) + bias_p)).astype(BF)
-
-    g = cotangent.astype(F32)
+
     gu = (mm_nt(gm_all, wp) * slope).astype(BF)
     gn2_part = mm_nt(gu, wf).astype(BF)
     gn2 = lax.psum_scatter(gn2_part, "seq", scatter_dimension=0, tiled=True)
-    gn2 = swap_blocks(gn2, dps, dp).astype(F32)
+    e, gn2 = lax.optimization_barrier((e, gn2))
+    mlp = lax.psum_scatter(mm(e, wp).astype(BF), "seq", scatter_dimension=0, tiled=True)
+    activations = (r + (mlp.astype(F32) + bias_p)).astype(BF)
     d_proj = mm_tn(e, gm_all)
     d_fc = mm_tn(n2_all, gu)
     sum_fc = jnp.sum(gu.astype(F32), axis=0)
-    gr = g + norm_back(gn2, z2, inv2, gain2)
-    go = gr.astype(BF)
-
-    ga = mm_nt(go, wo).astype(BF)
-    ga = lax.all_to_all(ga.reshape(rows, seqs, mine).transpose(1, 0, 2), "seq", 0, 0, tiled=True)
+
+    gr, go, ga, sums_two = out_back(where, gn2, r, cotangent, table, wo, owner)
+    ga = lax.all_to_all(ga, "seq", 0, 0, tiled=True)
     ga = ga.reshape(seqs * rows, mine)
-    d_out = mm_tn(att, go)
+    d_out = grad_out(where, att, go, dps, owner)
     gq, gk, gv = attend_back(qkv, ga, lse, slots)
     gqkv = jnp.concatenate([gq, gk, gv], axis=1)
-    gn1_part = mm_nt(gqkv, wq).astype(BF)
-    gn1 = lax.psum_scatter(gn1_part, "seq", scatter_dimension=0, tiled=True)
+    gn1_full = mm_nt(gqkv, wq)
+    gn1 = lax.psum_scatter(gn1_full.astype(BF), "seq", scatter_dimension=0, tiled=True)
     gn1 = swap_blocks(gn1, dps, dp).astype(F32)
     d_qkv = mm_tn(n1_all, gqkv)
     input_grad = (gr + norm_back(gn1, z1, inv1, gain1)).astype(BF)
@@ -354,41 +543,36 @@
     g_proj = lax.all_to_all(g_proj, "dp", 0, 0, tiled=True)
     g_proj = g_proj.transpose(1, 0, 2, 3).reshape(w_proj.shape).astype(F32)
 
-    d_out = d_out.reshape(seqs * slots, HD, model)
-    places = [int(np.where(order == h)[0][0]) for h in range(head_count)]
-    d_out = jnp.concatenate([d_out[i] for i in places], axis=0).astype(BF)
-    d_out = d_out.reshape(dps, w_out.shape[0], seqs, w_out.shape[1]).transpose(0, 2, 1, 3)
-    d_out = d_out.reshape(-1, w_out.shape[1])
-    g_out = lax.psum_scatter(d_out, ("dp", "seq"), scatter_dimension=0, tiled=True).astype(F32)
+    g_out = sum_out_blocks(d_out)
 
     gqkv_sums = jnp.sum(gqkv.astype(F32), axis=0)
-    vector_grads = jnp.stack(
+    both = jnp.stack([jnp.sum(gn1_full * n1_all.astype(F32), axis=0), jnp.sum(gn1_full, axis=0)])
+    both = swap_blocks(both, dps, dp)
+    vector_grads = jnp.concatenate(
         [
-            jnp.sum(gn1 * z1, axis=0),
-            jnp.sum(gn1, axis=0),
-            head_spread(gqkv_sums[:mine]),
-            head_spread(gqkv_sums[2 * mine :]),
-            jnp.sum(go.astype(F32), axis=0),
-            jnp.sum(gn2 * z2, axis=0),
-            jnp.sum(gn2, axis=0),
-            jnp.sum(g, axis=0),
+            ((both[0] - shift1 * both[1]) / gain1)[None],
+            both[1:],
+            head_spread(gqkv_sums[:mine])[None],
+            head_spread(gqkv_sums[2 * mine :])[None],
+            sums_two,
         ]
     )
-    vector_grads = vector_grads.reshape(dps, per, seqs, wide_vec).transpose(0, 2, 1, 3)
-    vector_grads = vector_grads.reshape(dps * seqs, per * wide_vec)
     fc_sums = lax.dynamic_update_slice_in_dim(
         jnp.zeros((dps * seqs * b_fc.shape[0],), F32), sum_fc, sq * ff_mine, axis=0
-    ).reshape(dps * seqs, -1)
-    sums = jnp.concatenate([vector_grads, fc_sums], axis=1)
-    sums = lax.psum_scatter(sums, ("dp", "seq"), scatter_dimension=0, tiled=True)[0]
+    ).reshape(-1, model)
+    sums = sum_all(jnp.concatenate([vector_grads, fc_sums]))
+    own_vec = lax.dynamic_slice(sums, (dp * per, sq * wide_vec), (per, wide_vec))
+    own_fc = lax.dynamic_slice_in_dim(
+        sums[8:].reshape(-1), (dp * seqs + sq) * b_fc.shape[0], b_fc.shape[0]
+    )
     return (
         activations,
         input_grad,
         g_qkv,
         g_out,
-        sums[: per * wide_vec].reshape(per, wide_vec),
+        own_vec,
         g_fc,
-        sums[per * wide_vec :],
+        own_fc,
         g_proj,
     )
 

time: 857 us -> 627 us (0.73)
  waiting for transfers between devices: 386 us -> 216 us
  local copies, waits for them, and re-layouts: 212 us -> 137 us
  blocking collectives: 60.8 us -> 15.2 us
  starting transfers between devices: 53.2 us -> 88.4 us
  Pallas kernels: 19.1 us -> 48.6 us
    unnamed x13 -> x6, waiting for transfers between devices: 93.5 us -> 0.76 us
    ppermute x9 -> x12, waiting for transfers between devices: 101 us -> 29.6 us  [scatter_rel(): lax.ppermute(chunks[k], axis, xor_perm(count, k)).astype(F32)]
    ppermute x0 -> x19, waiting for transfers between devices: none -> 58.6 us  [the longest x3 31.4 us: out_blocks(): lax.ppermute(w_out, 'seq', xor_perm(seqs, 2 * dz))]
    unnamed x143 -> x127, local copies, waits for them, and re-layouts: 87.9 us -> 41.9 us
    all_to_all x2 -> x0, blocking collectives: 45 us -> none  [the longest x1 27.1 us: body(): g_proj = lax.all_to_all(g_proj, 'seq', 0, 0, tiled=True)]
    all_gather x2 -> x1, waiting for transfers between devices: 42.8 us -> 0.01 us  [body(): gm_all = lax.all_gather(cot, 'seq', axis=0, tiled=True)]
    all_to_all x2, waiting for transfers between devices: 42.1 us -> 0.01 us  [body(): parts = lax.all_to_all(parts, 'seq', 0, 0, tiled=True)]
    pallas_call x0 -> x3, Pallas kernels: none -> 29.6 us  [the longest x1 10.4 us: grad_out(): pl.pallas_call(functools.partial(grad_out_kernel, dps, seqs, owner), in_s...]
  transfers between devices with their start and end apart: 37 -> 61, of which waited for: 22 -> 25; matrix products, arithmetic and copies ran while one was open for 29% -> 26% of each run, Pallas kernels for 1% -> 6%
where the time goes in v2:
time: 627 us; the launch traced here: 618 us
  waiting for transfers between devices  216 us (34%)
  local copies, waits for them, and re-layouts  137 us (22%)
  starting transfers between devices  88.4 us (14%)
  matrix products  68.9 us (11%)
  Pallas kernels  48.6 us (8%)
  other arithmetic  28.1 us (4%)
  between operations  15.3 us (2%)
  blocking collectives  15.2 us (2%)
    reduce_scatter x1, waiting for transfers between devices, body(): gn2 = lax.psum_scatter(gn2_part, 'seq', scatter_dimension=0, tiled=True)  42.8 us
    unnamed x127, local copies, waits for them, and re-layouts  41.9 us
    ppermute x3, waiting for transfers between devices, out_blocks(): lax.ppermute(w_out, 'seq', xor_perm(seqs, 2 * dz))  31.4 us
    ppermute x12, waiting for transfers between devices, scatter_rel(): lax.ppermute(chunks[k], axis, xor_perm(count, k)).astype(F32)  29.6 us
    ppermute x3, waiting for transfers between devices, sum_out_blocks(): lax.ppermute(line[dz], 'seq', xor_perm(seqs, 2 * dz)).astype(F32)  24.8 us
    ppermute x12, waiting for transfers between devices, gather_rel(): lax.ppermute(block, axis, xor_perm(count, k))  23.1 us
    dot_general x3, matrix products, mm(): return jnp.dot(a, b, preferred_element_type=F32)  22.5 us
    all_to_all x1, waiting for transfers between devices, body(): lax.all_to_all(pieces.reshape(seqs, ff_part, col), 'seq', 0, 0, tiled=True)  21.1 us
  transfers between devices with their start and end apart: 61, of which 25 were waited for; matrix products, arithmetic and copies ran while one was open for 26% of the time, Pallas kernels for 6%

profile of v2, /device:TPU:0, one launch (start us, length us, event | category | flops | bytes accessed | tf_op | source)
XLA Modules:
  0.0 617.6 jit_solution(8087431265767410425)
XLA Ops:
  27.6 6.0 collective-permute-done.3
  55.2 5.3 collective-permute-done.10
  60.4 22.6 %collective-permute-done.9 = bf16[400,200]{1,0:T(8,128)(2,1)S(1)} collective-permute-done((bf16[400,200]{1,0:T(8,128)(2,1)S(1)}, bf16[400,200]{1,0:T(8,128)(2,1)S(1)}, u32[]{:S(2)}, u32[]{:S(2)}) %collective-permute-start.9) | collective-permute-done | bytes 160032 | tf_op jit(solution)/shard_map/ppermute | solution.py:243
  94.9 5.7 add_convert_fusion.q_ref.k_ref.v_ref
  100.6 7.0 %shard_map.170 = (bf16[1024,256]{1,0:T(8,128)(2,1)S(1)}, f32[1024,256]{1,0:T(8,128)S(1)}) custom-call(bf16[1024,768]{1,0:T(8,128)(2,1)S(1)} %add_convert_fusion.q_ref.k_ref.v_ref, bf16[1024,768]{1,0:T(8,128)(2,1)S(1)} %add_convert_fusion.q_ref.k_ref.v_ref, bf16[1024,768]{1,0:T(8,128)(2,1)S(1)} %add_convert_fusion.q_ref.k_ref.v_ref), custom_call_target="tpu_custom_call" | custom-call | tf_op jit(solution)/shard_map/pallas_call | solution.py:170
  122.5 5.7 all-to-all-done.1.att_ref
  130.5 9.1 %shard_map.171 = (f32[128,1600]{1,0:T(8,128)}, bf16[128,1600]{1,0:T(8,128)(2,1)S(1)}) custom-call(s32[2]{0:T(128)S(1)} %pad_add_fusion.where, bf16[8,128,256]{2,1,0:T(8,128)(2,1)S(1)} %all-to-all-done.1.att_ref, bf16[128,1600]{1,0:T(8,128)(2,1)S(1)} %copy.157.x_ref, f32[8,1600]{1,0:T(8,128)S(1)} %reshape.732.vec_ref, ...), custom_call_target="tpu_custom_call" | custom-call | tf_op jit(solution)/shard_map/pallas_call | solution.py:300
  147.4 15.2 %all_to_all.40 = bf16[4,2,200,200]{2,1,3,0:T(2,128)(2,1)} all-to-all(bf16[4,2,200,200]{2,1,3,0:T(2,128)(2,1)S(1)} %copy.165), channel_id=1, replica_groups=mesh['dp'=4,'seq'=8] {'dp'}, dimensions={0} | all-to-all | bytes 1280000 | tf_op jit(solution)/shard_map/all_to_all | solution.py:475
  174.0 21.1 %all-to-all-done.3 = bf16[8,200,200]{2,1,0:T(8,128)(2,1)} async-done(((bf16[8,200,200]{2,1,0:T(8,128)(2,1)}), bf16[8,200,200]{2,1,0:T(8,128)(2,1)}, u32[]{:S(2)}, u32[]{:S(2)}) %all-to-all-start.3) | async-done | bytes 640032 | tf_op jit(solution)/shard_map/all_to_all | solution.py:476
  207.7 11.1 %collective-permute-done.19 = bf16[400,800]{1,0:T(8,128)(2,1)} collective-permute-done((bf16[400,800]{1,0:T(8,128)(2,1)}, bf16[400,800]{1,0:T(8,128)(2,1)}, u32[]{:S(2)}, u32[]{:S(2)}) %collective-permute-start.19) | collective-permute-done | bytes 640032 | tf_op jit(solution)/shard_map/ppermute | solution.py:65
  225.5 7.8 %collective-permute-done.22 = bf16[200,1600]{1,0:T(8,128)(2,1)} collective-permute-done((bf16[200,1600]{1,0:T(8,128)(2,1)}, bf16[200,1600]{1,0:T(8,128)(2,1)}, u32[]{:S(2)}, u32[]{:S(2)}) %collective-permute-start.22) | collective-permute-done | bytes 640032 | tf_op jit(solution)/shard_map/ppermute | solution.py:65
  237.0 9.2 %multiply_convert_fusion = (bf16[1024,800]{0,1:T(8,128)(2,1)}, f32[1024,800]{0,1:T(8,128)}) fusion(f32[800]{0:T(1024)S(1)} %dynamic_slice.87, bf16[1024,1600]{1,0:T(8,128)(2,1)} %all-gather.6.cloned.1.call-done, bf16[1600,800]{1,0:T(8,128)(2,1)} %constant_dynamic-update-slice_fusion.4), kind=kOutput, calls=%fused_computation.17 | convolution fusion | flops 2629632000 | bytes 10755200 | tf_op jit(solution)/shard_map/dot_general | solution.py:124
  246.2 8.2 %convert_reduce_fusion = (f32[800]{0:T(1024)S(1)}, bf16[1024,800]{0,1:T(8,128)(2,1)S(1)}) fusion(f32[1024,800]{0,1:T(8,128)} %get-tuple-element.160, f32[800]{0:T(1024)S(1)} %dynamic_slice.87, bf16[1024,1600]{0,1:T(8,128)(2,1)} %all-gather.8.cloned.1.call-done, bf16[200,1600]{1,0:T(8,128)(2,1)} %get-tuple-element.134, ...), kind=kOutput, calls=%fused_computation.16 | convolution fusion | flops 2649701632 | bytes 10758400 | tf_op jit(solution)/shard_map/dot_general | solution.py:128
  260.5 14.5 %copy.169 = bf16[1024,1600]{1,0:T(8,128)(2,1)} copy(bf16[1024,1600]{0,1:T(8,128)(2,1)} %convolution_convert_fusion) | data formatting | bytes 6553600 | tf_op jit(solution)/shard_map/convert_element_type | solution.py:504
  275.1 42.8 %reduce-scatter.4.cloned.1.call-done.gn2_ref = bf16[128,1600]{1,0:T(8,128)(2,1)} async-done(((bf16[1024,1600]{1,0:T(8,128)(2,1)}), bf16[128,1600]{1,0:T(8,128)(2,1)}) %reduce-scatter.4.cloned.1.call-update) | async-done | bytes 409616 | tf_op jit(solution)/shard_map/reduce_scatter | solution.py:505
  317.9 7.6 %convolution_convert_fusion.1 = bf16[1024,1600]{0,1:T(8,128)(2,1)} fusion(bf16[1024,800]{0,1:T(8,128)(2,1)} %get-tuple-element.40, bf16[200,1600]{1,0:T(8,128)(2,1)} %get-tuple-element.134, bf16[200,1600]{1,0:T(8,128)(2,1)} %get-tuple-element.135, bf16[200,1600]{1,0:T(8,128)(2,1)} %get-tuple-element.136, bf16[200,1600]{1,0:T(8,128)(2,1)} %get-tuple-element.133), kind=kOutput, calls=%fused_computation.4 | convolution fusion | flops 2633318400 | bytes 7475200 | tf_op jit(solution)/shard_map/dot_general | solution.py:124
  325.5 5.4 copy.170
  333.3 5.6 convolution_convert_fusion.2
  357.5 10.1 %shard_map.172 = (f32[128,1600]{1,0:T(8,128)}, bf16[128,1600]{1,0:T(8,128)(2,1)S(1)}, bf16[8,128,256]{2,1,0:T(8,128)(2,1)S(1)}, f32[4,1600]{1,0:T(4,128)S(1)}) custom-call(s32[2]{0:T(128)S(1)} %pad_add_fusion.where, bf16[128,1600]{1,0:T(8,128)(2,1)S(1)} %copy-done.22, f32[128,1600]{1,0:T(8,128)} %get-tuple-element.37.r_ref, bf16[128,1600]{1,0:T(8,128)(2,1)S(1)} %copy-done.8, ...), custom_call_target="tpu_custom_call" | custom-call | tf_op jit(solution)/shard_map/pallas_call | solution.py:356
  372.9 5.6 fusion.62
  383.3 10.4 %shard_map.174 = (bf16[4,400,200]{2,1,0:T(8,128)(2,1)S(1)}, bf16[4,400,200]{2,1,0:T(8,128)(2,1)S(1)}, bf16[4,400,200]{2,1,0:T(8,128)(2,1)S(1)}, bf16[4,400,200]{...) custom-call(s32[2]{0:T(128)S(1)} %pad_add_fusion.where, ...), custom_call_target="tpu_custom_call" | custom-call | tf_op jit(solution)/shard_map/pallas_call | solution.py:395
  400.5 12.0 %shard_map.173 = (bf16[1024,256]{1,0:T(8,128)(2,1)S(1)}, bf16[1024,256]{1,0:T(8,128)(2,1)S(1)}, bf16[1024,256]{1,0:T(8,128)(2,1)S(1)}) custom-call(bf16[1024,768]{1,0:T(8,128)(2,1)S(1)} %add_convert_fusion.q_ref.k_ref.v_ref, bf16[1024,768]{1,0:T(8,128)(2,1)S(1)} %add_convert_fusion.q_ref.k_ref.v_ref, ...), custom_call_target="tpu_custom_call" | custom-call | tf_op jit(solution)/shard_map/pallas_call | solution.py:223
  412.6 7.6 %fusion.57 = (f32[1600]{0:T(1024)S(1)}, bf16[1024,1600]{0,1:T(8,128)(2,1)}, f32[1024,1600]{0,1:T(8,128)}) fusion(bf16[1024,768]{1,0:T(8,128)(2,1)S(1)} %constant_dynamic-update-slice_fusion.8, bf16[1600,768]{1,0:T(8,128)(2,1)} %constant_dynamic-update-slice_fusion), kind=kOutput, calls=%fused_computation.157 | convolution fusion | flops 2519857664 | bytes 13867264 | tf_op jit(solution)/shard_map/dot_general | solution.py:128
  420.2 5.5 copy.172
  426.1 7.4 %copy.173 = f32[1024,1600]{1,0:T(8,128)} copy(f32[1024,1600]{0,1:T(8,128)} %get-tuple-element.161) | data formatting | bytes 13107200 | tf_op jit(solution)/shard_map/dot_general | solution.py:128
  446.6 5.5 all-to-all-start.6
  473.4 6.1 collective-permute-done.42
  481.8 10.8 %collective-permute-done.24 = bf16[400,768]{1,0:T(8,128)(2,1)S(1)} collective-permute-done((bf16[400,768]{1,0:T(8,128)(2,1)S(1)}, bf16[400,768]{1,0:T(8,128)(2,1)S(1)}, u32[]{:S(2)}, u32[]{:S(2)}) %collective-permute-start.24) | collective-permute-done | bytes 614432 | tf_op jit(solution)/shard_map/ppermute | solution.py:72
  493.2 12.6 %collective-permute-done.26 = bf16[400,768]{1,0:T(8,128)(2,1)S(1)} collective-permute-done((bf16[400,768]{1,0:T(8,128)(2,1)S(1)}, bf16[400,768]{1,0:T(8,128)(2,1)S(1)}, u32[]{:S(2)}, u32[]{:S(2)}) %collective-permute-start.26) | collective-permute-done | bytes 614432 | tf_op jit(solution)/shard_map/ppermute | solution.py:72
  529.4 19.8 %all-to-all-done.7 = bf16[4,2,200,200]{2,1,3,0:T(2,128)(2,1)} async-done(((bf16[4,2,200,200]{2,1,3,0:T(2,128)(2,1)}), bf16[4,2,200,200]{2,1,3,0:T(2,128)(2,1)}, u32[]{:S(2)}, u32[]{:S(2)}) %all-to-all-start.7) | async-done | bytes 640032 | tf_op jit(solution)/shard_map/all_to_all | solution.py:543
  573.1 8.7 %collective-permute-done.36 = bf16[400,200]{1,0:T(8,128)(2,1)S(1)} collective-permute-done((bf16[400,200]{1,0:T(8,128)(2,1)S(1)}, bf16[400,200]{1,0:T(8,128)(2,1)S(1)}, u32[]{:S(2)}, u32[]{:S(2)}) %collective-permute-start.36) | collective-permute-done | bytes 160032 | tf_op jit(solution)/shard_map/ppermute | solution.py:418
  581.8 11.7 %collective-permute-done.35 = bf16[400,200]{1,0:T(8,128)(2,1)S(1)} collective-permute-done((bf16[400,200]{1,0:T(8,128)(2,1)S(1)}, bf16[400,200]{1,0:T(8,128)(2,1)S(1)}, u32[]{:S(2)}, u32[]{:S(2)}) %collective-permute-start.35) | collective-permute-done | bytes 160032 | tf_op jit(solution)/shard_map/ppermute | solution.py:418
  (357 shorter events, 258.7 us)
Async XLA Ops:
  19.1 75.8 %all-gather.4.cloned.1.call-start = ((), (), s32[]{:S(2)}) async-start(), calls=%async_computation.11 | async-start | bytes 3833856 | tf_op jit(solution)/shard_map/all_gather | solution.py:490
  47.5 35.6 %collective-permute-start.9 = (bf16[400,200]{1,0:T(8,128)(2,1)S(1)}, bf16[400,200]{1,0:T(8,128)(2,1)S(1)}, u32[]{:S(2)}, u32[]{:S(2)}) collective-permute-start(bf16[400,200]{1,0:T(8,128)(2,1)S(1)} %copy-done.43), channel_id=1, source_target_pairs={{0,4},{1,5},{2,6},{3,7},{4,0},{5,1},{6,2},{7,3},{8,12},{9,13},{10,... | collective-permute-start | bytes 480008 | tf_op jit(solution)/shard_map/ppermute | solution.py:243
  48.9 38.9 %collective-permute-start.5 = (bf16[400,768]{1,0:T(8,128)(2,1)S(1)}, bf16[400,768]{1,0:T(8,128)(2,1)S(1)}, u32[]{:S(2)}, u32[]{:S(2)}) collective-permute-start(bf16[400,768]{1,0:T(8,128)(2,1)S(1)} %fusion.19), channel_id=1, source_target_pairs={{0,8},{8,0},{16,24},{24,16},{1,9},{9,1},{17,25},{25,17},{2,10},{10... | collective-permute-start | bytes 1843208 | tf_op jit(solution)/shard_map/ppermute | solution.py:65
  49.6 40.6 %collective-permute-start.6 = (bf16[400,768]{1,0:T(8,128)(2,1)S(1)}, bf16[400,768]{1,0:T(8,128)(2,1)}, u32[]{:S(2)}, u32[]{:S(2)}) collective-permute-start(bf16[400,768]{1,0:T(8,128)(2,1)S(1)} %fusion.19), channel_id=1, source_target_pairs={{0,16},{8,24},{16,0},{24,8},{1,17},{9,25},{17,1},{25,9},{2,18},{10... | collective-permute-start | bytes 1843208 | tf_op jit(solution)/shard_map/ppermute | solution.py:65
  54.9 37.2 %collective-permute-start.7 = (bf16[400,768]{1,0:T(8,128)(2,1)S(1)}, bf16[400,768]{1,0:T(8,128)(2,1)S(1)}, u32[]{:S(2)}, u32[]{:S(2)}) collective-permute-start(bf16[400,768]{1,0:T(8,128)(2,1)S(1)} %fusion.19), channel_id=1, source_target_pairs={{0,24},{8,16},{16,8},{24,0},{1,25},{9,17},{17,9},{25,1},{2,26},{10... | collective-permute-start | bytes 1843208 | tf_op jit(solution)/shard_map/ppermute | solution.py:65
  86.4 31.5 %collective-permute-start.14 = (bf16[4,400,200]{2,1,0:T(8,128)(2,1)S(1)}, bf16[4,400,200]{2,1,0:T(8,128)(2,1)}, u32[]{:S(2)}, u32[]{:S(2)}) collective-permute-start(bf16[4,400,200]{2,1,0:T(8,128)(2,1)S(1)} %pad_maximum_fusion.2.rest_0_), channel_id=1, source_target_pairs={{0,16},{8,24},{16,0},{24,8},{1,17},{9,25},{17,1},{25,9},{2,18},{10... | collective-permute-start | bytes 1920008 | tf_op jit(solution)/shard_map/ppermute | solution.py:65
  112.9 124.0 %all-gather.6.cloned.1.call-start = ((), (), s32[]{:S(2)}) async-start(), calls=%async_computation.12 | async-start | bytes 3833856 | tf_op jit(solution)/shard_map/all_gather | solution.py:498
  140.4 105.8 %all-gather.8.cloned.1.call-start = ((), (), s32[]{:S(2)}) async-start(), calls=%async_computation.13 | async-start | bytes 3686400 | tf_op jit(solution)/shard_map/all_gather | solution.py:493
  170.4 147.6 %reduce-scatter.4.cloned.1.call-start = ((), (), s32[]{:S(2)}) async-start(), calls=%async_computation.14 | async-start | bytes 3833856 | tf_op jit(solution)/shard_map/reduce_scatter | solution.py:505
  170.4 32.4 %collective-permute-start.18 = (bf16[400,800]{1,0:T(8,128)(2,1)}, bf16[400,800]{1,0:T(8,128)(2,1)}, u32[]{:S(2)}, u32[]{:S(2)}) collective-permute-start(bf16[400,800]{1,0:T(8,128)(2,1)} %param.15), channel_id=1, source_target_pairs={{0,8},{8,0},{16,24},{24,16},{1,9},{9,1},{17,25},{25,17},{2,10},{10... | collective-permute-start | bytes 1920008 | tf_op jit(solution)/shard_map/ppermute | solution.py:65
  171.1 47.7 %collective-permute-start.19 = (bf16[400,800]{1,0:T(8,128)(2,1)}, bf16[400,800]{1,0:T(8,128)(2,1)}, u32[]{:S(2)}, u32[]{:S(2)}) collective-permute-start(bf16[400,800]{1,0:T(8,128)(2,1)} %param.15), channel_id=1, source_target_pairs={{0,16},{8,24},{16,0},{24,8},{1,17},{9,25},{17,1},{25,9},{2,18},{10... | collective-permute-start | bytes 1920008 | tf_op jit(solution)/shard_map/ppermute | solution.py:65
  171.7 49.2 %collective-permute-start.20 = (bf16[400,800]{1,0:T(8,128)(2,1)}, bf16[400,800]{1,0:T(8,128)(2,1)}, u32[]{:S(2)}, u32[]{:S(2)}) collective-permute-start(bf16[400,800]{1,0:T(8,128)(2,1)} %param.15), channel_id=1, source_target_pairs={{0,24},{8,16},{16,8},{24,0},{1,25},{9,17},{17,9},{25,1},{2,26},{10... | collective-permute-start | bytes 1920008 | tf_op jit(solution)/shard_map/ppermute | solution.py:65
  202.3 31.0 %collective-permute-start.22 = (bf16[200,1600]{1,0:T(8,128)(2,1)}, bf16[200,1600]{1,0:T(8,128)(2,1)}, u32[]{:S(2)}, u32[]{:S(2)}) collective-permute-start(bf16[200,1600]{1,0:T(8,128)(2,1)} %reshape.739), channel_id=1, source_target_pairs={{0,16},{8,24},{16,0},{24,8},{1,17},{9,25},{17,1},{25,9},{2,18},{10... | collective-permute-start | bytes 1920008 | tf_op jit(solution)/shard_map/ppermute | solution.py:65
  275.1 329.8 %reduce-scatter.6.cloned.1.call-start = ((), (), s32[]{:S(2)}) async-start(), calls=%async_computation.15 | async-start | bytes 3833856 | tf_op jit(solution)/shard_map/reduce_scatter | solution.py:507
  350.3 110.0 %collective-permute-start.43 = (bf16[400,800]{1,0:T(8,128)(2,1)}, bf16[400,800]{1,0:T(8,128)(2,1)}, u32[]{:S(2)}, u32[]{:S(2)}) collective-permute-start(bf16[400,800]{1,0:T(8,128)(2,1)} %copy.176), channel_id=1, source_target_pairs={{0,16},{8,24},{16,0},{24,8},{1,17},{9,25},{17,1},{25,9},{2,18},{10... | collective-permute-start | bytes 1920008 | tf_op jit(solution)/shard_map/ppermute | solution.py:72
  351.7 110.3 %collective-permute-start.44 = (bf16[400,800]{1,0:T(8,128)(2,1)}, bf16[400,800]{1,0:T(8,128)(2,1)}, u32[]{:S(2)}, u32[]{:S(2)}) collective-permute-start(bf16[400,800]{1,0:T(8,128)(2,1)} %copy.178), channel_id=1, source_target_pairs={{0,24},{8,16},{16,8},{24,0},{1,25},{9,17},{17,9},{25,1},{2,26},{10... | collective-permute-start | bytes 1920008 | tf_op jit(solution)/shard_map/ppermute | solution.py:72
  372.6 234.4 %reduce-scatter.8.cloned.1.call-start = ((), (), s32[]{:S(2)}) async-start(), calls=%async_computation.16 | async-start | bytes 3833856 | tf_op jit(solution)/shard_map/reduce_scatter | solution.py:520
  379.8 59.2 %collective-permute-start.45 = (bf16[200,1600]{1,0:T(8,128)(2,1)}, bf16[200,1600]{1,0:T(8,128)(2,1)}, u32[]{:S(2)}, u32[]{:S(2)}) collective-permute-start(bf16[200,1600]{1,0:T(8,128)(2,1)} %get-tuple-element.127), channel_id=1, source_target_pairs={{0,8},{8,0},{16,24},{24,16},{1,9},{9,1},{17,25},{25,17},{2,10},{10... | collective-permute-start | bytes 1920008 | tf_op jit(solution)/shard_map/ppermute | solution.py:72
  380.4 58.6 %collective-permute-start.47 = (bf16[200,1600]{1,0:T(8,128)(2,1)}, bf16[200,1600]{1,0:T(8,128)(2,1)}, u32[]{:S(2)}, u32[]{:S(2)}) collective-permute-start(bf16[200,1600]{1,0:T(8,128)(2,1)} %get-tuple-element.128), channel_id=1, source_target_pairs={{0,24},{8,16},{16,8},{24,0},{1,25},{9,17},{17,9},{25,1},{2,26},{10... | collective-permute-start | bytes 1920008 | tf_op jit(solution)/shard_map/ppermute | solution.py:72
  382.8 56.8 %collective-permute-start.46 = (bf16[200,1600]{1,0:T(8,128)(2,1)}, bf16[200,1600]{1,0:T(8,128)(2,1)}, u32[]{:S(2)}, u32[]{:S(2)}) collective-permute-start(bf16[200,1600]{1,0:T(8,128)(2,1)} %get-tuple-element.129), channel_id=1, source_target_pairs={{0,16},{8,24},{16,0},{24,8},{1,17},{9,25},{17,1},{25,9},{2,18},{10... | collective-permute-start | bytes 1920008 | tf_op jit(solution)/shard_map/ppermute | solution.py:72
  446.6 62.4 %all-to-all-start.6 = ((bf16[8,200,200]{2,1,0:T(8,128)(2,1)}), bf16[8,200,200]{2,1,0:T(8,128)(2,1)}, u32[]{:S(2)}, u32[]{:S(2)}) async-start(bf16[8,200,200]{2,1,0:T(8,128)(2,1)} %bitcast.112), calls=%async_computation.9 | async-start | bytes 1638400 | tf_op jit(solution)/shard_map/all_to_all | solution.py:541
  462.1 30.6 %collective-permute-start.24 = (bf16[400,768]{1,0:T(8,128)(2,1)S(1)}, bf16[400,768]{1,0:T(8,128)(2,1)S(1)}, u32[]{:S(2)}, u32[]{:S(2)}) collective-permute-start(bf16[400,768]{1,0:T(8,128)(2,1)S(1)} %get-tuple-element.137), channel_id=1, source_target_pairs={{0,8},{8,0},{16,24},{24,16},{1,9},{9,1},{17,25},{25,17},{2,10},{10... | collective-permute-start | bytes 1843208 | tf_op jit(solution)/shard_map/ppermute | solution.py:72
  462.6 43.2 %collective-permute-start.26 = (bf16[400,768]{1,0:T(8,128)(2,1)S(1)}, bf16[400,768]{1,0:T(8,128)(2,1)S(1)}, u32[]{:S(2)}, u32[]{:S(2)}) collective-permute-start(bf16[400,768]{1,0:T(8,128)(2,1)S(1)} %get-tuple-element.138), channel_id=1, source_target_pairs={{0,24},{8,16},{16,8},{24,0},{1,25},{9,17},{17,9},{25,1},{2,26},{10... | collective-permute-start | bytes 1843208 | tf_op jit(solution)/shard_map/ppermute | solution.py:72
  466.4 56.4 %collective-permute-start.25 = (bf16[400,768]{1,0:T(8,128)(2,1)}, bf16[400,768]{1,0:T(8,128)(2,1)}, u32[]{:S(2)}, u32[]{:S(2)}) collective-permute-start(bf16[400,768]{1,0:T(8,128)(2,1)} %get-tuple-element.139), channel_id=1, source_target_pairs={{0,16},{8,24},{16,0},{24,8},{1,17},{9,25},{17,1},{25,9},{2,18},{10... | collective-permute-start | bytes 1843208 | tf_op jit(solution)/shard_map/ppermute | solution.py:72
  479.5 74.9 %collective-permute-start.27 = (bf16[4,400,200]{2,1,0:T(8,128)(2,1)S(1)}, bf16[4,400,200]{2,1,0:T(8,128)(2,1)}, u32[]{:S(2)}, u32[]{:S(2)}) collective-permute-start(bf16[4,400,200]{2,1,0:T(8,128)(2,1)S(1)} %copy-done.24), channel_id=1, source_target_pairs={{0,1},{1,0},{2,3},{3,2},{4,5},{5,4},{6,7},{7,6},{8,9},{9,8},{10,11... | collective-permute-start | bytes 1920008 | tf_op jit(solution)/shard_map/ppermute | solution.py:412
  480.5 73.9 %collective-permute-start.29 = (bf16[4,400,200]{2,1,0:T(8,128)(2,1)}, bf16[4,400,200]{2,1,0:T(8,128)(2,1)}, u32[]{:S(2)}, u32[]{:S(2)}) collective-permute-start(bf16[4,400,200]{2,1,0:T(8,128)(2,1)} %add_convert_fusion.4), channel_id=1, source_target_pairs={{0,8},{8,0},{16,24},{24,16},{1,9},{9,1},{17,25},{25,17},{2,10},{10... | collective-permute-start | bytes 1920008 | tf_op jit(solution)/shard_map/ppermute | solution.py:72
  492.6 61.7 %collective-permute-start.31 = (bf16[4,400,200]{2,1,0:T(8,128)(2,1)}, bf16[4,400,200]{2,1,0:T(8,128)(2,1)}, u32[]{:S(2)}, u32[]{:S(2)}) collective-permute-start(bf16[4,400,200]{2,1,0:T(8,128)(2,1)} %add_convert_fusion.3), channel_id=1, source_target_pairs={{0,16},{8,24},{16,0},{24,8},{1,17},{9,25},{17,1},{25,9},{2,18},{10... | collective-permute-start | bytes 1920008 | tf_op jit(solution)/shard_map/ppermute | solution.py:72
  506.7 47.7 %collective-permute-start.33 = (bf16[4,400,200]{2,1,0:T(8,128)(2,1)}, bf16[4,400,200]{2,1,0:T(8,128)(2,1)}, u32[]{:S(2)}, u32[]{:S(2)}) collective-permute-start(bf16[4,400,200]{2,1,0:T(8,128)(2,1)} %add_convert_fusion.2), channel_id=1, source_target_pairs={{0,24},{8,16},{16,8},{24,0},{1,25},{9,17},{17,9},{25,1},{2,26},{10... | collective-permute-start | bytes 1920008 | tf_op jit(solution)/shard_map/ppermute | solution.py:72
  512.6 36.6 %all-to-all-start.7 = ((bf16[4,2,200,200]{2,1,3,0:T(2,128)(2,1)}), bf16[4,2,200,200]{2,1,3,0:T(2,128)(2,1)}, u32[]{:S(2)}, u32[]{:S(2)}) async-start(bf16[4,2,200,200]{2,1,3,0:T(2,128)(2,1)} %copy.181), calls=%async_computation.10 | async-start | bytes 1638400 | tf_op jit(solution)/shard_map/all_to_all | solution.py:543
  522.8 44.5 %collective-permute-start.41 = (f32[12,1600]{1,0:T(8,128)S(1)}, f32[12,1600]{1,0:T(8,128)S(1)}, u32[]{:S(2)}, u32[]{:S(2)}) collective-permute-start(f32[12,1600]{1,0:T(8,128)S(1)} %add.255), channel_id=1, source_target_pairs={{0,4},{1,5},{2,6},{3,7},{4,0},{5,1},{6,2},{7,3},{8,12},{9,13},{10,... | collective-permute-start | bytes 230408 | tf_op jit(solution)/shard_map/ppermute | solution.py:426
  549.2 52.7 %all-to-all-start.5 = ((bf16[8,400,128]{2,1,0:T(8,128)(2,1)}), bf16[8,400,128]{2,1,0:T(8,128)(2,1)}, u32[]{:S(2)}, u32[]{:S(2)}) async-start(bf16[8,400,128]{2,1,0:T(8,128)(2,1)} %fusion.21), calls=%async_computation.8 | async-start | bytes 1638400 | tf_op jit(solution)/shard_map/all_to_all | solution.py:532
  561.4 32.0 %collective-permute-start.35 = (bf16[400,200]{1,0:T(8,128)(2,1)S(1)}, bf16[400,200]{1,0:T(8,128)(2,1)S(1)}, u32[]{:S(2)}, u32[]{:S(2)}) collective-permute-start(bf16[400,200]{1,0:T(8,128)(2,1)S(1)} %get-tuple-element.142), channel_id=1, source_target_pairs={{0,4},{1,5},{2,6},{3,7},{4,0},{5,1},{6,2},{7,3},{8,12},{9,13},{10,... | collective-permute-start | bytes 480008 | tf_op jit(solution)/shard_map/ppermute | solution.py:418
  (86 other events, 755.0 us)
Sparse Core Ops, SparseCore 0:
  44.8 50.0 all-gather.3
  140.5 41.1 all-gather.5
  183.3 43.2 all-gather.7
  275.2 42.7 reduce-scatter.3
  331.1 41.2 reduce-scatter.5
  426.1 53.2 reduce-scatter.7

commit v3 on v2

--- a/solution.py
+++ b/solution.py
@@ -88,12 +88,10 @@
     return stack
 
 
-def swap_blocks(matrix, count, me):
-    size = matrix.shape[1] // count
-    return jnp.concatenate(
-        [lax.dynamic_slice_in_dim(matrix, (me ^ k) * size, size, axis=1) for k in range(count)],
-        axis=1,
-    )
+ANY = pl.BlockSpec(memory_space=pl.ANY)
+WHOLE = pl.BlockSpec(memory_space=pltpu.VMEM)
+SCALAR = pl.BlockSpec(memory_space=pltpu.SMEM)
+ROOM = pltpu.CompilerParams(vmem_limit_bytes=56 * 1024 * 1024)
 
 
 def normalise(rows):
@@ -136,105 +134,370 @@
     return math.gcd(length, 256)
 
 
-def attend_kernel(q_ref, k_ref, v_ref, o_ref, lse_ref):
-    length = q_ref.shape[0]
-    rows = block_rows(length)
+def head_masks(rows):
     first = lax.broadcasted_iota(jnp.int32, (rows, PAIR), 1) < HD
     causal = lax.broadcasted_iota(jnp.int32, (rows, rows), 0) >= lax.broadcasted_iota(
         jnp.int32, (rows, rows), 1
     )
+    return first, causal
+
+
+def masked_scores(q, keys, causal):
+    rows, seen = q.shape[0], keys.shape[0]
+    s = mm_nt(q, keys)
+    tail = jnp.where(causal, s[:, seen - rows :], NEG_FILL)
+    return tail if seen == rows else jnp.concatenate([s[:, : seen - rows], tail], axis=1)
+
+
+def attend_rows(q, keys, values, first, causal):
+    q = q * BF(1.0 / math.sqrt(HD))
+    outs, logs = [], []
+    for mine in (first, ~first):
+        s = masked_scores(jnp.where(mine, q, BF(0)), keys, causal)
+        top = jnp.max(s, axis=-1, keepdims=True)
+        e = jnp.exp(s - top)
+        total = jnp.sum(e, axis=-1, keepdims=True)
+        outs.append(mm(e.astype(BF), values) / total)
+        logs.append(top + jnp.log(total))
+    return jnp.where(first, outs[0], outs[1]).astype(BF), jnp.where(first, logs[0], logs[1])
+
+
+def row_blocks_in(where, refs, store, sems):
+    copies = [
+        pltpu.make_async_copy(ref, store.at[where[0] ^ k], sems.at[k])
+        for k, ref in enumerate(refs)
+    ]
+    for c in copies:
+        c.start()
+    return copies
+
+
+def right_blocks(rows, store):
+    count, depth = store.shape[:2]
+    total = mm(rows[:, :depth], store[0])
+    for p in range(1, count):
+        total = total + mm(rows[:, p * depth : (p + 1) * depth], store[p])
+    return total
+
+
+def attend_kernel(dps, pairs, where, x_ref, vec_ref, bias_ref, *rest):
+    w_refs = rest[:dps]
+    n1_ref, qkv_ref, att_ref, lse_ref, w, qkv, sems = rest[dps:]
+    i = pl.program_id(0)
+    rows = x_ref.shape[0]
+    steps = qkv.shape[0] // rows
+
+    @pl.when(i == 0)
+    def _():
+        for c in row_blocks_in(where, w_refs, w, sems):
+            c.wait()
+
+    unit, _ = normalise(x_ref[...].astype(F32))
+    n1 = (unit * vec_ref[0:1, :] + vec_ref[1:2, :]).astype(BF)
+    n1_ref[...] = n1
+    tile = (right_blocks(n1, w) + bias_ref[...]).astype(BF)
+    qkv_ref[...] = tile
+    qkv[pl.ds(pl.multiple_of(i * rows, rows), rows), :] = tile
+    first, causal = head_masks(rows)
+    part = att_ref.shape[1]
+    for j in range(steps):
+
+        @pl.when(i == j)
+        def _(j=j):
+            seen = (j + 1) * rows
+            for g in range(pairs):
+                lanes = slice(g * PAIR, (g + 1) * PAIR)
+                keys = qkv[0:seen, (pairs + g) * PAIR : (pairs + g + 1) * PAIR]
+                values = qkv[0:seen, (2 * pairs + g) * PAIR : (2 * pairs + g + 1) * PAIR]
+                out, log = attend_rows(
+                    qkv[j * rows : seen, lanes], keys, values, first, causal
+                )
+                for b in range(rows // part):
+                    att_ref[b, :, lanes] = out[b * part : (b + 1) * part]
+                lse_ref[:, lanes] = log
+
+
+def attend(where, x_all, table, bias, weights, slots, part):
+    length, model = x_all.shape
+    dps = len(weights)
+    depth, width = weights[0].shape
+    mine = slots * HD
+    rows = block_rows(length)
+    whole = lambda shape: pl.BlockSpec(shape, lambda i: (0,) * len(shape))
+    tile = lambda cols: pl.BlockSpec((rows, cols), lambda i: (i, 0))
+    return pl.pallas_call(
+        functools.partial(attend_kernel, dps, mine // PAIR),
+        grid=(length // rows,),
+        in_specs=[SCALAR, tile(model), whole(table.shape), whole(bias.shape)] + [ANY] * dps,
+        out_specs=[
+            tile(model),
+            tile(width),
+            pl.BlockSpec((rows // part, part, mine), lambda i: (i, 0, 0)),
+            tile(mine),
+        ],
+        out_shape=[
+            jax.ShapeDtypeStruct((length, model), BF),
+            jax.ShapeDtypeStruct((length, width), BF),
+            jax.ShapeDtypeStruct((length // part, part, mine), BF),
+            jax.ShapeDtypeStruct((length, mine), F32),
+        ],
+        scratch_shapes=[
+            pltpu.VMEM((dps, depth, width), BF),
+            pltpu.VMEM((length, width), BF),
+            pltpu.SemaphoreType.DMA((dps,)),
+        ],
+        compiler_params=ROOM,
+    )(where, x_all, table, bias, *weights)
+
+
+def attend_back_kernel(dps, pairs, where, qkv_ref, ga_ref, lse_ref, *rest):
+    w_refs = rest[:dps]
+    gqkv_ref, gn1_ref, w, ak, av, sems = rest[dps:]
+    length = qkv_ref.shape[0]
+    rows = block_rows(length)
+    copies = row_blocks_in(where, w_refs, w, sems)
+    first, causal = head_masks(rows)
+    part = ga_ref.shape[1]
+    for g in range(pairs):
+        lanes = slice(g * PAIR, (g + 1) * PAIR)
+        k_lanes = slice((pairs + g) * PAIR, (pairs + g + 1) * PAIR)
+        v_lanes = slice((2 * pairs + g) * PAIR, (2 * pairs + g + 1) * PAIR)
+        ak[...] = jnp.zeros_like(ak)
+        av[...] = jnp.zeros_like(av)
+        for i in range(length // rows):
+            here = slice(i * rows, (i + 1) * rows)
+            seen = (i + 1) * rows
+            q = qkv_ref[here, lanes] * BF(1.0 / math.sqrt(HD))
+            ga = jnp.concatenate(
+                [ga_ref[b, :, lanes] for b in range(i * rows // part, seen // part)], axis=0
+            )
+            keys = qkv_ref[0:seen, k_lanes]
+            values = qkv_ref[0:seen, v_lanes]
+            grads = []
+            for h, mine in enumerate((first, ~first)):
+                q_h = jnp.where(mine, q, BF(0))
+                ga_h = jnp.where(mine, ga, BF(0))
+                s = masked_scores(q_h, keys, causal)
+                lane = g * PAIR + h * HD
+                p = jnp.exp(s - lse_ref[here, lane : lane + 1])
+                gp = mm_nt(ga_h, values)
+                centre = jnp.sum(p * gp, axis=-1, keepdims=True)
+                gs = (p * (gp - centre)).astype(BF)
+                av[0:seen, :] += mm_tn(p.astype(BF), ga_h)
+                ak[0:seen, :] += mm_tn(gs, q_h)
+                grads.append(mm(gs, keys))
+            gqkv_ref[here, lanes] = (
+                jnp.where(first, grads[0], grads[1]) * (1.0 / math.sqrt(HD))
+            ).astype(BF)
+        gqkv_ref[:, k_lanes] = ak[...].astype(BF)
+        gqkv_ref[:, v_lanes] = av[...].astype(BF)
+    for c in copies:
+        c.wait()
+    depth = w.shape[1]
     for i in range(length // rows):
-        here = pl.ds(i * rows, rows)
-        seen = (i + 1) * rows
-        q = q_ref[here, :] * BF(1.0 / math.sqrt(HD))
-        keys = k_ref[0:seen, :]
-        values = v_ref[0:seen, :]
-        outs, logs = [], []
-        for mine in (first, ~first):
-            s = mm_nt(jnp.where(mine, q, BF(0)), keys)
-            tail = jnp.where(causal, s[:, seen - rows :], NEG_FILL)
-            s = tail if i == 0 else jnp.concatenate([s[:, : seen - rows], tail], axis=1)
-            top = jnp.max(s, axis=-1, keepdims=True)
-            e = jnp.exp(s - top)
-            total = jnp.sum(e, axis=-1, keepdims=True)
-            outs.append(mm(e.astype(BF), values) / total)
-            logs.append(top + jnp.log(total))
-        o_ref[here, :] = jnp.where(first, outs[0], outs[1]).astype(BF)
-        lse_ref[here, :] = jnp.where(first, logs[0], logs[1])
-
-
-def attend(qkv, slots):
-    length = qkv.shape[0]
-    pairs = slots * HD // PAIR
-    spec = lambda shift: pl.BlockSpec((length, PAIR), lambda g: (0, g + shift))
+        here = slice(i * rows, (i + 1) * rows)
+        for p in range(dps):
+            gn1_ref[here, p * depth : (p + 1) * depth] = mm_nt(gqkv_ref[here, :], w[p]).astype(BF)
+
+
+def attend_back(where, qkv, grad, lse, weights):
+    length, width = qkv.shape
+    dps = len(weights)
+    depth = weights[0].shape[0]
     return pl.pallas_call(
-        attend_kernel,
-        grid=(pairs,),
-        in_specs=[spec(0), spec(pairs), spec(2 * pairs)],
-        out_specs=[spec(0), spec(0)],
+        functools.partial(attend_back_kernel, dps, grad.shape[2] // PAIR),
+        in_specs=[SCALAR, WHOLE, WHOLE, WHOLE] + [ANY] * dps,
+        out_specs=[WHOLE, WHOLE],
         out_shape=[
-            jax.ShapeDtypeStruct((length, slots * HD), BF),
-            jax.ShapeDtypeStruct((length, slots * HD), F32),
-        ],
-        compiler_params=pltpu.CompilerParams(vmem_limit_bytes=48 * 1024 * 1024),
-    )(qkv, qkv, qkv)
-
-
-def attend_back_kernel(q_ref, k_ref, v_ref, ga_ref, lse_ref, gq_ref, gk_ref, gv_ref, ak, av):
-    length = q_ref.shape[0]
+            jax.ShapeDtypeStruct((length, width), BF),
+            jax.ShapeDtypeStruct((length, dps * depth), BF),
+        ],
+        scratch_shapes=[
+            pltpu.VMEM((dps, depth, width), BF),
+            pltpu.VMEM((length, PAIR), F32),
+            pltpu.VMEM((length, PAIR), F32),
+            pltpu.SemaphoreType.DMA((dps,)),
+        ],
+        compiler_params=ROOM,
+    )(where, qkv, grad, lse, *weights)
+
+
+def grad_qkv_kernel(dps, where, n1_ref, gqkv_ref, gn1_ref, *rest):
+    outs = rest[:dps]
+    sums_ref, norm_ref, store, sems = rest[dps:]
+    depth = store.shape[1]
+    gqkv = gqkv_ref[...]
+    for p in range(dps):
+        store[p] = mm_tn(n1_ref[:, p * depth : (p + 1) * depth], gqkv).astype(BF)
+    copies = [
+        pltpu.make_async_copy(store.at[where[0] ^ k], ref, sems.at[k])
+        for k, ref in enumerate(outs)
+    ]
+    for c in copies:
+        c.start()
+    sums_ref[...] = jnp.sum(gqkv.astype(F32), axis=0, keepdims=True)
+    gn1 = gn1_ref[...].astype(F32)
+    norm_ref[0:1, :] = jnp.sum(gn1 * n1_ref[...].astype(F32), axis=0, keepdims=True)
+    norm_ref[1:2, :] = jnp.sum(gn1, axis=0, keepdims=True)
+    for c in copies:
+        c.wait()
+
+
+def grad_qkv(where, n1, gqkv, gn1, dps):
+    model, width = n1.shape[1], gqkv.shape[1]
+    depth = model // dps
+    *chunks, sums, norm = pl.pallas_call(
+        functools.partial(grad_qkv_kernel, dps),
+        in_specs=[SCALAR, WHOLE, WHOLE, WHOLE],
+        out_specs=[ANY] * dps + [WHOLE, WHOLE],
+        out_shape=[jax.ShapeDtypeStruct((depth, width), BF)] * dps
+        + [jax.ShapeDtypeStruct((1, width), F32), jax.ShapeDtypeStruct((2, model), F32)],
+        scratch_shapes=[pltpu.VMEM((dps, depth, width), BF), pltpu.SemaphoreType.DMA((dps,))],
+        compiler_params=ROOM,
+    )(where, n1, gqkv, gn1)
+    return chunks, sums, norm
+
+
+def piece_rows(total, count):
+    tiles = total // 16
+    return 16 * -(-tiles // count), lambda q: 16 * ((q * tiles) // count)
+
+
+def feed_kernel(dps, where, n2_ref, gm_ref, bias_ref, *rest):
+    f_refs, p_refs = rest[:dps], rest[dps : 2 * dps]
+    e_ref, gu_ref, gn2_ref, sum_ref, wf, wp, sems, sems2 = rest[2 * dps :]
+    i = pl.program_id(0)
+    size, start = piece_rows(wp.shape[0], dps)
+
+    @pl.when(i == 0)
+    def _():
+        copies = row_blocks_in(where, f_refs, wf, sems)
+        for k, ref in enumerate(p_refs):
+            here = pl.ds(pl.multiple_of(start(where[0] ^ k), 16), size)
+            one = pltpu.make_async_copy(ref, wp.at[here, :], sems2)
+            one.start()
+            one.wait()
+        for c in copies:
+            c.wait()
+        sum_ref[...] = jnp.zeros_like(sum_ref)
+
+    u = right_blocks(n2_ref[...], wf) + bias_ref[...]
+    ge = mm_nt(gm_ref[...], wp[...])
+    value, slope = gelu_parts(u)
+    e_ref[...] = value.astype(BF)
+    gu = (ge * slope).astype(BF)
+    gu_ref[...] = gu
+    sum_ref[...] += jnp.sum(gu.astype(F32), axis=0, keepdims=True)
+    depth = wf.shape[1]
+    for p in range(dps):
+        gn2_ref[:, p * depth : (p + 1) * depth] = mm_nt(gu, wf[p]).astype(BF)
+
+
+def feed(where, n2, gm, bias, fc, proj):
+    length, model = n2.shape
+    dps = len(fc)
+    depth, width = fc[0].shape
     rows = block_rows(length)
-    first = lax.broadcasted_iota(jnp.int32, (rows, PAIR), 1) < HD
-    causal = lax.broadcasted_iota(jnp.int32, (rows, rows), 0) >= lax.broadcasted_iota(
-        jnp.int32, (rows, rows), 1
-    )
-    ak[...] = jnp.zeros_like(ak)
-    av[...] = jnp.zeros_like(av)
-    for i in range(length // rows):
-        here = pl.ds(i * rows, rows)
-        seen = (i + 1) * rows
-        q = q_ref[here, :] * BF(1.0 / math.sqrt(HD))
-        ga = ga_ref[here, :]
-        keys = k_ref[0:seen, :]
-        values = v_ref[0:seen, :]
-        grads = []
-        for h, mine in enumerate((first, ~first)):
-            q_h = jnp.where(mine, q, BF(0))
-            ga_h = jnp.where(mine, ga, BF(0))
-            s = mm_nt(q_h, keys)
-            tail = jnp.where(causal, s[:, seen - rows :], NEG_FILL)
-            s = tail if i == 0 else jnp.concatenate([s[:, : seen - rows], tail], axis=1)
-            p = jnp.exp(s - lse_ref[here, h * HD : h * HD + 1])
-            gp = mm_nt(ga_h, values)
-            centre = jnp.sum(p * gp, axis=-1, keepdims=True)
-            gs = (p * (gp - centre)).astype(BF)
-            av[0:seen, :] += mm_tn(p.astype(BF), ga_h)
-            ak[0:seen, :] += mm_tn(gs, q_h)
-            grads.append(mm(gs, keys))
-        gq_ref[here, :] = (jnp.where(first, grads[0], grads[1]) * (1.0 / math.sqrt(HD))).astype(BF)
-    gk_ref[...] = ak[...].astype(BF)
-    gv_ref[...] = av[...].astype(BF)
-
-
-def attend_back(qkv, grad, lse, slots):
-    length = qkv.shape[0]
-    pairs = slots * HD // PAIR
-    spec = lambda shift: pl.BlockSpec((length, PAIR), lambda g: (0, g + shift))
-    shape = jax.ShapeDtypeStruct((length, slots * HD), BF)
+    whole = lambda shape: pl.BlockSpec(shape, lambda i: (0,) * len(shape))
+    tile = lambda cols: pl.BlockSpec((rows, cols), lambda i: (i, 0))
     return pl.pallas_call(
-        attend_back_kernel,
-        grid=(pairs,),
-        in_specs=[spec(0), spec(pairs), spec(2 * pairs), spec(0), spec(0)],
-        out_specs=[spec(0), spec(0), spec(0)],
-        out_shape=[shape, shape, shape],
-        scratch_shapes=[pltpu.VMEM((length, PAIR), F32), pltpu.VMEM((length, PAIR), F32)],
-        compiler_params=pltpu.CompilerParams(vmem_limit_bytes=48 * 1024 * 1024),
-    )(qkv, qkv, qkv, grad, lse)
-
-
-ANY = pl.BlockSpec(memory_space=pl.ANY)
-WHOLE = pl.BlockSpec(memory_space=pltpu.VMEM)
-SCALAR = pl.BlockSpec(memory_space=pltpu.SMEM)
-ROOM = pltpu.CompilerParams(vmem_limit_bytes=48 * 1024 * 1024)
+        functools.partial(feed_kernel, dps),
+        grid=(length // rows,),
+        in_specs=[SCALAR, tile(model), tile(model), whole(bias.shape)] + [ANY] * (2 * dps),
+        out_specs=[tile(width), tile(width), tile(model), whole((1, width))],
+        out_shape=[
+            jax.ShapeDtypeStruct((length, width), BF),
+            jax.ShapeDtypeStruct((length, width), BF),
+            jax.ShapeDtypeStruct((length, model), BF),
+            jax.ShapeDtypeStruct((1, width), F32),
+        ],
+        scratch_shapes=[
+            pltpu.VMEM((dps, depth, width), BF),
+            pltpu.VMEM((width, model), BF),
+            pltpu.SemaphoreType.DMA((dps,)),
+            pltpu.SemaphoreType.DMA,
+        ],
+        compiler_params=ROOM,
+    )(where, n2, gm, bias, *fc, *proj)
+
+
+def feed_grad_kernel(dps, where, n2_ref, gm_ref, e_ref, gu_ref, *rest):
+    p_refs = rest[:dps]
+    mlp_ref = rest[dps]
+    f_outs, p_outs = rest[dps + 1 : 2 * dps + 1], rest[2 * dps + 1 : 3 * dps + 1]
+    wp, df, dp_, sems, sems2 = rest[3 * dps + 1 :]
+    width = wp.shape[0]
+    size, start = piece_rows(width, dps)
+    spots = [pl.ds(pl.multiple_of(start(where[0] ^ k), 16), size) for k in range(dps)]
+    depth = df.shape[1]
+    for p in range(dps):
+        df[p] = mm_tn(n2_ref[:, p * depth : (p + 1) * depth], gu_ref[...]).astype(BF)
+    copies = [
+        pltpu.make_async_copy(df.at[where[0] ^ k], ref, sems.at[k]) for k, ref in enumerate(f_outs)
+    ]
+    for c in copies:
+        c.start()
+    for a in range(0, width, 256):
+        b = min(width, a + 256)
+        dp_[a:b, :] = mm_tn(e_ref[:, a:b], gm_ref[...]).astype(BF)
+    more = [
+        pltpu.make_async_copy(dp_.at[spots[k], :], ref, sems2.at[k])
+        for k, ref in enumerate(p_outs)
+    ]
+    for c in more:
+        c.start()
+    for c in copies:
+        c.wait()
+    for k, ref in enumerate(p_refs):
+        one = pltpu.make_async_copy(ref, wp.at[spots[k], :], sems.at[k])
+        one.start()
+        one.wait()
+    rows = block_rows(e_ref.shape[0])
+    for a in range(0, e_ref.shape[0], rows):
+        mlp_ref[a : a + rows, :] = mm(e_ref[a : a + rows, :], wp[...]).astype(BF)
+    for c in more:
+        c.wait()
+
+
+def feed_grad(where, n2, gm, e, gu, proj):
+    length, model = n2.shape
+    dps = len(proj)
+    width = e.shape[1]
+    depth = model // dps
+    size, _ = piece_rows(width, dps)
+    mlp, *chunks = pl.pallas_call(
+        functools.partial(feed_grad_kernel, dps),
+        in_specs=[SCALAR, WHOLE, WHOLE, WHOLE, WHOLE] + [ANY] * dps,
+        out_specs=[WHOLE] + [ANY] * (2 * dps),
+        out_shape=[jax.ShapeDtypeStruct((length, model), BF)]
+        + [jax.ShapeDtypeStruct((depth, width), BF)] * dps
+        + [jax.ShapeDtypeStruct((size, model), BF)] * dps,
+        scratch_shapes=[
+            pltpu.VMEM((width, model), BF),
+            pltpu.VMEM((dps, depth, width), BF),
+            pltpu.VMEM((width, model), BF),
+            pltpu.SemaphoreType.DMA((dps,)),
+            pltpu.SemaphoreType.DMA((dps,)),
+        ],
+        compiler_params=ROOM,
+    )(where, n2, gm, e, gu, *proj)
+    return mlp, chunks[:dps], chunks[dps:]
+
+
+def last_kernel(gn1_ref, x_ref, gr_ref, vec_ref, out_ref):
+    unit, inverse = normalise(x_ref[...].astype(F32))
+    grad = norm_back(gn1_ref[...].astype(F32), unit, inverse, vec_ref[0:1, :])
+    out_ref[...] = (gr_ref[...] + grad).astype(BF)
+
+
+def last_norm(gn1, x, gr, table):
+    return pl.pallas_call(
+        last_kernel,
+        in_specs=[WHOLE] * 4,
+        out_specs=WHOLE,
+        out_shape=jax.ShapeDtypeStruct(x.shape, BF),
+        compiler_params=ROOM,
+    )(gn1, x, gr, table)
 
 
 def out_blocks(w_out):
@@ -284,13 +547,7 @@
             total = total + mm(att[:, p * depth : (p + 1) * depth], store[p, n])
         r_ref[:, here] = total
     unit, _ = normalise(r_ref[...])
-    n2 = (unit * vec_ref[5:6, :] + vec_ref[6:7, :]).astype(BF)
-    me = where[0]
-    for k in range(dps):
-        piece = n2[:, k * depth : (k + 1) * depth]
-        for i in range(1, dps):
-            piece = jnp.where(me == i, n2[:, (i ^ k) * depth : ((i ^ k) + 1) * depth], piece)
-        n2_ref[:, k * depth : (k + 1) * depth] = piece
+    n2_ref[...] = (unit * vec_ref[5:6, :] + vec_ref[6:7, :]).astype(BF)
 
 
 def out_project(where, att, x, table, blocks, owner):
@@ -318,13 +575,7 @@
     for c in copies:
         c.start()
     depth, width = store.shape[2:]
-    me = where[0]
-    for k in range(dps):
-        piece = gn2_ref[:, k * depth : (k + 1) * depth]
-        for i in range(1, dps):
-            piece = jnp.where(me == i, gn2_ref[:, (i ^ k) * depth : ((i ^ k) + 1) * depth], piece)
-        gr_ref[:, k * depth : (k + 1) * depth] = piece.astype(F32)
-    gn2 = gr_ref[...]
+    gn2 = gn2_ref[...].astype(F32)
     unit, inverse = normalise(r_ref[...])
     gr = g_ref[...].astype(F32) + norm_back(gn2, unit, inverse, vec_ref[5:6, :])
     go = gr.astype(BF)
@@ -438,7 +689,6 @@
     slots, owner, wide, send, recv = head_plan(head_count, seqs, w_qkv.shape[1])
     mine = slots * HD
     ff_mine = w_fc.shape[1]
-    ff_part = ff_mine // dps
     ratio = seqs // dps
     col = w_proj.shape[1]
 
@@ -469,96 +719,72 @@
     parts = jnp.einsum("ac,cnw->naw", w_qkv, to_send, preferred_element_type=F32).astype(BF)
     parts = lax.all_to_all(parts, "seq", 0, 0, tiled=True)
     own_qkv = jnp.einsum("naw,nwd->ad", parts, to_recv, preferred_element_type=F32).astype(BF)
-    wf = jnp.concatenate(gather_rel(w_fc, "dp"), axis=0)
-
-    pieces = w_proj.reshape(ratio, dps, ff_part, col)
-    pieces = lax.all_to_all(pieces.transpose(1, 0, 2, 3), "dp", 0, 0, tiled=True)
-    pieces = lax.all_to_all(pieces.reshape(seqs, ff_part, col), "seq", 0, 0, tiled=True)
-    own_proj = pieces.transpose(1, 0, 2).reshape(ff_part, model)
-    wp_rel = jnp.stack(gather_rel(own_proj, "dp"))
-    wp = jnp.concatenate(
-        [lax.dynamic_index_in_dim(wp_rel, dp ^ k, 0, keepdims=False) for k in range(dps)], axis=0
-    )
+    wf = gather_rel(w_fc, "dp")
+
+    size, start = piece_rows(ff_mine, dps)
+    pieces = w_proj.reshape(ratio, ff_mine, col)
+    pieces = jnp.stack([pieces[:, start(q) : start(q) + size] for q in range(dps)])
+    pieces = lax.all_to_all(pieces, "dp", 0, 0, tiled=True)
+    pieces = lax.all_to_all(pieces.reshape(seqs, size, col), "seq", 0, 0, tiled=True)
+    wp = gather_rel(pieces.transpose(1, 0, 2).reshape(size, model), "dp")
 
     where = jnp.stack([dp, sq]).astype(jnp.int32)
     wo = out_blocks(w_out)
 
-    x = tokens.astype(F32)
-    z1, inv1 = normalise(x)
-    n1 = swap_blocks((z1 * gain1 + shift1).astype(BF), dps, dp)
-    n1, own_qkv = lax.optimization_barrier((n1, own_qkv))
-    n1_all = lax.all_gather(n1, "seq", axis=0, tiled=True)
-    wq = jnp.concatenate(gather_rel(own_qkv, "dp"), axis=0)
-    cot, n1_all = lax.optimization_barrier((cotangent, n1_all))
+    x_all = lax.all_gather(tokens, "seq", axis=0, tiled=True)
+    cot, own_qkv = lax.optimization_barrier((cotangent, own_qkv))
     gm_all = lax.all_gather(cot, "seq", axis=0, tiled=True)
-    qkv = (mm(n1_all, wq) + bias_qkv).astype(BF)
-    att, lse = attend(qkv, slots)
-    att = lax.all_to_all(att.reshape(seqs, rows, mine), "seq", 0, 0, tiled=True)
+    wq = gather_rel(own_qkv, "dp")
+    n1_all, qkv, att, lse = attend(where, x_all, table, bias_qkv[None], wq, slots, rows)
+    att = lax.all_to_all(att, "seq", 0, 0, tiled=True)
     r, n2 = out_project(where, att, tokens, table, wo, owner)
     n2_all = lax.all_gather(n2, "seq", axis=0, tiled=True)
-    u = mm(n2_all, wf) + bias_fc
-    value, slope = gelu_parts(u)
-    e = value.astype(BF)
-
-    gu = (mm_nt(gm_all, wp) * slope).astype(BF)
-    gn2_part = mm_nt(gu, wf).astype(BF)
+
+    e, gu, gn2_part, sum_fc = feed(where, n2_all, gm_all, bias_fc[None], wf, wp)
     gn2 = lax.psum_scatter(gn2_part, "seq", scatter_dimension=0, tiled=True)
-    e, gn2 = lax.optimization_barrier((e, gn2))
-    mlp = lax.psum_scatter(mm(e, wp).astype(BF), "seq", scatter_dimension=0, tiled=True)
+    mlp, d_fc, d_proj = feed_grad(where, n2_all, gm_all, e, gu, wp)
+    gn2, mlp = lax.optimization_barrier((gn2, mlp))
+    mlp = lax.psum_scatter(mlp, "seq", scatter_dimension=0, tiled=True)
     activations = (r + (mlp.astype(F32) + bias_p)).astype(BF)
-    d_proj = mm_tn(e, gm_all)
-    d_fc = mm_tn(n2_all, gu)
-    sum_fc = jnp.sum(gu.astype(F32), axis=0)
 
     gr, go, ga, sums_two = out_back(where, gn2, r, cotangent, table, wo, owner)
     ga = lax.all_to_all(ga, "seq", 0, 0, tiled=True)
-    ga = ga.reshape(seqs * rows, mine)
     d_out = grad_out(where, att, go, dps, owner)
-    gq, gk, gv = attend_back(qkv, ga, lse, slots)
-    gqkv = jnp.concatenate([gq, gk, gv], axis=1)
-    gn1_full = mm_nt(gqkv, wq)
-    gn1 = lax.psum_scatter(gn1_full.astype(BF), "seq", scatter_dimension=0, tiled=True)
-    gn1 = swap_blocks(gn1, dps, dp).astype(F32)
-    d_qkv = mm_tn(n1_all, gqkv)
-    input_grad = (gr + norm_back(gn1, z1, inv1, gain1)).astype(BF)
-
-    def row_chunks(matrix):
-        size = matrix.shape[0] // dps
-        return [matrix[k * size : (k + 1) * size].astype(BF) for k in range(dps)]
-
-    g_fc = scatter_rel(row_chunks(d_fc), "dp")
-    g_qkv = scatter_rel(row_chunks(d_qkv), "dp").astype(BF)
+    gqkv, gn1_part = attend_back(where, qkv, ga, lse, wq)
+    gn1 = lax.psum_scatter(gn1_part, "seq", scatter_dimension=0, tiled=True)
+    d_qkv, gqkv_sums, norm_sums = grad_qkv(where, n1_all, gqkv, gn1_part, dps)
+    input_grad = last_norm(gn1, tokens, gr, table)
+
+    g_fc = scatter_rel(d_fc, "dp")
+    g_qkv = scatter_rel(d_qkv, "dp").astype(BF)
     parts = jnp.einsum("ad,nwd->naw", g_qkv, to_recv, preferred_element_type=F32).astype(BF)
     parts = lax.all_to_all(parts, "seq", 0, 0, tiled=True)
     g_qkv = jnp.einsum("naw,cnw->ac", parts, to_send, preferred_element_type=F32)
 
-    chunks = [
-        lax.dynamic_slice_in_dim(d_proj, (dp ^ k) * ff_part, ff_part, axis=0).astype(BF)
-        for k in range(dps)
-    ]
-    g_proj = scatter_rel(chunks, "dp").astype(BF)
-    g_proj = g_proj.reshape(ff_part, seqs, col).transpose(1, 0, 2)
+    g_proj = scatter_rel(d_proj, "dp").astype(BF)
+    g_proj = g_proj.reshape(size, seqs, col).transpose(1, 0, 2)
     g_proj = lax.all_to_all(g_proj, "seq", 0, 0, tiled=True)
-    g_proj = g_proj.reshape(dps, ratio, ff_part, col)
+    g_proj = g_proj.reshape(dps, ratio, size, col)
     g_proj = lax.all_to_all(g_proj, "dp", 0, 0, tiled=True)
-    g_proj = g_proj.transpose(1, 0, 2, 3).reshape(w_proj.shape).astype(F32)
+    ends = [start(q) for q in range(dps)] + [ff_mine]
+    g_proj = jnp.concatenate(
+        [g_proj[q, :, : ends[q + 1] - ends[q]] for q in range(dps)], axis=1
+    )
+    g_proj = g_proj.reshape(w_proj.shape).astype(F32)
 
     g_out = sum_out_blocks(d_out)
 
-    gqkv_sums = jnp.sum(gqkv.astype(F32), axis=0)
-    both = jnp.stack([jnp.sum(gn1_full * n1_all.astype(F32), axis=0), jnp.sum(gn1_full, axis=0)])
-    both = swap_blocks(both, dps, dp)
     vector_grads = jnp.concatenate(
         [
-            ((both[0] - shift1 * both[1]) / gain1)[None],
-            both[1:],
-            head_spread(gqkv_sums[:mine])[None],
-            head_spread(gqkv_sums[2 * mine :])[None],
+            ((norm_sums[0] - shift1 * norm_sums[1]) / gain1)[None],
+            norm_sums[1:],
+            head_spread(gqkv_sums[0, :mine])[None],
+            head_spread(gqkv_sums[0, 2 * mine :])[None],
             sums_two,
         ]
     )
     fc_sums = lax.dynamic_update_slice_in_dim(
-        jnp.zeros((dps * seqs * b_fc.shape[0],), F32), sum_fc, sq * ff_mine, axis=0
+        jnp.zeros((dps * seqs * b_fc.shape[0],), F32), sum_fc[0], sq * ff_mine, axis=0
     ).reshape(-1, model)
     sums = sum_all(jnp.concatenate([vector_grads, fc_sums]))
     own_vec = lax.dynamic_slice(sums, (dp * per, sq * wide_vec), (per, wide_vec))

time: 627 us -> 611 us (0.974)
  local copies, waits for them, and re-layouts: 137 us -> 35.7 us
  waiting for transfers between devices: 216 us -> 290 us
  Pallas kernels: 48.6 us -> 112 us
  matrix products: 68.9 us -> 7.91 us
  blocking collectives: 15.2 us -> 44.1 us
  other arithmetic: 28.1 us -> 16.3 us
  starting transfers between devices: 88.4 us -> 79.3 us
    pallas_call x2 -> x6, Pallas kernels: 19.1 us -> 91.3 us  [the longest x1 22 us: feed_grad(): pl.pallas_call(functools.partial(feed_grad_kernel, dps), in_specs=[SCALAR...]
    dot_general x9 -> x0, matrix products: 59.6 us -> none  [the longest x3 22.5 us: mm(): return jnp.dot(a, b, preferred_element_type=F32)]
    ppermute x12, waiting for transfers between devices: 23.1 us -> 80.8 us  [gather_rel(): lax.ppermute(block, axis, xor_perm(count, k))]
    all_to_all x2, waiting for transfers between devices: 0.01 us -> 41.8 us  [body(): parts = lax.all_to_all(parts, 'seq', 0, 0, tiled=True)]
    ppermute x12, waiting for transfers between devices: 29.6 us -> 69.3 us  [scatter_rel(): lax.ppermute(chunks[k], axis, xor_perm(count, k)).astype(F32)]
    ppermute x5, waiting for transfers between devices: 0.99 us -> 37.8 us  [sum_all(): lax.ppermute(block, axis, xor_perm(lax.axis_size(axis), step))]
    convert_element_type x6 -> x2, local copies, waits for them, and re-layouts: 32.5 us -> 2.76 us  [body(): g_proj = g_proj.reshape(w_proj.shape).astype(F32)]
    ppermute x3, waiting for transfers between devices: 31.4 us -> 2.07 us  [out_blocks(): lax.ppermute(w_out, 'seq', xor_perm(seqs, 2 * dz))]
  transfers between devices with their start and end apart: 61 -> 60, of which waited for: 25 -> 24; matrix products, arithmetic and copies ran while one was open for 26% -> 8% of each run, Pallas kernels for 6% -> 15%
where the time goes in v3:
time: 611 us; the launch traced here: 601 us
  waiting for transfers between devices  290 us (47%)
  Pallas kernels  112 us (18%)
  starting transfers between devices  79.3 us (13%)
  blocking collectives  44.1 us (7%)
  local copies, waits for them, and re-layouts  35.7 us (6%)
  other arithmetic  16.3 us (3%)
  between operations  15.3 us (3%)
  matrix products  7.91 us (1%)
    ppermute x12, waiting for transfers between devices, gather_rel(): lax.ppermute(block, axis, xor_perm(count, k))  80.8 us
    ppermute x12, waiting for transfers between devices, scatter_rel(): lax.ppermute(chunks[k], axis, xor_perm(count, k)).astype(F32)  69.3 us
    all_to_all x2, waiting for transfers between devices, body(): parts = lax.all_to_all(parts, 'seq', 0, 0, tiled=True)  41.8 us
    ppermute x5, waiting for transfers between devices, sum_all(): lax.ppermute(block, axis, xor_perm(lax.axis_size(axis), step))  37.8 us
    all_to_all x1, waiting for transfers between devices, body(): lax.all_to_all(pieces.reshape(seqs, size, col), 'seq', 0, 0, tiled=True)  28.8 us
    all_to_all x1, blocking collectives, body(): ga = lax.all_to_all(ga, 'seq', 0, 0, tiled=True)  28.3 us
    pallas_call x1, Pallas kernels, feed_grad(): pl.pallas_call(functools.partial(feed_grad_kernel, dps), in_specs=[SCALAR...  22 us
    pallas_call x1, Pallas kernels, feed(): pl.pallas_call(functools.partial(feed_kernel, dps), grid=(length // rows,...  21.7 us
  transfers between devices with their start and end apart: 60, of which 24 were waited for; matrix products, arithmetic and copies ran while one was open for 8% of the time, Pallas kernels for 15%

profile of v3, /device:TPU:0, one launch (start us, length us, event | category | flops | bytes accessed | tf_op | source)
XLA Modules:
  0.0 600.9 jit_solution(12260617235518442389)
XLA Ops:
  11.7 6.3 %all-to-all-start = ((bf16[8,400,128]{2,1,0:T(8,128)(2,1)}), bf16[8,400,128]{2,1,0:T(8,128)(2,1)S(1)}, u32[]{:S(2)}, u32[]{:S(2)}) async-start(bf16[8,400,128]{2,1,0:T(8,128)(2,1)} %fusion.11), calls=%async_computation | async-start | bytes 1638400 | tf_op jit(solution)/shard_map/all_to_all | solution.py:720
  18.8 41.8 %all-to-all-done = bf16[8,400,128]{2,1,0:T(8,128)(2,1)S(1)} async-done(((bf16[8,400,128]{2,1,0:T(8,128)(2,1)}), bf16[8,400,128]{2,1,0:T(8,128)(2,1)S(1)}, u32[]{:S(2)}, u32[]{:S(2)}) %all-to-all-start) | async-done | bytes 819232 | tf_op jit(solution)/shard_map/all_to_all | solution.py:720
  63.2 3.8 collective-permute-start.8
  97.9 11.8 %collective-permute-done.6.rest_2_ = bf16[400,768]{1,0:T(8,128)(2,1)} collective-permute-done((bf16[400,768]{1,0:T(8,128)(2,1)S(1)}, bf16[400,768]{1,0:T(8,128)(2,1)}, u32[]{:S(2)}, u32[]{:S(2)}) %collective-permute-start.6) | collective-permute-done | bytes 614432 | tf_op jit(solution)/shard_map/ppermute | solution.py:65
  109.8 16.6 %shard_map.170 = (bf16[1024,1600]{1,0:T(8,128)(2,1)}, bf16[1024,768]{1,0:T(8,128)(2,1)}, bf16[8,128,256]{2,1,0:T(8,128)(2,1)}, f32[1024,256]{1,0:T(8,128)}) custom-call(s32[2]{0:T(128)} %pad_add_fusion.where, bf16[1024,1600]{1,0:T(8,128)(2,1)} %all-gather.4.cloned.1.call-done.x_ref, f32[8,1600]{1,0:T(8,128)} %copy-done.16, ...), custom_call_target="tpu_custom_call" | custom-call | tf_op jit(solution)/shard_map/pallas_call | solution.py:228
  126.4 3.5 all-to-all-start.1
  130.7 12.3 %collective-permute-done.14.rest_4_ = bf16[4,400,200]{2,1,0:T(8,128)(2,1)S(1)} collective-permute-done((bf16[4,400,200]{2,1,0:T(8,128)(2,1)S(1)}, bf16[4,400,200]{2,1,0:T(8,128)(2,1)S(1)}, u32[]{:S(2)}, u32[]{:S(2)}) %collective-permute-start.14) | collective-permute-done | bytes 640032 | tf_op jit(solution)/shard_map/ppermute | solution.py:65
  147.7 6.9 %shard_map.171 = (f32[128,1600]{1,0:T(8,128)}, bf16[128,1600]{1,0:T(8,128)(2,1)}) custom-call(s32[2]{0:T(128)} %pad_add_fusion.where, bf16[8,128,256]{2,1,0:T(8,128)(2,1)} %copy-done.4, bf16[128,1600]{1,0:T(8,128)(2,1)} %copy.79.x_ref, f32[8,1600]{1,0:T(8,128)} %copy-done.16, bf16[4,400,200]{2,1,0:T(8,128)(2,1)} %copy-done.2, ...), custom_call_target="tpu_custom_call" | custom-call | tf_op jit(solution)/shard_map/pallas_call | solution.py:557
  159.6 15.8 %all_to_all.40 = bf16[4,2,208,200]{2,1,3,0:T(2,128)(2,1)S(1)} all-to-all(bf16[4,2,208,200]{2,1,3,0:T(2,128)(2,1)S(1)} %pad_maximum_fusion.1), channel_id=1, replica_groups=mesh['dp'=4,'seq'=8] {'dp'}, dimensions={0} | all-to-all | bytes 1331200 | tf_op jit(solution)/shard_map/all_to_all | solution.py:727
  176.4 3.5 all-to-all-start.3
  180.7 28.8 %all-to-all-done.3 = bf16[8,208,200]{1,2,0:T(8,128)(2,1)S(1)} async-done(((bf16[8,208,200]{1,2,0:T(8,128)(2,1)}), bf16[8,208,200]{1,2,0:T(8,128)(2,1)S(1)}, u32[]{:S(2)}, u32[]{:S(2)}) %all-to-all-start.3) | async-done | bytes 665632 | tf_op jit(solution)/shard_map/all_to_all | solution.py:728
  219.3 54.9 %collective-permute-done.19.rest_2_ = bf16[400,800]{1,0:T(8,128)(2,1)} collective-permute-done((bf16[400,800]{1,0:T(8,128)(2,1)S(1)}, bf16[400,800]{1,0:T(8,128)(2,1)}, u32[]{:S(2)}, u32[]{:S(2)}) %collective-permute-start.19) | collective-permute-done | bytes 640032 | tf_op jit(solution)/shard_map/ppermute | solution.py:65
  275.6 21.7 %shard_map.172 = (bf16[1024,800]{1,0:T(8,128)(2,1)}, bf16[1024,800]{1,0:T(8,128)(2,1)}, bf16[1024,1600]{1,0:T(8,128)(2,1)}, f32[1,800]{1,0:T(1,128)}) custom-call(s32[2]{0:T(128)} %pad_add_fusion.where, bf16[1024,1600]{1,0:T(8,128)(2,1)} %all-gather.6.cloned.1.call-done.n2_ref, bf16[1024,1600]{1,0:T(8,128)(2,1)} %all-gather.8.cloned.1.call-done.gm_ref, ...), custom_call_target="tpu_custom_call" | custom-call | tf_op jit(solution)/shard_map/pallas_call | solution.py:403
  297.8 22.0 %shard_map.173 = (bf16[1024,1600]{1,0:T(8,128)(2,1)}, bf16[400,800]{1,0:T(8,128)(2,1)}, bf16[400,800]{1,0:T(8,128)(2,1)}, bf16[400,800]{1,0:T(8,128)(2,1)}, bf16...) custom-call(s32[2]{0:T(128)} %pad_add_fusion.where, ...), custom_call_target="tpu_custom_call" | custom-call | tf_op jit(solution)/shard_map/pallas_call | solution.py:468
  319.8 18.2 %reduce-scatter.4.cloned.1.call-done.gn2_ref = bf16[128,1600]{1,0:T(8,128)(2,1)} async-done(((bf16[1024,1600]{1,0:T(8,128)(2,1)}), bf16[128,1600]{1,0:T(8,128)(2,1)}) %reduce-scatter.4.cloned.1.call-update) | async-done | bytes 409616 | tf_op jit(solution)/shard_map/reduce_scatter | solution.py:744
  340.1 7.8 %shard_map.174 = (f32[128,1600]{1,0:T(8,128)}, bf16[128,1600]{1,0:T(8,128)(2,1)}, bf16[8,128,256]{2,1,0:T(8,128)(2,1)}, f32[4,1600]{1,0:T(4,128)}) custom-call(s32[2]{0:T(128)} %pad_add_fusion.where, bf16[128,1600]{1,0:T(8,128)(2,1)} %reduce-scatter.4.cloned.1.call-done.gn2_ref, f32[128,1600]{1,0:T(8,128)} %get-tuple-element.53.r_ref, ...), custom_call_target="tpu_custom_call" | custom-call | tf_op jit(solution)/shard_map/pallas_call | solution.py:607
  347.8 28.3 %all_to_all.41.ga_ref = bf16[8,128,256]{2,1,0:T(8,128)(2,1)} all-to-all(bf16[8,128,256]{2,1,0:T(8,128)(2,1)} %get-tuple-element.63), channel_id=1, replica_groups=mesh['dp'=4,'seq'=8] {'seq'}, dimensions={0} | all-to-all | bytes 1048576 | tf_op jit(solution)/shard_map/all_to_all | solution.py:751
  376.1 18.6 %shard_map.175 = (bf16[1024,768]{1,0:T(8,128)(2,1)}, bf16[1024,1600]{1,0:T(8,128)(2,1)}) custom-call(s32[2]{0:T(128)} %pad_add_fusion.where, bf16[1024,768]{1,0:T(8,128)(2,1)} %get-tuple-element.61.qkv_ref, bf16[8,128,256]{2,1,0:T(8,128)(2,1)} %all_to_all.41.ga_ref, f32[1024,256]{1,0:T(8,128)} %get-tuple-element.64.lse_ref, bf16[400,768]{1,0:T(8,128)(2,1)} %copy-done.14, ...), custom_call_target="tpu_custom_call" | custom-call | tf_op jit(solution)/shard_map/pallas_call | solution.py:307
  399.3 15.9 %collective-permute-done.47 = bf16[208,1600]{1,0:T(8,128)(2,1)S(1)} collective-permute-done((bf16[208,1600]{1,0:T(8,128)(2,1)S(1)}, bf16[208,1600]{1,0:T(8,128)(2,1)S(1)}, u32[]{:S(2)}, u32[]{:S(2)}) %collective-permute-start.47) | collective-permute-done | bytes 665632 | tf_op jit(solution)/shard_map/ppermute | solution.py:72
  415.2 13.5 %collective-permute-done.46 = bf16[208,1600]{1,0:T(8,128)(2,1)S(1)} collective-permute-done((bf16[208,1600]{1,0:T(8,128)(2,1)S(1)}, bf16[208,1600]{1,0:T(8,128)(2,1)S(1)}, u32[]{:S(2)}, u32[]{:S(2)}) %collective-permute-start.46) | collective-permute-done | bytes 665632 | tf_op jit(solution)/shard_map/ppermute | solution.py:72
  432.2 4.2 all-to-all-start.6
  438.7 6.3 %shard_map.178 = (bf16[4,400,200]{2,1,0:T(8,128)(2,1)}, bf16[4,400,200]{2,1,0:T(8,128)(2,1)}, bf16[4,400,200]{2,1,0:T(8,128)(2,1)}, bf16[4,400,200]{2,1,0:T(8,12...) custom-call(s32[2]{0:T(128)} %pad_add_fusion.where, ...), custom_call_target="tpu_custom_call" | custom-call | tf_op jit(solution)/shard_map/pallas_call | solution.py:646
  445.6 9.6 %shard_map.177 = (bf16[400,768]{1,0:T(8,128)(2,1)}, bf16[400,768]{1,0:T(8,128)(2,1)}, bf16[400,768]{1,0:T(8,128)(2,1)}, bf16[400,768]{1,0:T(8,128)(2,1)}, f32[1,768]{1,0:T(1,128)}, /*index=5*/f32[2,1600]{1,0:T(2,128)}) custom-call(s32[2]{0:T(128)} %pad_add_fusion.where, bf16[1024,1600]{1,0:T(8,128)(2,1)} %get-tuple-element.67.n1_ref, ...), custom_call_target="tpu_custom_call" | custom-call | tf_op jit(solution)/shard_map/pallas_call | solution.py:349
  460.2 3.7 all-to-all-start.7
  469.9 12.5 %collective-permute-done.43 = bf16[400,800]{1,0:T(8,128)(2,1)} collective-permute-done((bf16[400,800]{1,0:T(8,128)(2,1)}, bf16[400,800]{1,0:T(8,128)(2,1)}, u32[]{:S(2)}, u32[]{:S(2)}) %collective-permute-start.43) | collective-permute-done | bytes 640032 | tf_op jit(solution)/shard_map/ppermute | solution.py:72
  486.7 5.1 collective-permute-done.42
  491.8 22.2 %collective-permute-done.38 = f32[12,1600]{1,0:T(8,128)S(1)} collective-permute-done((f32[12,1600]{1,0:T(8,128)S(1)}, f32[12,1600]{1,0:T(8,128)S(1)}, u32[]{:S(2)}, u32[]{:S(2)}) %collective-permute-start.38) | collective-permute-done | bytes 76832 | tf_op jit(solution)/shard_map/ppermute | solution.py:677
  522.5 5.2 all-to-all-start.5
  529.8 6.7 %collective-permute-done.33 = bf16[4,400,200]{2,1,0:T(8,128)(2,1)} collective-permute-done((bf16[4,400,200]{2,1,0:T(8,128)(2,1)}, bf16[4,400,200]{2,1,0:T(8,128)(2,1)}, u32[]{:S(2)}, u32[]{:S(2)}) %collective-permute-start.33) | collective-permute-done | bytes 640032 | tf_op jit(solution)/shard_map/ppermute | solution.py:72
  536.5 15.6 %collective-permute-done.31 = bf16[4,400,200]{2,1,0:T(8,128)(2,1)} collective-permute-done((bf16[4,400,200]{2,1,0:T(8,128)(2,1)}, bf16[4,400,200]{2,1,0:T(8,128)(2,1)}, u32[]{:S(2)}, u32[]{:S(2)}) %collective-permute-start.31) | collective-permute-done | bytes 640032 | tf_op jit(solution)/shard_map/ppermute | solution.py:72
  556.1 3.7 collective-permute-start.36
  566.0 15.5 %collective-permute-done.41 = f32[12,1600]{1,0:T(8,128)S(1)} collective-permute-done((f32[12,1600]{1,0:T(8,128)S(1)}, f32[12,1600]{1,0:T(8,128)S(1)}, u32[]{:S(2)}, u32[]{:S(2)}) %collective-permute-start.41) | collective-permute-done | bytes 76832 | tf_op jit(solution)/shard_map/ppermute | solution.py:677
  (276 shorter events, 123.2 us)
Async XLA Ops:
  7.2 102.6 %all-gather.4.cloned.1.call-start = ((), (), s32[]{:S(2)}) async-start(), calls=%async_computation.11 | async-start | bytes 3833856 | tf_op jit(solution)/shard_map/all_gather | solution.py:734
  11.7 48.8 %all-to-all-start = ((bf16[8,400,128]{2,1,0:T(8,128)(2,1)}), bf16[8,400,128]{2,1,0:T(8,128)(2,1)S(1)}, u32[]{:S(2)}, u32[]{:S(2)}) async-start(bf16[8,400,128]{2,1,0:T(8,128)(2,1)} %fusion.11), calls=%async_computation | async-start | bytes 1638400 | tf_op jit(solution)/shard_map/all_to_all | solution.py:720
  18.1 256.2 %all-gather.8.cloned.1.call-start = ((), (), s32[]{:S(2)}) async-start(), calls=%async_computation.13 | async-start | bytes 3833856 | tf_op jit(solution)/shard_map/all_gather | solution.py:736
  79.6 30.1 %collective-permute-start.6 = (bf16[400,768]{1,0:T(8,128)(2,1)S(1)}, bf16[400,768]{1,0:T(8,128)(2,1)}, u32[]{:S(2)}, u32[]{:S(2)}) collective-permute-start(bf16[400,768]{1,0:T(8,128)(2,1)S(1)} %fusion.10.rest_0_), channel_id=1, source_target_pairs={{0,16},{8,24},{16,0},{24,8},{1,17},{9,25},{17,1},{25,9},{2,18},{10... | collective-permute-start | bytes 1843208 | tf_op jit(solution)/shard_map/ppermute | solution.py:65
  81.3 28.5 %collective-permute-start.7 = (bf16[400,768]{1,0:T(8,128)(2,1)S(1)}, bf16[400,768]{1,0:T(8,128)(2,1)}, u32[]{:S(2)}, u32[]{:S(2)}) collective-permute-start(bf16[400,768]{1,0:T(8,128)(2,1)S(1)} %fusion.10.rest_0_), channel_id=1, source_target_pairs={{0,24},{8,16},{16,8},{24,0},{1,25},{9,17},{17,9},{25,1},{2,26},{10... | collective-permute-start | bytes 1843208 | tf_op jit(solution)/shard_map/ppermute | solution.py:65
  85.0 45.6 %collective-permute-start.12 = (bf16[4,400,200]{2,1,0:T(8,128)(2,1)S(1)}, bf16[4,400,200]{2,1,0:T(8,128)(2,1)S(1)}, u32[]{:S(2)}, u32[]{:S(2)}) collective-permute-start(bf16[4,400,200]{2,1,0:T(8,128)(2,1)S(1)} %pad_maximum_fusion.rest_0_), channel_id=1, source_target_pairs={{0,8},{8,0},{16,24},{24,16},{1,9},{9,1},{17,25},{25,17},{2,10},{10... | collective-permute-start | bytes 1920008 | tf_op jit(solution)/shard_map/ppermute | solution.py:65
  89.5 53.6 %collective-permute-start.14 = (bf16[4,400,200]{2,1,0:T(8,128)(2,1)S(1)}, bf16[4,400,200]{2,1,0:T(8,128)(2,1)S(1)}, u32[]{:S(2)}, u32[]{:S(2)}) collective-permute-start(bf16[4,400,200]{2,1,0:T(8,128)(2,1)S(1)} %pad_maximum_fusion.rest_0_), channel_id=1, source_target_pairs={{0,16},{8,24},{16,0},{24,8},{1,17},{9,25},{17,1},{25,9},{2,18},{10... | collective-permute-start | bytes 1920008 | tf_op jit(solution)/shard_map/ppermute | solution.py:65
  93.4 49.6 %collective-permute-start.16 = (bf16[4,400,200]{2,1,0:T(8,128)(2,1)S(1)}, bf16[4,400,200]{2,1,0:T(8,128)(2,1)}, u32[]{:S(2)}, u32[]{:S(2)}) collective-permute-start(bf16[4,400,200]{2,1,0:T(8,128)(2,1)S(1)} %pad_maximum_fusion.rest_0_), channel_id=1, source_target_pairs={{0,24},{8,16},{16,8},{24,0},{1,25},{9,17},{17,9},{25,1},{2,26},{10... | collective-permute-start | bytes 1920008 | tf_op jit(solution)/shard_map/ppermute | solution.py:65
  129.9 144.5 %all-gather.6.cloned.1.call-start = ((), (), s32[]{:S(2)}) async-start(), calls=%async_computation.12 | async-start | bytes 3833856 | tf_op jit(solution)/shard_map/all_gather | solution.py:741
  176.4 33.1 %all-to-all-start.3 = ((bf16[8,208,200]{1,2,0:T(8,128)(2,1)}), bf16[8,208,200]{1,2,0:T(8,128)(2,1)S(1)}, u32[]{:S(2)}, u32[]{:S(2)}) async-start(bf16[8,208,200]{1,2,0:T(8,128)(2,1)} %bitcast.32), calls=%async_computation.3 | async-start | bytes 1638400 | tf_op jit(solution)/shard_map/all_to_all | solution.py:728
  180.0 158.1 %reduce-scatter.4.cloned.1.call-start = ((), (), s32[]{:S(2)}) async-start(), calls=%async_computation.14 | async-start | bytes 3833856 | tf_op jit(solution)/shard_map/reduce_scatter | solution.py:744
  180.0 34.9 %collective-permute-start.18 = (bf16[400,800]{1,0:T(8,128)(2,1)S(1)}, bf16[400,800]{1,0:T(8,128)(2,1)}, u32[]{:S(2)}, u32[]{:S(2)}) collective-permute-start(bf16[400,800]{1,0:T(8,128)(2,1)S(1)} %copy-done.24), channel_id=1, source_target_pairs={{0,8},{8,0},{16,24},{24,16},{1,9},{9,1},{17,25},{25,17},{2,10},{10... | collective-permute-start | bytes 1920008 | tf_op jit(solution)/shard_map/ppermute | solution.py:65
  209.9 64.4 %collective-permute-start.21 = (bf16[208,1600]{1,0:T(8,128)(2,1)S(1)}, bf16[208,1600]{1,0:T(8,128)(2,1)S(1)}, u32[]{:S(2)}, u32[]{:S(2)}) collective-permute-start(bf16[208,1600]{1,0:T(8,128)(2,1)S(1)} %copy.98.rest_4_.rest_0_), channel_id=1, source_target_pairs={{0,8},{8,0},{16,24},{24,16},{1,9},{9,1},{17,25},{25,17},{2,10},{10... | collective-permute-start | bytes 1996808 | tf_op jit(solution)/shard_map/ppermute | solution.py:65
  211.4 62.8 %collective-permute-start.22 = (bf16[208,1600]{1,0:T(8,128)(2,1)S(1)}, bf16[208,1600]{1,0:T(8,128)(2,1)S(1)}, u32[]{:S(2)}, u32[]{:S(2)}) collective-permute-start(bf16[208,1600]{1,0:T(8,128)(2,1)S(1)} %copy.98.rest_4_.rest_0_), channel_id=1, source_target_pairs={{0,16},{8,24},{16,0},{24,8},{1,17},{9,25},{17,1},{25,9},{2,18},{10... | collective-permute-start | bytes 1996808 | tf_op jit(solution)/shard_map/ppermute | solution.py:65
  212.9 61.4 %collective-permute-start.23 = (bf16[208,1600]{1,0:T(8,128)(2,1)S(1)}, bf16[208,1600]{1,0:T(8,128)(2,1)S(1)}, u32[]{:S(2)}, u32[]{:S(2)}) collective-permute-start(bf16[208,1600]{1,0:T(8,128)(2,1)S(1)} %copy.98.rest_4_.rest_0_), channel_id=1, source_target_pairs={{0,24},{8,16},{16,8},{24,0},{1,25},{9,17},{17,9},{25,1},{2,26},{10... | collective-permute-start | bytes 1996808 | tf_op jit(solution)/shard_map/ppermute | solution.py:65
  213.4 60.8 %collective-permute-start.19 = (bf16[400,800]{1,0:T(8,128)(2,1)S(1)}, bf16[400,800]{1,0:T(8,128)(2,1)}, u32[]{:S(2)}, u32[]{:S(2)}) collective-permute-start(bf16[400,800]{1,0:T(8,128)(2,1)S(1)} %copy-done.24), channel_id=1, source_target_pairs={{0,16},{8,24},{16,0},{24,8},{1,17},{9,25},{17,1},{25,9},{2,18},{10... | collective-permute-start | bytes 1920008 | tf_op jit(solution)/shard_map/ppermute | solution.py:65
  214.9 59.3 %collective-permute-start.20 = (bf16[400,800]{1,0:T(8,128)(2,1)S(1)}, bf16[400,800]{1,0:T(8,128)(2,1)}, u32[]{:S(2)}, u32[]{:S(2)}) collective-permute-start(bf16[400,800]{1,0:T(8,128)(2,1)S(1)} %copy-done.24), channel_id=1, source_target_pairs={{0,24},{8,16},{16,8},{24,0},{1,25},{9,17},{17,9},{25,1},{2,26},{10... | collective-permute-start | bytes 1920008 | tf_op jit(solution)/shard_map/ppermute | solution.py:65
  297.4 289.5 %reduce-scatter.6.cloned.1.call-start = ((), (), s32[]{:S(2)}) async-start(), calls=%async_computation.15 | async-start | bytes 3833856 | tf_op jit(solution)/shard_map/reduce_scatter | solution.py:747
  338.1 250.8 %reduce-scatter.8.cloned.1.call-start = ((), (), s32[]{:S(2)}) async-start(), calls=%async_computation.16 | async-start | bytes 3833856 | tf_op jit(solution)/shard_map/reduce_scatter | solution.py:754
  398.1 30.5 %collective-permute-start.46 = (bf16[208,1600]{1,0:T(8,128)(2,1)S(1)}, bf16[208,1600]{1,0:T(8,128)(2,1)S(1)}, u32[]{:S(2)}, u32[]{:S(2)}) collective-permute-start(bf16[208,1600]{1,0:T(8,128)(2,1)S(1)} %copy-done.36), channel_id=1, source_target_pairs={{0,16},{8,24},{16,0},{24,8},{1,17},{9,25},{17,1},{25,9},{2,18},{10... | collective-permute-start | bytes 1996808 | tf_op jit(solution)/shard_map/ppermute | solution.py:72
  398.7 30.0 %collective-permute-start.45 = (bf16[208,1600]{1,0:T(8,128)(2,1)S(1)}, bf16[208,1600]{1,0:T(8,128)(2,1)S(1)}, u32[]{:S(2)}, u32[]{:S(2)}) collective-permute-start(bf16[208,1600]{1,0:T(8,128)(2,1)S(1)} %copy-done.35), channel_id=1, source_target_pairs={{0,8},{8,0},{16,24},{24,16},{1,9},{9,1},{17,25},{25,17},{2,10},{10... | collective-permute-start | bytes 1996808 | tf_op jit(solution)/shard_map/ppermute | solution.py:72
  460.2 62.3 %all-to-all-start.7 = ((bf16[4,2,208,200]{2,3,1,0:T(8,128)(2,1)}), bf16[4,2,208,200]{2,3,1,0:T(8,128)(2,1)S(1)}, u32[]{:S(2)}, u32[]{:S(2)}) async-start(bf16[4,2,208,200]{2,3,1,0:T(8,128)(2,1)} %bitcast.44), calls=%async_computation.10 | async-start | bytes 1638400 | tf_op jit(solution)/shard_map/all_to_all | solution.py:768
  464.0 27.9 %collective-permute-start.42 = (bf16[400,800]{1,0:T(8,128)(2,1)}, bf16[400,800]{1,0:T(8,128)(2,1)S(1)}, u32[]{:S(2)}, u32[]{:S(2)}) collective-permute-start(bf16[400,800]{1,0:T(8,128)(2,1)} %get-tuple-element.87), channel_id=1, source_target_pairs={{0,8},{8,0},{16,24},{24,16},{1,9},{9,1},{17,25},{25,17},{2,10},{10... | collective-permute-start | bytes 1920008 | tf_op jit(solution)/shard_map/ppermute | solution.py:72
  466.0 49.6 %collective-permute-start.26 = (bf16[400,768]{1,0:T(8,128)(2,1)}, bf16[400,768]{1,0:T(8,128)(2,1)S(1)}, u32[]{:S(2)}, u32[]{:S(2)}) collective-permute-start(bf16[400,768]{1,0:T(8,128)(2,1)} %get-tuple-element.72), channel_id=1, source_target_pairs={{0,24},{8,16},{16,8},{24,0},{1,25},{9,17},{17,9},{25,1},{2,26},{10... | collective-permute-start | bytes 1843208 | tf_op jit(solution)/shard_map/ppermute | solution.py:72
  467.5 48.9 %collective-permute-start.25 = (bf16[400,768]{1,0:T(8,128)(2,1)}, bf16[400,768]{1,0:T(8,128)(2,1)S(1)}, u32[]{:S(2)}, u32[]{:S(2)}) collective-permute-start(bf16[400,768]{1,0:T(8,128)(2,1)} %get-tuple-element.71), channel_id=1, source_target_pairs={{0,16},{8,24},{16,0},{24,8},{1,17},{9,25},{17,1},{25,9},{2,18},{10... | collective-permute-start | bytes 1843208 | tf_op jit(solution)/shard_map/ppermute | solution.py:72
  482.4 37.9 %collective-permute-start.24 = (bf16[400,768]{1,0:T(8,128)(2,1)S(1)}, bf16[400,768]{1,0:T(8,128)(2,1)S(1)}, u32[]{:S(2)}, u32[]{:S(2)}) collective-permute-start(bf16[400,768]{1,0:T(8,128)(2,1)S(1)} %copy-done.39), channel_id=1, source_target_pairs={{0,8},{8,0},{16,24},{24,16},{1,9},{9,1},{17,25},{25,17},{2,10},{10... | collective-permute-start | bytes 1843208 | tf_op jit(solution)/shard_map/ppermute | solution.py:72
  483.2 30.9 %collective-permute-start.38 = (f32[12,1600]{1,0:T(8,128)S(1)}, f32[12,1600]{1,0:T(8,128)S(1)}, u32[]{:S(2)}, u32[]{:S(2)}) collective-permute-start(f32[12,1600]{1,0:T(8,128)S(1)} %add.132), channel_id=1, source_target_pairs={{0,16},{8,24},{16,0},{24,8},{1,17},{9,25},{17,1},{25,9},{2,18},{10... | collective-permute-start | bytes 230408 | tf_op jit(solution)/shard_map/ppermute | solution.py:677
  491.8 38.0 %collective-permute-start.27 = (bf16[4,400,200]{2,1,0:T(8,128)(2,1)}, bf16[4,400,200]{2,1,0:T(8,128)(2,1)}, u32[]{:S(2)}, u32[]{:S(2)}) collective-permute-start(bf16[4,400,200]{2,1,0:T(8,128)(2,1)} %get-tuple-element.75), channel_id=1, source_target_pairs={{0,1},{1,0},{2,3},{3,2},{4,5},{5,4},{6,7},{7,6},{8,9},{9,8},{10,11... | collective-permute-start | bytes 1920008 | tf_op jit(solution)/shard_map/ppermute | solution.py:663
  515.6 36.5 %collective-permute-start.31 = (bf16[4,400,200]{2,1,0:T(8,128)(2,1)}, bf16[4,400,200]{2,1,0:T(8,128)(2,1)}, u32[]{:S(2)}, u32[]{:S(2)}) collective-permute-start(bf16[4,400,200]{2,1,0:T(8,128)(2,1)} %add_convert_fusion.2), channel_id=1, source_target_pairs={{0,16},{8,24},{16,0},{24,8},{1,17},{9,25},{17,1},{25,9},{2,18},{10... | collective-permute-start | bytes 1920008 | tf_op jit(solution)/shard_map/ppermute | solution.py:72
  516.4 35.7 %collective-permute-start.29 = (bf16[4,400,200]{2,1,0:T(8,128)(2,1)}, bf16[4,400,200]{2,1,0:T(8,128)(2,1)S(1)}, u32[]{:S(2)}, u32[]{:S(2)}) collective-permute-start(bf16[4,400,200]{2,1,0:T(8,128)(2,1)} %add_convert_fusion.3), channel_id=1, source_target_pairs={{0,8},{8,0},{16,24},{24,16},{1,9},{9,1},{17,25},{25,17},{2,10},{10... | collective-permute-start | bytes 1920008 | tf_op jit(solution)/shard_map/ppermute | solution.py:72
  522.5 61.3 %all-to-all-start.5 = ((bf16[8,400,128]{2,1,0:T(8,128)(2,1)}), bf16[8,400,128]{2,1,0:T(8,128)(2,1)}, u32[]{:S(2)}, u32[]{:S(2)}) async-start(bf16[8,400,128]{2,1,0:T(8,128)(2,1)} %fusion.12), calls=%async_computation.8 | async-start | bytes 1638400 | tf_op jit(solution)/shard_map/all_to_all | solution.py:761
  527.7 32.8 %collective-permute-start.40 = (f32[12,1600]{1,0:T(8,128)S(1)}, f32[12,1600]{1,0:T(8,128)S(1)}, u32[]{:S(2)}, u32[]{:S(2)}) collective-permute-start(f32[12,1600]{1,0:T(8,128)S(1)} %add.134), channel_id=1, source_target_pairs={{0,2},{1,3},{2,0},{3,1},{4,6},{5,7},{6,4},{7,5},{8,10},{9,11},{10,... | collective-permute-start | bytes 230408 | tf_op jit(solution)/shard_map/ppermute | solution.py:677
  (68 other events, 1065.1 us)
Sparse Core Ops, SparseCore 0:
  9.7 71.6 all-gather.3
  83.0 38.6 all-gather.7
  154.8 46.2 all-gather.5
  297.5 40.5 reduce-scatter.3
  340.2 49.6 reduce-scatter.5
  394.9 41.4 reduce-scatter.7

commit v4 on v3

--- a/solution.py
+++ b/solution.py
@@ -58,6 +58,10 @@
 
 def xor_perm(count, k):
     return [(i, i ^ k) for i in range(count)]
+
+
+def after(value, *others):
+    return lax.optimization_barrier((value, *others))[0]
 
 
 def gather_rel(block, axis):
@@ -500,13 +504,17 @@
     )(gn1, x, gr, table)
 
 
-def out_blocks(w_out):
+def line_blocks(block):
     seqs = lax.axis_size("seq")
-    line = [w_out] + [
-        lax.ppermute(w_out, "seq", xor_perm(seqs, 2 * dz)) for dz in range(1, seqs // 2)
-    ]
-    near = gather_rel(jnp.stack(line), "dp")
-    return [[b, lax.ppermute(b, "seq", xor_perm(seqs, 1))] for b in near]
+    return jnp.stack(
+        [block]
+        + [lax.ppermute(block, "seq", xor_perm(seqs, 2 * dz)) for dz in range(1, seqs // 2)]
+    )
+
+
+def out_blocks(line):
+    seqs = lax.axis_size("seq")
+    return [[b, lax.ppermute(b, "seq", xor_perm(seqs, 1))] for b in gather_rel(line, "dp")]
 
 
 def block_copies(where, blocks, store, sems, outward):
@@ -725,20 +733,23 @@
     pieces = w_proj.reshape(ratio, ff_mine, col)
     pieces = jnp.stack([pieces[:, start(q) : start(q) + size] for q in range(dps)])
     pieces = lax.all_to_all(pieces, "dp", 0, 0, tiled=True)
-    pieces = lax.all_to_all(pieces.reshape(seqs, size, col), "seq", 0, 0, tiled=True)
+    own_qkv = after(own_qkv, pieces, *wf)
+
+    where = jnp.stack([dp, sq]).astype(jnp.int32)
+    x_all = lax.all_gather(after(tokens, parts), "seq", axis=0, tiled=True)
+    gm_all = lax.all_gather(after(cotangent, x_all), "seq", axis=0, tiled=True)
+    wq = gather_rel(own_qkv, "dp")
+    line = line_blocks(w_out)
+    wo = out_blocks(line)
+    pieces = lax.all_to_all(
+        after(pieces.reshape(seqs, size, col), x_all), "seq", 0, 0, tiled=True
+    )
+    x_all = after(x_all, line)
+    n1_all, qkv, att, lse = attend(where, x_all, table, bias_qkv[None], wq, slots, rows)
+    att = lax.all_to_all(after(att, pieces), "seq", 0, 0, tiled=True)
     wp = gather_rel(pieces.transpose(1, 0, 2).reshape(size, model), "dp")
-
-    where = jnp.stack([dp, sq]).astype(jnp.int32)
-    wo = out_blocks(w_out)
-
-    x_all = lax.all_gather(tokens, "seq", axis=0, tiled=True)
-    cot, own_qkv = lax.optimization_barrier((cotangent, own_qkv))
-    gm_all = lax.all_gather(cot, "seq", axis=0, tiled=True)
-    wq = gather_rel(own_qkv, "dp")
-    n1_all, qkv, att, lse = attend(where, x_all, table, bias_qkv[None], wq, slots, rows)
-    att = lax.all_to_all(att, "seq", 0, 0, tiled=True)
     r, n2 = out_project(where, att, tokens, table, wo, owner)
-    n2_all = lax.all_gather(n2, "seq", axis=0, tiled=True)
+    n2_all = lax.all_gather(after(n2, *wp), "seq", axis=0, tiled=True)
 
     e, gu, gn2_part, sum_fc = feed(where, n2_all, gm_all, bias_fc[None], wf, wp)
     gn2 = lax.psum_scatter(gn2_part, "seq", scatter_dimension=0, tiled=True)
@@ -750,18 +761,18 @@
     gr, go, ga, sums_two = out_back(where, gn2, r, cotangent, table, wo, owner)
     ga = lax.all_to_all(ga, "seq", 0, 0, tiled=True)
     d_out = grad_out(where, att, go, dps, owner)
-    gqkv, gn1_part = attend_back(where, qkv, ga, lse, wq)
+    g_proj = scatter_rel(d_proj, "dp").astype(BF)
+    g_fc = scatter_rel([after(d, g_proj) for d in d_fc], "dp")
+    gqkv, gn1_part = attend_back(where, qkv, after(ga, g_proj, *d_out[0]), lse, wq)
     gn1 = lax.psum_scatter(gn1_part, "seq", scatter_dimension=0, tiled=True)
     d_qkv, gqkv_sums, norm_sums = grad_qkv(where, n1_all, gqkv, gn1_part, dps)
     input_grad = last_norm(gn1, tokens, gr, table)
 
-    g_fc = scatter_rel(d_fc, "dp")
     g_qkv = scatter_rel(d_qkv, "dp").astype(BF)
     parts = jnp.einsum("ad,nwd->naw", g_qkv, to_recv, preferred_element_type=F32).astype(BF)
     parts = lax.all_to_all(parts, "seq", 0, 0, tiled=True)
     g_qkv = jnp.einsum("naw,cnw->ac", parts, to_send, preferred_element_type=F32)
 
-    g_proj = scatter_rel(d_proj, "dp").astype(BF)
     g_proj = g_proj.reshape(size, seqs, col).transpose(1, 0, 2)
     g_proj = lax.all_to_all(g_proj, "seq", 0, 0, tiled=True)
     g_proj = g_proj.reshape(dps, ratio, size, col)

time: 611 us -> 591 us (0.967)
  blocking collectives: 44.1 us -> 28 us
  starting transfers between devices: 79.3 us -> 88.7 us
  waiting for transfers between devices: 290 us -> 282 us
    all_gather x3, waiting for transfers between devices: 0.04 us -> 77.4 us  [the longest x1 39.5 us: body(): x_all = lax.all_gather(after(tokens, parts), 'seq', axis=0, tiled=True)]
    all_to_all x2 -> x1, waiting for transfers between devices: 41.8 us -> 0.01 us  [body(): parts = lax.all_to_all(parts, 'seq', 0, 0, tiled=True)]
    ppermute x12, waiting for transfers between devices: 80.8 us -> 39.2 us  [gather_rel(): lax.ppermute(block, axis, xor_perm(count, k))]
    all_to_all x2 -> x4, waiting for transfers between devices: 28.8 us -> 0.22 us  [the longest x1 0.21 us: body(): ga = lax.all_to_all(ga, 'seq', 0, 0, tiled=True)]
    ppermute x5, waiting for transfers between devices: 8.89 us -> 36.2 us  [gather_small(): other = lax.ppermute(stack, axis, xor_perm(count, step))]
    ppermute x5, waiting for transfers between devices: 37.8 us -> 13.3 us  [sum_all(): lax.ppermute(block, axis, xor_perm(lax.axis_size(axis), step))]
    all_to_all x2 -> x1, blocking collectives: 44.1 us -> 28 us  [body(): parts = lax.all_to_all(parts, 'seq', 0, 0, tiled=True)]
    all_to_all x1, waiting for transfers between devices: 0.01 us -> 15.4 us  [body(): g_proj = lax.all_to_all(g_proj, 'seq', 0, 0, tiled=True)]
  transfers between devices with their start and end apart: 60 -> 61, of which waited for: 24 -> 27; matrix products, arithmetic and copies ran while one was open for 8% -> 8% of each run, Pallas kernels for 15% -> 15%
where the time goes in v4:
time: 591 us; the launch traced here: 584 us
  waiting for transfers between devices  282 us (48%)
  Pallas kernels  112 us (19%)
  starting transfers between devices  88.7 us (15%)
  local copies, waits for them, and re-layouts  31.3 us (5%)
  blocking collectives  28 us (5%)
  other arithmetic  18.3 us (3%)
  between operations  15.3 us (3%)
  matrix products  8.18 us (1%)
    ppermute x12, waiting for transfers between devices, scatter_rel(): lax.ppermute(chunks[k], axis, xor_perm(count, k)).astype(F32)  70.2 us
    all_gather x1, waiting for transfers between devices, body(): x_all = lax.all_gather(after(tokens, parts), 'seq', axis=0, tiled=True)  39.5 us
    ppermute x12, waiting for transfers between devices, gather_rel(): lax.ppermute(block, axis, xor_perm(count, k))  39.2 us
    all_gather x1, waiting for transfers between devices, body(): n2_all = lax.all_gather(after(n2, *wp), 'seq', axis=0, tiled=True)  38 us
    ppermute x5, waiting for transfers between devices, gather_small(): other = lax.ppermute(stack, axis, xor_perm(count, step))  36.2 us
    all_to_all x1, blocking collectives, body(): parts = lax.all_to_all(parts, 'seq', 0, 0, tiled=True)  28 us
    ppermute x12, starting transfers between devices, scatter_rel(): lax.ppermute(chunks[k], axis, xor_perm(count, k)).astype(F32)  24.8 us
    pallas_call x1, Pallas kernels, feed_grad(): pl.pallas_call(functools.partial(feed_grad_kernel, dps), in_specs=[SCALAR...  21.7 us
  transfers between devices with their start and end apart: 61, of which 27 were waited for; matrix products, arithmetic and copies ran while one was open for 8% of the time, Pallas kernels for 15%

profile of v4, /device:TPU:0, one launch (start us, length us, event | category | flops | bytes accessed | tf_op | source)
XLA Modules:
  0.0 584.3 jit_solution(15190027678301796081)
XLA Ops:
  9.1 28.0 %all_to_all.40 = bf16[8,400,128]{2,1,0:T(8,128)(2,1)} all-to-all(bf16[8,400,128]{2,1,0:T(8,128)(2,1)S(1)} %fusion.11), channel_id=1, replica_groups=mesh['dp'=4,'seq'=8] {'seq'}, dimensions={0} | all-to-all | bytes 1638400 | tf_op jit(solution)/shard_map/all_to_all | solution.py:728
  38.3 39.5 %all-gather.4.cloned.1.call-done.x_ref = bf16[1024,1600]{1,0:T(8,128)(2,1)} async-done(((bf16[128,1600]{1,0:T(8,128)(2,1)}), bf16[1024,1600]{1,0:T(8,128)(2,1)}) %all-gather.4.cloned.1.call-update) | async-done | bytes 3276816 | tf_op jit(solution)/shard_map/all_gather | solution.py:739
  94.8 18.6 %collective-permute-done.3 = bf16[1,1,600]{2,0,1:T(2,128)(2,1)S(1)} collective-permute-done((bf16[1,1,600]{2,0,1:T(2,128)(2,1)S(1)}, bf16[1,1,600]{2,0,1:T(2,128)(2,1)S(1)}, u32[]{:S(2)}, u32[]{:S(2)}) %collective-permute-start.3) | collective-permute-done | bytes 1232 | tf_op jit(solution)/shard_map/ppermute | solution.py:86
  114.9 7.6 %collective-permute-done.4 = bf16[2,1,600]{2,0,1:T(2,128)(2,1)S(1)} collective-permute-done((bf16[2,1,600]{2,0,1:T(2,128)(2,1)S(1)}, bf16[2,1,600]{2,0,1:T(2,128)(2,1)S(1)}, u32[]{:S(2)}, u32[]{:S(2)}) %collective-permute-start.4) | collective-permute-done | bytes 2432 | tf_op jit(solution)/shard_map/ppermute | solution.py:86
  124.4 9.5 %collective-permute-done.1 = bf16[400,200]{1,0:T(8,128)(2,1)S(1)} collective-permute-done((bf16[400,200]{1,0:T(8,128)(2,1)S(1)}, bf16[400,200]{1,0:T(8,128)(2,1)S(1)}, u32[]{:S(2)}, u32[]{:S(2)}) %collective-permute-start.1) | collective-permute-done | bytes 160032 | tf_op jit(solution)/shard_map/ppermute | solution.py:511
  147.1 6.6 %collective-permute-done.6 = bf16[2,4,1,600]{3,1,2,0:T(4,128)(2,1)S(1)} collective-permute-done((bf16[2,4,1,600]{3,1,2,0:T(4,128)(2,1)S(1)}, bf16[2,4,1,600]{3,1,2,0:T(4,128)(2,1)S(1)}, u32[]{:S(2)}, u32[]{:S(2)}) %collective-permute-start.6) | collective-permute-done | bytes 9632 | tf_op jit(solution)/shard_map/ppermute | solution.py:86
  153.7 4.6 collective-permute-start.7
  163.1 5.4 collective-permute-done.11.rest_1_
  172.3 10.5 %collective-permute-done.13.rest_3_ = bf16[400,768]{1,0:T(8,128)(2,1)} collective-permute-done((bf16[400,768]{1,0:T(8,128)(2,1)S(1)}, bf16[400,768]{1,0:T(8,128)(2,1)}, u32[]{:S(2)}, u32[]{:S(2)}) %collective-permute-start.13) | collective-permute-done | bytes 614432 | tf_op jit(solution)/shard_map/ppermute | solution.py:69
  182.8 16.6 %shard_map.170 = (bf16[1024,1600]{1,0:T(8,128)(2,1)}, bf16[1024,768]{1,0:T(8,128)(2,1)}, bf16[8,128,256]{2,1,0:T(8,128)(2,1)}, f32[1024,256]{1,0:T(8,128)}) custom-call(s32[2]{0:T(128)} %pad_add_fusion.where, bf16[1024,1600]{1,0:T(8,128)(2,1)} %all-gather.4.cloned.1.call-done.x_ref, f32[8,1600]{1,0:T(8,128)} %copy-done.13, ...), custom_call_target="tpu_custom_call" | custom-call | tf_op jit(solution)/shard_map/pallas_call | solution.py:232
  204.3 9.2 %collective-permute-done.17.rest_4_ = bf16[4,400,200]{2,1,0:T(8,128)(2,1)} collective-permute-done((bf16[4,400,200]{2,1,0:T(8,128)(2,1)S(1)}, bf16[4,400,200]{2,1,0:T(8,128)(2,1)}, u32[]{:S(2)}, u32[]{:S(2)}) %collective-permute-start.17) | collective-permute-done | bytes 640032 | tf_op jit(solution)/shard_map/ppermute | solution.py:69
  221.8 6.9 %shard_map.171 = (f32[128,1600]{1,0:T(8,128)}, bf16[128,1600]{1,0:T(8,128)(2,1)}) custom-call(s32[2]{0:T(128)} %pad_add_fusion.where, bf16[8,128,256]{2,1,0:T(8,128)(2,1)} %copy-done.4, bf16[128,1600]{1,0:T(8,128)(2,1)} %copy.86.x_ref, f32[8,1600]{1,0:T(8,128)} %copy-done.13, bf16[4,400,200]{2,1,0:T(8,128)(2,1)} %copy-done.2, ...), custom_call_target="tpu_custom_call" | custom-call | tf_op jit(solution)/shard_map/pallas_call | solution.py:565
  228.7 14.1 %collective-permute-done.22.rest_6_.rest_2_ = bf16[208,1600]{1,0:T(8,128)(2,1)} collective-permute-done((bf16[208,1600]{1,0:T(8,128)(2,1)S(1)}, bf16[208,1600]{1,0:T(8,128)(2,1)}, u32[]{:S(2)}, u32[]{:S(2)}) %collective-permute-start.22) | collective-permute-done | bytes 665632 | tf_op jit(solution)/shard_map/ppermute | solution.py:69
  244.5 38.0 %all-gather.6.cloned.1.call-done.n2_ref = bf16[1024,1600]{1,0:T(8,128)(2,1)} async-done(((bf16[128,1600]{1,0:T(8,128)(2,1)}), bf16[1024,1600]{1,0:T(8,128)(2,1)}) %all-gather.6.cloned.1.call-update) | async-done | bytes 3276816 | tf_op jit(solution)/shard_map/all_gather | solution.py:752
  282.5 21.7 %shard_map.172 = (bf16[1024,800]{1,0:T(8,128)(2,1)}, bf16[1024,800]{1,0:T(8,128)(2,1)}, bf16[1024,1600]{1,0:T(8,128)(2,1)}, f32[1,800]{1,0:T(1,128)}) custom-call(s32[2]{0:T(128)} %pad_add_fusion.where, bf16[1024,1600]{1,0:T(8,128)(2,1)} %all-gather.6.cloned.1.call-done.n2_ref, bf16[1024,1600]{1,0:T(8,128)(2,1)} %all-gather.8.cloned.1.call-done.gm_ref, ...), custom_call_target="tpu_custom_call" | custom-call | tf_op jit(solution)/shard_map/pallas_call | solution.py:407
  304.8 21.7 %shard_map.173 = (bf16[1024,1600]{1,0:T(8,128)(2,1)}, bf16[400,800]{1,0:T(8,128)(2,1)}, bf16[400,800]{1,0:T(8,128)(2,1)}, bf16[400,800]{1,0:T(8,128)(2,1)}, bf16...) custom-call(s32[2]{0:T(128)} %pad_add_fusion.where, ...), custom_call_target="tpu_custom_call" | custom-call | tf_op jit(solution)/shard_map/pallas_call | solution.py:472
  326.5 19.3 %reduce-scatter.4.cloned.1.call-done.gn2_ref = bf16[128,1600]{1,0:T(8,128)(2,1)} async-done(((bf16[1024,1600]{1,0:T(8,128)(2,1)}), bf16[128,1600]{1,0:T(8,128)(2,1)}) %reduce-scatter.4.cloned.1.call-update) | async-done | bytes 409616 | tf_op jit(solution)/shard_map/reduce_scatter | solution.py:755
  350.4 8.1 %shard_map.174 = (f32[128,1600]{1,0:T(8,128)}, bf16[128,1600]{1,0:T(8,128)(2,1)}, bf16[8,128,256]{2,1,0:T(8,128)(2,1)}, f32[4,1600]{1,0:T(4,128)}) custom-call(s32[2]{0:T(128)} %pad_add_fusion.where, bf16[128,1600]{1,0:T(8,128)(2,1)} %reduce-scatter.4.cloned.1.call-done.gn2_ref, f32[128,1600]{1,0:T(8,128)} %get-tuple-element.67.r_ref, ...), custom_call_target="tpu_custom_call" | custom-call | tf_op jit(solution)/shard_map/pallas_call | solution.py:615
  365.5 11.5 %collective-permute-done.25 = bf16[208,1600]{1,0:T(8,128)(2,1)S(1)} collective-permute-done((bf16[208,1600]{1,0:T(8,128)(2,1)}, bf16[208,1600]{1,0:T(8,128)(2,1)S(1)}, u32[]{:S(2)}, u32[]{:S(2)}) %collective-permute-start.25) | collective-permute-done | bytes 665632 | tf_op jit(solution)/shard_map/ppermute | solution.py:76
  379.5 6.3 %shard_map.175 = (bf16[4,400,200]{2,1,0:T(8,128)(2,1)}, bf16[4,400,200]{2,1,0:T(8,128)(2,1)}, bf16[4,400,200]{2,1,0:T(8,128)(2,1)}, bf16[4,400,200]{2,1,0:T(8,12...) custom-call(s32[2]{0:T(128)} %pad_add_fusion.where, ...), custom_call_target="tpu_custom_call" | custom-call | tf_op jit(solution)/shard_map/pallas_call | solution.py:654
  386.9 18.5 %shard_map.176 = (bf16[1024,768]{1,0:T(8,128)(2,1)}, bf16[1024,1600]{1,0:T(8,128)(2,1)}) custom-call(s32[2]{0:T(128)} %pad_add_fusion.where, bf16[1024,768]{1,0:T(8,128)(2,1)} %get-tuple-element.76.qkv_ref, bf16[8,128,256]{2,1,0:T(8,128)(2,1)} %copy-done.12, f32[1024,256]{1,0:T(8,128)} %get-tuple-element.87.lse_ref, bf16[400,768]{1,0:T(8,128)(2,1)} %copy-done.9, ...), custom_call_target="tpu_custom_call" | custom-call | tf_op jit(solution)/shard_map/pallas_call | solution.py:311
  408.6 4.6 all-to-all-start.6
  416.3 9.7 %shard_map.178 = (bf16[400,768]{1,0:T(8,128)(2,1)}, bf16[400,768]{1,0:T(8,128)(2,1)}, bf16[400,768]{1,0:T(8,128)(2,1)}, bf16[400,768]{1,0:T(8,128)(2,1)}, f32[1,768]{1,0:T(1,128)}, /*index=5*/f32[2,1600]{1,0:T(2,128)}) custom-call(s32[2]{0:T(128)} %pad_add_fusion.where, bf16[1024,1600]{1,0:T(8,128)(2,1)} %get-tuple-element.90.n1_ref, ...), custom_call_target="tpu_custom_call" | custom-call | tf_op jit(solution)/shard_map/pallas_call | solution.py:353
  433.6 15.4 %all-to-all-done.6 = bf16[8,208,200]{1,2,0:T(8,128)(2,1)} async-done(((bf16[8,208,200]{1,2,0:T(8,128)(2,1)}), bf16[8,208,200]{1,2,0:T(8,128)(2,1)}, u32[]{:S(2)}, u32[]{:S(2)}) %all-to-all-start.6) | async-done | bytes 665632 | tf_op jit(solution)/shard_map/all_to_all | solution.py:777
  464.5 16.2 %collective-permute-done.45 = bf16[400,800]{1,0:T(8,128)(2,1)S(1)} collective-permute-done((bf16[400,800]{1,0:T(8,128)(2,1)}, bf16[400,800]{1,0:T(8,128)(2,1)S(1)}, u32[]{:S(2)}, u32[]{:S(2)}) %collective-permute-start.45) | collective-permute-done | bytes 640032 | tf_op jit(solution)/shard_map/ppermute | solution.py:76
  480.6 12.5 %collective-permute-start.36 = (bf16[4,400,200]{2,1,0:T(8,128)(2,1)}, bf16[4,400,200]{2,1,0:T(8,128)(2,1)}, u32[]{:S(2)}, u32[]{:S(2)}) collective-permute-start(bf16[4,400,200]{2,1,0:T(8,128)(2,1)} %add_convert_fusion.1), channel_id=1, source_target_pairs={{0,24},{8,16},{16,8},{24,0},{1,25},{9,17},{17,9},{25,1},{2,26},{10... | collective-permute-start | bytes 1920008 | tf_op jit(solution)/shard_map/ppermute | solution.py:76
  498.0 9.0 %collective-permute-done.27 = bf16[400,768]{1,0:T(8,128)(2,1)S(1)} collective-permute-done((bf16[400,768]{1,0:T(8,128)(2,1)S(1)}, bf16[400,768]{1,0:T(8,128)(2,1)S(1)}, u32[]{:S(2)}, u32[]{:S(2)}) %collective-permute-start.27) | collective-permute-done | bytes 614432 | tf_op jit(solution)/shard_map/ppermute | solution.py:76
  509.1 4.3 all-to-all-start.5
  515.5 10.1 %collective-permute-done.36 = bf16[4,400,200]{2,1,0:T(8,128)(2,1)} collective-permute-done((bf16[4,400,200]{2,1,0:T(8,128)(2,1)}, bf16[4,400,200]{2,1,0:T(8,128)(2,1)}, u32[]{:S(2)}, u32[]{:S(2)}) %collective-permute-start.36) | collective-permute-done | bytes 640032 | tf_op jit(solution)/shard_map/ppermute | solution.py:76
  525.6 4.4 collective-permute-done.34
  530.9 10.0 %collective-permute-done.32 = bf16[4,400,200]{2,1,0:T(8,128)(2,1)} collective-permute-done((bf16[4,400,200]{2,1,0:T(8,128)(2,1)}, bf16[4,400,200]{2,1,0:T(8,128)(2,1)}, u32[]{:S(2)}, u32[]{:S(2)}) %collective-permute-start.32) | collective-permute-done | bytes 640032 | tf_op jit(solution)/shard_map/ppermute | solution.py:76
  551.6 13.3 %collective-permute-done.44 = f32[12,1600]{1,0:T(8,128)S(1)} collective-permute-done((f32[12,1600]{1,0:T(8,128)S(1)}, f32[12,1600]{1,0:T(8,128)S(1)}, u32[]{:S(2)}, u32[]{:S(2)}) %collective-permute-start.44) | collective-permute-done | bytes 76832 | tf_op jit(solution)/shard_map/ppermute | solution.py:685
  (282 shorter events, 137.5 us)
Async XLA Ops:
  7.2 70.5 %all-gather.4.cloned.1.call-start = ((), (), s32[]{:S(2)}) async-start(), calls=%async_computation.11 | async-start | bytes 3833856 | tf_op jit(solution)/shard_map/all_gather | solution.py:739
  38.2 206.3 %all-gather.8.cloned.1.call-start = ((), (), s32[]{:S(2)}) async-start(), calls=%async_computation.13 | async-start | bytes 3833856 | tf_op jit(solution)/shard_map/all_gather | solution.py:740
  78.7 62.6 %collective-permute-start.8 = (bf16[400,800]{1,0:T(8,128)(2,1)}, bf16[400,800]{1,0:T(8,128)(2,1)}, u32[]{:S(2)}, u32[]{:S(2)}) collective-permute-start(bf16[400,800]{1,0:T(8,128)(2,1)} %rest_0_.1), channel_id=1, source_target_pairs={{0,8},{8,0},{16,24},{24,16},{1,9},{9,1},{17,25},{25,17},{2,10},{10... | collective-permute-start | bytes 1920008 | tf_op jit(solution)/shard_map/ppermute | solution.py:69
  80.3 61.1 %collective-permute-start.9 = (bf16[400,800]{1,0:T(8,128)(2,1)}, bf16[400,800]{1,0:T(8,128)(2,1)}, u32[]{:S(2)}, u32[]{:S(2)}) collective-permute-start(bf16[400,800]{1,0:T(8,128)(2,1)} %rest_0_.1), channel_id=1, source_target_pairs={{0,16},{8,24},{16,0},{24,8},{1,17},{9,25},{17,1},{25,9},{2,18},{10... | collective-permute-start | bytes 1920008 | tf_op jit(solution)/shard_map/ppermute | solution.py:69
  81.7 59.6 %collective-permute-start.10 = (bf16[400,800]{1,0:T(8,128)(2,1)}, bf16[400,800]{1,0:T(8,128)(2,1)}, u32[]{:S(2)}, u32[]{:S(2)}) collective-permute-start(bf16[400,800]{1,0:T(8,128)(2,1)} %rest_0_.1), channel_id=1, source_target_pairs={{0,24},{8,16},{16,8},{24,0},{1,25},{9,17},{17,9},{25,1},{2,26},{10... | collective-permute-start | bytes 1920008 | tf_op jit(solution)/shard_map/ppermute | solution.py:69
  82.3 41.6 %collective-permute-start.2 = (bf16[400,200]{1,0:T(8,128)(2,1)S(1)}, bf16[400,200]{1,0:T(8,128)(2,1)S(1)}, u32[]{:S(2)}, u32[]{:S(2)}) collective-permute-start(bf16[400,200]{1,0:T(8,128)(2,1)S(1)} %copy-done.29), channel_id=1, source_target_pairs={{0,6},{1,7},{2,4},{3,5},{4,2},{5,3},{6,0},{7,1},{8,14},{9,15},{10,... | collective-permute-start | bytes 480008 | tf_op jit(solution)/shard_map/ppermute | solution.py:511
  83.9 29.4 %collective-permute-start.3 = (bf16[1,1,600]{2,0,1:T(2,128)(2,1)S(1)}, bf16[1,1,600]{2,0,1:T(2,128)(2,1)S(1)}, u32[]{:S(2)}, u32[]{:S(2)}) collective-permute-start(bf16[1,1,600]{2,0,1:T(2,128)(2,1)S(1)} %broadcast_in_dim_broadcast_in_dim.3), channel_id=1, source_target_pairs={{0,8},{8,0},{16,24},{24,16},{1,9},{9,1},{17,25},{25,17},{2,10},{10... | collective-permute-start | bytes 3608 | tf_op jit(solution)/shard_map/ppermute | solution.py:86
  89.2 45.1 %all-to-all-start.1 = ((bf16[4,2,208,200]{2,1,3,0:T(2,128)(2,1)}), bf16[4,2,208,200]{2,1,3,0:T(2,128)(2,1)S(1)}, u32[]{:S(2)}, u32[]{:S(2)}) async-start(bf16[4,2,208,200]{2,1,3,0:T(2,128)(2,1)} %pad_maximum_fusion.1), calls=%async_computation.1 | async-start | bytes 1638400 | tf_op jit(solution)/shard_map/all_to_all | solution.py:735
  135.4 64.0 %all-to-all-start.2 = ((bf16[8,208,200]{1,2,0:T(8,128)(2,1)}), bf16[8,208,200]{1,2,0:T(8,128)(2,1)S(1)}, u32[]{:S(2)}, u32[]{:S(2)}) async-start(bf16[8,208,200]{1,2,0:T(8,128)(2,1)} %bitcast.31), calls=%async_computation.2 | async-start | bytes 1638400 | tf_op jit(solution)/shard_map/all_to_all | solution.py:744
  146.9 35.9 %collective-permute-start.13 = (bf16[400,768]{1,0:T(8,128)(2,1)S(1)}, bf16[400,768]{1,0:T(8,128)(2,1)}, u32[]{:S(2)}, u32[]{:S(2)}) collective-permute-start(bf16[400,768]{1,0:T(8,128)(2,1)S(1)} %fusion.10.rest_0_), channel_id=1, source_target_pairs={{0,24},{8,16},{16,8},{24,0},{1,25},{9,17},{17,9},{25,1},{2,26},{10... | collective-permute-start | bytes 1843208 | tf_op jit(solution)/shard_map/ppermute | solution.py:69
  161.6 42.1 %collective-permute-start.14 = (bf16[4,400,200]{2,1,0:T(8,128)(2,1)S(1)}, bf16[4,400,200]{2,1,0:T(8,128)(2,1)}, u32[]{:S(2)}, u32[]{:S(2)}) collective-permute-start(bf16[4,400,200]{2,1,0:T(8,128)(2,1)S(1)} %pad_maximum_fusion.rest_0_), channel_id=1, source_target_pairs={{0,1},{1,0},{2,3},{3,2},{4,5},{5,4},{6,7},{7,6},{8,9},{9,8},{10,11... | collective-permute-start | bytes 1920008 | tf_op jit(solution)/shard_map/ppermute | solution.py:517
  161.6 51.9 %collective-permute-start.17 = (bf16[4,400,200]{2,1,0:T(8,128)(2,1)S(1)}, bf16[4,400,200]{2,1,0:T(8,128)(2,1)}, u32[]{:S(2)}, u32[]{:S(2)}) collective-permute-start(bf16[4,400,200]{2,1,0:T(8,128)(2,1)S(1)} %pad_maximum_fusion.rest_0_), channel_id=1, source_target_pairs={{0,16},{8,24},{16,0},{24,8},{1,17},{9,25},{17,1},{25,9},{2,18},{10... | collective-permute-start | bytes 1920008 | tf_op jit(solution)/shard_map/ppermute | solution.py:69
  168.5 47.8 %collective-permute-start.19 = (bf16[4,400,200]{2,1,0:T(8,128)(2,1)S(1)}, bf16[4,400,200]{2,1,0:T(8,128)(2,1)}, u32[]{:S(2)}, u32[]{:S(2)}) collective-permute-start(bf16[4,400,200]{2,1,0:T(8,128)(2,1)S(1)} %pad_maximum_fusion.rest_0_), channel_id=1, source_target_pairs={{0,24},{8,16},{16,8},{24,0},{1,25},{9,17},{17,9},{25,1},{2,26},{10... | collective-permute-start | bytes 1920008 | tf_op jit(solution)/shard_map/ppermute | solution.py:69
  170.4 46.0 %collective-permute-start.16 = (bf16[4,400,200]{2,1,0:T(8,128)(2,1)}, bf16[4,400,200]{2,1,0:T(8,128)(2,1)}, u32[]{:S(2)}, u32[]{:S(2)}) collective-permute-start(bf16[4,400,200]{2,1,0:T(8,128)(2,1)} %collective-permute-done.15.rest_2_), channel_id=1, source_target_pairs={{0,1},{1,0},{2,3},{3,2},{4,5},{5,4},{6,7},{7,6},{8,9},{9,8},{10,11... | collective-permute-start | bytes 1920008 | tf_op jit(solution)/shard_map/ppermute | solution.py:517
  202.9 79.6 %all-gather.6.cloned.1.call-start = ((), (), s32[]{:S(2)}) async-start(), calls=%async_computation.12 | async-start | bytes 3833856 | tf_op jit(solution)/shard_map/all_gather | solution.py:752
  203.7 39.1 %collective-permute-start.22 = (bf16[208,1600]{1,0:T(8,128)(2,1)S(1)}, bf16[208,1600]{1,0:T(8,128)(2,1)}, u32[]{:S(2)}, u32[]{:S(2)}) collective-permute-start(bf16[208,1600]{1,0:T(8,128)(2,1)S(1)} %copy.98.rest_4_.rest_0_), channel_id=1, source_target_pairs={{0,16},{8,24},{16,0},{24,8},{1,17},{9,25},{17,1},{25,9},{2,18},{10... | collective-permute-start | bytes 1996808 | tf_op jit(solution)/shard_map/ppermute | solution.py:69
  242.8 103.0 %reduce-scatter.4.cloned.1.call-start = ((), (), s32[]{:S(2)}) async-start(), calls=%async_computation.14 | async-start | bytes 3833856 | tf_op jit(solution)/shard_map/reduce_scatter | solution.py:755
  304.2 266.0 %reduce-scatter.6.cloned.1.call-start = ((), (), s32[]{:S(2)}) async-start(), calls=%async_computation.15 | async-start | bytes 3833856 | tf_op jit(solution)/shard_map/reduce_scatter | solution.py:758
  362.0 210.3 %reduce-scatter.8.cloned.1.call-start = ((), (), s32[]{:S(2)}) async-start(), calls=%async_computation.16 | async-start | bytes 3833856 | tf_op jit(solution)/shard_map/reduce_scatter | solution.py:767
  408.6 40.4 %all-to-all-start.6 = ((bf16[8,208,200]{1,2,0:T(8,128)(2,1)}), bf16[8,208,200]{1,2,0:T(8,128)(2,1)}, u32[]{:S(2)}, u32[]{:S(2)}) async-start(bf16[8,208,200]{1,2,0:T(8,128)(2,1)} %copy.92), calls=%async_computation.9 | async-start | bytes 1638400 | tf_op jit(solution)/shard_map/all_to_all | solution.py:777
  415.8 36.9 %collective-permute-start.35 = (bf16[4,400,200]{2,1,0:T(8,128)(2,1)}, bf16[4,400,200]{2,1,0:T(8,128)(2,1)S(1)}, u32[]{:S(2)}, u32[]{:S(2)}) collective-permute-start(bf16[4,400,200]{2,1,0:T(8,128)(2,1)} %get-tuple-element.101), channel_id=1, source_target_pairs={{0,1},{1,0},{2,3},{3,2},{4,5},{5,4},{6,7},{7,6},{8,9},{9,8},{10,11... | collective-permute-start | bytes 1920008 | tf_op jit(solution)/shard_map/ppermute | solution.py:671
  415.9 38.9 %collective-permute-start.33 = (bf16[4,400,200]{2,1,0:T(8,128)(2,1)}, bf16[4,400,200]{2,1,0:T(8,128)(2,1)S(1)}, u32[]{:S(2)}, u32[]{:S(2)}) collective-permute-start(bf16[4,400,200]{2,1,0:T(8,128)(2,1)} %get-tuple-element.99), channel_id=1, source_target_pairs={{0,1},{1,0},{2,3},{3,2},{4,5},{5,4},{6,7},{7,6},{8,9},{9,8},{10,11... | collective-permute-start | bytes 1920008 | tf_op jit(solution)/shard_map/ppermute | solution.py:671
  449.0 60.2 %all-to-all-start.7 = ((bf16[4,2,208,200]{2,3,1,0:T(8,128)(2,1)}), bf16[4,2,208,200]{2,3,1,0:T(8,128)(2,1)S(1)}, u32[]{:S(2)}, u32[]{:S(2)}) async-start(bf16[4,2,208,200]{2,3,1,0:T(8,128)(2,1)} %bitcast.44), calls=%async_computation.10 | async-start | bytes 1638400 | tf_op jit(solution)/shard_map/all_to_all | solution.py:779
  454.8 39.9 %collective-permute-start.29 = (bf16[400,768]{1,0:T(8,128)(2,1)}, bf16[400,768]{1,0:T(8,128)(2,1)S(1)}, u32[]{:S(2)}, u32[]{:S(2)}) collective-permute-start(bf16[400,768]{1,0:T(8,128)(2,1)} %get-tuple-element.95), channel_id=1, source_target_pairs={{0,24},{8,16},{16,8},{24,0},{1,25},{9,17},{17,9},{25,1},{2,26},{10... | collective-permute-start | bytes 1843208 | tf_op jit(solution)/shard_map/ppermute | solution.py:76
  456.3 39.0 %collective-permute-start.28 = (bf16[400,768]{1,0:T(8,128)(2,1)}, bf16[400,768]{1,0:T(8,128)(2,1)S(1)}, u32[]{:S(2)}, u32[]{:S(2)}) collective-permute-start(bf16[400,768]{1,0:T(8,128)(2,1)} %get-tuple-element.94), channel_id=1, source_target_pairs={{0,16},{8,24},{16,0},{24,8},{1,17},{9,25},{17,1},{25,9},{2,18},{10... | collective-permute-start | bytes 1843208 | tf_op jit(solution)/shard_map/ppermute | solution.py:76
  458.7 48.3 %collective-permute-start.27 = (bf16[400,768]{1,0:T(8,128)(2,1)S(1)}, bf16[400,768]{1,0:T(8,128)(2,1)S(1)}, u32[]{:S(2)}, u32[]{:S(2)}) collective-permute-start(bf16[400,768]{1,0:T(8,128)(2,1)S(1)} %copy-done.41), channel_id=1, source_target_pairs={{0,8},{8,0},{16,24},{24,16},{1,9},{9,1},{17,25},{25,17},{2,10},{10... | collective-permute-start | bytes 1843208 | tf_op jit(solution)/shard_map/ppermute | solution.py:76
  480.6 34.9 %collective-permute-start.30 = (bf16[4,400,200]{2,1,0:T(8,128)(2,1)}, bf16[4,400,200]{2,1,0:T(8,128)(2,1)}, u32[]{:S(2)}, u32[]{:S(2)}) collective-permute-start(bf16[4,400,200]{2,1,0:T(8,128)(2,1)} %get-tuple-element.85), channel_id=1, source_target_pairs={{0,1},{1,0},{2,3},{3,2},{4,5},{5,4},{6,7},{7,6},{8,9},{9,8},{10,11... | collective-permute-start | bytes 1920008 | tf_op jit(solution)/shard_map/ppermute | solution.py:671
  480.6 44.9 %collective-permute-start.36 = (bf16[4,400,200]{2,1,0:T(8,128)(2,1)}, bf16[4,400,200]{2,1,0:T(8,128)(2,1)}, u32[]{:S(2)}, u32[]{:S(2)}) collective-permute-start(bf16[4,400,200]{2,1,0:T(8,128)(2,1)} %add_convert_fusion.1), channel_id=1, source_target_pairs={{0,24},{8,16},{16,8},{24,0},{1,25},{9,17},{17,9},{25,1},{2,26},{10... | collective-permute-start | bytes 1920008 | tf_op jit(solution)/shard_map/ppermute | solution.py:76
  494.7 35.3 %collective-permute-start.34 = (bf16[4,400,200]{2,1,0:T(8,128)(2,1)}, bf16[4,400,200]{2,1,0:T(8,128)(2,1)S(1)}, u32[]{:S(2)}, u32[]{:S(2)}) collective-permute-start(bf16[4,400,200]{2,1,0:T(8,128)(2,1)} %add_convert_fusion.2), channel_id=1, source_target_pairs={{0,16},{8,24},{16,0},{24,8},{1,17},{9,25},{17,1},{25,9},{2,18},{10... | collective-permute-start | bytes 1920008 | tf_op jit(solution)/shard_map/ppermute | solution.py:76
  495.3 45.6 %collective-permute-start.32 = (bf16[4,400,200]{2,1,0:T(8,128)(2,1)}, bf16[4,400,200]{2,1,0:T(8,128)(2,1)}, u32[]{:S(2)}, u32[]{:S(2)}) collective-permute-start(bf16[4,400,200]{2,1,0:T(8,128)(2,1)} %add_convert_fusion.3), channel_id=1, source_target_pairs={{0,8},{8,0},{16,24},{24,16},{1,9},{9,1},{17,25},{25,17},{2,10},{10... | collective-permute-start | bytes 1920008 | tf_op jit(solution)/shard_map/ppermute | solution.py:76
  509.1 58.0 %all-to-all-start.5 = ((bf16[8,400,128]{2,1,0:T(8,128)(2,1)}), bf16[8,400,128]{2,1,0:T(8,128)(2,1)}, u32[]{:S(2)}, u32[]{:S(2)}) async-start(bf16[8,400,128]{2,1,0:T(8,128)(2,1)} %fusion.12), calls=%async_computation.8 | async-start | bytes 1638400 | tf_op jit(solution)/shard_map/all_to_all | solution.py:773
  513.6 34.8 %collective-permute-start.43 = (f32[12,1600]{1,0:T(8,128)S(1)}, f32[12,1600]{1,0:T(8,128)S(1)}, u32[]{:S(2)}, u32[]{:S(2)}) collective-permute-start(f32[12,1600]{1,0:T(8,128)S(1)} %add.137), channel_id=1, source_target_pairs={{0,2},{1,3},{2,0},{3,1},{4,6},{5,7},{6,4},{7,5},{8,10},{9,11},{10,... | collective-permute-start | bytes 230408 | tf_op jit(solution)/shard_map/ppermute | solution.py:685
  (71 other events, 1494.1 us)
Sparse Core Ops, SparseCore 0:
  38.3 39.3 all-gather.3
  79.3 42.6 all-gather.7
  242.9 39.5 all-gather.5
  304.4 41.4 reduce-scatter.3
  348.0 49.6 reduce-scatter.5
  405.6 57.1 reduce-scatter.7

commit v5 on v4

v5 whole, which is shorter than its diff:
```python
import functools
import math

import jax
import jax.numpy as jnp
import numpy as np
from jax import lax
from jax.experimental import pallas as pl
from jax.experimental.pallas import tpu as pltpu
from jax.sharding import PartitionSpec as P

HD = 64
PAIR = 2 * HD
EPSILON = 1e-05
GELU_C = 0.7978845608028654
NEG_FILL = -1e30
BF = jnp.bfloat16
F32 = jnp.float32


def head_plan(head_count, seq_count, width):
    slots = -(-head_count // seq_count)
    slots += slots % 2
    model = head_count * HD

    def tables(turn):
        owner = np.full((seq_count, slots), -1, np.int32)
        for head in range(head_count):
            row = head // seq_count
            owner[(head + turn * row) % seq_count, row] = head
        place = {}
        for dev in range(seq_count):
            for slot in range(slots):
                if owner[dev, slot] >= 0:
                    place[int(owner[dev, slot])] = (dev, slot)
        lists = [[[] for _ in range(seq_count)] for _ in range(seq_count)]
        for col in range(3 * model):
            kind, rest = divmod(col, model)
            head, lane = divmod(rest, HD)
            dev, slot = place[head]
            src, local = divmod(col, width)
            lists[src][dev].append((local, (kind * slots + slot) * HD + lane))
        most = max(len(cell) for row in lists for cell in row)
        return most, owner, lists

    best = min((tables(turn) for turn in range(seq_count)), key=lambda t: t[0])
    most, owner, lists = best
    wide = -(-most // 128) * 128
    send = np.full((seq_count, seq_count, wide), -1, np.int32)
    recv = np.full((seq_count, seq_count, wide), -1, np.int32)
    for src in range(seq_count):
        for dev in range(seq_count):
            for i, (local, target) in enumerate(lists[src][dev]):
                send[src, dev, i] = local
                recv[src, dev, i] = target
    return slots, owner, wide, send, recv


ANY = pl.BlockSpec(memory_space=pl.ANY)
WHOLE = pl.BlockSpec(memory_space=pltpu.VMEM)
SCALAR = pl.BlockSpec(memory_space=pltpu.SMEM)


def blocks_of(*shapes):
    return [pl.BlockSpec(s.shape, lambda n=len(s.shape): (0,) * n) for s in shapes]


ROOM = pltpu.CompilerParams(vmem_limit_bytes=56 * 1024 * 1024)


def like(shape, kind=BF):
    return jax.ShapeDtypeStruct(shape, kind)


def phase(*values):
    return lax.optimization_barrier(values)


def xor_perm(count, k):
    return [(i, i ^ k) for i in range(count)]


def near_far(count):
    every = range(1, count)
    return [k for k in every if not k & (k - 1)], [k for k in every if k & (k - 1)]


def send_rel(blocks, axis, ks):
    count = lax.axis_size(axis)
    return {k: lax.ppermute(blocks[k], axis, xor_perm(count, k)) for k in ks}


def in_order(mine, *found):
    every = {0: mine}
    for part in found:
        every.update(part)
    return [every[k] for k in range(len(every))]


def can_halve(count, rows):
    return count == 4 and rows % 16 == 0


def cut(rows):
    return 16 * (rows // 16 - rows // 32)


def split_far(chunks):
    if len(chunks) != 4:
        return chunks
    far = chunks[3]
    half = far.shape[0] // 2 if far.ndim == 3 else cut(far.shape[0])
    return list(chunks[:3]) + [far[:half], far[half:]]


def reduce_first(chunks):
    if len(chunks) == 5:
        return [
            lax.ppermute(chunks[3], "dp", xor_perm(4, 1)),
            lax.ppermute(chunks[4], "dp", xor_perm(4, 2)),
        ]
    near, far = near_far(len(chunks))
    return list(send_rel(dict(enumerate(chunks)), "dp", far).values())


def reduce_second(chunks, found):
    if len(chunks) == 5:
        half = found[0].shape[0]
        first = jnp.concatenate(
            [chunks[1][:half], total_of([chunks[1][half:], found[1]]).astype(BF)]
        )
        second = jnp.concatenate(
            [total_of([chunks[2][:half], found[0]]).astype(BF), chunks[2][half:]]
        )
        return [
            chunks[0],
            lax.ppermute(first, "dp", xor_perm(4, 1)),
            lax.ppermute(second, "dp", xor_perm(4, 2)),
        ]
    near, far = near_far(len(chunks))
    return [chunks[0]] + found + list(send_rel(dict(enumerate(chunks)), "dp", near).values())


def swap_core(block):
    return lax.ppermute(block, "seq", xor_perm(lax.axis_size("seq"), 1))


def exchange(block):
    return lax.all_to_all(block, "seq", 0, 0, tiled=True)


def total_of(parts):
    total = parts[0].astype(F32)
    for part in parts[1:]:
        total = total + part.astype(F32)
    return total


def as_rows(values, lanes):
    size = -values.shape[1] % (16 * lanes)
    return jnp.pad(values, ((0, 0), (0, size))).reshape(values.shape[0], -1, lanes)


def normalise(rows):
    mean = jnp.mean(rows, axis=-1, keepdims=True)
    centred = rows - mean
    inverse = lax.rsqrt(jnp.mean(centred * centred, axis=-1, keepdims=True) + EPSILON)
    return centred * inverse, inverse


def norm_back(grad, unit, inverse, gain):
    scaled = grad * gain
    return (
        scaled
        - jnp.mean(scaled, axis=-1, keepdims=True)
        - unit * jnp.mean(scaled * unit, axis=-1, keepdims=True)
    ) * inverse


def gelu_parts(u):
    square = u * u
    t = jnp.tanh(u * (GELU_C + GELU_C * 0.044715 * square))
    half = 0.5 + 0.5 * t
    slope = half + u * (0.5 - 0.5 * t * t) * (GELU_C + 3 * 0.044715 * GELU_C * square)
    return u * half, slope


def mm(a, b):
    return jnp.dot(a, b, preferred_element_type=F32)


def mm_nt(a, b):
    return lax.dot_general(a, b, (((1,), (1,)), ((), ())), preferred_element_type=F32)


def mm_tn(a, b):
    return lax.dot_general(a, b, (((0,), (0,)), ((), ())), preferred_element_type=F32)


def run_copies(pairs, sems):
    found = [pltpu.make_async_copy(src, dst, sems.at[i]) for i, (src, dst) in enumerate(pairs)]
    for c in found:
        c.start()
    return found


def wait_for(copies):
    for c in copies:
        c.wait()


def stage_shape(dps, depth, width):
    return (dps, depth, width) if depth % 16 else (1, 16, 128)


def place_rows(where, refs, store, stage, sems, outward=False):
    depth = refs[0].shape[0]
    if outward and len(refs) == 5:
        pairs = []
        for k, ref in zip((0, 1, 2, 3, 3), refs):
            first = (where[0] ^ k) * depth
            if ref is refs[4]:
                first = first + refs[3].shape[0]
            pairs.append((store.at[pl.ds(pl.multiple_of(first, 16), ref.shape[0]), :], ref))
        return run_copies(pairs, sems)
    if depth % 16:
        spots = [stage.at[where[0] ^ k] for k in range(len(refs))]
    else:
        spots = [
            store.at[pl.ds(pl.multiple_of((where[0] ^ k) * depth, 16), depth), :]
            for k in range(len(refs))
        ]
    if outward:
        if depth % 16:
            for p in range(len(refs)):
                stage[p] = store[p * depth : (p + 1) * depth, :]
        return run_copies(list(zip(spots, refs)), sems)
    return run_copies(list(zip(refs, spots)), sems)


def settle_rows(copies, store, stage):
    wait_for(copies)
    depth = stage.shape[1]
    if depth % 16:
        for p in range(stage.shape[0]):
            store[p * depth : (p + 1) * depth, :] = stage[p]


def hot(row, count):
    return (
        lax.broadcasted_iota(jnp.int32, (count, row.shape[1]), 0) == row
    ).astype(BF)


def pack_kernel(where, w_ref, send_ref, more_ref, out_ref):
    depth = w_ref.shape[0]
    for n in range(out_ref.shape[0]):
        out_ref[n, 0:depth] = mm(w_ref[...], hot(send_ref[where[1], n], w_ref.shape[1])).astype(BF)
        out_ref[n, depth:] = more_ref[...]


def pack_columns(where, w_qkv, send, more):
    seqs, _, _, wide = send.shape
    shape = like((seqs, w_qkv.shape[0] + more.shape[0], wide))
    return pl.pallas_call(
        pack_kernel,
        in_specs=[SCALAR, WHOLE, WHOLE, WHOLE],
        out_specs=blocks_of(shape)[0],
        out_shape=shape,
        compiler_params=ROOM,
    )(where, w_qkv, send, more)


def unpack_kernel(where, recv_ref, in_ref, out_ref):
    total = None
    for n in range(in_ref.shape[0]):
        part = mm_nt(in_ref[n, 0 : out_ref.shape[0]], hot(recv_ref[n, where[1]], out_ref.shape[1]))
        total = part if total is None else total + part
    out_ref[...] = total.astype(BF)


def unpack_columns(where, parts, recv, depth, width):
    return pl.pallas_call(
        unpack_kernel,
        in_specs=[SCALAR, WHOLE, WHOLE],
        out_specs=blocks_of(like((depth, width)))[0],
        out_shape=like((depth, width)),
        compiler_params=ROOM,
    )(where, recv, parts)


def repack_kernel(where, recv_ref, more_ref, *rest):
    parts, out_ref = rest[:-1], rest[-1]
    grad = total_of([p[...] for p in parts]).astype(BF)
    depth = grad.shape[0]
    for n in range(out_ref.shape[0]):
        out_ref[n, 0:depth] = mm(grad, hot(recv_ref[n, where[1]], grad.shape[1])).astype(BF)
        out_ref[n, depth:] = more_ref[n]


def repack_columns(where, parts, recv, more):
    seqs, _, _, wide = recv.shape
    shape = like((seqs, parts[0].shape[0] + more.shape[1], wide))
    return pl.pallas_call(
        repack_kernel,
        in_specs=[SCALAR] + [WHOLE] * (2 + len(parts)),
        out_specs=blocks_of(shape)[0],
        out_shape=shape,
        compiler_params=ROOM,
    )(where, recv, more, *parts)


def restore_kernel(where, send_ref, in_ref, out_ref):
    depth = out_ref.shape[0]
    total = None
    for n in range(in_ref.shape[0]):
        part = mm_nt(in_ref[n, 0:depth], hot(send_ref[where[1], n], out_ref.shape[1]))
        total = part if total is None else total + part
    out_ref[...] = total


def restore_columns(where, parts, send, depth, width):
    return pl.pallas_call(
        restore_kernel,
        in_specs=[SCALAR, WHOLE, WHOLE],
        out_specs=blocks_of(like((depth, width)))[0],
        out_shape=like((depth, width), F32),
        compiler_params=ROOM,
    )(where, send, parts)


def piece_rows(total, count):
    tiles = total // 16
    return 16 * -(-tiles // count), lambda q: 16 * ((q * tiles) // count)


def pieces_kernel(where, w_ref, *outs):
    size, start = piece_rows(w_ref.shape[1], len(outs))
    for k, ref in enumerate(outs):
        first = pl.multiple_of(start(where[0] ^ k), 16)
        ref[...] = w_ref[:, pl.ds(first, size), :]


def proj_pieces(where, w_proj, dps):
    ratio, ff_mine, col = w_proj.shape
    size, _ = piece_rows(ff_mine, dps)
    return pl.pallas_call(
        pieces_kernel,
        in_specs=[SCALAR, WHOLE],
        out_specs=blocks_of(*[like((ratio, size, col))] * dps),
        out_shape=[like((ratio, size, col))] * dps,
        compiler_params=ROOM,
    )(where, w_proj)


def turn_kernel(where, *rest):
    ins, (out_ref, sems) = rest[:-2], rest[-2:]
    ratio = ins[0].shape[0]
    spots = [out_ref.at[pl.ds((where[0] ^ k) * ratio, ratio)] for k in range(len(ins))]
    wait_for(run_copies(list(zip(ins, spots)), sems))


def turn_pieces(where, parts):
    ratio, size, col = parts[0].shape
    return pl.pallas_call(
        turn_kernel,
        in_specs=[SCALAR] + [WHOLE] * len(parts),
        out_specs=blocks_of(like((ratio * len(parts), size, col)))[0],
        out_shape=like((ratio * len(parts), size, col)),
        scratch_shapes=[pltpu.SemaphoreType.DMA((len(parts),))],
        compiler_params=ROOM,
    )(where, *parts)


def join_kernel(in_ref, out_ref):
    width = in_ref.shape[2]
    for n in range(in_ref.shape[0]):
        out_ref[:, n * width : (n + 1) * width] = in_ref[n]


def join_columns(parts):
    seqs, size, col = parts.shape
    return pl.pallas_call(
        join_kernel,
        in_specs=[WHOLE],
        out_specs=blocks_of(like((size, col * seqs)))[0],
        out_shape=like((size, col * seqs)),
        compiler_params=ROOM,
    )(parts)


def split_kernel(*refs):
    out_ref = refs[-1]
    total = total_of([r[...] for r in refs[:-1]]).astype(BF)
    width = out_ref.shape[2]
    for n in range(out_ref.shape[0]):
        out_ref[n] = total[:, n * width : (n + 1) * width]


def split_columns(parts, seqs):
    size, model = parts[0].shape
    return pl.pallas_call(
        split_kernel,
        in_specs=[WHOLE] * len(parts),
        out_specs=blocks_of(like((seqs, size, model // seqs)))[0],
        out_shape=like((seqs, size, model // seqs)),
        compiler_params=ROOM,
    )(*parts)


def rows_kernel(where, *rest):
    ins, (out_ref, store, sems) = rest[:-3], rest[-3:]
    dps, ratio, size, _ = store.shape
    ff_mine = out_ref.shape[0] // ratio
    _, start = piece_rows(ff_mine, dps)
    wait_for(run_copies([(ref, store.at[where[0] ^ k]) for k, ref in enumerate(ins)], sems))
    for q in range(dps):
        for b in range(ratio):
            first = b * ff_mine + start(q)
            out_ref[first : first + size, :] = store[q, b].astype(F32)


def proj_rows(where, parts, ff_mine):
    ratio, size, col = parts[0].shape
    return pl.pallas_call(
        rows_kernel,
        in_specs=[SCALAR] + [ANY] * len(parts),
        out_specs=blocks_of(like((ratio * ff_mine, col)))[0],
        out_shape=like((ratio * ff_mine, col), F32),
        scratch_shapes=[
            pltpu.VMEM((len(parts), ratio, size, col), BF),
            pltpu.SemaphoreType.DMA((len(parts),)),
        ],
        compiler_params=ROOM,
    )(where, *parts)


def head_masks(rows):
    first = lax.broadcasted_iota(jnp.int32, (rows, PAIR), 1) < HD
    causal = lax.broadcasted_iota(jnp.int32, (rows, rows), 0) >= lax.broadcasted_iota(
        jnp.int32, (rows, rows), 1
    )
    return first, causal


def masked_scores(q, keys, causal):
    rows, seen = q.shape[0], keys.shape[0]
    s = mm_nt(q, keys)
    tail = jnp.where(causal, s[:, seen - rows :], NEG_FILL)
    return tail if seen == rows else jnp.concatenate([s[:, : seen - rows], tail], axis=1)


def attend_rows(q, keys, values, first, causal):
    q = q * BF(1.0 / math.sqrt(HD))
    outs, logs = [], []
    for mine in (first, ~first):
        s = masked_scores(jnp.where(mine, q, BF(0)), keys, causal)
        top = jnp.max(s, axis=-1, keepdims=True)
        e = jnp.exp(s - top)
        total = jnp.sum(e, axis=-1, keepdims=True)
        outs.append(mm(e.astype(BF), values) / total)
        logs.append(top + jnp.log(total))
    return jnp.where(first, outs[0], outs[1]).astype(BF), jnp.where(first, logs[0], logs[1])


def attend_kernel(pairs, dps, where, x_ref, vec_ref, bias_ref, *rest):
    w_refs = rest[:dps]
    n1_ref, qkv_ref, att_ref, lse_ref, w, stage, qkv, sems = rest[dps:]
    i = pl.program_id(0)
    rows = x_ref.shape[0]
    part = rows // 2

    @pl.when(i == 0)
    def _():
        settle_rows(place_rows(where, w_refs, w, stage, sems), w, stage)

    unit, _ = normalise(x_ref[...].astype(F32))
    n1 = (unit * vec_ref[0:1, :] + vec_ref[1:2, :]).astype(BF)
    n1_ref[...] = n1
    tile = (mm(n1, w[...]) + bias_ref[...]).astype(BF)
    qkv_ref[...] = tile
    qkv[pl.ds(pl.multiple_of(i * rows, rows), rows), :] = tile
    first, causal = head_masks(rows)
    for j in range(qkv.shape[0] // rows):

        @pl.when(i == j)
        def _(j=j):
            seen = (j + 1) * rows
            for g in range(pairs):
                lanes = slice(g * PAIR, (g + 1) * PAIR)
                keys = qkv[0:seen, (pairs + g) * PAIR : (pairs + g + 1) * PAIR]
                values = qkv[0:seen, (2 * pairs + g) * PAIR : (2 * pairs + g + 1) * PAIR]
                out, log = attend_rows(qkv[j * rows : seen, lanes], keys, values, first, causal)
                for b in range(2):
                    att_ref[b, :, lanes] = out[b * part : (b + 1) * part]
                lse_ref[:, lanes] = log


def attend(where, x_all, table, bias, weights, part):
    length, model = x_all.shape
    depth, width = weights[0].shape
    dps = len(weights)
    heads = width // 3
    rows = 2 * part
    whole = lambda a: pl.BlockSpec(a.shape, lambda i: (0,) * a.ndim)
    tile = lambda cols: pl.BlockSpec((rows, cols), lambda i: (i, 0))
    return pl.pallas_call(
        functools.partial(attend_kernel, heads // PAIR, dps),
        grid=(length // rows,),
        in_specs=[SCALAR, tile(model), whole(table), whole(bias)] + [ANY] * dps,
        out_specs=[
            tile(model),
            tile(width),
            pl.BlockSpec((2, part, heads), lambda i: (i, 0, 0)),
            tile(heads),
        ],
        out_shape=[
            like((length, model)),
            like((length, width)),
            like((length // part, part, heads)),
            like((length, heads), F32),
        ],
        scratch_shapes=[
            pltpu.VMEM((model, width), BF),
            pltpu.VMEM(stage_shape(dps, depth, width), BF),
            pltpu.VMEM((length, width), BF),
            pltpu.SemaphoreType.DMA((dps,)),
        ],
        compiler_params=ROOM,
    )(where, x_all, table, bias, *weights)


def attend_back_kernel(pairs, qkv_ref, ga_ref, lse_ref, gqkv_ref, sums_ref, ak, av):
    length = qkv_ref.shape[0]
    part = ga_ref.shape[1]
    rows = 2 * part
    first, causal = head_masks(rows)
    for g in range(pairs):
        lanes = slice(g * PAIR, (g + 1) * PAIR)
        k_lanes = slice((pairs + g) * PAIR, (pairs + g + 1) * PAIR)
        v_lanes = slice((2 * pairs + g) * PAIR, (2 * pairs + g + 1) * PAIR)
        ak[...] = jnp.zeros_like(ak)
        av[...] = jnp.zeros_like(av)
        for i in range(length // rows):
            here = slice(i * rows, (i + 1) * rows)
            seen = (i + 1) * rows
            q = qkv_ref[here, lanes] * BF(1.0 / math.sqrt(HD))
            ga = jnp.concatenate([ga_ref[b, :, lanes] for b in (2 * i, 2 * i + 1)], axis=0)
            keys = qkv_ref[0:seen, k_lanes]
            values = qkv_ref[0:seen, v_lanes]
            grads = []
            for h, mine in enumerate((first, ~first)):
                q_h = jnp.where(mine, q, BF(0))
                ga_h = jnp.where(mine, ga, BF(0))
                s = masked_scores(q_h, keys, causal)
                lane = g * PAIR + h * HD
                p = jnp.exp(s - lse_ref[here, lane : lane + 1])
                gp = mm_nt(ga_h, values)
                centre = jnp.sum(p * gp, axis=-1, keepdims=True)
                gs = (p * (gp - centre)).astype(BF)
                av[0:seen, :] += mm_tn(p.astype(BF), ga_h)
                ak[0:seen, :] += mm_tn(gs, q_h)
                grads.append(mm(gs, keys))
            gqkv_ref[here, lanes] = (
                jnp.where(first, grads[0], grads[1]) * (1.0 / math.sqrt(HD))
            ).astype(BF)
        gqkv_ref[:, k_lanes] = ak[...].astype(BF)
        gqkv_ref[:, v_lanes] = av[...].astype(BF)
    sums_ref[...] = jnp.sum(gqkv_ref[...].astype(F32), axis=0, keepdims=True)


def attend_back(qkv, grad, lse):
    length, width = qkv.shape
    return pl.pallas_call(
        functools.partial(attend_back_kernel, grad.shape[2] // PAIR),
        in_specs=[WHOLE] * 3,
        out_specs=[WHOLE, WHOLE],
        out_shape=[like((length, width)), like((1, width), F32)],
        scratch_shapes=[pltpu.VMEM((length, PAIR), F32), pltpu.VMEM((length, PAIR), F32)],
        compiler_params=ROOM,
    )(qkv, grad, lse)


def grad_blocks_kernel(where, a_ref, g_ref, *rest):
    outs, (store, stage, sems) = rest[:-3], rest[-3:]
    g = g_ref[...]
    model = a_ref.shape[1]
    for a in range(0, model, 256):
        b = min(model, a + 256)
        store[a:b, :] = mm_tn(a_ref[:, a:b], g).astype(BF)
    wait_for(place_rows(where, outs, store, stage, sems, True))


def chunk_shapes(count, rows, cols):
    shapes = [like((rows, cols))] * count
    if can_halve(count, rows):
        shapes[3:] = [like((cut(rows), cols)), like((rows - cut(rows), cols))]
    return shapes


def grad_blocks(where, a, g, dps):
    model, width = a.shape[1], g.shape[1]
    depth = model // dps
    shapes = chunk_shapes(dps, depth, width)
    return pl.pallas_call(
        grad_blocks_kernel,
        in_specs=[SCALAR, WHOLE, WHOLE],
        out_specs=[ANY] * len(shapes),
        out_shape=shapes,
        scratch_shapes=[
            pltpu.VMEM((model, width), BF),
            pltpu.VMEM(stage_shape(dps, depth, width), BF),
            pltpu.SemaphoreType.DMA((len(shapes),)),
        ],
        compiler_params=ROOM,
    )(where, a, g)


def grad_rows_kernel(dps, where, g_ref, n1_ref, *rest):
    w_refs = rest[:dps]
    out_ref, sums_ref, w, stage, sems = rest[dps:]

    @pl.when(pl.program_id(0) == 0)
    def _():
        settle_rows(place_rows(where, w_refs, w, stage, sems), w, stage)
        sums_ref[...] = jnp.zeros_like(sums_ref)

    grad = mm_nt(g_ref[...], w[...])
    sums_ref[0:1, :] += jnp.sum(grad * n1_ref[...].astype(F32), axis=0, keepdims=True)
    sums_ref[1:2, :] += jnp.sum(grad, axis=0, keepdims=True)
    out_ref[...] = grad.astype(BF)


def grad_rows(where, gqkv, weights, n1, rows):
    length, model = n1.shape
    depth, width = weights[0].shape
    dps = len(weights)
    tile = lambda cols: pl.BlockSpec((rows, cols), lambda i: (i, 0))
    return pl.pallas_call(
        functools.partial(grad_rows_kernel, dps),
        grid=(length // rows,),
        in_specs=[SCALAR, tile(width), tile(model)] + [ANY] * dps,
        out_specs=[tile(model), pl.BlockSpec((2, model), lambda i: (0, 0))],
        out_shape=[like((length, model)), like((2, model), F32)],
        scratch_shapes=[
            pltpu.VMEM((model, width), BF),
            pltpu.VMEM(stage_shape(dps, depth, width), BF),
            pltpu.SemaphoreType.DMA((dps,)),
        ],
        compiler_params=ROOM,
    )(where, gqkv, n1, *weights)


def place_pieces(where, refs, store, sem):
    size, start = piece_rows(store.shape[0], len(refs))
    for k, ref in enumerate(refs):
        spot = store.at[pl.ds(pl.multiple_of(start(where[0] ^ k), 16), size), :]
        one = pltpu.make_async_copy(ref, spot, sem)
        one.start()
        one.wait()


def feed_kernel(dps, where, n2_ref, gm_ref, bias_ref, *rest):
    f_refs, p_refs = rest[:dps], rest[dps : 2 * dps]
    e_ref, gu_ref, gn2_ref, sum_ref, wf, stage, wp, sems, sem = rest[2 * dps :]

    @pl.when(pl.program_id(0) == 0)
    def _():
        copies = place_rows(where, f_refs, wf, stage, sems)
        place_pieces(where, p_refs, wp, sem)
        settle_rows(copies, wf, stage)
        sum_ref[...] = jnp.zeros_like(sum_ref)

    u = mm(n2_ref[...], wf[...]) + bias_ref[...]
    ge = mm_nt(gm_ref[...], wp[...])
    value, slope = gelu_parts(u)
    e_ref[...] = value.astype(BF)
    gu = (ge * slope).astype(BF)
    gu_ref[...] = gu
    sum_ref[...] += jnp.sum(gu.astype(F32), axis=0, keepdims=True)
    gn2_ref[...] = mm_nt(gu, wf[...]).astype(BF)


def feed(where, n2, gm, bias, fc, proj, rows):
    length, model = n2.shape
    dps = len(fc)
    depth, width = fc[0].shape
    whole = lambda shape: pl.BlockSpec(shape, lambda i: (0,) * len(shape))
    tile = lambda cols: pl.BlockSpec((rows, cols), lambda i: (i, 0))
    return pl.pallas_call(
        functools.partial(feed_kernel, dps),
        grid=(length // rows,),
        in_specs=[SCALAR, tile(model), tile(model), whole(bias.shape)] + [ANY] * (2 * dps),
        out_specs=[tile(width), tile(width), tile(model), whole((1, width))],
        out_shape=[
            like((length, width)),
            like((length, width)),
            like((length, model)),
            like((1, width), F32),
        ],
        scratch_shapes=[
            pltpu.VMEM((model, width), BF),
            pltpu.VMEM(stage_shape(dps, depth, width), BF),
            pltpu.VMEM((width, model), BF),
            pltpu.SemaphoreType.DMA((dps,)),
            pltpu.SemaphoreType.DMA,
        ],
        compiler_params=ROOM,
    )(where, n2, gm, bias, *fc, *proj)


def grad_proj_kernel(dps, where, gm_ref, e_ref, *rest):
    outs, (store, sems) = rest[:-2], rest[-2:]
    width = store.shape[0]
    for a in range(0, width, 256):
        b = min(width, a + 256)
        store[a:b, :] = mm_tn(e_ref[:, a:b], gm_ref[...]).astype(BF)
    _, start = piece_rows(width, dps)
    pairs = []
    for i, ref in enumerate(outs):
        first = start(where[0] ^ min(i, dps - 1))
        if i == dps:
            first = first + outs[i - 1].shape[0]
        pairs.append((store.at[pl.ds(pl.multiple_of(first, 16), ref.shape[0]), :], ref))
    wait_for(run_copies(pairs, sems))


def grad_proj(where, gm, e, dps):
    model, width = gm.shape[1], e.shape[1]
    size, _ = piece_rows(width, dps)
    shapes = chunk_shapes(dps, size, model)
    return pl.pallas_call(
        functools.partial(grad_proj_kernel, dps),
        in_specs=[SCALAR, WHOLE, WHOLE],
        out_specs=[ANY] * len(shapes),
        out_shape=shapes,
        scratch_shapes=[
            pltpu.VMEM((width, model), BF),
            pltpu.SemaphoreType.DMA((len(shapes),)),
        ],
        compiler_params=ROOM,
    )(where, gm, e)


def feed_out_kernel(dps, where, e_ref, *rest):
    p_refs = rest[:dps]
    out_ref, wp, sem = rest[dps:]

    @pl.when(pl.program_id(0) == 0)
    def _():
        place_pieces(where, p_refs, wp, sem)

    out_ref[...] = mm(e_ref[...], wp[...]).astype(BF)


def feed_out(where, e, proj, rows):
    length, width = e.shape
    model = proj[0].shape[1]
    return pl.pallas_call(
        functools.partial(feed_out_kernel, len(proj)),
        grid=(length // rows,),
        in_specs=[SCALAR, pl.BlockSpec((rows, width), lambda i: (i, 0))] + [ANY] * len(proj),
        out_specs=pl.BlockSpec((rows, model), lambda i: (i, 0)),
        out_shape=like((length, model)),
        scratch_shapes=[pltpu.VMEM((width, model), BF), pltpu.SemaphoreType.DMA],
        compiler_params=ROOM,
    )(where, e, *proj)


def last_kernel(gn1_ref, gr_ref, vec_ref, x_hbm, out_ref, x_ref, sem):
    copy = pltpu.make_async_copy(x_hbm, x_ref, sem)
    copy.start()
    copy.wait()
    unit, inverse = normalise(x_ref[...].astype(F32))
    grad = norm_back(gn1_ref[...].astype(F32), unit, inverse, vec_ref[0:1, :])
    out_ref[...] = (gr_ref[...] + grad).T.astype(BF)


def last_norm(gn1, x, gr, table):
    shape = like(x.shape[::-1])
    return pl.pallas_call(
        last_kernel,
        in_specs=[WHOLE] * 3 + [ANY],
        out_specs=blocks_of(shape)[0],
        out_shape=shape,
        scratch_shapes=[pltpu.VMEM(x.shape, BF), pltpu.SemaphoreType.DMA],
        compiler_params=ROOM,
    )(gn1, gr, table, x)


def line_blocks(block):
    seqs = lax.axis_size("seq")
    return jnp.stack(
        [block]
        + [lax.ppermute(block, "seq", xor_perm(seqs, 2 * dz)) for dz in range(1, seqs // 2)]
    )


def block_pairs(where, flat, store):
    return [
        (ref.at[dz], store.at[where[0] ^ (i // 2), where[1] ^ (2 * dz + i % 2)])
        for i, ref in enumerate(flat)
        for dz in range(ref.shape[0])
    ]


def head_columns(att_ref, owner):
    count = int(owner.max()) + 1
    parts = []
    for h in range(count):
        dev, slot = [int(i[0]) for i in np.where(owner == h)]
        parts.append(att_ref[dev, :, slot * HD : (slot + 1) * HD])
    return jnp.concatenate(parts, axis=1)


def block_scratch(flat):
    line, depth, width = flat[0].shape
    dps = len(flat) // 2
    return [
        pltpu.VMEM((dps, 2 * line, depth, width), BF),
        pltpu.SemaphoreType.DMA((dps * 2 * line + 1,)),
    ]


def out_kernel(owner, where, att_ref, vec_ref, x_hbm, *rest):
    flat, (r_ref, n2_ref, store, sems, x_ref) = rest[:-5], rest[-5:]
    copies = run_copies(block_pairs(where, flat, store) + [(x_hbm, x_ref)], sems)
    att = head_columns(att_ref, owner)
    dps, seqs, depth, width = store.shape
    wait_for(copies)
    for n in range(seqs):
        here = slice(n * width, (n + 1) * width)
        total = x_ref[:, here].astype(F32) + vec_ref[4:5, here]
        for p in range(dps):
            total = total + mm(att[:, p * depth : (p + 1) * depth], store[p, n])
        r_ref[:, here] = total
    unit, _ = normalise(r_ref[...])
    n2_ref[...] = (unit * vec_ref[5:6, :] + vec_ref[6:7, :]).astype(BF)


def out_project(where, att, x, table, flat, owner):
    return pl.pallas_call(
        functools.partial(out_kernel, owner),
        in_specs=[SCALAR, WHOLE, WHOLE, ANY] + [ANY] * len(flat),
        out_specs=blocks_of(x, x),
        out_shape=[like(x.shape, F32), like(x.shape)],
        scratch_shapes=block_scratch(flat) + [pltpu.VMEM(x.shape, BF)],
        compiler_params=ROOM,
    )(where, att, table, x, *flat)


def back_kernel(owner, where, gn2_ref, r_ref, vec_ref, g_hbm, *rest):
    flat = rest[:-7]
    gr_ref, go_ref, ga_ref, sums_ref, store, sems, g_ref = rest[-7:]
    copies = run_copies([(g_hbm, g_ref)] + block_pairs(where, flat, store), sems)
    copies[0].wait()
    dps, seqs, depth, width = store.shape
    gn2 = gn2_ref[...].astype(F32)
    unit, inverse = normalise(r_ref[...])
    gr = g_ref[...].astype(F32) + norm_back(gn2, unit, inverse, vec_ref[5:6, :])
    go = gr.astype(BF)
    gr_ref[...] = gr
    go_ref[...] = go
    sums_ref[0:1, :] = jnp.sum(go.astype(F32), axis=0, keepdims=True)
    sums_ref[1:2, :] = jnp.sum(gn2 * unit, axis=0, keepdims=True)
    sums_ref[2:3, :] = jnp.sum(gn2, axis=0, keepdims=True)
    sums_ref[3:4, :] = jnp.sum(g_ref[...].astype(F32), axis=0, keepdims=True)
    wait_for(copies[1:])
    found = []
    for p in range(dps):
        total = mm_nt(go[:, 0:width], store[p, 0])
        for n in range(1, seqs):
            total = total + mm_nt(go[:, n * width : (n + 1) * width], store[p, n])
        found.append(total)
    ga = jnp.concatenate(found, axis=1).astype(BF)
    ga_ref[...] = jnp.zeros_like(ga_ref)
    for h in range(int(owner.max()) + 1):
        dev, slot = [int(i[0]) for i in np.where(owner == h)]
        ga_ref[dev, :, slot * HD : (slot + 1) * HD] = ga[:, h * HD : (h + 1) * HD]


def out_back(where, gn2, r, g, table, flat, owner):
    shapes = [
        like(r.shape, F32),
        like(r.shape),
        like((owner.shape[0], r.shape[0], owner.shape[1] * HD)),
        like((4, r.shape[1]), F32),
    ]
    return pl.pallas_call(
        functools.partial(back_kernel, owner),
        in_specs=[SCALAR, WHOLE, WHOLE, WHOLE, ANY] + [ANY] * len(flat),
        out_specs=blocks_of(*shapes),
        out_shape=shapes,
        scratch_shapes=block_scratch(flat) + [pltpu.VMEM(g.shape, BF)],
        compiler_params=ROOM,
    )(where, gn2, r, table, g, *flat)


def grad_out_kernel(owner, where, att_ref, far_att_ref, go_ref, far_go_ref, *rest):
    outs, (store, sems) = rest[:-2], rest[-2:]
    att = jnp.concatenate([head_columns(r, owner) for r in (att_ref, far_att_ref)], axis=0)
    go = jnp.concatenate([go_ref[...], far_go_ref[...]], axis=0)
    dps, line, depth, width = store.shape
    even = where[1] % 2 == 0
    for z in range(line):
        a, b = 2 * z * width, (2 * z + 1) * width
        cols = jnp.where(even, go[:, a : a + width], go[:, b : b + width])
        for p in range(dps):
            store[p, z] = mm_tn(att[:, p * depth : (p + 1) * depth], cols).astype(BF)
    pairs = [
        (store.at[where[0] ^ k, (where[1] // 2) ^ dz], ref.at[dz])
        for k, ref in enumerate(outs)
        for dz in range(line)
    ]
    wait_for(run_copies(pairs, sems))


def grad_out(where, att, far_att, go, far_go, dps, owner):
    seqs = att.shape[0]
    line, depth, width = seqs // 2, go.shape[1] // dps, go.shape[1] // seqs
    return pl.pallas_call(
        functools.partial(grad_out_kernel, owner),
        in_specs=[SCALAR] + [WHOLE] * 4,
        out_specs=[ANY] * dps,
        out_shape=[like((line, depth, width))] * dps,
        scratch_shapes=[
            pltpu.VMEM((dps, line, depth, width), BF),
            pltpu.SemaphoreType.DMA((dps * line,)),
        ],
        compiler_params=ROOM,
    )(where, att, far_att, go, far_go)


def body(tokens, w_qkv, w_out, vectors, w_fc, b_fc, w_proj, cotangent):
    dps = lax.axis_size("dp")
    seqs = lax.axis_size("seq")
    dp = lax.axis_index("dp")
    sq = lax.axis_index("seq")
    rows, model = tokens.shape
    head_count = model // HD
    slots, owner, wide, send, recv = head_plan(head_count, seqs, w_qkv.shape[1])
    send = jnp.asarray(send)[:, :, None, :]
    recv = jnp.asarray(recv)[:, :, None, :]
    mine = slots * HD
    ff_mine = w_fc.shape[1]
    ratio = seqs // dps
    col = w_proj.shape[1]
    where = jnp.stack([dp, sq]).astype(jnp.int32)
    per, wide_vec = vectors.shape
    own_heads = jnp.asarray(owner)[sq]
    pick = (own_heads[:, None] == jnp.arange(head_count)[None, :]).astype(F32)

    def head_rows(vector):
        return jnp.sum(pick[:, :, None] * vector.reshape(1, head_count, HD), axis=1).reshape(-1)

    def head_spread(vector):
        return jnp.sum(pick[:, :, None] * vector.reshape(slots, 1, HD), axis=0).reshape(-1)

    near, far = near_far(dps)
    copies = lambda block: {k: block for k in range(dps)}
    chunks = lambda blocks: dict(enumerate(blocks))

    lanes = send.shape[3]
    small = jnp.concatenate([vectors.reshape(-1), b_fc])
    count = small.shape[0]
    small = jnp.stack(in_order(small, send_rel(copies(small), "dp", near + far)))
    small = as_rows(small.reshape(1, -1), lanes)[0]
    parts = exchange(pack_columns(where, w_qkv, send, small))
    wf_near = send_rel(copies(w_fc), "dp", near)
    pieces = proj_pieces(where, w_proj.reshape(ratio, ff_mine, col), dps)
    pieces = in_order(pieces[0], send_rel(chunks(pieces), "dp", near + far))
    parts, wf_near, x_own, out_own, pieces, fc_own = phase(
        parts, wf_near, tokens, w_out, pieces, w_fc
    )

    x_all = lax.all_gather(x_own, "seq", axis=0, tiled=True)
    own_qkv = unpack_columns(where, parts, recv, w_qkv.shape[0], 3 * mine)
    wq = in_order(own_qkv, send_rel(copies(own_qkv), "dp", near + far))
    wf_far = send_rel(copies(fc_own), "dp", far)
    line = line_blocks(out_own)
    pieces = exchange(turn_pieces(where, pieces))
    small = parts[:, w_qkv.shape[0] :].reshape(seqs, -1)[:, : dps * count].astype(F32)
    small = jnp.take(small.reshape(seqs, dps, count), dp ^ jnp.arange(dps), axis=1)
    table = small[:, :, : per * wide_vec].reshape(seqs, dps, per, wide_vec)
    table = table.transpose(1, 2, 0, 3).reshape(dps * per, model)
    bias_fc = small[:, :, per * wide_vec :].transpose(1, 0, 2).reshape(-1)
    bias_fc = lax.dynamic_slice_in_dim(bias_fc, sq * ff_mine, ff_mine)[None]
    bias_qkv = jnp.concatenate(
        [head_rows(table[2]), jnp.zeros((mine,), F32), head_rows(table[3])]
    )[None]
    x_all, wq, wf_far, line, pieces, table, bias_qkv, cot = phase(
        x_all, wq, wf_far, line, pieces, table, bias_qkv, cotangent
    )

    gm_all = lax.all_gather(cot, "seq", axis=0, tiled=True)
    wo = {0: line, **send_rel(copies(line), "dp", near)}
    n1_all, qkv, att, lse = attend(where, x_all, table, bias_qkv, wq, rows)
    att, wo, pieces = phase(att, wo, pieces)

    att = exchange(att)
    wo.update(send_rel(copies(wo[0]), "dp", far))
    wo_other = {k: swap_core(wo[k]) for k in [0] + near}
    own_proj = join_columns(pieces)
    att, wo, wo_other, own_proj = phase(att, wo, wo_other, own_proj)
    wo_other.update({k: swap_core(wo[k]) for k in far})
    wp_near = send_rel(copies(own_proj), "dp", near)
    flat = [b for k in range(dps) for b in (wo[k], wo_other[k])]
    r, n2 = out_project(where, att, x_own, table, flat, owner)
    n2, att, own_proj = phase(n2, att, own_proj)

    n2_all = lax.all_gather(n2, "seq", axis=0, tiled=True)
    wp = in_order(own_proj, wp_near, send_rel(copies(own_proj), "dp", far))
    far_att = swap_core(att)
    n2_all, gm_all, wp, far_att = phase(n2_all, gm_all, wp, far_att)
    wf = in_order(fc_own, wf_near, wf_far)
    e, gu, gn2_part, sum_fc = feed(where, n2_all, gm_all, bias_fc, wf, wp, 2 * rows)

    gn2 = lax.psum_scatter(gn2_part, "seq", scatter_dimension=0, tiled=True)
    d_proj = grad_proj(where, gm_all, e, dps)
    proj_first = reduce_first(d_proj)
    d_fc = grad_blocks(where, n2_all, gu, dps)
    d_fc, proj_first, e_late = phase(d_fc, proj_first, e)
    proj_in = reduce_second(d_proj, proj_first)
    mlp = feed_out(where, e_late, wp, 2 * rows)
    gn2, d_fc, mlp, proj_in = phase(gn2, d_fc, mlp, proj_in)

    mlp = lax.psum_scatter(mlp, "seq", scatter_dimension=0, tiled=True)
    activations = (r + (mlp.astype(F32) + table[7])).astype(BF)
    gr, go, ga, sums_two = out_back(where, gn2, r, cot, table, flat, owner)
    fc_first = reduce_first(d_fc)
    ga, go, fc_first = phase(ga, go, fc_first)

    ga = exchange(ga)
    fc_in = reduce_second(d_fc, fc_first)
    d_out = grad_out(where, att, far_att, go, swap_core(go), dps, owner)
    g_proj = split_columns(proj_in, seqs)
    d_out = split_far(d_out)
    ga, d_out, fc_in, g_proj = phase(ga, d_out, fc_in, g_proj)

    out_first = reduce_first(d_out)
    g_proj = exchange(g_proj)
    gqkv, gqkv_sums = attend_back(qkv, ga, lse)
    gqkv, out_first = phase(gqkv, out_first)
    d_qkv = grad_blocks(where, n1_all, gqkv, dps)
    out_in = reduce_second(d_out, out_first)
    d_qkv, gqkv, g_proj = phase(d_qkv, gqkv, g_proj)

    qkv_first = reduce_first(d_qkv)
    gn1_part, norm_sums = grad_rows(where, gqkv, wq, n1_all, 2 * rows)
    gn1_part, qkv_first = phase(gn1_part, qkv_first)
    gn1 = lax.psum_scatter(gn1_part, "seq", scatter_dimension=0, tiled=True)
    qkv_in = reduce_second(d_qkv, qkv_first)
    g_line = total_of(out_in).astype(BF)
    g_fc = total_of(fc_in)
    vector_grads = jnp.concatenate(
        [
            ((norm_sums[0] - table[1] * norm_sums[1]) / table[0])[None],
            norm_sums[1:],
            head_spread(gqkv_sums[0, :mine])[None],
            head_spread(gqkv_sums[0, 2 * mine :])[None],
            sums_two,
        ]
    )
    fc_sums = lax.dynamic_update_slice_in_dim(
        jnp.zeros((dps * seqs * b_fc.shape[0],), F32), sum_fc[0], sq * ff_mine, axis=0
    )
    sums = jnp.concatenate(
        [
            vector_grads.reshape(dps, per, seqs, wide_vec).transpose(0, 2, 1, 3).reshape(
                dps, seqs, per * wide_vec
            ),
            fc_sums.reshape(dps, seqs, -1),
        ],
        axis=2,
    )
    sums = as_rows(sums.transpose(1, 0, 2).reshape(seqs, -1).astype(BF), lanes)
    qkv_in, sums, g_proj, g_fc, g_line = phase(qkv_in, sums, g_proj, g_fc, g_line)

    parts = exchange(repack_columns(where, qkv_in, recv, sums))
    g_proj = {
        k: lax.dynamic_slice_in_dim(g_proj, (dp ^ k) * ratio, ratio, axis=0) for k in range(dps)
    }
    g_proj = in_order(g_proj[0], send_rel(g_proj, "dp", near + far))
    g_proj = proj_rows(where, g_proj, ff_mine)
    g_out = total_of(
        [g_line[0]]
        + [
            lax.ppermute(g_line[dz], "seq", xor_perm(seqs, 2 * dz))
            for dz in range(1, seqs // 2)
        ]
    )
    input_grad = last_norm(gn1, x_own, gr, table)
    parts, g_proj, input_grad, activations = phase(parts, g_proj, input_grad, activations)
    g_qkv = restore_columns(where, parts, send, *w_qkv.shape)
    sums = parts[:, w_qkv.shape[0] :].reshape(seqs, -1)[:, : dps * count].astype(F32)
    sums = sums.sum(axis=0).reshape(dps, count)
    sums = {k: lax.dynamic_index_in_dim(sums, dp ^ k, 0, keepdims=False) for k in range(dps)}
    sums = total_of(in_order(sums[0], send_rel(sums, "dp", near + far)))
    return (
        activations,
        input_grad.T,
        g_qkv,
        g_out,
        sums[: per * wide_vec].reshape(per, wide_vec),
        g_fc,
        sums[per * wide_vec :],
        g_proj,
    )


def solution(mesh):
    rows = P(("dp", "seq"), None)
    grid = P("dp", "seq")
    line = P(("dp", "seq"))
    return jax.shard_map(
        body,
        mesh=mesh,
        in_specs=(rows, grid, grid, grid, grid, line, grid, rows),
        out_specs=(rows, rows, grid, grid, grid, grid, line, grid),
        check_vma=False,
    )
```

time: 591 us -> 486 us (0.82)
  waiting for transfers between devices: 282 us -> 184 us
  Pallas kernels: 112 us -> 145 us
  blocking collectives: 28 us -> 0 us
  matrix products: 8.18 us -> 0 us
    all_gather x3, waiting for transfers between devices: 77.4 us -> 5.22 us  [the longest x1 5.19 us: body(): n2_all = lax.all_gather(n2, 'seq', axis=0, tiled=True)]
    ppermute x45 -> x49, waiting for transfers between devices: 160 us -> 111 us  [the longest x24 71.7 us: send_rel(): return {k: lax.ppermute(blocks[k], axis, xor_perm(count, k)) for k in ks}]
    pallas_call x8 -> x20, Pallas kernels: 90.6 us -> 125 us  [the longest x1 15.7 us: attend(): pl.pallas_call(functools.partial(attend_kernel, heads // PAIR, dps), grid...]
    ppermute x3, waiting for transfers between devices: 9.6 us -> 41.1 us  [line_blocks(): lax.ppermute(block, 'seq', xor_perm(seqs, 2 * dz))]
    all_to_all x1 -> x0, blocking collectives: 28 us -> none  [body(): parts = lax.all_to_all(parts, 'seq', 0, 0, tiled=True)]
    reduce_scatter x1, waiting for transfers between devices: 19.3 us -> 4.11 us  [body(): gn2 = lax.psum_scatter(gn2_part, 'seq', scatter_dimension=0, tiled=True)]
    dot_general x4 -> x0, matrix products: 8.18 us -> none  [the longest x1 3.04 us: body(): jnp.einsum('naw,cnw->ac', parts, to_send, preferred_element_type=F32)]
    all_to_all x7 -> x6, waiting for transfers between devices: 15.6 us -> 22.2 us  [exchange(): return lax.all_to_all(block, 'seq', 0, 0, tiled=True)]
  transfers between devices with their start and end apart: 61 -> 64, of which waited for: 27 -> 29; matrix products, arithmetic and copies ran while one was open for 8% -> 7% of each run, Pallas kernels for 15% -> 25%
where the time goes in v5:
time: 486 us; the launch traced here: 480 us
  waiting for transfers between devices  184 us (38%)
  Pallas kernels  145 us (30%)
  starting transfers between devices  84.5 us (17%)
  local copies, waits for them, and re-layouts  34.9 us (7%)
  other arithmetic  15.8 us (3%)
  between operations  15.4 us (3%)
    ppermute x24, waiting for transfers between devices, send_rel(): return {k: lax.ppermute(blocks[k], axis, xor_perm(count, k)) for k in ks}  71.7 us
    ppermute x3, waiting for transfers between devices, line_blocks(): lax.ppermute(block, 'seq', xor_perm(seqs, 2 * dz))  41.1 us
    ppermute x24, starting transfers between devices, send_rel(): return {k: lax.ppermute(blocks[k], axis, xor_perm(count, k)) for k in ks}  29.7 us
    all_to_all x6, starting transfers between devices, exchange(): return lax.all_to_all(block, 'seq', 0, 0, tiled=True)  24.1 us
    all_to_all x6, waiting for transfers between devices, exchange(): return lax.all_to_all(block, 'seq', 0, 0, tiled=True)  22.2 us
    pallas_call x1, Pallas kernels, feed(): pl.pallas_call(functools.partial(feed_kernel, dps), grid=(length // rows,...  20.2 us
    ppermute x4, waiting for transfers between devices, reduce_second(): lax.ppermute(first, 'dp', xor_perm(4, 1))  18.2 us
    pallas_call x1, Pallas kernels, attend(): pl.pallas_call(functools.partial(attend_kernel, heads // PAIR, dps), grid...  15.7 us
  transfers between devices with their start and end apart: 64, of which 29 were waited for; matrix products, arithmetic and copies ran while one was open for 7% of the time, Pallas kernels for 25%

profile of v5, /device:TPU:0, one launch (start us, length us, event | category | flops | bytes accessed | tf_op | source)
XLA Modules:
  0.0 479.6 jit_solution(12461487047656616600)
XLA Ops:
  8.7 3.9 collective-permute-start.2
  20.9 4.9 %all-to-all-start = ((bf16[8,432,128]{2,1,0:T(8,128)(2,1)}), bf16[8,432,128]{2,1,0:T(8,128)(2,1)S(1)}, u32[]{:S(2)}, u32[]{:S(2)}) async-start(bf16[8,432,128]{2,1,0:T(8,128)(2,1)} %shard_map.170), calls=%async_computation | async-start | bytes 1769472 | tf_op jit(solution)/shard_map/all_to_all | solution.py:149
  34.8 14.8 %collective-permute-done.5.rest_1_ = bf16[2,208,200]{2,1,0:T(8,128)(2,1)S(1)} collective-permute-done((bf16[2,208,200]{2,1,0:T(8,128)(2,1)}, bf16[2,208,200]{2,1,0:T(8,128)(2,1)S(1)}, u32[]{:S(2)}, u32[]{:S(2)}) %collective-permute-start.5) | collective-permute-done | bytes 166432 | tf_op jit(solution)/shard_map/ppermute | solution.py:90
  72.7 4.2 all-to-all-start.1
  81.1 33.9 %collective-permute-done.13 = bf16[400,200]{1,0:T(8,128)(2,1)S(1)} collective-permute-done((bf16[400,200]{1,0:T(8,128)(2,1)}, bf16[400,200]{1,0:T(8,128)(2,1)S(1)}, u32[]{:S(2)}, u32[]{:S(2)}) %collective-permute-start.13) | collective-permute-done | bytes 160032 | tf_op jit(solution)/shard_map/ppermute | solution.py:795
  115.8 7.3 %collective-permute-done.12 = bf16[400,200]{1,0:T(8,128)(2,1)S(1)} collective-permute-done((bf16[400,200]{1,0:T(8,128)(2,1)}, bf16[400,200]{1,0:T(8,128)(2,1)S(1)}, u32[]{:S(2)}, u32[]{:S(2)}) %collective-permute-start.12) | collective-permute-done | bytes 160032 | tf_op jit(solution)/shard_map/ppermute | solution.py:795
  124.5 4.1 all-to-all-done.1
  132.7 15.7 %shard_map.174 = (bf16[1024,1600]{1,0:T(8,128)(2,1)}, bf16[1024,768]{1,0:T(8,128)(2,1)}, bf16[8,128,256]{2,1,0:T(8,128)(2,1)}, f32[1024,256]{1,0:T(8,128)}) custom-call(s32[2]{0:T(128)} %pad_add_fusion.where, bf16[1024,1600]{1,0:T(8,128)(2,1)} %all-gather.4.cloned.1.call-done.x_ref, f32[8,1600]{1,0:T(8,128)} %copy-done.17, ...), custom_call_target="tpu_custom_call" | custom-call | tf_op jit(solution)/shard_map/pallas_call | solution.py:507
  151.1 4.3 all-to-all-start.2
  161.2 15.9 %collective-permute-done.17.rest_6_ = bf16[4,400,200]{2,1,0:T(8,128)(2,1)} collective-permute-done((bf16[4,400,200]{2,1,0:T(8,128)(2,1)S(1)}, bf16[4,400,200]{2,1,0:T(8,128)(2,1)}, u32[]{:S(2)}, u32[]{:S(2)}) %collective-permute-start.17) | collective-permute-done | bytes 640032 | tf_op jit(solution)/shard_map/ppermute | solution.py:90
  183.3 6.9 %shard_map.176 = (f32[128,1600]{1,0:T(8,128)}, bf16[128,1600]{1,0:T(8,128)(2,1)}) custom-call(s32[2]{0:T(128)} %pad_add_fusion.where, bf16[8,128,256]{2,1,0:T(8,128)(2,1)} %copy-done.3, f32[8,1600]{1,0:T(8,128)} %copy-done.17, bf16[128,1600]{1,0:T(8,128)(2,1)} %copy.69.x_hbm, bf16[4,400,200]{2,1,0:T(8,128)(2,1)} %copy-done, ...), custom_call_target="tpu_custom_call" | custom-call | tf_op jit(solution)/shard_map/pallas_call | solution.py:842
  195.9 13.3 %collective-permute-done.22.rest_5_.rest_1_ = bf16[208,1600]{1,0:T(8,128)(2,1)S(1)} collective-permute-done((bf16[208,1600]{1,0:T(8,128)(2,1)S(1)}, bf16[208,1600]{1,0:T(8,128)(2,1)S(1)}, u32[]{:S(2)}, u32[]{:S(2)}) %collective-permute-start.22) | collective-permute-done | bytes 665632 | tf_op jit(solution)/shard_map/ppermute | solution.py:90
  209.1 15.2 %collective-permute-done.23.rest_6_.rest_2_ = bf16[208,1600]{1,0:T(8,128)(2,1)S(1)} collective-permute-done((bf16[208,1600]{1,0:T(8,128)(2,1)S(1)}, bf16[208,1600]{1,0:T(8,128)(2,1)S(1)}, u32[]{:S(2)}, u32[]{:S(2)}) %collective-permute-start.23) | collective-permute-done | bytes 665632 | tf_op jit(solution)/shard_map/ppermute | solution.py:90
  224.4 5.2 %all-gather.6.cloned.1.call-done.n2_ref.a_ref = bf16[1024,1600]{1,0:T(8,128)(2,1)} async-done(((bf16[128,1600]{1,0:T(8,128)(2,1)}), bf16[1024,1600]{1,0:T(8,128)(2,1)}) %all-gather.6.cloned.1.call-update) | async-done | bytes 3276816 | tf_op jit(solution)/shard_map/all_gather | solution.py:1011
  229.6 20.2 %shard_map.177 = (bf16[1024,800]{1,0:T(8,128)(2,1)}, bf16[1024,800]{1,0:T(8,128)(2,1)}, bf16[1024,1600]{1,0:T(8,128)(2,1)}, f32[1,800]{1,0:T(1,128)}) custom-call(s32[2]{0:T(128)} %pad_add_fusion.where, bf16[1024,1600]{1,0:T(8,128)(2,1)} %all-gather.6.cloned.1.call-done.n2_ref.a_ref, bf16[1024,1600]{1,0:T(8,128)(2,1)} %all-gather.8.cloned.1.call-done.gm_ref, ...), custom_call_target="tpu_custom_call" | custom-call | tf_op jit(solution)/shard_map/pallas_call | solution.py:690
  249.9 7.7 %shard_map.179 = (bf16[208,1600]{1,0:T(8,128)(2,1)}, bf16[208,1600]{1,0:T(8,128)(2,1)}, bf16[208,1600]{1,0:T(8,128)(2,1)}, bf16[112,1600]{1,0:T(8,128)(2,1)}, bf16[96,1600]{1,0:T(8,128)(2,1)}) custom-call(s32[2]{0:T(128)} %pad_add_fusion.where, bf16[1024,1600]{1,0:T(8,128)(2,1)} %all-gather.8.cloned.1.call-done.gm_ref, ...), custom_call_target="tpu_custom_call" | custom-call | tf_op jit(solution)/shard_map/pallas_call | solution.py:732
  260.6 8.0 %shard_map.178 = (bf16[400,800]{1,0:T(8,128)(2,1)}, bf16[400,800]{1,0:T(8,128)(2,1)}, bf16[400,800]{1,0:T(8,128)(2,1)}, bf16[208,800]{1,0:T(8,128)(2,1)}, bf16[192,800]{1,0:T(8,128)(2,1)}) custom-call(s32[2]{0:T(128)} %pad_add_fusion.where, bf16[1024,1600]{1,0:T(8,128)(2,1)} %all-gather.6.cloned.1.call-done.n2_ref.a_ref, ...), custom_call_target="tpu_custom_call" | custom-call | tf_op jit(solution)/shard_map/pallas_call | solution.py:605
  272.1 11.2 %shard_map.180 = bf16[1024,1600]{1,0:T(8,128)(2,1)} custom-call(s32[2]{0:T(128)} %pad_add_fusion.where, bf16[1024,800]{1,0:T(8,128)(2,1)} %get-tuple-element.217.e_ref, bf16[208,1600]{1,0:T(8,128)(2,1)} %shard_map.175.rest_4_.rest_0_, bf16[208,1600]{1,0:T(8,128)(2,1)} %copy-done.11, bf16[208,1600]{1,0:T(8,128)(2,1)} %copy-done.12, bf16[208,1600]{1,0:T(8,128)(2,1)} %copy-done.13), custom_call_target="tpu_custom_call" | custom-call | tf_op jit(solution)/shard_map/pallas_call | solution.py:759
  287.3 4.1 reduce-scatter.4.cloned.1.call-done.gn2_ref
  294.6 8.0 %shard_map.181 = (f32[128,1600]{1,0:T(8,128)}, bf16[128,1600]{1,0:T(8,128)(2,1)}, bf16[8,128,256]{2,1,0:T(8,128)(2,1)}, f32[4,1600]{1,0:T(4,128)}) custom-call(s32[2]{0:T(128)} %pad_add_fusion.where, bf16[128,1600]{1,0:T(8,128)(2,1)} %reduce-scatter.4.cloned.1.call-done.gn2_ref, f32[128,1600]{1,0:T(8,128)} %get-tuple-element.224.r_ref, ...), custom_call_target="tpu_custom_call" | custom-call | tf_op jit(solution)/shard_map/pallas_call | solution.py:889
  313.6 5.4 %shard_map.182 = (bf16[4,400,200]{2,1,0:T(8,128)(2,1)}, bf16[4,400,200]{2,1,0:T(8,128)(2,1)}, bf16[4,400,200]{2,1,0:T(8,128)(2,1)}, bf16[4,400,200]{2,1,0:T(8,128)(2,1)}) custom-call(s32[2]{0:T(128)} %pad_add_fusion.where, bf16[8,128,256]{2,1,0:T(8,128)(2,1)} %copy-done.3, bf16[8,128,256]{2,1,0:T(8,128)(2,1)} %copy-done.36, ...), custom_call_target="tpu_custom_call" | custom-call | tf_op jit(solution)/shard_map/pallas_call | solution.py:921
  320.2 5.6 %collective-permute-done.33 = bf16[400,800]{1,0:T(8,128)(2,1)S(1)} collective-permute-done((bf16[400,800]{1,0:T(8,128)(2,1)S(1)}, bf16[400,800]{1,0:T(8,128)(2,1)S(1)}, u32[]{:S(2)}, u32[]{:S(2)}) %collective-permute-start.33) | collective-permute-done | bytes 640032 | tf_op jit(solution)/shard_map/ppermute | solution.py:137
  326.8 4.3 all-to-all-done.3.ga_ref
  338.0 14.2 %shard_map.184 = (bf16[1024,768]{1,0:T(8,128)(2,1)}, f32[1,768]{1,0:T(1,128)}) custom-call(bf16[1024,768]{1,0:T(8,128)(2,1)} %get-tuple-element.170.qkv_ref, bf16[8,128,256]{2,1,0:T(8,128)(2,1)} %copy-done.16, f32[1024,256]{1,0:T(8,128)} %get-tuple-element.245.lse_ref), custom_call_target="tpu_custom_call" | custom-call | tf_op jit(solution)/shard_map/pallas_call | solution.py:574
  353.1 7.0 %shard_map.185 = (bf16[400,768]{1,0:T(8,128)(2,1)}, bf16[400,768]{1,0:T(8,128)(2,1)}, bf16[400,768]{1,0:T(8,128)(2,1)}, bf16[208,768]{1,0:T(8,128)(2,1)}, bf16[192,768]{1,0:T(8,128)(2,1)}) custom-call(s32[2]{0:T(128)} %pad_add_fusion.where, bf16[1024,1600]{1,0:T(8,128)(2,1)} %get-tuple-element.169.a_ref.n1_ref, bf16[1024,768]{1,0:T(8,128)(2,1)} %get-tuple-element.258.g_ref), custom_call_target="tpu_custom_call" | custom-call | tf_op jit(solution)/shard_map/pallas_call | solution.py:605
  365.3 8.4 %shard_map.186 = (bf16[1024,1600]{1,0:T(8,128)(2,1)}, f32[2,1600]{1,0:T(2,128)}) custom-call(s32[2]{0:T(128)} %pad_add_fusion.where, bf16[1024,768]{1,0:T(8,128)(2,1)} %get-tuple-element.258.g_ref, bf16[1024,1600]{1,0:T(8,128)(2,1)} %get-tuple-element.169.a_ref.n1_ref, bf16[400,768]{1,0:T(8,128)(2,1)} %shard_map.172.rest_0_, bf16[400,768]{1,0:T(8,128)(2,1)} %copy-done.14, ...), custom_call_target="tpu_custom_call" | custom-call | tf_op jit(solution)/shard_map/pallas_call | solution.py:639
  387.8 12.9 %collective-permute-done.42 = bf16[4,400,200]{2,1,0:T(8,128)(2,1)S(1)} collective-permute-done((bf16[4,400,200]{2,1,0:T(8,128)(2,1)S(1)}, bf16[4,400,200]{2,1,0:T(8,128)(2,1)S(1)}, u32[]{:S(2)}, u32[]{:S(2)}) %collective-permute-start.42) | collective-permute-done | bytes 640032 | tf_op jit(solution)/shard_map/ppermute | solution.py:138
  404.3 8.9 %collective-permute-done.39.rest_1_ = bf16[400,768]{1,0:T(8,128)(2,1)S(1)} collective-permute-done((bf16[400,768]{1,0:T(8,128)(2,1)}, bf16[400,768]{1,0:T(8,128)(2,1)S(1)}, u32[]{:S(2)}, u32[]{:S(2)}) %collective-permute-start.39) | collective-permute-done | bytes 614432 | tf_op jit(solution)/shard_map/ppermute | solution.py:137
  414.0 3.9 shard_map.187
  444.9 8.8 %all-to-all-done.5.in_ref = bf16[8,432,128]{2,1,0:T(8,128)(2,1)S(1)} async-done(((bf16[8,432,128]{2,1,0:T(8,128)(2,1)}), bf16[8,432,128]{2,1,0:T(8,128)(2,1)S(1)}, u32[]{:S(2)}, u32[]{:S(2)}) %all-to-all-start.5) | async-done | bytes 884768 | tf_op jit(solution)/shard_map/all_to_all | solution.py:149
  457.4 4.6 collective-permute-done.47
  464.0 3.7 shard_map.190
  (350 shorter events, 167.8 us)
Async XLA Ops:
  20.9 33.7 %all-to-all-start = ((bf16[8,432,128]{2,1,0:T(8,128)(2,1)}), bf16[8,432,128]{2,1,0:T(8,128)(2,1)S(1)}, u32[]{:S(2)}, u32[]{:S(2)}) async-start(bf16[8,432,128]{2,1,0:T(8,128)(2,1)} %shard_map.170), calls=%async_computation | async-start | bytes 1769472 | tf_op jit(solution)/shard_map/all_to_all | solution.py:149
  25.8 102.8 %all-gather.4.cloned.1.call-start = ((), (), s32[]{:S(2)}) async-start(), calls=%async_computation.9 | async-start | bytes 3833856 | tf_op jit(solution)/shard_map/all_gather | solution.py:976
  25.8 28.8 %collective-permute-start.3 = (bf16[400,800]{1,0:T(8,128)(2,1)}, bf16[400,800]{1,0:T(8,128)(2,1)S(1)}, u32[]{:S(2)}, u32[]{:S(2)}) collective-permute-start(bf16[400,800]{1,0:T(8,128)(2,1)} %rest_0_), channel_id=1, source_target_pairs={{0,8},{8,0},{16,24},{24,16},{1,9},{9,1},{17,25},{25,17},{2,10},{10... | collective-permute-start | bytes 1920008 | tf_op jit(solution)/shard_map/ppermute | solution.py:90
  26.4 28.2 %collective-permute-start.4 = (bf16[400,800]{1,0:T(8,128)(2,1)}, bf16[400,800]{1,0:T(8,128)(2,1)S(1)}, u32[]{:S(2)}, u32[]{:S(2)}) collective-permute-start(bf16[400,800]{1,0:T(8,128)(2,1)} %rest_0_), channel_id=1, source_target_pairs={{0,16},{8,24},{16,0},{24,8},{1,17},{9,25},{17,1},{25,9},{2,18},{10... | collective-permute-start | bytes 1920008 | tf_op jit(solution)/shard_map/ppermute | solution.py:90
  32.8 20.3 %collective-permute-start.6 = (bf16[2,208,200]{2,1,0:T(8,128)(2,1)}, bf16[2,208,200]{2,1,0:T(8,128)(2,1)S(1)}, u32[]{:S(2)}, u32[]{:S(2)}) collective-permute-start(bf16[2,208,200]{2,1,0:T(8,128)(2,1)} %get-tuple-element.152), channel_id=1, source_target_pairs={{0,16},{8,24},{16,0},{24,8},{1,17},{9,25},{17,1},{25,9},{2,18},{10... | collective-permute-start | bytes 499208 | tf_op jit(solution)/shard_map/ppermute | solution.py:90
  33.3 21.3 %collective-permute-start.7 = (bf16[2,208,200]{2,1,0:T(8,128)(2,1)}, bf16[2,208,200]{2,1,0:T(8,128)(2,1)S(1)}, u32[]{:S(2)}, u32[]{:S(2)}) collective-permute-start(bf16[2,208,200]{2,1,0:T(8,128)(2,1)} %get-tuple-element.153), channel_id=1, source_target_pairs={{0,24},{8,16},{16,8},{24,0},{1,25},{9,17},{17,9},{25,1},{2,26},{10... | collective-permute-start | bytes 499208 | tf_op jit(solution)/shard_map/ppermute | solution.py:90
  60.2 64.2 %collective-permute-start.8 = (bf16[400,768]{1,0:T(8,128)(2,1)}, bf16[400,768]{1,0:T(8,128)(2,1)S(1)}, u32[]{:S(2)}, u32[]{:S(2)}) collective-permute-start(bf16[400,768]{1,0:T(8,128)(2,1)} %shard_map.172.rest_0_), channel_id=1, source_target_pairs={{0,8},{8,0},{16,24},{24,16},{1,9},{9,1},{17,25},{25,17},{2,10},{10... | collective-permute-start | bytes 1843208 | tf_op jit(solution)/shard_map/ppermute | solution.py:90
  61.0 63.4 %collective-permute-start.9 = (bf16[400,768]{1,0:T(8,128)(2,1)}, bf16[400,768]{1,0:T(8,128)(2,1)S(1)}, u32[]{:S(2)}, u32[]{:S(2)}) collective-permute-start(bf16[400,768]{1,0:T(8,128)(2,1)} %shard_map.172.rest_0_), channel_id=1, source_target_pairs={{0,16},{8,24},{16,0},{24,8},{1,17},{9,25},{17,1},{25,9},{2,18},{10... | collective-permute-start | bytes 1843208 | tf_op jit(solution)/shard_map/ppermute | solution.py:90
  62.5 61.9 %collective-permute-start.10 = (bf16[400,768]{1,0:T(8,128)(2,1)}, bf16[400,768]{1,0:T(8,128)(2,1)}, u32[]{:S(2)}, u32[]{:S(2)}) collective-permute-start(bf16[400,768]{1,0:T(8,128)(2,1)} %shard_map.172.rest_0_), channel_id=1, source_target_pairs={{0,24},{8,16},{16,8},{24,0},{1,25},{9,17},{17,9},{25,1},{2,26},{10... | collective-permute-start | bytes 1843208 | tf_op jit(solution)/shard_map/ppermute | solution.py:90
  67.1 47.8 %collective-permute-start.13 = (bf16[400,200]{1,0:T(8,128)(2,1)}, bf16[400,200]{1,0:T(8,128)(2,1)S(1)}, u32[]{:S(2)}, u32[]{:S(2)}) collective-permute-start(bf16[400,200]{1,0:T(8,128)(2,1)} %param.13), channel_id=1, source_target_pairs={{0,4},{1,5},{2,6},{3,7},{4,0},{5,1},{6,2},{7,3},{8,12},{9,13},{10,... | collective-permute-start | bytes 480008 | tf_op jit(solution)/shard_map/ppermute | solution.py:795
  72.7 55.9 %all-to-all-start.1 = ((bf16[8,208,200]{1,2,0:T(8,128)(2,1)}), bf16[8,208,200]{1,2,0:T(8,128)(2,1)S(1)}, u32[]{:S(2)}, u32[]{:S(2)}) async-start(bf16[8,208,200]{1,2,0:T(8,128)(2,1)} %copy.70), calls=%async_computation.1 | async-start | bytes 1638400 | tf_op jit(solution)/shard_map/all_to_all | solution.py:149
  76.9 147.6 %all-gather.8.cloned.1.call-start = ((), (), s32[]{:S(2)}) async-start(), calls=%async_computation.11 | async-start | bytes 3833856 | tf_op jit(solution)/shard_map/all_gather | solution.py:995
  78.7 45.8 %collective-permute-start.11 = (bf16[400,800]{1,0:T(8,128)(2,1)}, bf16[400,800]{1,0:T(8,128)(2,1)}, u32[]{:S(2)}, u32[]{:S(2)}) collective-permute-start(bf16[400,800]{1,0:T(8,128)(2,1)} %rest_0_), channel_id=1, source_target_pairs={{0,24},{8,16},{16,8},{24,0},{1,25},{9,17},{17,9},{25,1},{2,26},{10... | collective-permute-start | bytes 1920008 | tf_op jit(solution)/shard_map/ppermute | solution.py:90
  151.1 28.7 %all-to-all-start.2 = ((bf16[8,128,256]{2,1,0:T(8,128)(2,1)}), bf16[8,128,256]{2,1,0:T(8,128)(2,1)S(1)}, u32[]{:S(2)}, u32[]{:S(2)}) async-start(bf16[8,128,256]{2,1,0:T(8,128)(2,1)} %get-tuple-element.174), calls=%async_computation.2 | async-start | bytes 1048576 | tf_op jit(solution)/shard_map/all_to_all | solution.py:149
  155.4 74.2 %all-gather.6.cloned.1.call-start = ((), (), s32[]{:S(2)}) async-start(), calls=%async_computation.10 | async-start | bytes 3833856 | tf_op jit(solution)/shard_map/all_gather | solution.py:1011
  155.4 21.6 %collective-permute-start.17 = (bf16[4,400,200]{2,1,0:T(8,128)(2,1)S(1)}, bf16[4,400,200]{2,1,0:T(8,128)(2,1)}, u32[]{:S(2)}, u32[]{:S(2)}) collective-permute-start(bf16[4,400,200]{2,1,0:T(8,128)(2,1)S(1)} %pad_maximum_fusion.rest_0_), channel_id=1, source_target_pairs={{0,24},{8,16},{16,8},{24,0},{1,25},{9,17},{17,9},{25,1},{2,26},{10... | collective-permute-start | bytes 1920008 | tf_op jit(solution)/shard_map/ppermute | solution.py:90
  190.3 101.2 %reduce-scatter.4.cloned.1.call-start = ((), (), s32[]{:S(2)}) async-start(), calls=%async_computation.12 | async-start | bytes 3833856 | tf_op jit(solution)/shard_map/reduce_scatter | solution.py:1018
  192.2 32.1 %collective-permute-start.23 = (bf16[208,1600]{1,0:T(8,128)(2,1)S(1)}, bf16[208,1600]{1,0:T(8,128)(2,1)S(1)}, u32[]{:S(2)}, u32[]{:S(2)}) collective-permute-start(bf16[208,1600]{1,0:T(8,128)(2,1)S(1)} %copy-done.2), channel_id=1, source_target_pairs={{0,16},{8,24},{16,0},{24,8},{1,17},{9,25},{17,1},{25,9},{2,18},{10... | collective-permute-start | bytes 1996808 | tf_op jit(solution)/shard_map/ppermute | solution.py:90
  193.7 30.7 %collective-permute-start.24 = (bf16[208,1600]{1,0:T(8,128)(2,1)S(1)}, bf16[208,1600]{1,0:T(8,128)(2,1)S(1)}, u32[]{:S(2)}, u32[]{:S(2)}) collective-permute-start(bf16[208,1600]{1,0:T(8,128)(2,1)S(1)} %copy-done.2), channel_id=1, source_target_pairs={{0,24},{8,16},{16,8},{24,0},{1,25},{9,17},{17,9},{25,1},{2,26},{10... | collective-permute-start | bytes 1996808 | tf_op jit(solution)/shard_map/ppermute | solution.py:90
  194.3 30.1 %collective-permute-start.25 = (bf16[8,128,256]{2,1,0:T(8,128)(2,1)}, bf16[8,128,256]{2,1,0:T(8,128)(2,1)S(1)}, u32[]{:S(2)}, u32[]{:S(2)}) collective-permute-start(bf16[8,128,256]{2,1,0:T(8,128)(2,1)} %copy-done.3), channel_id=1, source_target_pairs={{0,1},{1,0},{2,3},{3,2},{4,5},{5,4},{6,7},{7,6},{8,9},{9,8},{10,11... | collective-permute-start | bytes 1572872 | tf_op jit(solution)/shard_map/ppermute | solution.py:145
  249.9 189.4 %reduce-scatter.8.cloned.1.call-start = ((), (), s32[]{:S(2)}) async-start(), calls=%async_computation.14 | async-start | bytes 3833856 | tf_op jit(solution)/shard_map/reduce_scatter | solution.py:1027
  303.4 27.7 %all-to-all-start.3 = ((bf16[8,128,256]{2,1,0:T(8,128)(2,1)}), bf16[8,128,256]{2,1,0:T(8,128)(2,1)S(1)}, u32[]{:S(2)}, u32[]{:S(2)}) async-start(bf16[8,128,256]{2,1,0:T(8,128)(2,1)} %get-tuple-element.229), calls=%async_computation.4 | async-start | bytes 1048576 | tf_op jit(solution)/shard_map/all_to_all | solution.py:149
  332.3 30.0 %all-to-all-start.4 = ((bf16[8,208,200]{1,2,0:T(8,128)(2,1)}), bf16[8,208,200]{1,2,0:T(8,128)(2,1)S(1)}, u32[]{:S(2)}, u32[]{:S(2)}) async-start(bf16[8,208,200]{1,2,0:T(8,128)(2,1)} %copy.77), calls=%async_computation.5 | async-start | bytes 1638400 | tf_op jit(solution)/shard_map/all_to_all | solution.py:149
  335.9 105.3 %reduce-scatter.6.cloned.1.call-start = ((), (), s32[]{:S(2)}) async-start(), calls=%async_computation.13 | async-start | bytes 3833856 | tf_op jit(solution)/shard_map/reduce_scatter | solution.py:1051
  379.5 21.2 %collective-permute-start.42 = (bf16[4,400,200]{2,1,0:T(8,128)(2,1)S(1)}, bf16[4,400,200]{2,1,0:T(8,128)(2,1)S(1)}, u32[]{:S(2)}, u32[]{:S(2)}) collective-permute-start(bf16[4,400,200]{2,1,0:T(8,128)(2,1)S(1)} %pad_maximum_fusion.2), channel_id=1, source_target_pairs={{0,16},{8,24},{16,0},{24,8},{1,17},{9,25},{17,1},{25,9},{2,18},{10... | collective-permute-start | bytes 1920008 | tf_op jit(solution)/shard_map/ppermute | solution.py:138
  380.5 21.2 %collective-permute-start.41 = (bf16[4,400,200]{2,1,0:T(8,128)(2,1)S(1)}, bf16[4,400,200]{2,1,0:T(8,128)(2,1)S(1)}, u32[]{:S(2)}, u32[]{:S(2)}) collective-permute-start(bf16[4,400,200]{2,1,0:T(8,128)(2,1)S(1)} %pad_maximum_fusion.1), channel_id=1, source_target_pairs={{0,8},{8,0},{16,24},{24,16},{1,9},{9,1},{17,25},{25,17},{2,10},{10... | collective-permute-start | bytes 1920008 | tf_op jit(solution)/shard_map/ppermute | solution.py:137
  383.4 29.8 %collective-permute-start.39 = (bf16[400,768]{1,0:T(8,128)(2,1)}, bf16[400,768]{1,0:T(8,128)(2,1)S(1)}, u32[]{:S(2)}, u32[]{:S(2)}) collective-permute-start(bf16[400,768]{1,0:T(8,128)(2,1)} %pad_maximum_fusion.7), channel_id=1, source_target_pairs={{0,8},{8,0},{16,24},{24,16},{1,9},{9,1},{17,25},{25,17},{2,10},{10... | collective-permute-start | bytes 1843208 | tf_op jit(solution)/shard_map/ppermute | solution.py:137
  386.5 26.7 %collective-permute-start.40 = (bf16[400,768]{1,0:T(8,128)(2,1)}, bf16[400,768]{1,0:T(8,128)(2,1)}, u32[]{:S(2)}, u32[]{:S(2)}) collective-permute-start(bf16[400,768]{1,0:T(8,128)(2,1)} %pad_maximum_fusion.8), channel_id=1, source_target_pairs={{0,16},{8,24},{16,0},{24,8},{1,17},{9,25},{17,1},{25,9},{2,18},{10... | collective-permute-start | bytes 1843208 | tf_op jit(solution)/shard_map/ppermute | solution.py:138
  417.9 35.8 %all-to-all-start.5 = ((bf16[8,432,128]{2,1,0:T(8,128)(2,1)}), bf16[8,432,128]{2,1,0:T(8,128)(2,1)S(1)}, u32[]{:S(2)}, u32[]{:S(2)}) async-start(bf16[8,432,128]{2,1,0:T(8,128)(2,1)} %shard_map.187), calls=%async_computation.6 | async-start | bytes 1769472 | tf_op jit(solution)/shard_map/all_to_all | solution.py:149
  427.1 28.9 %collective-permute-start.48 = (bf16[400,200]{1,0:T(8,128)(2,1)}, bf16[400,200]{1,0:T(8,128)(2,1)}, u32[]{:S(2)}, u32[]{:S(2)}) collective-permute-start(bf16[400,200]{1,0:T(8,128)(2,1)} %get-tuple-element.349), channel_id=1, source_target_pairs={{0,6},{1,7},{2,4},{3,5},{4,2},{5,3},{6,0},{7,1},{8,14},{9,15},{10,... | collective-permute-start | bytes 480008 | tf_op jit(solution)/shard_map/ppermute | solution.py:1088
  430.8 31.3 %collective-permute-start.47 = (bf16[400,200]{1,0:T(8,128)(2,1)}, bf16[400,200]{1,0:T(8,128)(2,1)}, u32[]{:S(2)}, u32[]{:S(2)}) collective-permute-start(bf16[400,200]{1,0:T(8,128)(2,1)} %get-tuple-element.350), channel_id=1, source_target_pairs={{0,4},{1,5},{2,6},{3,7},{4,0},{5,1},{6,2},{7,3},{8,12},{9,13},{10,... | collective-permute-start | bytes 480008 | tf_op jit(solution)/shard_map/ppermute | solution.py:1088
  430.8 31.3 %collective-permute-start.46 = (bf16[400,200]{1,0:T(8,128)(2,1)}, bf16[400,200]{1,0:T(8,128)(2,1)S(1)}, u32[]{:S(2)}, u32[]{:S(2)}) collective-permute-start(bf16[400,200]{1,0:T(8,128)(2,1)} %get-tuple-element.348), channel_id=1, source_target_pairs={{0,2},{1,3},{2,0},{3,1},{4,6},{5,7},{6,4},{7,5},{8,10},{9,11},{10,... | collective-permute-start | bytes 480008 | tf_op jit(solution)/shard_map/ppermute | solution.py:1088
  (90 other events, 953.6 us)
Sparse Core Ops, SparseCore 0:
  56.1 71.3 all-gather.3
  130.7 49.6 all-gather.7
  190.4 39.2 all-gather.5
  250.0 41.4 reduce-scatter.3
  293.6 50.8 reduce-scatter.7
  374.0 40.1 reduce-scatter.5

commit v6 on v5

--- a/solution.py
+++ b/solution.py
@@ -125,13 +125,7 @@
 
 def reduce_second(chunks, found):
     if len(chunks) == 5:
-        half = found[0].shape[0]
-        first = jnp.concatenate(
-            [chunks[1][:half], total_of([chunks[1][half:], found[1]]).astype(BF)]
-        )
-        second = jnp.concatenate(
-            [total_of([chunks[2][:half], found[0]]).astype(BF), chunks[2][half:]]
-        )
+        first, second = merge_halves(chunks[1], chunks[2], *found)
         return [
             chunks[0],
             lax.ppermute(first, "dp", xor_perm(4, 1)),
@@ -139,6 +133,25 @@
         ]
     near, far = near_far(len(chunks))
     return [chunks[0]] + found + list(send_rel(dict(enumerate(chunks)), "dp", near).values())
+
+
+def merge_kernel(one_ref, two_ref, top_ref, low_ref, first_ref, second_ref):
+    half = top_ref.shape[0]
+    first_ref[:half] = one_ref[:half]
+    first_ref[half:] = (one_ref[half:].astype(F32) + low_ref[...].astype(F32)).astype(BF)
+    second_ref[:half] = (two_ref[:half].astype(F32) + top_ref[...].astype(F32)).astype(BF)
+    second_ref[half:] = two_ref[half:]
+
+
+def merge_halves(one, two, top, low):
+    shape = like(one.shape)
+    return pl.pallas_call(
+        merge_kernel,
+        in_specs=[WHOLE] * 4,
+        out_specs=blocks_of(shape, shape),
+        out_shape=[shape, shape],
+        compiler_params=ROOM,
+    )(one, two, top, low)
 
 
 def swap_core(block):
@@ -411,13 +424,13 @@
 def rows_kernel(where, *rest):
     ins, (out_ref, store, sems) = rest[:-3], rest[-3:]
     dps, ratio, size, _ = store.shape
-    ff_mine = out_ref.shape[0] // ratio
+    ff_mine = out_ref.shape[1] // ratio
     _, start = piece_rows(ff_mine, dps)
     wait_for(run_copies([(ref, store.at[where[0] ^ k]) for k, ref in enumerate(ins)], sems))
     for q in range(dps):
         for b in range(ratio):
             first = b * ff_mine + start(q)
-            out_ref[first : first + size, :] = store[q, b].astype(F32)
+            out_ref[:, first : first + size] = store[q, b].astype(F32).T
 
 
 def proj_rows(where, parts, ff_mine):
@@ -425,8 +438,8 @@
     return pl.pallas_call(
         rows_kernel,
         in_specs=[SCALAR] + [ANY] * len(parts),
-        out_specs=blocks_of(like((ratio * ff_mine, col)))[0],
-        out_shape=like((ratio * ff_mine, col), F32),
+        out_specs=blocks_of(like((col, ratio * ff_mine)))[0],
+        out_shape=like((col, ratio * ff_mine), F32),
         scratch_shapes=[
             pltpu.VMEM((len(parts), ratio, size, col), BF),
             pltpu.SemaphoreType.DMA((len(parts),)),
@@ -513,15 +526,16 @@
             tile(width),
             pl.BlockSpec((2, part, heads), lambda i: (i, 0, 0)),
             tile(heads),
+            pl.BlockSpec((model, width), lambda i: (0, 0)),
         ],
         out_shape=[
             like((length, model)),
             like((length, width)),
             like((length // part, part, heads)),
             like((length, heads), F32),
+            like((model, width)),
         ],
         scratch_shapes=[
-            pltpu.VMEM((model, width), BF),
             pltpu.VMEM(stage_shape(dps, depth, width), BF),
             pltpu.VMEM((length, width), BF),
             pltpu.SemaphoreType.DMA((dps,)),
@@ -616,59 +630,102 @@
     )(where, a, g)
 
 
-def grad_rows_kernel(dps, where, g_ref, n1_ref, *rest):
-    w_refs = rest[:dps]
-    out_ref, sums_ref, w, stage, sems = rest[dps:]
-
+def grad_rows_kernel(g_ref, n1_ref, w_ref, out_ref, sums_ref):
     @pl.when(pl.program_id(0) == 0)
     def _():
-        settle_rows(place_rows(where, w_refs, w, stage, sems), w, stage)
         sums_ref[...] = jnp.zeros_like(sums_ref)
 
-    grad = mm_nt(g_ref[...], w[...])
+    grad = mm_nt(g_ref[...], w_ref[...])
     sums_ref[0:1, :] += jnp.sum(grad * n1_ref[...].astype(F32), axis=0, keepdims=True)
     sums_ref[1:2, :] += jnp.sum(grad, axis=0, keepdims=True)
     out_ref[...] = grad.astype(BF)
 
 
-def grad_rows(where, gqkv, weights, n1, rows):
+def grad_rows(gqkv, weights, n1, rows):
     length, model = n1.shape
-    depth, width = weights[0].shape
-    dps = len(weights)
+    width = weights.shape[1]
     tile = lambda cols: pl.BlockSpec((rows, cols), lambda i: (i, 0))
     return pl.pallas_call(
-        functools.partial(grad_rows_kernel, dps),
+        grad_rows_kernel,
         grid=(length // rows,),
-        in_specs=[SCALAR, tile(width), tile(model)] + [ANY] * dps,
+        in_specs=[tile(width), tile(model), WHOLE],
         out_specs=[tile(model), pl.BlockSpec((2, model), lambda i: (0, 0))],
         out_shape=[like((length, model)), like((2, model), F32)],
+        compiler_params=ROOM,
+    )(gqkv, n1, weights)
+
+
+def place_pieces(where, refs, store, sems):
+    size, start = piece_rows(store.shape[0], len(refs))
+    starts = [start(q) for q in range(len(refs))] + [store.shape[0]]
+    least = min(b - a for a, b in zip(starts, starts[1:]))
+    count = len(refs)
+    copies, more = [], []
+    for k, ref in enumerate(refs):
+        first = start(where[0] ^ k)
+        spot = pl.ds(pl.multiple_of(first, 16), least)
+        copies.append(
+            pltpu.make_async_copy(ref.at[pl.ds(0, least), :], store.at[spot, :], sems.at[k])
+        )
+        if size > least:
+            spot = pl.ds(pl.multiple_of(first + least, 16), size - least)
+            rest = ref.at[pl.ds(least, size - least), :]
+            more.append(
+                (
+                    start((where[0] ^ k) + 1) - first > least,
+                    pltpu.make_async_copy(rest, store.at[spot, :], sems.at[count + k]),
+                )
+            )
+    for c in copies:
+        c.start()
+    for needed, c in more:
+        pl.when(needed)(c.start)
+    wait_for(copies)
+    for needed, c in more:
+        pl.when(needed)(c.wait)
+
+
+def gather_fc_kernel(where, *rest):
+    f_refs, (wf, stage, sems) = rest[:-3], rest[-3:]
+    settle_rows(place_rows(where, f_refs, wf, stage, sems), wf, stage)
+
+
+def gather_fc(where, fc):
+    dps = len(fc)
+    depth, width = fc[0].shape
+    return pl.pallas_call(
+        gather_fc_kernel,
+        in_specs=[SCALAR] + [ANY] * dps,
+        out_specs=WHOLE,
+        out_shape=like((depth * dps, width)),
         scratch_shapes=[
-            pltpu.VMEM((model, width), BF),
             pltpu.VMEM(stage_shape(dps, depth, width), BF),
             pltpu.SemaphoreType.DMA((dps,)),
         ],
         compiler_params=ROOM,
-    )(where, gqkv, n1, *weights)
-
-
-def place_pieces(where, refs, store, sem):
-    size, start = piece_rows(store.shape[0], len(refs))
-    for k, ref in enumerate(refs):
-        spot = store.at[pl.ds(pl.multiple_of(start(where[0] ^ k), 16), size), :]
-        one = pltpu.make_async_copy(ref, spot, sem)
-        one.start()
-        one.wait()
-
-
-def feed_kernel(dps, where, n2_ref, gm_ref, bias_ref, *rest):
-    f_refs, p_refs = rest[:dps], rest[dps : 2 * dps]
-    e_ref, gu_ref, gn2_ref, sum_ref, wf, stage, wp, sems, sem = rest[2 * dps :]
-
+    )(where, *fc)
+
+
+def gather_proj_kernel(where, *rest):
+    p_refs, (wp, sems) = rest[:-2], rest[-2:]
+    place_pieces(where, p_refs, wp, sems)
+
+
+def gather_proj(where, proj, ff_mine):
+    dps = len(proj)
+    return pl.pallas_call(
+        gather_proj_kernel,
+        in_specs=[SCALAR] + [ANY] * dps,
+        out_specs=WHOLE,
+        out_shape=like((ff_mine, proj[0].shape[1])),
+        scratch_shapes=[pltpu.SemaphoreType.DMA((2 * dps,))],
+        compiler_params=ROOM,
+    )(where, *proj)
+
+
+def feed_kernel(n2_ref, gm_ref, bias_ref, wf, wp, e_ref, gu_ref, gn2_ref, sum_ref):
     @pl.when(pl.program_id(0) == 0)
     def _():
-        copies = place_rows(where, f_refs, wf, stage, sems)
-        place_pieces(where, p_refs, wp, sem)
-        settle_rows(copies, wf, stage)
         sum_ref[...] = jnp.zeros_like(sum_ref)
 
     u = mm(n2_ref[...], wf[...]) + bias_ref[...]
@@ -681,16 +738,15 @@
     gn2_ref[...] = mm_nt(gu, wf[...]).astype(BF)
 
 
-def feed(where, n2, gm, bias, fc, proj, rows):
+def feed(n2, gm, bias, fc, proj, rows):
     length, model = n2.shape
-    dps = len(fc)
-    depth, width = fc[0].shape
+    width = fc.shape[1]
     whole = lambda shape: pl.BlockSpec(shape, lambda i: (0,) * len(shape))
     tile = lambda cols: pl.BlockSpec((rows, cols), lambda i: (i, 0))
     return pl.pallas_call(
-        functools.partial(feed_kernel, dps),
+        feed_kernel,
         grid=(length // rows,),
-        in_specs=[SCALAR, tile(model), tile(model), whole(bias.shape)] + [ANY] * (2 * dps),
+        in_specs=[tile(model), tile(model), whole(bias.shape), WHOLE, WHOLE],
         out_specs=[tile(width), tile(width), tile(model), whole((1, width))],
         out_shape=[
             like((length, width)),
@@ -698,15 +754,8 @@
             like((length, model)),
             like((1, width), F32),
         ],
-        scratch_shapes=[
-            pltpu.VMEM((model, width), BF),
-            pltpu.VMEM(stage_shape(dps, depth, width), BF),
-            pltpu.VMEM((width, model), BF),
-            pltpu.SemaphoreType.DMA((dps,)),
-            pltpu.SemaphoreType.DMA,
-        ],
-        compiler_params=ROOM,
-    )(where, n2, gm, bias, *fc, *proj)
+        compiler_params=ROOM,
+    )(n2, gm, bias, fc, proj)
 
 
 def grad_proj_kernel(dps, where, gm_ref, e_ref, *rest):
@@ -742,29 +791,21 @@
     )(where, gm, e)
 
 
-def feed_out_kernel(dps, where, e_ref, *rest):
-    p_refs = rest[:dps]
-    out_ref, wp, sem = rest[dps:]
-
-    @pl.when(pl.program_id(0) == 0)
-    def _():
-        place_pieces(where, p_refs, wp, sem)
-
+def feed_out_kernel(e_ref, wp, out_ref):
     out_ref[...] = mm(e_ref[...], wp[...]).astype(BF)
 
 
-def feed_out(where, e, proj, rows):
+def feed_out(e, proj, rows):
     length, width = e.shape
-    model = proj[0].shape[1]
-    return pl.pallas_call(
-        functools.partial(feed_out_kernel, len(proj)),
+    model = proj.shape[1]
+    return pl.pallas_call(
+        feed_out_kernel,
         grid=(length // rows,),
-        in_specs=[SCALAR, pl.BlockSpec((rows, width), lambda i: (i, 0))] + [ANY] * len(proj),
+        in_specs=[pl.BlockSpec((rows, width), lambda i: (i, 0)), WHOLE],
         out_specs=pl.BlockSpec((rows, model), lambda i: (i, 0)),
         out_shape=like((length, model)),
-        scratch_shapes=[pltpu.VMEM((width, model), BF), pltpu.SemaphoreType.DMA],
-        compiler_params=ROOM,
-    )(where, e, *proj)
+        compiler_params=ROOM,
+    )(e, proj)
 
 
 def last_kernel(gn1_ref, gr_ref, vec_ref, x_hbm, out_ref, x_ref, sem):
@@ -786,6 +827,22 @@
         scratch_shapes=[pltpu.VMEM(x.shape, BF), pltpu.SemaphoreType.DMA],
         compiler_params=ROOM,
     )(gn1, gr, table, x)
+
+
+def output_kernel(r_ref, mlp_ref, vec_ref, out_ref):
+    out = r_ref[...] + (mlp_ref[...].astype(F32) + vec_ref[7:8, :])
+    out_ref[...] = out.T.astype(BF)
+
+
+def output_rows(r, mlp, table):
+    shape = like(r.shape[::-1])
+    return pl.pallas_call(
+        output_kernel,
+        in_specs=[WHOLE] * 3,
+        out_specs=blocks_of(shape)[0],
+        out_shape=shape,
+        compiler_params=ROOM,
+    )(r, mlp, table)
 
 
 def line_blocks(block):
@@ -994,7 +1051,7 @@
 
     gm_all = lax.all_gather(cot, "seq", axis=0, tiled=True)
     wo = {0: line, **send_rel(copies(line), "dp", near)}
-    n1_all, qkv, att, lse = attend(where, x_all, table, bias_qkv, wq, rows)
+    n1_all, qkv, att, lse, wq = attend(where, x_all, table, bias_qkv, wq, rows)
     att, wo, pieces = phase(att, wo, pieces)
 
     att = exchange(att)
@@ -1011,9 +1068,12 @@
     n2_all = lax.all_gather(n2, "seq", axis=0, tiled=True)
     wp = in_order(own_proj, wp_near, send_rel(copies(own_proj), "dp", far))
     far_att = swap_core(att)
+    wf = in_order(fc_own, wf_near, wf_far)
+    wf = gather_fc(where, wf)
+    wf, wp = phase(wf, wp)
+    wp = gather_proj(where, wp, ff_mine)
     n2_all, gm_all, wp, far_att = phase(n2_all, gm_all, wp, far_att)
-    wf = in_order(fc_own, wf_near, wf_far)
-    e, gu, gn2_part, sum_fc = feed(where, n2_all, gm_all, bias_fc, wf, wp, 2 * rows)
+    e, gu, gn2_part, sum_fc = feed(n2_all, gm_all, bias_fc, wf, wp, 2 * rows)
 
     gn2 = lax.psum_scatter(gn2_part, "seq", scatter_dimension=0, tiled=True)
     d_proj = grad_proj(where, gm_all, e, dps)
@@ -1021,37 +1081,44 @@
     d_fc = grad_blocks(where, n2_all, gu, dps)
     d_fc, proj_first, e_late = phase(d_fc, proj_first, e)
     proj_in = reduce_second(d_proj, proj_first)
-    mlp = feed_out(where, e_late, wp, 2 * rows)
+    mlp = feed_out(e_late, wp, 2 * rows)
     gn2, d_fc, mlp, proj_in = phase(gn2, d_fc, mlp, proj_in)
 
     mlp = lax.psum_scatter(mlp, "seq", scatter_dimension=0, tiled=True)
-    activations = (r + (mlp.astype(F32) + table[7])).astype(BF)
     gr, go, ga, sums_two = out_back(where, gn2, r, cot, table, flat, owner)
     fc_first = reduce_first(d_fc)
     ga, go, fc_first = phase(ga, go, fc_first)
 
     ga = exchange(ga)
+    d_out = split_far(grad_out(where, att, far_att, go, swap_core(go), dps, owner))
+    g_proj = split_columns(proj_in, seqs)
     fc_in = reduce_second(d_fc, fc_first)
-    d_out = grad_out(where, att, far_att, go, swap_core(go), dps, owner)
-    g_proj = split_columns(proj_in, seqs)
-    d_out = split_far(d_out)
     ga, d_out, fc_in, g_proj = phase(ga, d_out, fc_in, g_proj)
 
     out_first = reduce_first(d_out)
     g_proj = exchange(g_proj)
     gqkv, gqkv_sums = attend_back(qkv, ga, lse)
     gqkv, out_first = phase(gqkv, out_first)
+    gn1_part, norm_sums = grad_rows(gqkv, wq, n1_all, 2 * rows)
+    gn1_part, gqkv, mlp, g_proj, d_out = phase(gn1_part, gqkv, mlp, g_proj, d_out)
+
+    gn1 = lax.psum_scatter(gn1_part, "seq", scatter_dimension=0, tiled=True)
+    out_in = reduce_second(d_out, out_first)
     d_qkv = grad_blocks(where, n1_all, gqkv, dps)
-    out_in = reduce_second(d_out, out_first)
-    d_qkv, gqkv, g_proj = phase(d_qkv, gqkv, g_proj)
-
+    d_qkv, out_in = phase(d_qkv, out_in)
     qkv_first = reduce_first(d_qkv)
-    gn1_part, norm_sums = grad_rows(where, gqkv, wq, n1_all, 2 * rows)
-    gn1_part, qkv_first = phase(gn1_part, qkv_first)
-    gn1 = lax.psum_scatter(gn1_part, "seq", scatter_dimension=0, tiled=True)
+    g_line = total_of(out_in).astype(BF)
+    out_in = [g_line[0]] + [
+        lax.ppermute(g_line[dz], "seq", xor_perm(seqs, 2 * dz)) for dz in range(1, seqs // 2)
+    ]
     qkv_in = reduce_second(d_qkv, qkv_first)
-    g_line = total_of(out_in).astype(BF)
+    activations = output_rows(r, mlp, table)
     g_fc = total_of(fc_in)
+    g_proj = {
+        k: lax.dynamic_slice_in_dim(g_proj, (dp ^ k) * ratio, ratio, axis=0) for k in range(dps)
+    }
+    g_proj = in_order(g_proj[0], send_rel(g_proj, "dp", near + far))
+    g_proj = proj_rows(where, g_proj, ff_mine)
     vector_grads = jnp.concatenate(
         [
             ((norm_sums[0] - table[1] * norm_sums[1]) / table[0])[None],
@@ -1074,37 +1141,26 @@
         axis=2,
     )
     sums = as_rows(sums.transpose(1, 0, 2).reshape(seqs, -1).astype(BF), lanes)
-    qkv_in, sums, g_proj, g_fc, g_line = phase(qkv_in, sums, g_proj, g_fc, g_line)
+    qkv_in, sums, activations, g_fc, out_in = phase(qkv_in, sums, activations, g_fc, out_in)
+    g_out = total_of(out_in)
 
     parts = exchange(repack_columns(where, qkv_in, recv, sums))
-    g_proj = {
-        k: lax.dynamic_slice_in_dim(g_proj, (dp ^ k) * ratio, ratio, axis=0) for k in range(dps)
-    }
-    g_proj = in_order(g_proj[0], send_rel(g_proj, "dp", near + far))
-    g_proj = proj_rows(where, g_proj, ff_mine)
-    g_out = total_of(
-        [g_line[0]]
-        + [
-            lax.ppermute(g_line[dz], "seq", xor_perm(seqs, 2 * dz))
-            for dz in range(1, seqs // 2)
-        ]
-    )
     input_grad = last_norm(gn1, x_own, gr, table)
-    parts, g_proj, input_grad, activations = phase(parts, g_proj, input_grad, activations)
+    parts, input_grad, g_proj, g_out = phase(parts, input_grad, g_proj, g_out)
     g_qkv = restore_columns(where, parts, send, *w_qkv.shape)
     sums = parts[:, w_qkv.shape[0] :].reshape(seqs, -1)[:, : dps * count].astype(F32)
     sums = sums.sum(axis=0).reshape(dps, count)
     sums = {k: lax.dynamic_index_in_dim(sums, dp ^ k, 0, keepdims=False) for k in range(dps)}
     sums = total_of(in_order(sums[0], send_rel(sums, "dp", near + far)))
     return (
-        activations,
+        activations.T,
         input_grad.T,
         g_qkv,
         g_out,
         sums[: per * wide_vec].reshape(per, wide_vec),
         g_fc,
         sums[per * wide_vec :],
-        g_proj,
+        g_proj.T,
     )
 
 

time: 486 us -> 465 us (0.957)
  waiting for transfers between devices: 184 us -> 151 us
  Pallas kernels: 145 us -> 159 us
  other arithmetic: 15.8 us -> 9.48 us
  starting transfers between devices: 84.5 us -> 89.4 us
    ppermute x3, waiting for transfers between devices: 41.1 us -> 22.7 us  [line_blocks(): lax.ppermute(block, 'seq', xor_perm(seqs, 2 * dz))]
    pallas_call x3 -> x10, Pallas kernels: 39.9 us -> 53.5 us  [the longest x1 16.6 us: feed(): pl.pallas_call(feed_kernel, grid=(length // rows,), in_specs=[tile(model)...]
    all_to_all x6, waiting for transfers between devices: 22.2 us -> 8.91 us  [exchange(): return lax.all_to_all(block, 'seq', 0, 0, tiled=True)]
    ppermute x4, waiting for transfers between devices: 14.1 us -> 2.27 us  [reduce_second(): lax.ppermute(second, 'dp', xor_perm(4, 2))]
    ppermute x3, waiting for transfers between devices: 4.65 us -> 11.5 us  [body(): lax.ppermute(g_line[dz], 'seq', xor_perm(seqs, 2 * dz))]
    ppermute x4, waiting for transfers between devices: 0.04 us -> 5.49 us  [reduce_first(): lax.ppermute(chunks[4], 'dp', xor_perm(4, 2))]
    all_gather x1, waiting for transfers between devices: 5.19 us -> 0.02 us  [body(): n2_all = lax.all_gather(n2, 'seq', axis=0, tiled=True)]
    unnamed x125 -> x113, local copies, waits for them, and re-layouts: 15.3 us -> 13.1 us
  transfers between devices with their start and end apart: 64 -> 64, of which waited for: 29 -> 29; matrix products, arithmetic and copies ran while one was open for 7% -> 6% of each run, Pallas kernels for 25% -> 30%
where the time goes in v6:
time: 465 us; the launch traced here: 460 us
  Pallas kernels  159 us (34%)
  waiting for transfers between devices  151 us (32%)
  starting transfers between devices  89.4 us (19%)
  local copies, waits for them, and re-layouts  35.2 us (8%)
  between operations  15.1 us (3%)
  other arithmetic  9.48 us (2%)
    ppermute x24, waiting for transfers between devices, send_rel(): return {k: lax.ppermute(blocks[k], axis, xor_perm(count, k)) for k in ks}  75.7 us
    ppermute x24, starting transfers between devices, send_rel(): return {k: lax.ppermute(blocks[k], axis, xor_perm(count, k)) for k in ks}  28 us
    all_to_all x6, starting transfers between devices, exchange(): return lax.all_to_all(block, 'seq', 0, 0, tiled=True)  27.6 us
    ppermute x3, waiting for transfers between devices, line_blocks(): lax.ppermute(block, 'seq', xor_perm(seqs, 2 * dz))  22.7 us
    ppermute x4, waiting for transfers between devices, reduce_second(): lax.ppermute(first, 'dp', xor_perm(4, 1))  20 us
    pallas_call x1, Pallas kernels, feed(): pl.pallas_call(feed_kernel, grid=(length // rows,), in_specs=[tile(model)...  16.6 us
    pallas_call x1, Pallas kernels, attend(): pl.pallas_call(functools.partial(attend_kernel, heads // PAIR, dps), grid...  16.5 us
    pallas_call x2, Pallas kernels, grad_blocks(): pl.pallas_call(grad_blocks_kernel, in_specs=[SCALAR, WHOLE, WHOLE], out_s...  14.7 us
  transfers between devices with their start and end apart: 64, of which 29 were waited for; matrix products, arithmetic and copies ran while one was open for 6% of the time, Pallas kernels for 30%

profile of v6, /device:TPU:0, one launch (start us, length us, event | category | flops | bytes accessed | tf_op | source)
XLA Modules:
  0.0 459.6 jit_solution(1669526533927804116)
XLA Ops:
  21.8 5.0 %all-to-all-start = ((bf16[8,432,128]{2,1,0:T(8,128)(2,1)}), bf16[8,432,128]{2,1,0:T(8,128)(2,1)S(1)}, u32[]{:S(2)}, u32[]{:S(2)}) async-start(bf16[8,432,128]{2,1,0:T(8,128)(2,1)} %shard_map.170), calls=%async_computation | async-start | bytes 1769472 | tf_op jit(solution)/shard_map/all_to_all | solution.py:162
  35.8 14.5 %collective-permute-done.5.rest_1_ = bf16[2,208,200]{2,1,0:T(8,128)(2,1)S(1)} collective-permute-done((bf16[2,208,200]{2,1,0:T(8,128)(2,1)}, bf16[2,208,200]{2,1,0:T(8,128)(2,1)S(1)}, u32[]{:S(2)}, u32[]{:S(2)}) %collective-permute-start.5) | collective-permute-done | bytes 166432 | tf_op jit(solution)/shard_map/ppermute | solution.py:90
  50.3 4.4 collective-permute-done.6.rest_2_
  88.1 3.7 collective-permute-start.14
  92.6 22.7 %collective-permute-done.14 = bf16[400,200]{1,0:T(8,128)(2,1)S(1)} collective-permute-done((bf16[400,200]{1,0:T(8,128)(2,1)}, bf16[400,200]{1,0:T(8,128)(2,1)S(1)}, u32[]{:S(2)}, u32[]{:S(2)}) %collective-permute-start.14) | collective-permute-done | bytes 160032 | tf_op jit(solution)/shard_map/ppermute | solution.py:852
  123.8 16.5 %shard_map.174 = (bf16[1024,1600]{1,0:T(8,128)(2,1)}, bf16[1024,768]{1,0:T(8,128)(2,1)}, bf16[8,128,256]{2,1,0:T(8,128)(2,1)}, f32[1024,256]{1,0:T(8,128)}, bf16[1600,768]{1,0:T(8,128)(2,1)}) custom-call(s32[2]{0:T(128)} %pad_add_fusion.where, bf16[1024,1600]{1,0:T(8,128)(2,1)} %all-gather.4.cloned.1.call-done.x_ref, f32[8,1600]{1,0:T(8,128)} %copy-done.9, ...), custom_call_target="tpu_custom_call" | custom-call | tf_op jit(solution)/shard_map/pallas_call | solution.py:520
  144.5 7.5 %all-to-all-start.2 = ((bf16[8,128,256]{2,1,0:T(8,128)(2,1)}), bf16[8,128,256]{2,1,0:T(8,128)(2,1)S(1)}, u32[]{:S(2)}, u32[]{:S(2)}) async-start(bf16[8,128,256]{2,1,0:T(8,128)(2,1)} %get-tuple-element.193), calls=%async_computation.2 | async-start | bytes 1048576 | tf_op jit(solution)/shard_map/all_to_all | solution.py:162
  157.8 15.9 %collective-permute-done.17.rest_6_ = bf16[4,400,200]{2,1,0:T(8,128)(2,1)} collective-permute-done((bf16[4,400,200]{2,1,0:T(8,128)(2,1)S(1)}, bf16[4,400,200]{2,1,0:T(8,128)(2,1)}, u32[]{:S(2)}, u32[]{:S(2)}) %collective-permute-start.17) | collective-permute-done | bytes 640032 | tf_op jit(solution)/shard_map/ppermute | solution.py:90
  178.7 7.0 %shard_map.176 = (f32[128,1600]{1,0:T(8,128)}, bf16[128,1600]{1,0:T(8,128)(2,1)}) custom-call(s32[2]{0:T(128)} %pad_add_fusion.where, bf16[8,128,256]{2,1,0:T(8,128)(2,1)} %copy-done.1, f32[8,1600]{1,0:T(8,128)} %copy-done.9, bf16[128,1600]{1,0:T(8,128)(2,1)} %copy.61.x_hbm, bf16[4,400,200]{2,1,0:T(8,128)(2,1)} %copy-done, ...), custom_call_target="tpu_custom_call" | custom-call | tf_op jit(solution)/shard_map/pallas_call | solution.py:899
  191.3 4.3 shard_map.177.wf
  195.6 9.0 %collective-permute-done.22.rest_1_ = bf16[208,1600]{1,0:T(8,128)(2,1)S(1)} collective-permute-done((bf16[208,1600]{1,0:T(8,128)(2,1)S(1)}, bf16[208,1600]{1,0:T(8,128)(2,1)S(1)}, u32[]{:S(2)}, u32[]{:S(2)}) %collective-permute-start.22) | collective-permute-done | bytes 665632 | tf_op jit(solution)/shard_map/ppermute | solution.py:90
  204.6 15.2 %collective-permute-done.23.rest_2_ = bf16[208,1600]{1,0:T(8,128)(2,1)S(1)} collective-permute-done((bf16[208,1600]{1,0:T(8,128)(2,1)S(1)}, bf16[208,1600]{1,0:T(8,128)(2,1)S(1)}, u32[]{:S(2)}, u32[]{:S(2)}) %collective-permute-start.23) | collective-permute-done | bytes 665632 | tf_op jit(solution)/shard_map/ppermute | solution.py:90
  221.5 3.9 shard_map.178.wp
  225.5 16.6 %shard_map.179 = (bf16[1024,800]{1,0:T(8,128)(2,1)}, bf16[1024,800]{1,0:T(8,128)(2,1)}, bf16[1024,1600]{1,0:T(8,128)(2,1)}, f32[1,800]{1,0:T(1,128)}) custom-call(bf16[1024,1600]{1,0:T(8,128)(2,1)} %all-gather.6.cloned.1.call-done.n2_ref.a_ref, bf16[1024,1600]{1,0:T(8,128)(2,1)} %all-gather.8.cloned.1.call-done.gm_ref, f32[1,800]{1,0:T(1,128)} %broadcast_in_dim.40.bias_ref, ...), custom_call_target="tpu_custom_call" | custom-call | tf_op jit(solution)/shard_map/pallas_call | solution.py:746
  242.2 7.7 %shard_map.181 = (bf16[208,1600]{1,0:T(8,128)(2,1)}, bf16[208,1600]{1,0:T(8,128)(2,1)}, bf16[208,1600]{1,0:T(8,128)(2,1)}, bf16[112,1600]{1,0:T(8,128)(2,1)}, bf16[96,1600]{1,0:T(8,128)(2,1)}) custom-call(s32[2]{0:T(128)} %pad_add_fusion.where, bf16[1024,1600]{1,0:T(8,128)(2,1)} %all-gather.8.cloned.1.call-done.gm_ref, ...), custom_call_target="tpu_custom_call" | custom-call | tf_op jit(solution)/shard_map/pallas_call | solution.py:781
  252.3 7.9 %shard_map.180 = (bf16[400,800]{1,0:T(8,128)(2,1)}, bf16[400,800]{1,0:T(8,128)(2,1)}, bf16[400,800]{1,0:T(8,128)(2,1)}, bf16[208,800]{1,0:T(8,128)(2,1)}, bf16[192,800]{1,0:T(8,128)(2,1)}) custom-call(s32[2]{0:T(128)} %pad_add_fusion.where, bf16[1024,1600]{1,0:T(8,128)(2,1)} %all-gather.6.cloned.1.call-done.n2_ref.a_ref, ...), custom_call_target="tpu_custom_call" | custom-call | tf_op jit(solution)/shard_map/pallas_call | solution.py:619
  266.9 7.5 %shard_map.182 = bf16[1024,1600]{1,0:T(8,128)(2,1)} custom-call(bf16[1024,800]{1,0:T(8,128)(2,1)} %get-tuple-element.238.e_ref, bf16[800,1600]{1,0:T(8,128)(2,1)} %shard_map.178.wp), custom_call_target="tpu_custom_call" | custom-call | tf_op jit(solution)/shard_map/pallas_call | solution.py:801
  274.4 6.8 %collective-permute-done.28.refs_1_ = bf16[208,1600]{1,0:T(8,128)(2,1)S(1)} collective-permute-done((bf16[208,1600]{1,0:T(8,128)(2,1)}, bf16[208,1600]{1,0:T(8,128)(2,1)S(1)}, u32[]{:S(2)}, u32[]{:S(2)}) %collective-permute-start.28) | collective-permute-done | bytes 665632 | tf_op jit(solution)/shard_map/ppermute | solution.py:131
  287.1 8.0 %shard_map.184 = (f32[128,1600]{1,0:T(8,128)}, bf16[128,1600]{1,0:T(8,128)(2,1)}, bf16[8,128,256]{2,1,0:T(8,128)(2,1)}, f32[4,1600]{1,0:T(4,128)}) custom-call(s32[2]{0:T(128)} %pad_add_fusion.where, bf16[128,1600]{1,0:T(8,128)(2,1)} %reduce-scatter.4.cloned.1.call-done.gn2_ref, f32[128,1600]{1,0:T(8,128)} %get-tuple-element.247.r_ref, f32[8,1600]{1,0:T(8,128)} %copy-done.9, ...), custom_call_target="tpu_custom_call" | custom-call | tf_op jit(solution)/shard_map/pallas_call | solution.py:946
  307.6 5.5 %shard_map.185 = (bf16[4,400,200]{2,1,0:T(8,128)(2,1)}, bf16[4,400,200]{2,1,0:T(8,128)(2,1)}, bf16[4,400,200]{2,1,0:T(8,128)(2,1)}, bf16[4,400,200]{2,1,0:T(8,128)(2,1)}) custom-call(s32[2]{0:T(128)} %pad_add_fusion.where, bf16[8,128,256]{2,1,0:T(8,128)(2,1)} %copy-done.1, bf16[8,128,256]{2,1,0:T(8,128)(2,1)} %copy-done.22, ...), custom_call_target="tpu_custom_call" | custom-call | tf_op jit(solution)/shard_map/pallas_call | solution.py:978
  314.2 6.2 %collective-permute-done.33 = bf16[400,800]{1,0:T(8,128)(2,1)S(1)} collective-permute-done((bf16[400,800]{1,0:T(8,128)(2,1)}, bf16[400,800]{1,0:T(8,128)(2,1)S(1)}, u32[]{:S(2)}, u32[]{:S(2)}) %collective-permute-start.33) | collective-permute-done | bytes 640032 | tf_op jit(solution)/shard_map/ppermute | solution.py:131
  329.6 14.1 %shard_map.188 = (bf16[1024,768]{1,0:T(8,128)(2,1)}, f32[1,768]{1,0:T(1,128)}) custom-call(bf16[1024,768]{1,0:T(8,128)(2,1)} %get-tuple-element.189.qkv_ref, bf16[8,128,256]{2,1,0:T(8,128)(2,1)} %copy-done.10, f32[1024,256]{1,0:T(8,128)} %get-tuple-element.270.lse_ref), custom_call_target="tpu_custom_call" | custom-call | tf_op jit(solution)/shard_map/pallas_call | solution.py:588
  343.8 7.8 %shard_map.189 = (bf16[1024,1600]{1,0:T(8,128)(2,1)}, f32[2,1600]{1,0:T(2,128)}) custom-call(bf16[1024,768]{1,0:T(8,128)(2,1)} %get-tuple-element.282.g_ref, bf16[1024,1600]{1,0:T(8,128)(2,1)} %get-tuple-element.188.n1_ref.a_ref, bf16[1600,768]{1,0:T(8,128)(2,1)} %get-tuple-element.275.w_ref), custom_call_target="tpu_custom_call" | custom-call | tf_op jit(solution)/shard_map/pallas_call | solution.py:648
  363.7 6.8 %shard_map.190 = (bf16[400,768]{1,0:T(8,128)(2,1)}, bf16[400,768]{1,0:T(8,128)(2,1)}, bf16[400,768]{1,0:T(8,128)(2,1)}, bf16[208,768]{1,0:T(8,128)(2,1)}, bf16[192,768]{1,0:T(8,128)(2,1)}) custom-call(s32[2]{0:T(128)} %pad_add_fusion.where, bf16[1024,1600]{1,0:T(8,128)(2,1)} %get-tuple-element.188.n1_ref.a_ref, bf16[1024,768]{1,0:T(8,128)(2,1)} %get-tuple-element.282.g_ref), custom_call_target="tpu_custom_call" | custom-call | tf_op jit(solution)/shard_map/pallas_call | solution.py:619
  370.6 7.0 %collective-permute-done.37 = bf16[4,400,200]{2,1,0:T(8,128)(2,1)S(1)} collective-permute-done((bf16[4,400,200]{2,1,0:T(8,128)(2,1)}, bf16[4,400,200]{2,1,0:T(8,128)(2,1)S(1)}, u32[]{:S(2)}, u32[]{:S(2)}) %collective-permute-start.37) | collective-permute-done | bytes 640032 | tf_op jit(solution)/shard_map/ppermute | solution.py:131
  382.0 5.3 %collective-permute-done.40.low_ref = bf16[192,768]{1,0:T(8,128)(2,1)} collective-permute-done((bf16[192,768]{1,0:T(8,128)(2,1)}, bf16[192,768]{1,0:T(8,128)(2,1)}, u32[]{:S(2)}, u32[]{:S(2)}) %collective-permute-start.40) | collective-permute-done | bytes 294944 | tf_op jit(solution)/shard_map/ppermute | solution.py:120
  403.0 9.1 %collective-permute-done.44 = bf16[400,200]{1,0:T(8,128)(2,1)S(1)} collective-permute-done((bf16[400,200]{1,0:T(8,128)(2,1)S(1)}, bf16[400,200]{1,0:T(8,128)(2,1)S(1)}, u32[]{:S(2)}, u32[]{:S(2)}) %collective-permute-start.44) | collective-permute-done | bytes 160032 | tf_op jit(solution)/shard_map/ppermute | solution.py:1112
  412.2 4.0 shard_map.194
  416.2 4.3 all-to-all-start.5
  425.2 4.6 collective-permute-done.46.rest_1_
  429.8 5.1 %collective-permute-done.47.rest_2_ = bf16[2,208,200]{2,1,0:T(8,128)(2,1)S(1)} collective-permute-done((bf16[2,208,200]{2,1,0:T(8,128)(2,1)S(1)}, bf16[2,208,200]{2,1,0:T(8,128)(2,1)S(1)}, u32[]{:S(2)}, u32[]{:S(2)}) %collective-permute-start.47) | collective-permute-done | bytes 166432 | tf_op jit(solution)/shard_map/ppermute | solution.py:90
  440.1 3.7 shard_map.195
  (320 shorter events, 177.1 us)
Async XLA Ops:
  21.8 33.7 %all-to-all-start = ((bf16[8,432,128]{2,1,0:T(8,128)(2,1)}), bf16[8,432,128]{2,1,0:T(8,128)(2,1)S(1)}, u32[]{:S(2)}, u32[]{:S(2)}) async-start(bf16[8,432,128]{2,1,0:T(8,128)(2,1)} %shard_map.170), calls=%async_computation | async-start | bytes 1769472 | tf_op jit(solution)/shard_map/all_to_all | solution.py:162
  26.8 94.1 %all-gather.4.cloned.1.call-start = ((), (), s32[]{:S(2)}) async-start(), calls=%async_computation.9 | async-start | bytes 3833856 | tf_op jit(solution)/shard_map/all_gather | solution.py:1033
  26.9 27.9 %collective-permute-start.3 = (bf16[400,800]{1,0:T(8,128)(2,1)S(1)}, bf16[400,800]{1,0:T(8,128)(2,1)S(1)}, u32[]{:S(2)}, u32[]{:S(2)}) collective-permute-start(bf16[400,800]{1,0:T(8,128)(2,1)S(1)} %copy-done.12), channel_id=1, source_target_pairs={{0,8},{8,0},{16,24},{24,16},{1,9},{9,1},{17,25},{25,17},{2,10},{10... | collective-permute-start | bytes 1920008 | tf_op jit(solution)/shard_map/ppermute | solution.py:90
  27.5 28.0 %collective-permute-start.4 = (bf16[400,800]{1,0:T(8,128)(2,1)S(1)}, bf16[400,800]{1,0:T(8,128)(2,1)S(1)}, u32[]{:S(2)}, u32[]{:S(2)}) collective-permute-start(bf16[400,800]{1,0:T(8,128)(2,1)S(1)} %copy-done.12), channel_id=1, source_target_pairs={{0,16},{8,24},{16,0},{24,8},{1,17},{9,25},{17,1},{25,9},{2,18},{10... | collective-permute-start | bytes 1920008 | tf_op jit(solution)/shard_map/ppermute | solution.py:90
  33.8 20.9 %collective-permute-start.6 = (bf16[2,208,200]{2,1,0:T(8,128)(2,1)}, bf16[2,208,200]{2,1,0:T(8,128)(2,1)S(1)}, u32[]{:S(2)}, u32[]{:S(2)}) collective-permute-start(bf16[2,208,200]{2,1,0:T(8,128)(2,1)} %get-tuple-element.171), channel_id=1, source_target_pairs={{0,16},{8,24},{16,0},{24,8},{1,17},{9,25},{17,1},{25,9},{2,18},{10... | collective-permute-start | bytes 499208 | tf_op jit(solution)/shard_map/ppermute | solution.py:90
  57.5 27.1 %collective-permute-start.12 = (bf16[400,200]{1,0:T(8,128)(2,1)}, bf16[400,200]{1,0:T(8,128)(2,1)}, u32[]{:S(2)}, u32[]{:S(2)}) collective-permute-start(bf16[400,200]{1,0:T(8,128)(2,1)} %param.13), channel_id=1, source_target_pairs={{0,2},{1,3},{2,0},{3,1},{4,6},{5,7},{6,4},{7,5},{8,10},{9,11},{10,... | collective-permute-start | bytes 480008 | tf_op jit(solution)/shard_map/ppermute | solution.py:852
  59.2 28.9 %collective-permute-start.13 = (bf16[400,200]{1,0:T(8,128)(2,1)}, bf16[400,200]{1,0:T(8,128)(2,1)}, u32[]{:S(2)}, u32[]{:S(2)}) collective-permute-start(bf16[400,200]{1,0:T(8,128)(2,1)} %param.13), channel_id=1, source_target_pairs={{0,4},{1,5},{2,6},{3,7},{4,0},{5,1},{6,2},{7,3},{8,12},{9,13},{10,... | collective-permute-start | bytes 480008 | tf_op jit(solution)/shard_map/ppermute | solution.py:852
  65.0 51.6 %collective-permute-start.10 = (bf16[400,768]{1,0:T(8,128)(2,1)}, bf16[400,768]{1,0:T(8,128)(2,1)}, u32[]{:S(2)}, u32[]{:S(2)}) collective-permute-start(bf16[400,768]{1,0:T(8,128)(2,1)} %shard_map.172.rest_0_), channel_id=1, source_target_pairs={{0,24},{8,16},{16,8},{24,0},{1,25},{9,17},{17,9},{25,1},{2,26},{10... | collective-permute-start | bytes 1843208 | tf_op jit(solution)/shard_map/ppermute | solution.py:90
  66.5 50.2 %collective-permute-start.8 = (bf16[400,768]{1,0:T(8,128)(2,1)}, bf16[400,768]{1,0:T(8,128)(2,1)}, u32[]{:S(2)}, u32[]{:S(2)}) collective-permute-start(bf16[400,768]{1,0:T(8,128)(2,1)} %shard_map.172.rest_0_), channel_id=1, source_target_pairs={{0,8},{8,0},{16,24},{24,16},{1,9},{9,1},{17,25},{25,17},{2,10},{10... | collective-permute-start | bytes 1843208 | tf_op jit(solution)/shard_map/ppermute | solution.py:90
  67.6 49.0 %collective-permute-start.9 = (bf16[400,768]{1,0:T(8,128)(2,1)}, bf16[400,768]{1,0:T(8,128)(2,1)}, u32[]{:S(2)}, u32[]{:S(2)}) collective-permute-start(bf16[400,768]{1,0:T(8,128)(2,1)} %shard_map.172.rest_0_), channel_id=1, source_target_pairs={{0,16},{8,24},{16,0},{24,8},{1,17},{9,25},{17,1},{25,9},{2,18},{10... | collective-permute-start | bytes 1843208 | tf_op jit(solution)/shard_map/ppermute | solution.py:90
  74.9 45.1 %all-to-all-start.1 = ((bf16[8,208,200]{1,2,0:T(8,128)(2,1)}), bf16[8,208,200]{1,2,0:T(8,128)(2,1)S(1)}, u32[]{:S(2)}, u32[]{:S(2)}) async-start(bf16[8,208,200]{1,2,0:T(8,128)(2,1)} %copy.62), calls=%async_computation.1 | async-start | bytes 1638400 | tf_op jit(solution)/shard_map/all_to_all | solution.py:162
  78.5 147.0 %all-gather.8.cloned.1.call-start = ((), (), s32[]{:S(2)}) async-start(), calls=%async_computation.11 | async-start | bytes 3833856 | tf_op jit(solution)/shard_map/all_gather | solution.py:1052
  84.6 32.1 %collective-permute-start.11 = (bf16[400,800]{1,0:T(8,128)(2,1)S(1)}, bf16[400,800]{1,0:T(8,128)(2,1)}, u32[]{:S(2)}, u32[]{:S(2)}) collective-permute-start(bf16[400,800]{1,0:T(8,128)(2,1)S(1)} %copy-done.12), channel_id=1, source_target_pairs={{0,24},{8,16},{16,8},{24,0},{1,25},{9,17},{17,9},{25,1},{2,26},{10... | collective-permute-start | bytes 1920008 | tf_op jit(solution)/shard_map/ppermute | solution.py:90
  88.1 27.2 %collective-permute-start.14 = (bf16[400,200]{1,0:T(8,128)(2,1)}, bf16[400,200]{1,0:T(8,128)(2,1)S(1)}, u32[]{:S(2)}, u32[]{:S(2)}) collective-permute-start(bf16[400,200]{1,0:T(8,128)(2,1)} %param.13), channel_id=1, source_target_pairs={{0,6},{1,7},{2,4},{3,5},{4,2},{5,3},{6,0},{7,1},{8,14},{9,15},{10,... | collective-permute-start | bytes 480008 | tf_op jit(solution)/shard_map/ppermute | solution.py:852
  121.9 20.4 %collective-permute-start.15 = (bf16[4,400,200]{2,1,0:T(8,128)(2,1)S(1)}, bf16[4,400,200]{2,1,0:T(8,128)(2,1)S(1)}, u32[]{:S(2)}, u32[]{:S(2)}) collective-permute-start(bf16[4,400,200]{2,1,0:T(8,128)(2,1)S(1)} %pad_maximum_fusion.rest_0_), channel_id=1, source_target_pairs={{0,8},{8,0},{16,24},{24,16},{1,9},{9,1},{17,25},{25,17},{2,10},{10... | collective-permute-start | bytes 1920008 | tf_op jit(solution)/shard_map/ppermute | solution.py:90
  123.5 20.1 %collective-permute-start.16 = (bf16[4,400,200]{2,1,0:T(8,128)(2,1)S(1)}, bf16[4,400,200]{2,1,0:T(8,128)(2,1)S(1)}, u32[]{:S(2)}, u32[]{:S(2)}) collective-permute-start(bf16[4,400,200]{2,1,0:T(8,128)(2,1)S(1)} %pad_maximum_fusion.rest_0_), channel_id=1, source_target_pairs={{0,16},{8,24},{16,0},{24,8},{1,17},{9,25},{17,1},{25,9},{2,18},{10... | collective-permute-start | bytes 1920008 | tf_op jit(solution)/shard_map/ppermute | solution.py:90
  144.5 30.7 %all-to-all-start.2 = ((bf16[8,128,256]{2,1,0:T(8,128)(2,1)}), bf16[8,128,256]{2,1,0:T(8,128)(2,1)S(1)}, u32[]{:S(2)}, u32[]{:S(2)}) async-start(bf16[8,128,256]{2,1,0:T(8,128)(2,1)} %get-tuple-element.193), calls=%async_computation.2 | async-start | bytes 1048576 | tf_op jit(solution)/shard_map/all_to_all | solution.py:162
  152.0 73.5 %all-gather.6.cloned.1.call-start = ((), (), s32[]{:S(2)}) async-start(), calls=%async_computation.10 | async-start | bytes 3833856 | tf_op jit(solution)/shard_map/all_gather | solution.py:1068
  152.0 21.6 %collective-permute-start.17 = (bf16[4,400,200]{2,1,0:T(8,128)(2,1)S(1)}, bf16[4,400,200]{2,1,0:T(8,128)(2,1)}, u32[]{:S(2)}, u32[]{:S(2)}) collective-permute-start(bf16[4,400,200]{2,1,0:T(8,128)(2,1)S(1)} %pad_maximum_fusion.rest_0_), channel_id=1, source_target_pairs={{0,24},{8,16},{16,8},{24,0},{1,25},{9,17},{17,9},{25,1},{2,26},{10... | collective-permute-start | bytes 1920008 | tf_op jit(solution)/shard_map/ppermute | solution.py:90
  153.6 20.1 %collective-permute-start.18 = (bf16[4,400,200]{2,1,0:T(8,128)(2,1)S(1)}, bf16[4,400,200]{2,1,0:T(8,128)(2,1)}, u32[]{:S(2)}, u32[]{:S(2)}) collective-permute-start(bf16[4,400,200]{2,1,0:T(8,128)(2,1)S(1)} %pad_maximum_fusion.rest_0_), channel_id=1, source_target_pairs={{0,1},{1,0},{2,3},{3,2},{4,5},{5,4},{6,7},{7,6},{8,9},{9,8},{10,11... | collective-permute-start | bytes 1920008 | tf_op jit(solution)/shard_map/ppermute | solution.py:158
  185.7 97.4 %reduce-scatter.4.cloned.1.call-start = ((), (), s32[]{:S(2)}) async-start(), calls=%async_computation.12 | async-start | bytes 3833856 | tf_op jit(solution)/shard_map/reduce_scatter | solution.py:1078
  187.7 32.1 %collective-permute-start.23 = (bf16[208,1600]{1,0:T(8,128)(2,1)S(1)}, bf16[208,1600]{1,0:T(8,128)(2,1)S(1)}, u32[]{:S(2)}, u32[]{:S(2)}) collective-permute-start(bf16[208,1600]{1,0:T(8,128)(2,1)S(1)} %copy-done.8), channel_id=1, source_target_pairs={{0,16},{8,24},{16,0},{24,8},{1,17},{9,25},{17,1},{25,9},{2,18},{10... | collective-permute-start | bytes 1996808 | tf_op jit(solution)/shard_map/ppermute | solution.py:90
  189.2 30.6 %collective-permute-start.24 = (bf16[208,1600]{1,0:T(8,128)(2,1)S(1)}, bf16[208,1600]{1,0:T(8,128)(2,1)S(1)}, u32[]{:S(2)}, u32[]{:S(2)}) collective-permute-start(bf16[208,1600]{1,0:T(8,128)(2,1)S(1)} %copy-done.8), channel_id=1, source_target_pairs={{0,24},{8,16},{16,8},{24,0},{1,25},{9,17},{17,9},{25,1},{2,26},{10... | collective-permute-start | bytes 1996808 | tf_op jit(solution)/shard_map/ppermute | solution.py:90
  189.7 35.7 %collective-permute-start.25 = (bf16[8,128,256]{2,1,0:T(8,128)(2,1)}, bf16[8,128,256]{2,1,0:T(8,128)(2,1)S(1)}, u32[]{:S(2)}, u32[]{:S(2)}) collective-permute-start(bf16[8,128,256]{2,1,0:T(8,128)(2,1)} %copy-done.1), channel_id=1, source_target_pairs={{0,1},{1,0},{2,3},{3,2},{4,5},{5,4},{6,7},{7,6},{8,9},{9,8},{10,11... | collective-permute-start | bytes 1572872 | tf_op jit(solution)/shard_map/ppermute | solution.py:158
  242.1 111.9 %reduce-scatter.6.cloned.1.call-start = ((), (), s32[]{:S(2)}) async-start(), calls=%async_computation.13 | async-start | bytes 3833856 | tf_op jit(solution)/shard_map/reduce_scatter | solution.py:1087
  295.2 27.7 %all-to-all-start.3 = ((bf16[8,128,256]{2,1,0:T(8,128)(2,1)}), bf16[8,128,256]{2,1,0:T(8,128)(2,1)S(1)}, u32[]{:S(2)}, u32[]{:S(2)}) async-start(bf16[8,128,256]{2,1,0:T(8,128)(2,1)} %get-tuple-element.252), calls=%async_computation.4 | async-start | bytes 1048576 | tf_op jit(solution)/shard_map/all_to_all | solution.py:162
  324.2 29.9 %all-to-all-start.4 = ((bf16[8,208,200]{1,2,0:T(8,128)(2,1)}), bf16[8,208,200]{1,2,0:T(8,128)(2,1)S(1)}, u32[]{:S(2)}, u32[]{:S(2)}) async-start(bf16[8,208,200]{1,2,0:T(8,128)(2,1)} %copy.69), calls=%async_computation.6 | async-start | bytes 1638400 | tf_op jit(solution)/shard_map/all_to_all | solution.py:162
  327.7 112.4 %reduce-scatter.8.cloned.1.call-start = ((), (), s32[]{:S(2)}) async-start(), calls=%async_computation.14 | async-start | bytes 3833856 | tf_op jit(solution)/shard_map/reduce_scatter | solution.py:1105
  357.1 20.4 %collective-permute-start.37 = (bf16[4,400,200]{2,1,0:T(8,128)(2,1)}, bf16[4,400,200]{2,1,0:T(8,128)(2,1)S(1)}, u32[]{:S(2)}, u32[]{:S(2)}) collective-permute-start(bf16[4,400,200]{2,1,0:T(8,128)(2,1)} %get-tuple-element.293), channel_id=1, source_target_pairs={{0,8},{8,0},{16,24},{24,16},{1,9},{9,1},{17,25},{25,17},{2,10},{10... | collective-permute-start | bytes 1920008 | tf_op jit(solution)/shard_map/ppermute | solution.py:131
  390.0 22.1 %collective-permute-start.41 = (bf16[400,768]{1,0:T(8,128)(2,1)}, bf16[400,768]{1,0:T(8,128)(2,1)}, u32[]{:S(2)}, u32[]{:S(2)}) collective-permute-start(bf16[400,768]{1,0:T(8,128)(2,1)} %get-tuple-element.300), channel_id=1, source_target_pairs={{0,8},{8,0},{16,24},{24,16},{1,9},{9,1},{17,25},{25,17},{2,10},{10... | collective-permute-start | bytes 1843208 | tf_op jit(solution)/shard_map/ppermute | solution.py:131
  391.2 20.9 %collective-permute-start.42 = (bf16[400,768]{1,0:T(8,128)(2,1)}, bf16[400,768]{1,0:T(8,128)(2,1)}, u32[]{:S(2)}, u32[]{:S(2)}) collective-permute-start(bf16[400,768]{1,0:T(8,128)(2,1)} %get-tuple-element.301), channel_id=1, source_target_pairs={{0,16},{8,24},{16,0},{24,8},{1,17},{9,25},{17,1},{25,9},{2,18},{10... | collective-permute-start | bytes 1843208 | tf_op jit(solution)/shard_map/ppermute | solution.py:132
  416.2 27.6 %all-to-all-start.5 = ((bf16[8,432,128]{2,1,0:T(8,128)(2,1)}), bf16[8,432,128]{2,1,0:T(8,128)(2,1)S(1)}, u32[]{:S(2)}, u32[]{:S(2)}) async-start(bf16[8,432,128]{2,1,0:T(8,128)(2,1)} %shard_map.194), calls=%async_computation.7 | async-start | bytes 1769472 | tf_op jit(solution)/shard_map/all_to_all | solution.py:162
  (85 other events, 951.4 us)
Sparse Core Ops, SparseCore 0:
  56.8 64.0 all-gather.3
  122.5 52.6 all-gather.7
  185.8 39.1 all-gather.5
  242.2 40.8 reduce-scatter.3
  285.3 50.6 reduce-scatter.5
  354.2 44.7 reduce-scatter.7

commit v7 on v6

--- a/solution.py
+++ b/solution.py
@@ -152,6 +152,16 @@
         out_shape=[shape, shape],
         compiler_params=ROOM,
     )(one, two, top, low)
+
+
+def gather_far(found, far):
+    if len(found) + len(far) != 4:
+        return {(k, 0): b for k, b in send_rel({k: found[0, 0] for k in far}, "dp", far).items()}
+    half = found[0, 0].shape[0] // 2
+    return {
+        (3, 0): lax.ppermute(found[2, 0][:half], "dp", xor_perm(4, 1)),
+        (3, half): lax.ppermute(found[1, 0][half:], "dp", xor_perm(4, 2)),
+    }
 
 
 def swap_core(block):
@@ -853,11 +863,14 @@
     )
 
 
-def block_pairs(where, flat, store):
+def block_pairs(where, places, flat, store):
     return [
-        (ref.at[dz], store.at[where[0] ^ (i // 2), where[1] ^ (2 * dz + i % 2)])
+        (
+            ref.at[j],
+            store.at[where[0] ^ places[i // 2][0], where[1] ^ (2 * (places[i // 2][1] + j) + i % 2)],
+        )
         for i, ref in enumerate(flat)
-        for dz in range(ref.shape[0])
+        for j in range(ref.shape[0])
     ]
 
 
@@ -870,18 +883,17 @@
     return jnp.concatenate(parts, axis=1)
 
 
-def block_scratch(flat):
+def block_scratch(dps, flat):
     line, depth, width = flat[0].shape
-    dps = len(flat) // 2
     return [
         pltpu.VMEM((dps, 2 * line, depth, width), BF),
         pltpu.SemaphoreType.DMA((dps * 2 * line + 1,)),
     ]
 
 
-def out_kernel(owner, where, att_ref, vec_ref, x_hbm, *rest):
+def out_kernel(owner, places, where, att_ref, vec_ref, x_hbm, *rest):
     flat, (r_ref, n2_ref, store, sems, x_ref) = rest[:-5], rest[-5:]
-    copies = run_copies(block_pairs(where, flat, store) + [(x_hbm, x_ref)], sems)
+    copies = run_copies(block_pairs(where, places, flat, store) + [(x_hbm, x_ref)], sems)
     att = head_columns(att_ref, owner)
     dps, seqs, depth, width = store.shape
     wait_for(copies)
@@ -895,21 +907,22 @@
     n2_ref[...] = (unit * vec_ref[5:6, :] + vec_ref[6:7, :]).astype(BF)
 
 
-def out_project(where, att, x, table, flat, owner):
-    return pl.pallas_call(
-        functools.partial(out_kernel, owner),
+def out_project(where, att, x, table, places, flat, owner):
+    dps = max(k for k, _ in places) + 1
+    return pl.pallas_call(
+        functools.partial(out_kernel, owner, places),
         in_specs=[SCALAR, WHOLE, WHOLE, ANY] + [ANY] * len(flat),
         out_specs=blocks_of(x, x),
         out_shape=[like(x.shape, F32), like(x.shape)],
-        scratch_shapes=block_scratch(flat) + [pltpu.VMEM(x.shape, BF)],
+        scratch_shapes=block_scratch(dps, flat) + [pltpu.VMEM(x.shape, BF)],
         compiler_params=ROOM,
     )(where, att, table, x, *flat)
 
 
-def back_kernel(owner, where, gn2_ref, r_ref, vec_ref, g_hbm, *rest):
+def back_kernel(owner, places, where, gn2_ref, r_ref, vec_ref, g_hbm, *rest):
     flat = rest[:-7]
     gr_ref, go_ref, ga_ref, sums_ref, store, sems, g_ref = rest[-7:]
-    copies = run_copies([(g_hbm, g_ref)] + block_pairs(where, flat, store), sems)
+    copies = run_copies([(g_hbm, g_ref)] + block_pairs(where, places, flat, store), sems)
     copies[0].wait()
     dps, seqs, depth, width = store.shape
     gn2 = gn2_ref[...].astype(F32)
@@ -936,7 +949,8 @@
         ga_ref[dev, :, slot * HD : (slot + 1) * HD] = ga[:, h * HD : (h + 1) * HD]
 
 
-def out_back(where, gn2, r, g, table, flat, owner):
+def out_back(where, gn2, r, g, table, places, flat, owner):
+    dps = max(k for k, _ in places) + 1
     shapes = [
         like(r.shape, F32),
         like(r.shape),
@@ -944,11 +958,11 @@
         like((4, r.shape[1]), F32),
     ]
     return pl.pallas_call(
-        functools.partial(back_kernel, owner),
+        functools.partial(back_kernel, owner, places),
         in_specs=[SCALAR, WHOLE, WHOLE, WHOLE, ANY] + [ANY] * len(flat),
         out_specs=blocks_of(*shapes),
         out_shape=shapes,
-        scratch_shapes=block_scratch(flat) + [pltpu.VMEM(g.shape, BF)],
+        scratch_shapes=block_scratch(dps, flat) + [pltpu.VMEM(g.shape, BF)],
         compiler_params=ROOM,
     )(where, gn2, r, table, g, *flat)
 
@@ -1018,6 +1032,7 @@
     chunks = lambda blocks: dict(enumerate(blocks))
 
     lanes = send.shape[3]
+    gm_all = lax.all_gather(cotangent, "seq", axis=0, tiled=True)
     small = jnp.concatenate([vectors.reshape(-1), b_fc])
     count = small.shape[0]
     small = jnp.stack(in_order(small, send_rel(copies(small), "dp", near + far)))
@@ -1026,8 +1041,8 @@
     wf_near = send_rel(copies(w_fc), "dp", near)
     pieces = proj_pieces(where, w_proj.reshape(ratio, ff_mine, col), dps)
     pieces = in_order(pieces[0], send_rel(chunks(pieces), "dp", near + far))
-    parts, wf_near, x_own, out_own, pieces, fc_own = phase(
-        parts, wf_near, tokens, w_out, pieces, w_fc
+    parts, wf_near, x_own, out_own, pieces, fc_own, gm_all = phase(
+        parts, wf_near, tokens, w_out, pieces, w_fc, gm_all
     )
 
     x_all = lax.all_gather(x_own, "seq", axis=0, tiled=True)
@@ -1035,7 +1050,7 @@
     wq = in_order(own_qkv, send_rel(copies(own_qkv), "dp", near + far))
     wf_far = send_rel(copies(fc_own), "dp", far)
     line = line_blocks(out_own)
-    pieces = exchange(turn_pieces(where, pieces))
+    pieces = turn_pieces(where, pieces)
     small = parts[:, w_qkv.shape[0] :].reshape(seqs, -1)[:, : dps * count].astype(F32)
     small = jnp.take(small.reshape(seqs, dps, count), dp ^ jnp.arange(dps), axis=1)
     table = small[:, :, : per * wide_vec].reshape(seqs, dps, per, wide_vec)
@@ -1045,24 +1060,27 @@
     bias_qkv = jnp.concatenate(
         [head_rows(table[2]), jnp.zeros((mine,), F32), head_rows(table[3])]
     )[None]
-    x_all, wq, wf_far, line, pieces, table, bias_qkv, cot = phase(
-        x_all, wq, wf_far, line, pieces, table, bias_qkv, cotangent
+    x_all, wq, wf_far, line, pieces, table, bias_qkv = phase(
+        x_all, wq, wf_far, line, pieces, table, bias_qkv
     )
 
-    gm_all = lax.all_gather(cot, "seq", axis=0, tiled=True)
-    wo = {0: line, **send_rel(copies(line), "dp", near)}
+    pieces = exchange(pieces)
+    wo = {(0, 0): line}
+    wo.update({(k, 0): b for k, b in send_rel(copies(line), "dp", near).items()})
     n1_all, qkv, att, lse, wq = attend(where, x_all, table, bias_qkv, wq, rows)
     att, wo, pieces = phase(att, wo, pieces)
 
     att = exchange(att)
-    wo.update(send_rel(copies(wo[0]), "dp", far))
-    wo_other = {k: swap_core(wo[k]) for k in [0] + near}
+    wo_other = {place: swap_core(b) for place, b in wo.items()}
+    found = gather_far(wo, far)
+    wo.update(found)
     own_proj = join_columns(pieces)
     att, wo, wo_other, own_proj = phase(att, wo, wo_other, own_proj)
-    wo_other.update({k: swap_core(wo[k]) for k in far})
+    wo_other.update({place: swap_core(wo[place]) for place in found})
     wp_near = send_rel(copies(own_proj), "dp", near)
-    flat = [b for k in range(dps) for b in (wo[k], wo_other[k])]
-    r, n2 = out_project(where, att, x_own, table, flat, owner)
+    places = sorted(wo)
+    flat = [b for place in places for b in (wo[place], wo_other[place])]
+    r, n2 = out_project(where, att, x_own, table, places, flat, owner)
     n2, att, own_proj = phase(n2, att, own_proj)
 
     n2_all = lax.all_gather(n2, "seq", axis=0, tiled=True)
@@ -1072,7 +1090,7 @@
     wf = gather_fc(where, wf)
     wf, wp = phase(wf, wp)
     wp = gather_proj(where, wp, ff_mine)
-    n2_all, gm_all, wp, far_att = phase(n2_all, gm_all, wp, far_att)
+    n2_all, wp, far_att = phase(n2_all, wp, far_att)
     e, gu, gn2_part, sum_fc = feed(n2_all, gm_all, bias_fc, wf, wp, 2 * rows)
 
     gn2 = lax.psum_scatter(gn2_part, "seq", scatter_dimension=0, tiled=True)
@@ -1085,7 +1103,7 @@
     gn2, d_fc, mlp, proj_in = phase(gn2, d_fc, mlp, proj_in)
 
     mlp = lax.psum_scatter(mlp, "seq", scatter_dimension=0, tiled=True)
-    gr, go, ga, sums_two = out_back(where, gn2, r, cot, table, flat, owner)
+    gr, go, ga, sums_two = out_back(where, gn2, r, cotangent, table, places, flat, owner)
     fc_first = reduce_first(d_fc)
     ga, go, fc_first = phase(ga, go, fc_first)
 

time: 465 us -> 465 us (level)
  waiting for transfers between devices: 151 us -> 159 us
    all_to_all x6, waiting for transfers between devices: 8.91 us -> 17.7 us  [exchange(): return lax.all_to_all(block, 'seq', 0, 0, tiled=True)]
    ppermute x3, waiting for transfers between devices: 22.7 us -> 14.2 us  [line_blocks(): lax.ppermute(block, 'seq', xor_perm(seqs, 2 * dz))]
    ppermute x3, starting transfers between devices: 7.78 us -> 1.77 us  [line_blocks(): lax.ppermute(block, 'seq', xor_perm(seqs, 2 * dz))]
    ppermute x0 -> x2, waiting for transfers between devices: none -> 5.34 us  [the longest x1 5.11 us: gather_far(): lax.ppermute(found[2, 0][:half], 'dp', xor_perm(4, 1))]
    ppermute x24 -> x23, starting transfers between devices: 28 us -> 29.6 us  [send_rel(): return {k: lax.ppermute(blocks[k], axis, xor_perm(count, k)) for k in ks}]
    unnamed x113 -> x120, local copies, waits for them, and re-layouts: 13.1 us -> 14.6 us
    ppermute x24 -> x23, waiting for transfers between devices: 75.7 us -> 75.7 us  [send_rel(): return {k: lax.ppermute(blocks[k], axis, xor_perm(count, k)) for k in ks}]
  transfers between devices with their start and end apart: 64 -> 66, of which waited for: 29 -> 36; matrix products, arithmetic and copies ran while one was open for 6% -> 6% of each run, Pallas kernels for 30% -> 30%
where the time goes in v7:
time: 465 us; the launch traced here: 458 us
  waiting for transfers between devices  159 us (34%)
  Pallas kernels  159 us (34%)
  starting transfers between devices  86 us (18%)
  local copies, waits for them, and re-layouts  31.8 us (7%)
  between operations  15.1 us (3%)
  other arithmetic  7.92 us (2%)
    ppermute x23, waiting for transfers between devices, send_rel(): return {k: lax.ppermute(blocks[k], axis, xor_perm(count, k)) for k in ks}  75.7 us
    ppermute x23, starting transfers between devices, send_rel(): return {k: lax.ppermute(blocks[k], axis, xor_perm(count, k)) for k in ks}  29.6 us
    all_to_all x6, starting transfers between devices, exchange(): return lax.all_to_all(block, 'seq', 0, 0, tiled=True)  25.4 us
    ppermute x4, waiting for transfers between devices, reduce_second(): lax.ppermute(first, 'dp', xor_perm(4, 1))  20 us
    all_to_all x6, waiting for transfers between devices, exchange(): return lax.all_to_all(block, 'seq', 0, 0, tiled=True)  17.7 us
    pallas_call x1, Pallas kernels, attend(): pl.pallas_call(functools.partial(attend_kernel, heads // PAIR, dps), grid...  16.5 us
    pallas_call x1, Pallas kernels, feed(): pl.pallas_call(feed_kernel, grid=(length // rows,), in_specs=[tile(model)...  16.4 us
    pallas_call x2, Pallas kernels, grad_blocks(): pl.pallas_call(grad_blocks_kernel, in_specs=[SCALAR, WHOLE, WHOLE], out_s...  14.7 us
  transfers between devices with their start and end apart: 66, of which 36 were waited for; matrix products, arithmetic and copies ran while one was open for 6% of the time, Pallas kernels for 30%

profile of v7, /device:TPU:0, one launch (start us, length us, event | category | flops | bytes accessed | tf_op | source)
XLA Modules:
  0.0 458.5 jit_solution(87429808598680976)
XLA Ops:
  23.9 5.0 %all-to-all-start = ((bf16[8,432,128]{2,1,0:T(8,128)(2,1)}), bf16[8,432,128]{2,1,0:T(8,128)(2,1)S(1)}, u32[]{:S(2)}, u32[]{:S(2)}) async-start(bf16[8,432,128]{2,1,0:T(8,128)(2,1)} %shard_map.170), calls=%async_computation | async-start | bytes 1769472 | tf_op jit(solution)/shard_map/all_to_all | solution.py:172
  37.9 14.5 %collective-permute-done.5.rest_1_ = bf16[2,208,200]{2,1,0:T(8,128)(2,1)S(1)} collective-permute-done((bf16[2,208,200]{2,1,0:T(8,128)(2,1)}, bf16[2,208,200]{2,1,0:T(8,128)(2,1)S(1)}, u32[]{:S(2)}, u32[]{:S(2)}) %collective-permute-start.5) | collective-permute-done | bytes 166432 | tf_op jit(solution)/shard_map/ppermute | solution.py:90
  52.5 4.4 collective-permute-done.6.rest_2_
  57.6 12.6 %all-to-all-done.in_ref = bf16[8,432,128]{2,1,0:T(8,128)(2,1)S(1)} async-done(((bf16[8,432,128]{2,1,0:T(8,128)(2,1)}), bf16[8,432,128]{2,1,0:T(8,128)(2,1)S(1)}, u32[]{:S(2)}, u32[]{:S(2)}) %all-to-all-start) | async-done | bytes 884768 | tf_op jit(solution)/shard_map/all_to_all | solution.py:172
  88.8 4.5 collective-permute-done.13
  97.5 8.2 %collective-permute-done.14 = bf16[400,200]{1,0:T(8,128)(2,1)S(1)} collective-permute-done((bf16[400,200]{1,0:T(8,128)(2,1)}, bf16[400,200]{1,0:T(8,128)(2,1)S(1)}, u32[]{:S(2)}, u32[]{:S(2)}) %collective-permute-start.14) | collective-permute-done | bytes 160032 | tf_op jit(solution)/shard_map/ppermute | solution.py:862
  110.0 13.8 %collective-permute-done.11.rest_3_ = bf16[400,800]{1,0:T(8,128)(2,1)} collective-permute-done((bf16[400,800]{1,0:T(8,128)(2,1)S(1)}, bf16[400,800]{1,0:T(8,128)(2,1)}, u32[]{:S(2)}, u32[]{:S(2)}) %collective-permute-start.11) | collective-permute-done | bytes 640032 | tf_op jit(solution)/shard_map/ppermute | solution.py:90
  125.1 4.1 all-to-all-start.1
  132.4 16.5 %shard_map.174 = (bf16[1024,1600]{1,0:T(8,128)(2,1)}, bf16[1024,768]{1,0:T(8,128)(2,1)}, bf16[8,128,256]{2,1,0:T(8,128)(2,1)}, f32[1024,256]{1,0:T(8,128)}, bf16[1600,768]{1,0:T(8,128)(2,1)}) custom-call(s32[2]{0:T(128)} %pad_add_fusion.where, bf16[1024,1600]{1,0:T(8,128)(2,1)} %all-gather.6.cloned.1.call-done.x_ref, f32[8,1600]{1,0:T(8,128)} %copy-done.10, ...), custom_call_target="tpu_custom_call" | custom-call | tf_op jit(solution)/shard_map/pallas_call | solution.py:530
  152.3 4.7 %all-to-all-start.2 = ((bf16[8,128,256]{2,1,0:T(8,128)(2,1)}), bf16[8,128,256]{2,1,0:T(8,128)(2,1)S(1)}, u32[]{:S(2)}, u32[]{:S(2)}) async-start(bf16[8,128,256]{2,1,0:T(8,128)(2,1)} %get-tuple-element.193), calls=%async_computation.2 | async-start | bytes 1048576 | tf_op jit(solution)/shard_map/all_to_all | solution.py:172
  166.2 5.1 %collective-permute-done.17.rest_6_ = bf16[2,400,200]{2,1,0:T(8,128)(2,1)S(1)} collective-permute-done((bf16[2,400,200]{2,1,0:T(8,128)(2,1)}, bf16[2,400,200]{2,1,0:T(8,128)(2,1)S(1)}, u32[]{:S(2)}, u32[]{:S(2)}) %collective-permute-start.17) | collective-permute-done | bytes 320032 | tf_op jit(solution)/shard_map/ppermute | solution.py:162
  176.2 6.9 %shard_map.176 = (f32[128,1600]{1,0:T(8,128)}, bf16[128,1600]{1,0:T(8,128)(2,1)}) custom-call(s32[2]{0:T(128)} %pad_add_fusion.where, bf16[8,128,256]{2,1,0:T(8,128)(2,1)} %copy-done.3, f32[8,1600]{1,0:T(8,128)} %copy-done.10, bf16[128,1600]{1,0:T(8,128)(2,1)} %copy.62.x_hbm, bf16[4,400,200]{2,1,0:T(8,128)(2,1)} %copy-done, ...), custom_call_target="tpu_custom_call" | custom-call | tf_op jit(solution)/shard_map/pallas_call | solution.py:912
  187.6 4.1 shard_map.177.wf
  191.7 9.9 %collective-permute-done.24.rest_1_ = bf16[208,1600]{1,0:T(8,128)(2,1)S(1)} collective-permute-done((bf16[208,1600]{1,0:T(8,128)(2,1)S(1)}, bf16[208,1600]{1,0:T(8,128)(2,1)S(1)}, u32[]{:S(2)}, u32[]{:S(2)}) %collective-permute-start.24) | collective-permute-done | bytes 665632 | tf_op jit(solution)/shard_map/ppermute | solution.py:90
  201.6 14.9 %collective-permute-done.26.rest_3_ = bf16[208,1600]{1,0:T(8,128)(2,1)S(1)} collective-permute-done((bf16[208,1600]{1,0:T(8,128)(2,1)S(1)}, bf16[208,1600]{1,0:T(8,128)(2,1)S(1)}, u32[]{:S(2)}, u32[]{:S(2)}) %collective-permute-start.26) | collective-permute-done | bytes 665632 | tf_op jit(solution)/shard_map/ppermute | solution.py:90
  224.0 16.4 %shard_map.179 = (bf16[1024,800]{1,0:T(8,128)(2,1)}, bf16[1024,800]{1,0:T(8,128)(2,1)}, bf16[1024,1600]{1,0:T(8,128)(2,1)}, f32[1,800]{1,0:T(1,128)}) custom-call(bf16[1024,1600]{1,0:T(8,128)(2,1)} %all-gather.8.cloned.1.call-done.n2_ref.a_ref, bf16[1024,1600]{1,0:T(8,128)(2,1)} %all-gather.4.cloned.1.call-done.gm_ref, f32[1,800]{1,0:T(1,128)} %broadcast_in_dim.40.bias_ref, ...), custom_call_target="tpu_custom_call" | custom-call | tf_op jit(solution)/shard_map/pallas_call | solution.py:756
  240.9 7.7 %shard_map.181 = (bf16[208,1600]{1,0:T(8,128)(2,1)}, bf16[208,1600]{1,0:T(8,128)(2,1)}, bf16[208,1600]{1,0:T(8,128)(2,1)}, bf16[112,1600]{1,0:T(8,128)(2,1)}, bf16[96,1600]{1,0:T(8,128)(2,1)}) custom-call(s32[2]{0:T(128)} %pad_add_fusion.where, bf16[1024,1600]{1,0:T(8,128)(2,1)} %all-gather.4.cloned.1.call-done.gm_ref, ...), custom_call_target="tpu_custom_call" | custom-call | tf_op jit(solution)/shard_map/pallas_call | solution.py:791
  251.7 7.9 %shard_map.180 = (bf16[400,800]{1,0:T(8,128)(2,1)}, bf16[400,800]{1,0:T(8,128)(2,1)}, bf16[400,800]{1,0:T(8,128)(2,1)}, bf16[208,800]{1,0:T(8,128)(2,1)}, bf16[192,800]{1,0:T(8,128)(2,1)}) custom-call(s32[2]{0:T(128)} %pad_add_fusion.where, bf16[1024,1600]{1,0:T(8,128)(2,1)} %all-gather.8.cloned.1.call-done.n2_ref.a_ref, ...), custom_call_target="tpu_custom_call" | custom-call | tf_op jit(solution)/shard_map/pallas_call | solution.py:629
  266.2 7.5 %shard_map.182 = bf16[1024,1600]{1,0:T(8,128)(2,1)} custom-call(bf16[1024,800]{1,0:T(8,128)(2,1)} %get-tuple-element.238.e_ref, bf16[800,1600]{1,0:T(8,128)(2,1)} %shard_map.178.wp), custom_call_target="tpu_custom_call" | custom-call | tf_op jit(solution)/shard_map/pallas_call | solution.py:811
  273.8 6.8 %collective-permute-done.30.refs_1_ = bf16[208,1600]{1,0:T(8,128)(2,1)S(1)} collective-permute-done((bf16[208,1600]{1,0:T(8,128)(2,1)}, bf16[208,1600]{1,0:T(8,128)(2,1)S(1)}, u32[]{:S(2)}, u32[]{:S(2)}) %collective-permute-start.30) | collective-permute-done | bytes 665632 | tf_op jit(solution)/shard_map/ppermute | solution.py:131
  286.0 8.1 %shard_map.184 = (f32[128,1600]{1,0:T(8,128)}, bf16[128,1600]{1,0:T(8,128)(2,1)}, bf16[8,128,256]{2,1,0:T(8,128)(2,1)}, f32[4,1600]{1,0:T(4,128)}) custom-call(s32[2]{0:T(128)} %pad_add_fusion.where, bf16[128,1600]{1,0:T(8,128)(2,1)} %reduce-scatter.4.cloned.1.call-done.gn2_ref, f32[128,1600]{1,0:T(8,128)} %get-tuple-element.247.r_ref, ...), custom_call_target="tpu_custom_call" | custom-call | tf_op jit(solution)/shard_map/pallas_call | solution.py:960
  306.5 5.5 %shard_map.185 = (bf16[4,400,200]{2,1,0:T(8,128)(2,1)}, bf16[4,400,200]{2,1,0:T(8,128)(2,1)}, bf16[4,400,200]{2,1,0:T(8,128)(2,1)}, bf16[4,400,200]{2,1,0:T(8,128)(2,1)}) custom-call(s32[2]{0:T(128)} %pad_add_fusion.where, bf16[8,128,256]{2,1,0:T(8,128)(2,1)} %copy-done.3, bf16[8,128,256]{2,1,0:T(8,128)(2,1)} %copy-done.26, ...), custom_call_target="tpu_custom_call" | custom-call | tf_op jit(solution)/shard_map/pallas_call | solution.py:992
  313.1 6.2 %collective-permute-done.35 = bf16[400,800]{1,0:T(8,128)(2,1)S(1)} collective-permute-done((bf16[400,800]{1,0:T(8,128)(2,1)}, bf16[400,800]{1,0:T(8,128)(2,1)S(1)}, u32[]{:S(2)}, u32[]{:S(2)}) %collective-permute-start.35) | collective-permute-done | bytes 640032 | tf_op jit(solution)/shard_map/ppermute | solution.py:131
  328.5 14.1 %shard_map.188 = (bf16[1024,768]{1,0:T(8,128)(2,1)}, f32[1,768]{1,0:T(1,128)}) custom-call(bf16[1024,768]{1,0:T(8,128)(2,1)} %get-tuple-element.189.qkv_ref, bf16[8,128,256]{2,1,0:T(8,128)(2,1)} %copy-done.11, f32[1024,256]{1,0:T(8,128)} %get-tuple-element.270.lse_ref), custom_call_target="tpu_custom_call" | custom-call | tf_op jit(solution)/shard_map/pallas_call | solution.py:598
  342.7 7.7 %shard_map.189 = (bf16[1024,1600]{1,0:T(8,128)(2,1)}, f32[2,1600]{1,0:T(2,128)}) custom-call(bf16[1024,768]{1,0:T(8,128)(2,1)} %get-tuple-element.282.g_ref, bf16[1024,1600]{1,0:T(8,128)(2,1)} %get-tuple-element.188.n1_ref.a_ref, bf16[1600,768]{1,0:T(8,128)(2,1)} %get-tuple-element.275.w_ref), custom_call_target="tpu_custom_call" | custom-call | tf_op jit(solution)/shard_map/pallas_call | solution.py:658
  362.7 6.8 %shard_map.190 = (bf16[400,768]{1,0:T(8,128)(2,1)}, bf16[400,768]{1,0:T(8,128)(2,1)}, bf16[400,768]{1,0:T(8,128)(2,1)}, bf16[208,768]{1,0:T(8,128)(2,1)}, bf16[192,768]{1,0:T(8,128)(2,1)}) custom-call(s32[2]{0:T(128)} %pad_add_fusion.where, bf16[1024,1600]{1,0:T(8,128)(2,1)} %get-tuple-element.188.n1_ref.a_ref, bf16[1024,768]{1,0:T(8,128)(2,1)} %get-tuple-element.282.g_ref), custom_call_target="tpu_custom_call" | custom-call | tf_op jit(solution)/shard_map/pallas_call | solution.py:629
  369.5 7.0 %collective-permute-done.39 = bf16[4,400,200]{2,1,0:T(8,128)(2,1)S(1)} collective-permute-done((bf16[4,400,200]{2,1,0:T(8,128)(2,1)}, bf16[4,400,200]{2,1,0:T(8,128)(2,1)S(1)}, u32[]{:S(2)}, u32[]{:S(2)}) %collective-permute-start.39) | collective-permute-done | bytes 640032 | tf_op jit(solution)/shard_map/ppermute | solution.py:131
  380.9 5.3 %collective-permute-done.42.low_ref = bf16[192,768]{1,0:T(8,128)(2,1)} collective-permute-done((bf16[192,768]{1,0:T(8,128)(2,1)}, bf16[192,768]{1,0:T(8,128)(2,1)}, u32[]{:S(2)}, u32[]{:S(2)}) %collective-permute-start.42) | collective-permute-done | bytes 294944 | tf_op jit(solution)/shard_map/ppermute | solution.py:120
  402.0 8.9 %collective-permute-done.46 = bf16[400,200]{1,0:T(8,128)(2,1)S(1)} collective-permute-done((bf16[400,200]{1,0:T(8,128)(2,1)S(1)}, bf16[400,200]{1,0:T(8,128)(2,1)S(1)}, u32[]{:S(2)}, u32[]{:S(2)}) %collective-permute-start.46) | collective-permute-done | bytes 160032 | tf_op jit(solution)/shard_map/ppermute | solution.py:1130
  415.0 4.4 all-to-all-start.5
  424.1 4.6 collective-permute-done.48.rest_1_
  428.7 5.1 %collective-permute-done.49.rest_2_ = bf16[2,208,200]{2,1,0:T(8,128)(2,1)S(1)} collective-permute-done((bf16[2,208,200]{2,1,0:T(8,128)(2,1)S(1)}, bf16[2,208,200]{2,1,0:T(8,128)(2,1)S(1)}, u32[]{:S(2)}, u32[]{:S(2)}) %collective-permute-start.49) | collective-permute-done | bytes 166432 | tf_op jit(solution)/shard_map/ppermute | solution.py:90
  (332 shorter events, 184.2 us)
Async XLA Ops:
  7.2 64.2 %all-gather.4.cloned.1.call-start = ((), (), s32[]{:S(2)}) async-start(), calls=%async_computation.9 | async-start | bytes 3833856 | tf_op jit(solution)/shard_map/all_gather | solution.py:1035
  23.9 46.3 %all-to-all-start = ((bf16[8,432,128]{2,1,0:T(8,128)(2,1)}), bf16[8,432,128]{2,1,0:T(8,128)(2,1)S(1)}, u32[]{:S(2)}, u32[]{:S(2)}) async-start(bf16[8,432,128]{2,1,0:T(8,128)(2,1)} %shard_map.170), calls=%async_computation | async-start | bytes 1769472 | tf_op jit(solution)/shard_map/all_to_all | solution.py:172
  28.9 94.9 %all-gather.6.cloned.1.call-start = ((), (), s32[]{:S(2)}) async-start(), calls=%async_computation.10 | async-start | bytes 3833856 | tf_op jit(solution)/shard_map/all_gather | solution.py:1048
  29.0 27.9 %collective-permute-start.3 = (bf16[400,800]{1,0:T(8,128)(2,1)S(1)}, bf16[400,800]{1,0:T(8,128)(2,1)S(1)}, u32[]{:S(2)}, u32[]{:S(2)}) collective-permute-start(bf16[400,800]{1,0:T(8,128)(2,1)S(1)} %copy-done.16), channel_id=1, source_target_pairs={{0,8},{8,0},{16,24},{24,16},{1,9},{9,1},{17,25},{25,17},{2,10},{10... | collective-permute-start | bytes 1920008 | tf_op jit(solution)/shard_map/ppermute | solution.py:90
  29.6 28.0 %collective-permute-start.4 = (bf16[400,800]{1,0:T(8,128)(2,1)S(1)}, bf16[400,800]{1,0:T(8,128)(2,1)S(1)}, u32[]{:S(2)}, u32[]{:S(2)}) collective-permute-start(bf16[400,800]{1,0:T(8,128)(2,1)S(1)} %copy-done.16), channel_id=1, source_target_pairs={{0,16},{8,24},{16,0},{24,8},{1,17},{9,25},{17,1},{25,9},{2,18},{10... | collective-permute-start | bytes 1920008 | tf_op jit(solution)/shard_map/ppermute | solution.py:90
  36.0 20.9 %collective-permute-start.6 = (bf16[2,208,200]{2,1,0:T(8,128)(2,1)}, bf16[2,208,200]{2,1,0:T(8,128)(2,1)S(1)}, u32[]{:S(2)}, u32[]{:S(2)}) collective-permute-start(bf16[2,208,200]{2,1,0:T(8,128)(2,1)} %get-tuple-element.171), channel_id=1, source_target_pairs={{0,16},{8,24},{16,0},{24,8},{1,17},{9,25},{17,1},{25,9},{2,18},{10... | collective-permute-start | bytes 499208 | tf_op jit(solution)/shard_map/ppermute | solution.py:90
  37.5 19.3 %collective-permute-start.7 = (bf16[2,208,200]{2,1,0:T(8,128)(2,1)}, bf16[2,208,200]{2,1,0:T(8,128)(2,1)S(1)}, u32[]{:S(2)}, u32[]{:S(2)}) collective-permute-start(bf16[2,208,200]{2,1,0:T(8,128)(2,1)} %get-tuple-element.172), channel_id=1, source_target_pairs={{0,24},{8,16},{16,8},{24,0},{1,25},{9,17},{17,9},{25,1},{2,26},{10... | collective-permute-start | bytes 499208 | tf_op jit(solution)/shard_map/ppermute | solution.py:90
  73.2 20.0 %collective-permute-start.13 = (bf16[400,200]{1,0:T(8,128)(2,1)}, bf16[400,200]{1,0:T(8,128)(2,1)}, u32[]{:S(2)}, u32[]{:S(2)}) collective-permute-start(bf16[400,200]{1,0:T(8,128)(2,1)} %param.13), channel_id=1, source_target_pairs={{0,4},{1,5},{2,6},{3,7},{4,0},{5,1},{6,2},{7,3},{8,12},{9,13},{10,... | collective-permute-start | bytes 480008 | tf_op jit(solution)/shard_map/ppermute | solution.py:862
  78.4 29.3 %collective-permute-start.10 = (bf16[400,768]{1,0:T(8,128)(2,1)}, bf16[400,768]{1,0:T(8,128)(2,1)}, u32[]{:S(2)}, u32[]{:S(2)}) collective-permute-start(bf16[400,768]{1,0:T(8,128)(2,1)} %shard_map.172.rest_0_), channel_id=1, source_target_pairs={{0,24},{8,16},{16,8},{24,0},{1,25},{9,17},{17,9},{25,1},{2,26},{10... | collective-permute-start | bytes 1843208 | tf_op jit(solution)/shard_map/ppermute | solution.py:90
  81.2 28.8 %collective-permute-start.8 = (bf16[400,768]{1,0:T(8,128)(2,1)}, bf16[400,768]{1,0:T(8,128)(2,1)}, u32[]{:S(2)}, u32[]{:S(2)}) collective-permute-start(bf16[400,768]{1,0:T(8,128)(2,1)} %shard_map.172.rest_0_), channel_id=1, source_target_pairs={{0,8},{8,0},{16,24},{24,16},{1,9},{9,1},{17,25},{25,17},{2,10},{10... | collective-permute-start | bytes 1843208 | tf_op jit(solution)/shard_map/ppermute | solution.py:90
  81.8 28.3 %collective-permute-start.9 = (bf16[400,768]{1,0:T(8,128)(2,1)}, bf16[400,768]{1,0:T(8,128)(2,1)}, u32[]{:S(2)}, u32[]{:S(2)}) collective-permute-start(bf16[400,768]{1,0:T(8,128)(2,1)} %shard_map.172.rest_0_), channel_id=1, source_target_pairs={{0,16},{8,24},{16,0},{24,8},{1,17},{9,25},{17,1},{25,9},{2,18},{10... | collective-permute-start | bytes 1843208 | tf_op jit(solution)/shard_map/ppermute | solution.py:90
  85.1 38.7 %collective-permute-start.11 = (bf16[400,800]{1,0:T(8,128)(2,1)S(1)}, bf16[400,800]{1,0:T(8,128)(2,1)}, u32[]{:S(2)}, u32[]{:S(2)}) collective-permute-start(bf16[400,800]{1,0:T(8,128)(2,1)S(1)} %copy-done.16), channel_id=1, source_target_pairs={{0,24},{8,16},{16,8},{24,0},{1,25},{9,17},{17,9},{25,1},{2,26},{10... | collective-permute-start | bytes 1920008 | tf_op jit(solution)/shard_map/ppermute | solution.py:90
  125.1 26.3 %all-to-all-start.1 = ((bf16[8,208,200]{1,2,0:T(8,128)(2,1)}), bf16[8,208,200]{1,2,0:T(8,128)(2,1)S(1)}, u32[]{:S(2)}, u32[]{:S(2)}) async-start(bf16[8,208,200]{1,2,0:T(8,128)(2,1)} %copy.65), calls=%async_computation.1 | async-start | bytes 1638400 | tf_op jit(solution)/shard_map/all_to_all | solution.py:172
  129.2 20.7 %collective-permute-start.15 = (bf16[4,400,200]{2,1,0:T(8,128)(2,1)S(1)}, bf16[4,400,200]{2,1,0:T(8,128)(2,1)S(1)}, u32[]{:S(2)}, u32[]{:S(2)}) collective-permute-start(bf16[4,400,200]{2,1,0:T(8,128)(2,1)S(1)} %pad_maximum_fusion.rest_0_), channel_id=1, source_target_pairs={{0,8},{8,0},{16,24},{24,16},{1,9},{9,1},{17,25},{25,17},{2,10},{10... | collective-permute-start | bytes 1920008 | tf_op jit(solution)/shard_map/ppermute | solution.py:90
  131.0 20.4 %collective-permute-start.16 = (bf16[4,400,200]{2,1,0:T(8,128)(2,1)S(1)}, bf16[4,400,200]{2,1,0:T(8,128)(2,1)S(1)}, u32[]{:S(2)}, u32[]{:S(2)}) collective-permute-start(bf16[4,400,200]{2,1,0:T(8,128)(2,1)S(1)} %pad_maximum_fusion.rest_0_), channel_id=1, source_target_pairs={{0,16},{8,24},{16,0},{24,8},{1,17},{9,25},{17,1},{25,9},{2,18},{10... | collective-permute-start | bytes 1920008 | tf_op jit(solution)/shard_map/ppermute | solution.py:90
  152.3 20.1 %all-to-all-start.2 = ((bf16[8,128,256]{2,1,0:T(8,128)(2,1)}), bf16[8,128,256]{2,1,0:T(8,128)(2,1)S(1)}, u32[]{:S(2)}, u32[]{:S(2)}) async-start(bf16[8,128,256]{2,1,0:T(8,128)(2,1)} %get-tuple-element.193), calls=%async_computation.2 | async-start | bytes 1048576 | tf_op jit(solution)/shard_map/all_to_all | solution.py:172
  157.0 67.0 %all-gather.8.cloned.1.call-start = ((), (), s32[]{:S(2)}) async-start(), calls=%async_computation.11 | async-start | bytes 3833856 | tf_op jit(solution)/shard_map/all_gather | solution.py:1086
  183.1 98.9 %reduce-scatter.4.cloned.1.call-start = ((), (), s32[]{:S(2)}) async-start(), calls=%async_computation.12 | async-start | bytes 3833856 | tf_op jit(solution)/shard_map/reduce_scatter | solution.py:1096
  183.2 18.4 %collective-permute-start.24 = (bf16[208,1600]{1,0:T(8,128)(2,1)S(1)}, bf16[208,1600]{1,0:T(8,128)(2,1)S(1)}, u32[]{:S(2)}, u32[]{:S(2)}) collective-permute-start(bf16[208,1600]{1,0:T(8,128)(2,1)S(1)} %copy-done.9), channel_id=1, source_target_pairs={{0,8},{8,0},{16,24},{24,16},{1,9},{9,1},{17,25},{25,17},{2,10},{10... | collective-permute-start | bytes 1996808 | tf_op jit(solution)/shard_map/ppermute | solution.py:90
  185.2 31.4 %collective-permute-start.26 = (bf16[208,1600]{1,0:T(8,128)(2,1)S(1)}, bf16[208,1600]{1,0:T(8,128)(2,1)S(1)}, u32[]{:S(2)}, u32[]{:S(2)}) collective-permute-start(bf16[208,1600]{1,0:T(8,128)(2,1)S(1)} %copy-done.9), channel_id=1, source_target_pairs={{0,24},{8,16},{16,8},{24,0},{1,25},{9,17},{17,9},{25,1},{2,26},{10... | collective-permute-start | bytes 1996808 | tf_op jit(solution)/shard_map/ppermute | solution.py:90
  186.7 34.6 %collective-permute-start.27 = (bf16[8,128,256]{2,1,0:T(8,128)(2,1)}, bf16[8,128,256]{2,1,0:T(8,128)(2,1)S(1)}, u32[]{:S(2)}, u32[]{:S(2)}) collective-permute-start(bf16[8,128,256]{2,1,0:T(8,128)(2,1)} %copy-done.3), channel_id=1, source_target_pairs={{0,1},{1,0},{2,3},{3,2},{4,5},{5,4},{6,7},{7,6},{8,9},{9,8},{10,11... | collective-permute-start | bytes 1572872 | tf_op jit(solution)/shard_map/ppermute | solution.py:168
  240.5 112.6 %reduce-scatter.6.cloned.1.call-start = ((), (), s32[]{:S(2)}) async-start(), calls=%async_computation.13 | async-start | bytes 3833856 | tf_op jit(solution)/shard_map/reduce_scatter | solution.py:1105
  294.1 27.7 %all-to-all-start.3 = ((bf16[8,128,256]{2,1,0:T(8,128)(2,1)}), bf16[8,128,256]{2,1,0:T(8,128)(2,1)S(1)}, u32[]{:S(2)}, u32[]{:S(2)}) async-start(bf16[8,128,256]{2,1,0:T(8,128)(2,1)} %get-tuple-element.252), calls=%async_computation.4 | async-start | bytes 1048576 | tf_op jit(solution)/shard_map/all_to_all | solution.py:172
  301.1 18.2 %collective-permute-start.35 = (bf16[400,800]{1,0:T(8,128)(2,1)}, bf16[400,800]{1,0:T(8,128)(2,1)S(1)}, u32[]{:S(2)}, u32[]{:S(2)}) collective-permute-start(bf16[400,800]{1,0:T(8,128)(2,1)} %get-tuple-element.264), channel_id=1, source_target_pairs={{0,8},{8,0},{16,24},{24,16},{1,9},{9,1},{17,25},{25,17},{2,10},{10... | collective-permute-start | bytes 1920008 | tf_op jit(solution)/shard_map/ppermute | solution.py:131
  301.5 18.7 %collective-permute-start.36 = (bf16[400,800]{1,0:T(8,128)(2,1)}, bf16[400,800]{1,0:T(8,128)(2,1)}, u32[]{:S(2)}, u32[]{:S(2)}) collective-permute-start(bf16[400,800]{1,0:T(8,128)(2,1)} %get-tuple-element.265), channel_id=1, source_target_pairs={{0,16},{8,24},{16,0},{24,8},{1,17},{9,25},{17,1},{25,9},{2,18},{10... | collective-permute-start | bytes 1920008 | tf_op jit(solution)/shard_map/ppermute | solution.py:132
  323.1 29.9 %all-to-all-start.4 = ((bf16[8,208,200]{1,2,0:T(8,128)(2,1)}), bf16[8,208,200]{1,2,0:T(8,128)(2,1)S(1)}, u32[]{:S(2)}, u32[]{:S(2)}) async-start(bf16[8,208,200]{1,2,0:T(8,128)(2,1)} %copy.69), calls=%async_computation.6 | async-start | bytes 1638400 | tf_op jit(solution)/shard_map/all_to_all | solution.py:172
  326.7 112.3 %reduce-scatter.8.cloned.1.call-start = ((), (), s32[]{:S(2)}) async-start(), calls=%async_computation.14 | async-start | bytes 3833856 | tf_op jit(solution)/shard_map/reduce_scatter | solution.py:1123
  356.1 20.4 %collective-permute-start.39 = (bf16[4,400,200]{2,1,0:T(8,128)(2,1)}, bf16[4,400,200]{2,1,0:T(8,128)(2,1)S(1)}, u32[]{:S(2)}, u32[]{:S(2)}) collective-permute-start(bf16[4,400,200]{2,1,0:T(8,128)(2,1)} %get-tuple-element.293), channel_id=1, source_target_pairs={{0,8},{8,0},{16,24},{24,16},{1,9},{9,1},{17,25},{25,17},{2,10},{10... | collective-permute-start | bytes 1920008 | tf_op jit(solution)/shard_map/ppermute | solution.py:131
  357.5 20.1 %collective-permute-start.40 = (bf16[4,400,200]{2,1,0:T(8,128)(2,1)}, bf16[4,400,200]{2,1,0:T(8,128)(2,1)S(1)}, u32[]{:S(2)}, u32[]{:S(2)}) collective-permute-start(bf16[4,400,200]{2,1,0:T(8,128)(2,1)} %get-tuple-element.294), channel_id=1, source_target_pairs={{0,16},{8,24},{16,0},{24,8},{1,17},{9,25},{17,1},{25,9},{2,18},{10... | collective-permute-start | bytes 1920008 | tf_op jit(solution)/shard_map/ppermute | solution.py:132
  389.0 22.0 %collective-permute-start.43 = (bf16[400,768]{1,0:T(8,128)(2,1)}, bf16[400,768]{1,0:T(8,128)(2,1)}, u32[]{:S(2)}, u32[]{:S(2)}) collective-permute-start(bf16[400,768]{1,0:T(8,128)(2,1)} %get-tuple-element.300), channel_id=1, source_target_pairs={{0,8},{8,0},{16,24},{24,16},{1,9},{9,1},{17,25},{25,17},{2,10},{10... | collective-permute-start | bytes 1843208 | tf_op jit(solution)/shard_map/ppermute | solution.py:131
  390.2 20.8 %collective-permute-start.44 = (bf16[400,768]{1,0:T(8,128)(2,1)}, bf16[400,768]{1,0:T(8,128)(2,1)}, u32[]{:S(2)}, u32[]{:S(2)}) collective-permute-start(bf16[400,768]{1,0:T(8,128)(2,1)} %get-tuple-element.301), channel_id=1, source_target_pairs={{0,16},{8,24},{16,0},{24,8},{1,17},{9,25},{17,1},{25,9},{2,18},{10... | collective-permute-start | bytes 1843208 | tf_op jit(solution)/shard_map/ppermute | solution.py:132
  415.0 27.7 %all-to-all-start.5 = ((bf16[8,432,128]{2,1,0:T(8,128)(2,1)}), bf16[8,432,128]{2,1,0:T(8,128)(2,1)S(1)}, u32[]{:S(2)}, u32[]{:S(2)}) async-start(bf16[8,432,128]{2,1,0:T(8,128)(2,1)} %shard_map.194), calls=%async_computation.7 | async-start | bytes 1769472 | tf_op jit(solution)/shard_map/all_to_all | solution.py:172
  (90 other events, 936.7 us)
Sparse Core Ops, SparseCore 0:
  9.6 61.7 all-gather.3
  73.1 50.7 all-gather.5
  183.3 40.7 all-gather.7
  240.6 41.4 reduce-scatter.3
  284.2 50.7 reduce-scatter.5
  353.2 44.9 reduce-scatter.7

commit v8 on v7

--- a/solution.py
+++ b/solution.py
@@ -170,6 +170,56 @@
 
 def exchange(block):
     return lax.all_to_all(block, "seq", 0, 0, tiled=True)
+
+
+def chip_permute(block, pairs):
+    return lax.ppermute(
+        block, "seq", [(2 * a + core, 2 * b + core) for a, b in pairs for core in range(2)]
+    )
+
+
+def chips():
+    return lax.axis_size("seq") // 2
+
+
+def gather_first(block):
+    count = chips()
+    fetch = lambda off: chip_permute(block, [((z + off) % count, z) for z in range(count)])
+    if count != 4:
+        return [block] + [fetch(off) for off in range(1, count)]
+    return [block, fetch(1), None, fetch(3)]
+
+
+def gather_second(found):
+    if len(found) != 4:
+        return found
+    above = chip_permute(found[3], [(1, 2), (2, 3)])
+    below = chip_permute(found[1], [(2, 1), (1, 0)])
+    far = jnp.where(lax.axis_index("seq") >= 4, above, below)
+    return [found[0], found[1], far, found[3]]
+
+
+def scatter_first(chunks):
+    count = chips()
+    if count != 4:
+        return [
+            chip_permute(chunks[off], [(z, (z + off) % count) for z in range(count)])
+            for off in range(1, count)
+        ]
+    above = chip_permute(chunks[2], [(0, 1), (1, 2)])
+    below = chip_permute(chunks[2], [(3, 2), (2, 1)])
+    return [above, below]
+
+
+def scatter_second(chunks, found):
+    count = chips()
+    if count != 4:
+        return [chunks[0]] + found
+    up = total_of([chunks[1], found[0]]).astype(BF)
+    down = total_of([chunks[3], found[1]]).astype(BF)
+    up = chip_permute(up, [(z, (z + 1) % 4) for z in range(4)])
+    down = chip_permute(down, [(z, (z - 1) % 4) for z in range(4)])
+    return [chunks[0], up, down]
 
 
 def total_of(parts):
@@ -857,10 +907,12 @@
 
 def line_blocks(block):
     seqs = lax.axis_size("seq")
-    return jnp.stack(
-        [block]
-        + [lax.ppermute(block, "seq", xor_perm(seqs, 2 * dz)) for dz in range(1, seqs // 2)]
-    )
+    if seqs != 8:
+        others = [lax.ppermute(block, "seq", xor_perm(seqs, 2 * dz)) for dz in range(1, seqs // 2)]
+        return jnp.stack([block] + others)
+    _, above, far, below = gather_second(gather_first(block))
+    even = (lax.axis_index("seq") // 2) % 2 == 0
+    return jnp.stack([block, jnp.where(even, above, below), far, jnp.where(even, below, above)])
 
 
 def block_pairs(where, places, flat, store):
@@ -1038,18 +1090,17 @@
     small = jnp.stack(in_order(small, send_rel(copies(small), "dp", near + far)))
     small = as_rows(small.reshape(1, -1), lanes)[0]
     parts = exchange(pack_columns(where, w_qkv, send, small))
-    wf_near = send_rel(copies(w_fc), "dp", near)
+    wf = in_order(w_fc, send_rel(copies(w_fc), "dp", near + far))
     pieces = proj_pieces(where, w_proj.reshape(ratio, ff_mine, col), dps)
-    pieces = in_order(pieces[0], send_rel(chunks(pieces), "dp", near + far))
-    parts, wf_near, x_own, out_own, pieces, fc_own, gm_all = phase(
-        parts, wf_near, tokens, w_out, pieces, w_fc, gm_all
+    parts, wf, x_own, out_own, pieces, gm_all = phase(
+        parts, wf, tokens, w_out, pieces, gm_all
     )
 
     x_all = lax.all_gather(x_own, "seq", axis=0, tiled=True)
     own_qkv = unpack_columns(where, parts, recv, w_qkv.shape[0], 3 * mine)
     wq = in_order(own_qkv, send_rel(copies(own_qkv), "dp", near + far))
-    wf_far = send_rel(copies(fc_own), "dp", far)
     line = line_blocks(out_own)
+    pieces = in_order(pieces[0], send_rel(chunks(pieces), "dp", near + far))
     pieces = turn_pieces(where, pieces)
     small = parts[:, w_qkv.shape[0] :].reshape(seqs, -1)[:, : dps * count].astype(F32)
     small = jnp.take(small.reshape(seqs, dps, count), dp ^ jnp.arange(dps), axis=1)
@@ -1060,9 +1111,7 @@
     bias_qkv = jnp.concatenate(
         [head_rows(table[2]), jnp.zeros((mine,), F32), head_rows(table[3])]
     )[None]
-    x_all, wq, wf_far, line, pieces, table, bias_qkv = phase(
-        x_all, wq, wf_far, line, pieces, table, bias_qkv
-    )
+    x_all, wq, line, pieces, table, bias_qkv = phase(x_all, wq, line, pieces, table, bias_qkv)
 
     pieces = exchange(pieces)
     wo = {(0, 0): line}
@@ -1086,7 +1135,6 @@
     n2_all = lax.all_gather(n2, "seq", axis=0, tiled=True)
     wp = in_order(own_proj, wp_near, send_rel(copies(own_proj), "dp", far))
     far_att = swap_core(att)
-    wf = in_order(fc_own, wf_near, wf_far)
     wf = gather_fc(where, wf)
     wf, wp = phase(wf, wp)
     wp = gather_proj(where, wp, ff_mine)
@@ -1126,9 +1174,19 @@
     d_qkv, out_in = phase(d_qkv, out_in)
     qkv_first = reduce_first(d_qkv)
     g_line = total_of(out_in).astype(BF)
-    out_in = [g_line[0]] + [
-        lax.ppermute(g_line[dz], "seq", xor_perm(seqs, 2 * dz)) for dz in range(1, seqs // 2)
-    ]
+    if seqs == 8:
+        even = (sq // 2) % 2 == 0
+        above = jnp.where(even, g_line[1], g_line[3])
+        below = jnp.where(even, g_line[3], g_line[1])
+        line_out = [g_line[0], above, g_line[2], below]
+    else:
+        line_out = [
+            lax.dynamic_index_in_dim(
+                g_line, ((sq // 2 + off) % (seqs // 2)) ^ (sq // 2), 0, keepdims=False
+            )
+            for off in range(seqs // 2)
+        ]
+    out_in = scatter_second(line_out, scatter_first(line_out))
     qkv_in = reduce_second(d_qkv, qkv_first)
     activations = output_rows(r, mlp, table)
     g_fc = total_of(fc_in)

time: 465 us -> 457 us (0.983)
  waiting for transfers between devices: 159 us -> 141 us
  starting transfers between devices: 86 us -> 93.6 us
    ppermute x6 -> x8, starting transfers between devices: 6.23 us -> 13.6 us  [chip_permute(): lax.ppermute(block, 'seq', [(2 * a + core, 2 * b + core) for a, b in pair...]
    ppermute x6 -> x8, waiting for transfers between devices: 25.6 us -> 19.8 us  [chip_permute(): lax.ppermute(block, 'seq', [(2 * a + core, 2 * b + core) for a, b in pair...]
    all_to_all x6, waiting for transfers between devices: 17.7 us -> 12.2 us  [exchange(): return lax.all_to_all(block, 'seq', 0, 0, tiled=True)]
    unnamed x120 -> x124, local copies, waits for them, and re-layouts: 14.6 us -> 14.7 us
  transfers between devices with their start and end apart: 66 -> 68, of which waited for: 36 -> 34; matrix products, arithmetic and copies ran while one was open for 6% -> 6% of each run, Pallas kernels for 30% -> 30%
where the time goes in v8:
time: 457 us; the launch traced here: 450 us
  Pallas kernels  159 us (35%)
  waiting for transfers between devices  141 us (31%)
  starting transfers between devices  93.6 us (20%)
  local copies, waits for them, and re-layouts  31.8 us (7%)
  between operations  15.2 us (3%)
  other arithmetic  9.73 us (2%)
    ppermute x23, waiting for transfers between devices, send_rel(): return {k: lax.ppermute(blocks[k], axis, xor_perm(count, k)) for k in ks}  72.4 us
    ppermute x23, starting transfers between devices, send_rel(): return {k: lax.ppermute(blocks[k], axis, xor_perm(count, k)) for k in ks}  30.7 us
    all_to_all x6, starting transfers between devices, exchange(): return lax.all_to_all(block, 'seq', 0, 0, tiled=True)  24.4 us
    ppermute x4, waiting for transfers between devices, reduce_second(): lax.ppermute(first, 'dp', xor_perm(4, 1))  19.9 us
    ppermute x8, waiting for transfers between devices, chip_permute(): lax.ppermute(block, 'seq', [(2 * a + core, 2 * b + core) for a, b in pair...  19.8 us
    pallas_call x1, Pallas kernels, attend(): pl.pallas_call(functools.partial(attend_kernel, heads // PAIR, dps), grid...  16.5 us
    pallas_call x1, Pallas kernels, feed(): pl.pallas_call(feed_kernel, grid=(length // rows,), in_specs=[tile(model)...  16.4 us
    pallas_call x2, Pallas kernels, grad_blocks(): pl.pallas_call(grad_blocks_kernel, in_specs=[SCALAR, WHOLE, WHOLE], out_s...  14.8 us
  transfers between devices with their start and end apart: 68, of which 34 were waited for; matrix products, arithmetic and copies ran while one was open for 6% of the time, Pallas kernels for 30%

profile of v8, /device:TPU:0, one launch (start us, length us, event | category | flops | bytes accessed | tf_op | source)
XLA Modules:
  0.0 450.1 jit_solution(11863068228306591829)
XLA Ops:
  23.9 5.0 %all-to-all-start = ((bf16[8,432,128]{2,1,0:T(8,128)(2,1)}), bf16[8,432,128]{2,1,0:T(8,128)(2,1)S(1)}, u32[]{:S(2)}, u32[]{:S(2)}) async-start(bf16[8,432,128]{2,1,0:T(8,128)(2,1)} %shard_map.170), calls=%async_computation | async-start | bytes 1769472 | tf_op jit(solution)/shard_map/all_to_all | solution.py:172
  36.9 11.0 %collective-permute-done.3.rest_1_ = bf16[400,800]{1,0:T(8,128)(2,1)S(1)} collective-permute-done((bf16[400,800]{1,0:T(8,128)(2,1)S(1)}, bf16[400,800]{1,0:T(8,128)(2,1)S(1)}, u32[]{:S(2)}, u32[]{:S(2)}) %collective-permute-start.3) | collective-permute-done | bytes 640032 | tf_op jit(solution)/shard_map/ppermute | solution.py:90
  47.9 15.2 %collective-permute-done.4.rest_2_ = bf16[400,800]{1,0:T(8,128)(2,1)S(1)} collective-permute-done((bf16[400,800]{1,0:T(8,128)(2,1)S(1)}, bf16[400,800]{1,0:T(8,128)(2,1)S(1)}, u32[]{:S(2)}, u32[]{:S(2)}) %collective-permute-start.4) | collective-permute-done | bytes 640032 | tf_op jit(solution)/shard_map/ppermute | solution.py:90
  63.1 7.1 %all-to-all-done.in_ref = bf16[8,432,128]{2,1,0:T(8,128)(2,1)S(1)} async-done(((bf16[8,432,128]{2,1,0:T(8,128)(2,1)}), bf16[8,432,128]{2,1,0:T(8,128)(2,1)S(1)}, u32[]{:S(2)}, u32[]{:S(2)}) %all-to-all-start) | async-done | bytes 884768 | tf_op jit(solution)/shard_map/all_to_all | solution.py:172
  73.2 3.8 collective-permute-start.9
  88.1 4.4 collective-permute-done.9
  102.4 10.3 %collective-permute-done.12 = bf16[400,200]{1,0:T(8,128)(2,1)S(1)} collective-permute-done((bf16[400,200]{1,0:T(8,128)(2,1)}, bf16[400,200]{1,0:T(8,128)(2,1)S(1)}, u32[]{:S(2)}, u32[]{:S(2)}) %collective-permute-start.12) | collective-permute-done | bytes 160032 | tf_op jit(solution)/shard_map/ppermute | solution.py:176
  113.0 5.6 %collective-permute-done.7.rest_2_ = bf16[400,768]{1,0:T(8,128)(2,1)} collective-permute-done((bf16[400,768]{1,0:T(8,128)(2,1)}, bf16[400,768]{1,0:T(8,128)(2,1)}, u32[]{:S(2)}, u32[]{:S(2)}) %collective-permute-start.7) | collective-permute-done | bytes 614432 | tf_op jit(solution)/shard_map/ppermute | solution.py:90
  119.9 3.7 all-to-all-start.1
  126.9 16.5 %shard_map.174 = (bf16[1024,1600]{1,0:T(8,128)(2,1)}, bf16[1024,768]{1,0:T(8,128)(2,1)}, bf16[8,128,256]{2,1,0:T(8,128)(2,1)}, f32[1024,256]{1,0:T(8,128)}, bf16[1600,768]{1,0:T(8,128)(2,1)}) custom-call(s32[2]{0:T(128)} %pad_add_fusion.where, bf16[1024,1600]{1,0:T(8,128)(2,1)} %all-gather.6.cloned.1.call-done.x_ref, f32[8,1600]{1,0:T(8,128)} %copy-done.10, ...), custom_call_target="tpu_custom_call" | custom-call | tf_op jit(solution)/shard_map/pallas_call | solution.py:580
  146.7 4.8 %all-to-all-start.2 = ((bf16[8,128,256]{2,1,0:T(8,128)(2,1)}), bf16[8,128,256]{2,1,0:T(8,128)(2,1)S(1)}, u32[]{:S(2)}, u32[]{:S(2)}) async-start(bf16[8,128,256]{2,1,0:T(8,128)(2,1)} %get-tuple-element.191), calls=%async_computation.2 | async-start | bytes 1048576 | tf_op jit(solution)/shard_map/all_to_all | solution.py:172
  160.7 5.1 %collective-permute-done.18.rest_6_ = bf16[2,400,200]{2,1,0:T(8,128)(2,1)S(1)} collective-permute-done((bf16[2,400,200]{2,1,0:T(8,128)(2,1)}, bf16[2,400,200]{2,1,0:T(8,128)(2,1)S(1)}, u32[]{:S(2)}, u32[]{:S(2)}) %collective-permute-start.18) | collective-permute-done | bytes 320032 | tf_op jit(solution)/shard_map/ppermute | solution.py:162
  170.6 6.9 %shard_map.176 = (f32[128,1600]{1,0:T(8,128)}, bf16[128,1600]{1,0:T(8,128)(2,1)}) custom-call(s32[2]{0:T(128)} %pad_add_fusion.where, bf16[8,128,256]{2,1,0:T(8,128)(2,1)} %copy-done.3, f32[8,1600]{1,0:T(8,128)} %copy-done.10, bf16[128,1600]{1,0:T(8,128)(2,1)} %copy.62.x_hbm, bf16[4,400,200]{2,1,0:T(8,128)(2,1)} %copy-done, ...), custom_call_target="tpu_custom_call" | custom-call | tf_op jit(solution)/shard_map/pallas_call | solution.py:964
  182.0 4.1 shard_map.177.wf
  186.1 9.9 %collective-permute-done.25.rest_1_ = bf16[208,1600]{1,0:T(8,128)(2,1)S(1)} collective-permute-done((bf16[208,1600]{1,0:T(8,128)(2,1)S(1)}, bf16[208,1600]{1,0:T(8,128)(2,1)S(1)}, u32[]{:S(2)}, u32[]{:S(2)}) %collective-permute-start.25) | collective-permute-done | bytes 665632 | tf_op jit(solution)/shard_map/ppermute | solution.py:90
  196.1 14.9 %collective-permute-done.27.rest_3_ = bf16[208,1600]{1,0:T(8,128)(2,1)S(1)} collective-permute-done((bf16[208,1600]{1,0:T(8,128)(2,1)S(1)}, bf16[208,1600]{1,0:T(8,128)(2,1)S(1)}, u32[]{:S(2)}, u32[]{:S(2)}) %collective-permute-start.27) | collective-permute-done | bytes 665632 | tf_op jit(solution)/shard_map/ppermute | solution.py:90
  211.9 3.9 shard_map.178.wp
  218.4 16.4 %shard_map.179 = (bf16[1024,800]{1,0:T(8,128)(2,1)}, bf16[1024,800]{1,0:T(8,128)(2,1)}, bf16[1024,1600]{1,0:T(8,128)(2,1)}, f32[1,800]{1,0:T(1,128)}) custom-call(bf16[1024,1600]{1,0:T(8,128)(2,1)} %all-gather.8.cloned.1.call-done.n2_ref.a_ref, bf16[1024,1600]{1,0:T(8,128)(2,1)} %all-gather.4.cloned.1.call-done.gm_ref, f32[1,800]{1,0:T(1,128)} %broadcast_in_dim.40.bias_ref, ...), custom_call_target="tpu_custom_call" | custom-call | tf_op jit(solution)/shard_map/pallas_call | solution.py:806
  235.3 7.7 %shard_map.181 = (bf16[208,1600]{1,0:T(8,128)(2,1)}, bf16[208,1600]{1,0:T(8,128)(2,1)}, bf16[208,1600]{1,0:T(8,128)(2,1)}, bf16[112,1600]{1,0:T(8,128)(2,1)}, bf16[96,1600]{1,0:T(8,128)(2,1)}) custom-call(s32[2]{0:T(128)} %pad_add_fusion.where, bf16[1024,1600]{1,0:T(8,128)(2,1)} %all-gather.4.cloned.1.call-done.gm_ref, ...), custom_call_target="tpu_custom_call" | custom-call | tf_op jit(solution)/shard_map/pallas_call | solution.py:841
  246.1 7.9 %shard_map.180 = (bf16[400,800]{1,0:T(8,128)(2,1)}, bf16[400,800]{1,0:T(8,128)(2,1)}, bf16[400,800]{1,0:T(8,128)(2,1)}, bf16[208,800]{1,0:T(8,128)(2,1)}, bf16[192,800]{1,0:T(8,128)(2,1)}) custom-call(s32[2]{0:T(128)} %pad_add_fusion.where, bf16[1024,1600]{1,0:T(8,128)(2,1)} %all-gather.8.cloned.1.call-done.n2_ref.a_ref, ...), custom_call_target="tpu_custom_call" | custom-call | tf_op jit(solution)/shard_map/pallas_call | solution.py:679
  260.6 7.6 %shard_map.182 = bf16[1024,1600]{1,0:T(8,128)(2,1)} custom-call(bf16[1024,800]{1,0:T(8,128)(2,1)} %get-tuple-element.237.e_ref, bf16[800,1600]{1,0:T(8,128)(2,1)} %shard_map.178.wp), custom_call_target="tpu_custom_call" | custom-call | tf_op jit(solution)/shard_map/pallas_call | solution.py:861
  268.2 6.8 %collective-permute-done.31.refs_1_ = bf16[208,1600]{1,0:T(8,128)(2,1)S(1)} collective-permute-done((bf16[208,1600]{1,0:T(8,128)(2,1)}, bf16[208,1600]{1,0:T(8,128)(2,1)S(1)}, u32[]{:S(2)}, u32[]{:S(2)}) %collective-permute-start.31) | collective-permute-done | bytes 665632 | tf_op jit(solution)/shard_map/ppermute | solution.py:131
  280.5 8.0 %shard_map.184 = (f32[128,1600]{1,0:T(8,128)}, bf16[128,1600]{1,0:T(8,128)(2,1)}, bf16[8,128,256]{2,1,0:T(8,128)(2,1)}, f32[4,1600]{1,0:T(4,128)}) custom-call(s32[2]{0:T(128)} %pad_add_fusion.where, bf16[128,1600]{1,0:T(8,128)(2,1)} %reduce-scatter.4.cloned.1.call-done.gn2_ref, f32[128,1600]{1,0:T(8,128)} %get-tuple-element.246.r_ref, ...), custom_call_target="tpu_custom_call" | custom-call | tf_op jit(solution)/shard_map/pallas_call | solution.py:1012
  300.9 5.4 %shard_map.185 = (bf16[4,400,200]{2,1,0:T(8,128)(2,1)}, bf16[4,400,200]{2,1,0:T(8,128)(2,1)}, bf16[4,400,200]{2,1,0:T(8,128)(2,1)}, bf16[4,400,200]{2,1,0:T(8,128)(2,1)}) custom-call(s32[2]{0:T(128)} %pad_add_fusion.where, bf16[8,128,256]{2,1,0:T(8,128)(2,1)} %copy-done.3, bf16[8,128,256]{2,1,0:T(8,128)(2,1)} %copy-done.29, ...), custom_call_target="tpu_custom_call" | custom-call | tf_op jit(solution)/shard_map/pallas_call | solution.py:1044
  307.5 6.2 %collective-permute-done.36 = bf16[400,800]{1,0:T(8,128)(2,1)S(1)} collective-permute-done((bf16[400,800]{1,0:T(8,128)(2,1)}, bf16[400,800]{1,0:T(8,128)(2,1)S(1)}, u32[]{:S(2)}, u32[]{:S(2)}) %collective-permute-start.36) | collective-permute-done | bytes 640032 | tf_op jit(solution)/shard_map/ppermute | solution.py:131
  323.0 14.1 %shard_map.188 = (bf16[1024,768]{1,0:T(8,128)(2,1)}, f32[1,768]{1,0:T(1,128)}) custom-call(bf16[1024,768]{1,0:T(8,128)(2,1)} %get-tuple-element.187.qkv_ref, bf16[8,128,256]{2,1,0:T(8,128)(2,1)} %copy-done.11, f32[1024,256]{1,0:T(8,128)} %get-tuple-element.269.lse_ref), custom_call_target="tpu_custom_call" | custom-call | tf_op jit(solution)/shard_map/pallas_call | solution.py:648
  337.1 7.7 %shard_map.189 = (bf16[1024,1600]{1,0:T(8,128)(2,1)}, f32[2,1600]{1,0:T(2,128)}) custom-call(bf16[1024,768]{1,0:T(8,128)(2,1)} %get-tuple-element.281.g_ref, bf16[1024,1600]{1,0:T(8,128)(2,1)} %get-tuple-element.186.n1_ref.a_ref, bf16[1600,768]{1,0:T(8,128)(2,1)} %get-tuple-element.274.w_ref), custom_call_target="tpu_custom_call" | custom-call | tf_op jit(solution)/shard_map/pallas_call | solution.py:708
  357.1 6.9 %shard_map.190 = (bf16[400,768]{1,0:T(8,128)(2,1)}, bf16[400,768]{1,0:T(8,128)(2,1)}, bf16[400,768]{1,0:T(8,128)(2,1)}, bf16[208,768]{1,0:T(8,128)(2,1)}, bf16[192,768]{1,0:T(8,128)(2,1)}) custom-call(s32[2]{0:T(128)} %pad_add_fusion.where, bf16[1024,1600]{1,0:T(8,128)(2,1)} %get-tuple-element.186.n1_ref.a_ref, bf16[1024,768]{1,0:T(8,128)(2,1)} %get-tuple-element.281.g_ref), custom_call_target="tpu_custom_call" | custom-call | tf_op jit(solution)/shard_map/pallas_call | solution.py:679
  364.0 6.9 %collective-permute-done.40 = bf16[4,400,200]{2,1,0:T(8,128)(2,1)S(1)} collective-permute-done((bf16[4,400,200]{2,1,0:T(8,128)(2,1)}, bf16[4,400,200]{2,1,0:T(8,128)(2,1)S(1)}, u32[]{:S(2)}, u32[]{:S(2)}) %collective-permute-start.40) | collective-permute-done | bytes 640032 | tf_op jit(solution)/shard_map/ppermute | solution.py:131
  403.6 3.9 shard_map.194
  415.9 4.6 %collective-permute-done.50.rest_1_ = bf16[2,208,200]{2,1,0:T(8,128)(2,1)S(1)} collective-permute-done((bf16[2,208,200]{2,1,0:T(8,128)(2,1)S(1)}, bf16[2,208,200]{2,1,0:T(8,128)(2,1)S(1)}, u32[]{:S(2)}, u32[]{:S(2)}) %collective-permute-start.50) | collective-permute-done | bytes 166432 | tf_op jit(solution)/shard_map/ppermute | solution.py:90
  420.5 5.0 %collective-permute-done.51.rest_2_ = bf16[2,208,200]{2,1,0:T(8,128)(2,1)S(1)} collective-permute-done((bf16[2,208,200]{2,1,0:T(8,128)(2,1)S(1)}, bf16[2,208,200]{2,1,0:T(8,128)(2,1)S(1)}, u32[]{:S(2)}, u32[]{:S(2)}) %collective-permute-start.51) | collective-permute-done | bytes 166432 | tf_op jit(solution)/shard_map/ppermute | solution.py:90
  (343 shorter events, 187.4 us)
Async XLA Ops:
  7.2 64.2 %all-gather.4.cloned.1.call-start = ((), (), s32[]{:S(2)}) async-start(), calls=%async_computation.9 | async-start | bytes 3833856 | tf_op jit(solution)/shard_map/all_gather | solution.py:1087
  23.9 46.3 %all-to-all-start = ((bf16[8,432,128]{2,1,0:T(8,128)(2,1)}), bf16[8,432,128]{2,1,0:T(8,128)(2,1)S(1)}, u32[]{:S(2)}, u32[]{:S(2)}) async-start(bf16[8,432,128]{2,1,0:T(8,128)(2,1)} %shard_map.170), calls=%async_computation | async-start | bytes 1769472 | tf_op jit(solution)/shard_map/all_to_all | solution.py:172
  28.9 89.7 %all-gather.6.cloned.1.call-start = ((), (), s32[]{:S(2)}) async-start(), calls=%async_computation.10 | async-start | bytes 3833856 | tf_op jit(solution)/shard_map/all_gather | solution.py:1099
  29.0 18.9 %collective-permute-start.3 = (bf16[400,800]{1,0:T(8,128)(2,1)S(1)}, bf16[400,800]{1,0:T(8,128)(2,1)S(1)}, u32[]{:S(2)}, u32[]{:S(2)}) collective-permute-start(bf16[400,800]{1,0:T(8,128)(2,1)S(1)} %copy-done.16), channel_id=1, source_target_pairs={{0,8},{8,0},{16,24},{24,16},{1,9},{9,1},{17,25},{25,17},{2,10},{10... | collective-permute-start | bytes 1920008 | tf_op jit(solution)/shard_map/ppermute | solution.py:90
  29.6 33.5 %collective-permute-start.4 = (bf16[400,800]{1,0:T(8,128)(2,1)S(1)}, bf16[400,800]{1,0:T(8,128)(2,1)S(1)}, u32[]{:S(2)}, u32[]{:S(2)}) collective-permute-start(bf16[400,800]{1,0:T(8,128)(2,1)S(1)} %copy-done.16), channel_id=1, source_target_pairs={{0,16},{8,24},{16,0},{24,8},{1,17},{9,25},{17,1},{25,9},{2,18},{10... | collective-permute-start | bytes 1920008 | tf_op jit(solution)/shard_map/ppermute | solution.py:90
  30.1 33.0 %collective-permute-start.5 = (bf16[400,800]{1,0:T(8,128)(2,1)S(1)}, bf16[400,800]{1,0:T(8,128)(2,1)}, u32[]{:S(2)}, u32[]{:S(2)}) collective-permute-start(bf16[400,800]{1,0:T(8,128)(2,1)S(1)} %copy-done.16), channel_id=1, source_target_pairs={{0,24},{8,16},{16,8},{24,0},{1,25},{9,17},{17,9},{25,1},{2,26},{10... | collective-permute-start | bytes 1920008 | tf_op jit(solution)/shard_map/ppermute | solution.py:90
  73.2 19.3 %collective-permute-start.9 = (bf16[400,200]{1,0:T(8,128)(2,1)}, bf16[400,200]{1,0:T(8,128)(2,1)}, u32[]{:S(2)}, u32[]{:S(2)}) collective-permute-start(bf16[400,200]{1,0:T(8,128)(2,1)} %param.13), channel_id=1, source_target_pairs={{2,0},{3,1},{4,2},{5,3},{6,4},{7,5},{0,6},{1,7},{10,8},{11,9},{12,... | collective-permute-start | bytes 480008 | tf_op jit(solution)/shard_map/ppermute | solution.py:176
  86.2 26.8 %collective-permute-start.6 = (bf16[400,768]{1,0:T(8,128)(2,1)}, bf16[400,768]{1,0:T(8,128)(2,1)S(1)}, u32[]{:S(2)}, u32[]{:S(2)}) collective-permute-start(bf16[400,768]{1,0:T(8,128)(2,1)} %shard_map.172.rest_0_), channel_id=1, source_target_pairs={{0,8},{8,0},{16,24},{24,16},{1,9},{9,1},{17,25},{25,17},{2,10},{10... | collective-permute-start | bytes 1843208 | tf_op jit(solution)/shard_map/ppermute | solution.py:90
  92.6 26.1 %collective-permute-start.7 = (bf16[400,768]{1,0:T(8,128)(2,1)}, bf16[400,768]{1,0:T(8,128)(2,1)}, u32[]{:S(2)}, u32[]{:S(2)}) collective-permute-start(bf16[400,768]{1,0:T(8,128)(2,1)} %shard_map.172.rest_0_), channel_id=1, source_target_pairs={{0,16},{8,24},{16,0},{24,8},{1,17},{9,25},{17,1},{25,9},{2,18},{10... | collective-permute-start | bytes 1843208 | tf_op jit(solution)/shard_map/ppermute | solution.py:90
  94.5 24.1 %collective-permute-start.8 = (bf16[400,768]{1,0:T(8,128)(2,1)}, bf16[400,768]{1,0:T(8,128)(2,1)}, u32[]{:S(2)}, u32[]{:S(2)}) collective-permute-start(bf16[400,768]{1,0:T(8,128)(2,1)} %shard_map.172.rest_0_), channel_id=1, source_target_pairs={{0,24},{8,16},{16,8},{24,0},{1,25},{9,17},{17,9},{25,1},{2,26},{10... | collective-permute-start | bytes 1843208 | tf_op jit(solution)/shard_map/ppermute | solution.py:90
  119.9 25.8 %all-to-all-start.1 = ((bf16[8,208,200]{1,2,0:T(8,128)(2,1)}), bf16[8,208,200]{1,2,0:T(8,128)(2,1)S(1)}, u32[]{:S(2)}, u32[]{:S(2)}) async-start(bf16[8,208,200]{1,2,0:T(8,128)(2,1)} %copy.65), calls=%async_computation.1 | async-start | bytes 1638400 | tf_op jit(solution)/shard_map/all_to_all | solution.py:172
  123.6 20.7 %collective-permute-start.16 = (bf16[4,400,200]{2,1,0:T(8,128)(2,1)S(1)}, bf16[4,400,200]{2,1,0:T(8,128)(2,1)S(1)}, u32[]{:S(2)}, u32[]{:S(2)}) collective-permute-start(bf16[4,400,200]{2,1,0:T(8,128)(2,1)S(1)} %pad_maximum_fusion.rest_0_), channel_id=1, source_target_pairs={{0,8},{8,0},{16,24},{24,16},{1,9},{9,1},{17,25},{25,17},{2,10},{10... | collective-permute-start | bytes 1920008 | tf_op jit(solution)/shard_map/ppermute | solution.py:90
  125.4 20.3 %collective-permute-start.17 = (bf16[4,400,200]{2,1,0:T(8,128)(2,1)S(1)}, bf16[4,400,200]{2,1,0:T(8,128)(2,1)S(1)}, u32[]{:S(2)}, u32[]{:S(2)}) collective-permute-start(bf16[4,400,200]{2,1,0:T(8,128)(2,1)S(1)} %pad_maximum_fusion.rest_0_), channel_id=1, source_target_pairs={{0,16},{8,24},{16,0},{24,8},{1,17},{9,25},{17,1},{25,9},{2,18},{10... | collective-permute-start | bytes 1920008 | tf_op jit(solution)/shard_map/ppermute | solution.py:90
  146.7 20.1 %all-to-all-start.2 = ((bf16[8,128,256]{2,1,0:T(8,128)(2,1)}), bf16[8,128,256]{2,1,0:T(8,128)(2,1)S(1)}, u32[]{:S(2)}, u32[]{:S(2)}) async-start(bf16[8,128,256]{2,1,0:T(8,128)(2,1)} %get-tuple-element.191), calls=%async_computation.2 | async-start | bytes 1048576 | tf_op jit(solution)/shard_map/all_to_all | solution.py:172
  151.4 67.0 %all-gather.8.cloned.1.call-start = ((), (), s32[]{:S(2)}) async-start(), calls=%async_computation.11 | async-start | bytes 3833856 | tf_op jit(solution)/shard_map/all_gather | solution.py:1135
  177.6 98.9 %reduce-scatter.4.cloned.1.call-start = ((), (), s32[]{:S(2)}) async-start(), calls=%async_computation.12 | async-start | bytes 3833856 | tf_op jit(solution)/shard_map/reduce_scatter | solution.py:1144
  177.6 18.4 %collective-permute-start.25 = (bf16[208,1600]{1,0:T(8,128)(2,1)S(1)}, bf16[208,1600]{1,0:T(8,128)(2,1)S(1)}, u32[]{:S(2)}, u32[]{:S(2)}) collective-permute-start(bf16[208,1600]{1,0:T(8,128)(2,1)S(1)} %copy-done.9), channel_id=1, source_target_pairs={{0,8},{8,0},{16,24},{24,16},{1,9},{9,1},{17,25},{25,17},{2,10},{10... | collective-permute-start | bytes 1996808 | tf_op jit(solution)/shard_map/ppermute | solution.py:90
  178.1 18.0 %collective-permute-start.26 = (bf16[208,1600]{1,0:T(8,128)(2,1)S(1)}, bf16[208,1600]{1,0:T(8,128)(2,1)S(1)}, u32[]{:S(2)}, u32[]{:S(2)}) collective-permute-start(bf16[208,1600]{1,0:T(8,128)(2,1)S(1)} %copy-done.9), channel_id=1, source_target_pairs={{0,16},{8,24},{16,0},{24,8},{1,17},{9,25},{17,1},{25,9},{2,18},{10... | collective-permute-start | bytes 1996808 | tf_op jit(solution)/shard_map/ppermute | solution.py:90
  179.6 31.4 %collective-permute-start.27 = (bf16[208,1600]{1,0:T(8,128)(2,1)S(1)}, bf16[208,1600]{1,0:T(8,128)(2,1)S(1)}, u32[]{:S(2)}, u32[]{:S(2)}) collective-permute-start(bf16[208,1600]{1,0:T(8,128)(2,1)S(1)} %copy-done.9), channel_id=1, source_target_pairs={{0,24},{8,16},{16,8},{24,0},{1,25},{9,17},{17,9},{25,1},{2,26},{10... | collective-permute-start | bytes 1996808 | tf_op jit(solution)/shard_map/ppermute | solution.py:90
  181.2 34.6 %collective-permute-start.28 = (bf16[8,128,256]{2,1,0:T(8,128)(2,1)}, bf16[8,128,256]{2,1,0:T(8,128)(2,1)S(1)}, u32[]{:S(2)}, u32[]{:S(2)}) collective-permute-start(bf16[8,128,256]{2,1,0:T(8,128)(2,1)} %copy-done.3), channel_id=1, source_target_pairs={{0,1},{1,0},{2,3},{3,2},{4,5},{5,4},{6,7},{7,6},{8,9},{9,8},{10,11... | collective-permute-start | bytes 1572872 | tf_op jit(solution)/shard_map/ppermute | solution.py:168
  234.9 112.5 %reduce-scatter.6.cloned.1.call-start = ((), (), s32[]{:S(2)}) async-start(), calls=%async_computation.13 | async-start | bytes 3833856 | tf_op jit(solution)/shard_map/reduce_scatter | solution.py:1153
  257.8 17.1 %collective-permute-start.31 = (bf16[208,1600]{1,0:T(8,128)(2,1)}, bf16[208,1600]{1,0:T(8,128)(2,1)S(1)}, u32[]{:S(2)}, u32[]{:S(2)}) collective-permute-start(bf16[208,1600]{1,0:T(8,128)(2,1)} %get-tuple-element.243), channel_id=1, source_target_pairs={{0,8},{8,0},{16,24},{24,16},{1,9},{9,1},{17,25},{25,17},{2,10},{10... | collective-permute-start | bytes 1996808 | tf_op jit(solution)/shard_map/ppermute | solution.py:131
  259.1 16.9 %collective-permute-start.32 = (bf16[208,1600]{1,0:T(8,128)(2,1)}, bf16[208,1600]{1,0:T(8,128)(2,1)S(1)}, u32[]{:S(2)}, u32[]{:S(2)}) collective-permute-start(bf16[208,1600]{1,0:T(8,128)(2,1)} %get-tuple-element.244), channel_id=1, source_target_pairs={{0,16},{8,24},{16,0},{24,8},{1,17},{9,25},{17,1},{25,9},{2,18},{10... | collective-permute-start | bytes 1996808 | tf_op jit(solution)/shard_map/ppermute | solution.py:132
  288.5 27.7 %all-to-all-start.3 = ((bf16[8,128,256]{2,1,0:T(8,128)(2,1)}), bf16[8,128,256]{2,1,0:T(8,128)(2,1)S(1)}, u32[]{:S(2)}, u32[]{:S(2)}) async-start(bf16[8,128,256]{2,1,0:T(8,128)(2,1)} %get-tuple-element.251), calls=%async_computation.4 | async-start | bytes 1048576 | tf_op jit(solution)/shard_map/all_to_all | solution.py:172
  295.5 18.2 %collective-permute-start.36 = (bf16[400,800]{1,0:T(8,128)(2,1)}, bf16[400,800]{1,0:T(8,128)(2,1)S(1)}, u32[]{:S(2)}, u32[]{:S(2)}) collective-permute-start(bf16[400,800]{1,0:T(8,128)(2,1)} %get-tuple-element.263), channel_id=1, source_target_pairs={{0,8},{8,0},{16,24},{24,16},{1,9},{9,1},{17,25},{25,17},{2,10},{10... | collective-permute-start | bytes 1920008 | tf_op jit(solution)/shard_map/ppermute | solution.py:131
  295.9 18.7 %collective-permute-start.37 = (bf16[400,800]{1,0:T(8,128)(2,1)}, bf16[400,800]{1,0:T(8,128)(2,1)}, u32[]{:S(2)}, u32[]{:S(2)}) collective-permute-start(bf16[400,800]{1,0:T(8,128)(2,1)} %get-tuple-element.264), channel_id=1, source_target_pairs={{0,16},{8,24},{16,0},{24,8},{1,17},{9,25},{17,1},{25,9},{2,18},{10... | collective-permute-start | bytes 1920008 | tf_op jit(solution)/shard_map/ppermute | solution.py:132
  317.5 29.9 %all-to-all-start.4 = ((bf16[8,208,200]{1,2,0:T(8,128)(2,1)}), bf16[8,208,200]{1,2,0:T(8,128)(2,1)S(1)}, u32[]{:S(2)}, u32[]{:S(2)}) async-start(bf16[8,208,200]{1,2,0:T(8,128)(2,1)} %copy.69), calls=%async_computation.6 | async-start | bytes 1638400 | tf_op jit(solution)/shard_map/all_to_all | solution.py:172
  321.1 109.6 %reduce-scatter.8.cloned.1.call-start = ((), (), s32[]{:S(2)}) async-start(), calls=%async_computation.14 | async-start | bytes 3833856 | tf_op jit(solution)/shard_map/reduce_scatter | solution.py:1171
  350.5 20.4 %collective-permute-start.40 = (bf16[4,400,200]{2,1,0:T(8,128)(2,1)}, bf16[4,400,200]{2,1,0:T(8,128)(2,1)S(1)}, u32[]{:S(2)}, u32[]{:S(2)}) collective-permute-start(bf16[4,400,200]{2,1,0:T(8,128)(2,1)} %get-tuple-element.292), channel_id=1, source_target_pairs={{0,8},{8,0},{16,24},{24,16},{1,9},{9,1},{17,25},{25,17},{2,10},{10... | collective-permute-start | bytes 1920008 | tf_op jit(solution)/shard_map/ppermute | solution.py:131
  352.0 20.1 %collective-permute-start.41 = (bf16[4,400,200]{2,1,0:T(8,128)(2,1)}, bf16[4,400,200]{2,1,0:T(8,128)(2,1)S(1)}, u32[]{:S(2)}, u32[]{:S(2)}) collective-permute-start(bf16[4,400,200]{2,1,0:T(8,128)(2,1)} %get-tuple-element.293), channel_id=1, source_target_pairs={{0,16},{8,24},{16,0},{24,8},{1,17},{9,25},{17,1},{25,9},{2,18},{10... | collective-permute-start | bytes 1920008 | tf_op jit(solution)/shard_map/ppermute | solution.py:132
  384.5 18.0 %collective-permute-start.44 = (bf16[400,768]{1,0:T(8,128)(2,1)}, bf16[400,768]{1,0:T(8,128)(2,1)S(1)}, u32[]{:S(2)}, u32[]{:S(2)}) collective-permute-start(bf16[400,768]{1,0:T(8,128)(2,1)} %get-tuple-element.299), channel_id=1, source_target_pairs={{0,8},{8,0},{16,24},{24,16},{1,9},{9,1},{17,25},{25,17},{2,10},{10... | collective-permute-start | bytes 1843208 | tf_op jit(solution)/shard_map/ppermute | solution.py:131
  407.5 26.8 %all-to-all-start.5 = ((bf16[8,432,128]{2,1,0:T(8,128)(2,1)}), bf16[8,432,128]{2,1,0:T(8,128)(2,1)S(1)}, u32[]{:S(2)}, u32[]{:S(2)}) async-start(bf16[8,432,128]{2,1,0:T(8,128)(2,1)} %shard_map.194), calls=%async_computation.7 | async-start | bytes 1769472 | tf_op jit(solution)/shard_map/all_to_all | solution.py:172
  (94 other events, 915.6 us)
Sparse Core Ops, SparseCore 0:
  9.6 61.7 all-gather.3
  73.0 45.4 all-gather.5
  177.7 40.7 all-gather.7
  235.0 41.4 reduce-scatter.3
  278.6 50.7 reduce-scatter.5
  347.6 48.0 reduce-scatter.7

commit v9 on v8

--- a/solution.py
+++ b/solution.py
@@ -510,30 +510,31 @@
 
 def head_masks(rows):
     first = lax.broadcasted_iota(jnp.int32, (rows, PAIR), 1) < HD
-    causal = lax.broadcasted_iota(jnp.int32, (rows, rows), 0) >= lax.broadcasted_iota(
+    causal = lax.broadcasted_iota(jnp.int32, (rows, rows), 0) <= lax.broadcasted_iota(
         jnp.int32, (rows, rows), 1
     )
     return first, causal
 
 
-def masked_scores(q, keys, causal):
+def masked_scores(keys, q, causal):
     rows, seen = q.shape[0], keys.shape[0]
-    s = mm_nt(q, keys)
-    tail = jnp.where(causal, s[:, seen - rows :], NEG_FILL)
-    return tail if seen == rows else jnp.concatenate([s[:, : seen - rows], tail], axis=1)
+    s = mm_nt(keys, q)
+    tail = jnp.where(causal, s[seen - rows :], NEG_FILL)
+    return tail if seen == rows else jnp.concatenate([s[: seen - rows], tail], axis=0)
 
 
 def attend_rows(q, keys, values, first, causal):
     q = q * BF(1.0 / math.sqrt(HD))
+    values = jnp.concatenate([values, jnp.ones_like(values)], axis=1)
     outs, logs = [], []
     for mine in (first, ~first):
-        s = masked_scores(jnp.where(mine, q, BF(0)), keys, causal)
-        top = jnp.max(s, axis=-1, keepdims=True)
+        s = masked_scores(keys, jnp.where(mine, q, BF(0)), causal)
+        top = jnp.max(s, axis=0, keepdims=True)
         e = jnp.exp(s - top)
-        total = jnp.sum(e, axis=-1, keepdims=True)
-        outs.append(mm(e.astype(BF), values) / total)
-        logs.append(top + jnp.log(total))
-    return jnp.where(first, outs[0], outs[1]).astype(BF), jnp.where(first, logs[0], logs[1])
+        logs.append(top + jnp.log(jnp.sum(e, axis=0, keepdims=True)))
+        both = mm_tn(e.astype(BF), values)
+        outs.append(both[:, :PAIR] / both[:, PAIR:])
+    return jnp.where(first, outs[0], outs[1]).astype(BF), logs
 
 
 def attend_kernel(pairs, dps, where, x_ref, vec_ref, bias_ref, *rest):
@@ -563,10 +564,11 @@
                 lanes = slice(g * PAIR, (g + 1) * PAIR)
                 keys = qkv[0:seen, (pairs + g) * PAIR : (pairs + g + 1) * PAIR]
                 values = qkv[0:seen, (2 * pairs + g) * PAIR : (2 * pairs + g + 1) * PAIR]
-                out, log = attend_rows(qkv[j * rows : seen, lanes], keys, values, first, causal)
+                out, logs = attend_rows(qkv[j * rows : seen, lanes], keys, values, first, causal)
                 for b in range(2):
                     att_ref[b, :, lanes] = out[b * part : (b + 1) * part]
-                lse_ref[:, lanes] = log
+                for h in range(2):
+                    lse_ref[2 * g + h : 2 * g + h + 1, :] = logs[h]
 
 
 def attend(where, x_all, table, bias, weights, part):
@@ -585,17 +587,16 @@
             tile(model),
             tile(width),
             pl.BlockSpec((2, part, heads), lambda i: (i, 0, 0)),
-            tile(heads),
-            pl.BlockSpec((model, width), lambda i: (0, 0)),
+            pl.BlockSpec((heads // HD, rows), lambda i: (0, i)),
         ],
         out_shape=[
             like((length, model)),
             like((length, width)),
             like((length // part, part, heads)),
-            like((length, heads), F32),
-            like((model, width)),
+            like((heads // HD, length), F32),
         ],
         scratch_shapes=[
+            pltpu.VMEM((model, width), BF),
             pltpu.VMEM(stage_shape(dps, depth, width), BF),
             pltpu.VMEM((length, width), BF),
             pltpu.SemaphoreType.DMA((dps,)),
@@ -604,10 +605,14 @@
     )(where, x_all, table, bias, *weights)
 
 
-def attend_back_kernel(pairs, qkv_ref, ga_ref, lse_ref, gqkv_ref, sums_ref, ak, av):
+def attend_back_kernel(pairs, dps, where, qkv_ref, ga_ref, lse_ref, n1_hbm, *rest):
+    w_refs, rest = rest[:dps], rest[dps:]
+    gqkv_ref, gn1_hbm, sums_ref, norm_ref, ak, av, w, stage, n1, gn1, sems, sems2 = rest
     length = qkv_ref.shape[0]
     part = ga_ref.shape[1]
     rows = 2 * part
+    copies = place_rows(where, w_refs, w, stage, sems)
+    late = run_copies([(n1_hbm, n1)], sems2)
     first, causal = head_masks(rows)
     for g in range(pairs):
         lanes = slice(g * PAIR, (g + 1) * PAIR)
@@ -626,33 +631,63 @@
             for h, mine in enumerate((first, ~first)):
                 q_h = jnp.where(mine, q, BF(0))
                 ga_h = jnp.where(mine, ga, BF(0))
-                s = masked_scores(q_h, keys, causal)
-                lane = g * PAIR + h * HD
-                p = jnp.exp(s - lse_ref[here, lane : lane + 1])
-                gp = mm_nt(ga_h, values)
-                centre = jnp.sum(p * gp, axis=-1, keepdims=True)
+                s = masked_scores(keys, q_h, causal)
+                p = jnp.exp(s - lse_ref[2 * g + h : 2 * g + h + 1, here])
+                gp = mm_nt(values, ga_h)
+                centre = jnp.sum(p * gp, axis=0, keepdims=True)
                 gs = (p * (gp - centre)).astype(BF)
-                av[0:seen, :] += mm_tn(p.astype(BF), ga_h)
-                ak[0:seen, :] += mm_tn(gs, q_h)
-                grads.append(mm(gs, keys))
+                av[0:seen, :] += mm(p.astype(BF), ga_h)
+                ak[0:seen, :] += mm(gs, q_h)
+                grads.append(mm_tn(gs, keys))
             gqkv_ref[here, lanes] = (
                 jnp.where(first, grads[0], grads[1]) * (1.0 / math.sqrt(HD))
             ).astype(BF)
         gqkv_ref[:, k_lanes] = ak[...].astype(BF)
         gqkv_ref[:, v_lanes] = av[...].astype(BF)
-    sums_ref[...] = jnp.sum(gqkv_ref[...].astype(F32), axis=0, keepdims=True)
-
-
-def attend_back(qkv, grad, lse):
+    settle_rows(copies, w, stage)
+    wait_for(late)
+    out = []
+    norm_ref[...] = jnp.zeros_like(norm_ref)
+    sums_ref[...] = jnp.zeros_like(sums_ref)
+    for i in range(length // rows):
+        here = slice(i * rows, (i + 1) * rows)
+        grad = mm_nt(gqkv_ref[here, :], w[...])
+        gn1[here, :] = grad.astype(BF)
+        out.append(pltpu.make_async_copy(gn1.at[here, :], gn1_hbm.at[here, :], sems2.at[i]))
+        out[-1].start()
+        norm_ref[0:1, :] += jnp.sum(grad * n1[here, :].astype(F32), axis=0, keepdims=True)
+        norm_ref[1:2, :] += jnp.sum(grad, axis=0, keepdims=True)
+        sums_ref[...] += jnp.sum(gqkv_ref[here, :].astype(F32), axis=0, keepdims=True)
+    wait_for(out)
+
+
+def attend_back(where, qkv, grad, lse, n1, weights):
     length, width = qkv.shape
-    return pl.pallas_call(
-        functools.partial(attend_back_kernel, grad.shape[2] // PAIR),
-        in_specs=[WHOLE] * 3,
-        out_specs=[WHOLE, WHOLE],
-        out_shape=[like((length, width)), like((1, width), F32)],
-        scratch_shapes=[pltpu.VMEM((length, PAIR), F32), pltpu.VMEM((length, PAIR), F32)],
-        compiler_params=ROOM,
-    )(qkv, grad, lse)
+    model = n1.shape[1]
+    dps = len(weights)
+    depth = weights[0].shape[0]
+    return pl.pallas_call(
+        functools.partial(attend_back_kernel, grad.shape[2] // PAIR, dps),
+        in_specs=[SCALAR, WHOLE, WHOLE, WHOLE] + [ANY] * (1 + dps),
+        out_specs=[WHOLE, ANY, WHOLE, WHOLE],
+        out_shape=[
+            like((length, width)),
+            like((length, model)),
+            like((1, width), F32),
+            like((2, model), F32),
+        ],
+        scratch_shapes=[
+            pltpu.VMEM((length, PAIR), F32),
+            pltpu.VMEM((length, PAIR), F32),
+            pltpu.VMEM((model, width), BF),
+            pltpu.VMEM(stage_shape(dps, depth, width), BF),
+            pltpu.VMEM((length, model), BF),
+            pltpu.VMEM((length, model), BF),
+            pltpu.SemaphoreType.DMA((dps,)),
+            pltpu.SemaphoreType.DMA((length // (2 * grad.shape[1]),)),
+        ],
+        compiler_params=ROOM,
+    )(where, qkv, grad, lse, n1, *weights)
 
 
 def grad_blocks_kernel(where, a_ref, g_ref, *rest):
@@ -688,31 +723,6 @@
         ],
         compiler_params=ROOM,
     )(where, a, g)
-
-
-def grad_rows_kernel(g_ref, n1_ref, w_ref, out_ref, sums_ref):
-    @pl.when(pl.program_id(0) == 0)
-    def _():
-        sums_ref[...] = jnp.zeros_like(sums_ref)
-
-    grad = mm_nt(g_ref[...], w_ref[...])
-    sums_ref[0:1, :] += jnp.sum(grad * n1_ref[...].astype(F32), axis=0, keepdims=True)
-    sums_ref[1:2, :] += jnp.sum(grad, axis=0, keepdims=True)
-    out_ref[...] = grad.astype(BF)
-
-
-def grad_rows(gqkv, weights, n1, rows):
-    length, model = n1.shape
-    width = weights.shape[1]
-    tile = lambda cols: pl.BlockSpec((rows, cols), lambda i: (i, 0))
-    return pl.pallas_call(
-        grad_rows_kernel,
-        grid=(length // rows,),
-        in_specs=[tile(width), tile(model), WHOLE],
-        out_specs=[tile(model), pl.BlockSpec((2, model), lambda i: (0, 0))],
-        out_shape=[like((length, model)), like((2, model), F32)],
-        compiler_params=ROOM,
-    )(gqkv, n1, weights)
 
 
 def place_pieces(where, refs, store, sems):
@@ -1116,7 +1126,7 @@
     pieces = exchange(pieces)
     wo = {(0, 0): line}
     wo.update({(k, 0): b for k, b in send_rel(copies(line), "dp", near).items()})
-    n1_all, qkv, att, lse, wq = attend(where, x_all, table, bias_qkv, wq, rows)
+    n1_all, qkv, att, lse = attend(where, x_all, table, bias_qkv, wq, rows)
     att, wo, pieces = phase(att, wo, pieces)
 
     att = exchange(att)
@@ -1163,10 +1173,10 @@
 
     out_first = reduce_first(d_out)
     g_proj = exchange(g_proj)
-    gqkv, gqkv_sums = attend_back(qkv, ga, lse)
-    gqkv, out_first = phase(gqkv, out_first)
-    gn1_part, norm_sums = grad_rows(gqkv, wq, n1_all, 2 * rows)
-    gn1_part, gqkv, mlp, g_proj, d_out = phase(gn1_part, gqkv, mlp, g_proj, d_out)
+    gqkv, gn1_part, gqkv_sums, norm_sums = attend_back(where, qkv, ga, lse, n1_all, wq)
+    gn1_part, gqkv, mlp, g_proj, d_out, out_first = phase(
+        gn1_part, gqkv, mlp, g_proj, d_out, out_first
+    )
 
     gn1 = lax.psum_scatter(gn1_part, "seq", scatter_dimension=0, tiled=True)
     out_in = reduce_second(d_out, out_first)

time: 457 us -> 456 us (level)
  waiting for transfers between devices: 141 us -> 150 us
  Pallas kernels: 159 us -> 152 us
    pallas_call x1 -> x0, Pallas kernels: 7.73 us -> none  [grad_rows(): pl.pallas_call(grad_rows_kernel, grid=(length // rows,), in_specs=[tile(w...]
    all_to_all x6, waiting for transfers between devices: 12.2 us -> 17.2 us  [exchange(): return lax.all_to_all(block, 'seq', 0, 0, tiled=True)]
    unnamed x124 -> x120, local copies, waits for them, and re-layouts: 14.7 us -> 14.1 us
  transfers between devices with their start and end apart: 68 -> 68, of which waited for: 34 -> 34; matrix products, arithmetic and copies ran while one was open for 6% -> 5% of each run, Pallas kernels for 30% -> 29%
where the time goes in v9:
time: 456 us; the launch traced here: 450 us
  Pallas kernels  152 us (33%)
  waiting for transfers between devices  150 us (33%)
  starting transfers between devices  93.4 us (20%)
  local copies, waits for them, and re-layouts  31.3 us (7%)
  between operations  15.2 us (3%)
  other arithmetic  7.84 us (2%)
    ppermute x23, waiting for transfers between devices, send_rel(): return {k: lax.ppermute(blocks[k], axis, xor_perm(count, k)) for k in ks}  74.4 us
    ppermute x23, starting transfers between devices, send_rel(): return {k: lax.ppermute(blocks[k], axis, xor_perm(count, k)) for k in ks}  30.7 us
    all_to_all x6, starting transfers between devices, exchange(): return lax.all_to_all(block, 'seq', 0, 0, tiled=True)  24.6 us
    ppermute x4, waiting for transfers between devices, reduce_second(): lax.ppermute(first, 'dp', xor_perm(4, 1))  21.8 us
    ppermute x8, waiting for transfers between devices, chip_permute(): lax.ppermute(block, 'seq', [(2 * a + core, 2 * b + core) for a, b in pair...  18.6 us
    all_to_all x6, waiting for transfers between devices, exchange(): return lax.all_to_all(block, 'seq', 0, 0, tiled=True)  17.2 us
    pallas_call x1, Pallas kernels, attend_back(): pl.pallas_call(functools.partial(attend_back_kernel, grad.shape[2] // PAI...  16.9 us
    pallas_call x1, Pallas kernels, feed(): pl.pallas_call(feed_kernel, grid=(length // rows,), in_specs=[tile(model)...  16.4 us
  transfers between devices with their start and end apart: 68, of which 34 were waited for; matrix products, arithmetic and copies ran while one was open for 5% of the time, Pallas kernels for 29%

profile of v9, /device:TPU:0, one launch (start us, length us, event | category | flops | bytes accessed | tf_op | source)
XLA Modules:
  0.0 449.9 jit_solution(13045539527173834420)
XLA Ops:
  23.9 5.0 %all-to-all-start = ((bf16[8,432,128]{2,1,0:T(8,128)(2,1)}), bf16[8,432,128]{2,1,0:T(8,128)(2,1)S(1)}, u32[]{:S(2)}, u32[]{:S(2)}) async-start(bf16[8,432,128]{2,1,0:T(8,128)(2,1)} %shard_map.170), calls=%async_computation | async-start | bytes 1769472 | tf_op jit(solution)/shard_map/all_to_all | solution.py:172
  36.9 11.0 %collective-permute-done.3.rest_1_ = bf16[400,800]{1,0:T(8,128)(2,1)S(1)} collective-permute-done((bf16[400,800]{1,0:T(8,128)(2,1)S(1)}, bf16[400,800]{1,0:T(8,128)(2,1)S(1)}, u32[]{:S(2)}, u32[]{:S(2)}) %collective-permute-start.3) | collective-permute-done | bytes 640032 | tf_op jit(solution)/shard_map/ppermute | solution.py:90
  47.9 15.2 %collective-permute-done.4.rest_2_ = bf16[400,800]{1,0:T(8,128)(2,1)S(1)} collective-permute-done((bf16[400,800]{1,0:T(8,128)(2,1)S(1)}, bf16[400,800]{1,0:T(8,128)(2,1)S(1)}, u32[]{:S(2)}, u32[]{:S(2)}) %collective-permute-start.4) | collective-permute-done | bytes 640032 | tf_op jit(solution)/shard_map/ppermute | solution.py:90
  63.0 7.2 %all-to-all-done.in_ref = bf16[8,432,128]{2,1,0:T(8,128)(2,1)S(1)} async-done(((bf16[8,432,128]{2,1,0:T(8,128)(2,1)}), bf16[8,432,128]{2,1,0:T(8,128)(2,1)S(1)}, u32[]{:S(2)}, u32[]{:S(2)}) %all-to-all-start) | async-done | bytes 884768 | tf_op jit(solution)/shard_map/all_to_all | solution.py:172
  88.1 4.5 collective-permute-done.9
  102.5 10.3 %collective-permute-done.12 = bf16[400,200]{1,0:T(8,128)(2,1)S(1)} collective-permute-done((bf16[400,200]{1,0:T(8,128)(2,1)}, bf16[400,200]{1,0:T(8,128)(2,1)S(1)}, u32[]{:S(2)}, u32[]{:S(2)}) %collective-permute-start.12) | collective-permute-done | bytes 160032 | tf_op jit(solution)/shard_map/ppermute | solution.py:176
  113.0 5.6 %collective-permute-done.7.rest_2_ = bf16[400,768]{1,0:T(8,128)(2,1)} collective-permute-done((bf16[400,768]{1,0:T(8,128)(2,1)}, bf16[400,768]{1,0:T(8,128)(2,1)}, u32[]{:S(2)}, u32[]{:S(2)}) %collective-permute-start.7) | collective-permute-done | bytes 614432 | tf_op jit(solution)/shard_map/ppermute | solution.py:90
  126.9 14.8 %shard_map.174 = (bf16[1024,1600]{1,0:T(8,128)(2,1)}, bf16[1024,768]{1,0:T(8,128)(2,1)}, bf16[8,128,256]{2,1,0:T(8,128)(2,1)}, f32[4,1024]{1,0:T(4,128)}) custom-call(s32[2]{0:T(128)} %pad_add_fusion.where, bf16[1024,1600]{1,0:T(8,128)(2,1)} %all-gather.6.cloned.1.call-done.x_ref, f32[8,1600]{1,0:T(8,128)} %copy-done.10, ...), custom_call_target="tpu_custom_call" | custom-call | tf_op jit(solution)/shard_map/pallas_call | solution.py:582
  146.8 4.8 %all-to-all-start.2 = ((bf16[8,128,256]{2,1,0:T(8,128)(2,1)}), bf16[8,128,256]{2,1,0:T(8,128)(2,1)S(1)}, u32[]{:S(2)}, u32[]{:S(2)}) async-start(bf16[8,128,256]{2,1,0:T(8,128)(2,1)} %get-tuple-element.189), calls=%async_computation.2 | async-start | bytes 1048576 | tf_op jit(solution)/shard_map/all_to_all | solution.py:172
  160.7 5.1 %collective-permute-done.18.rest_6_ = bf16[2,400,200]{2,1,0:T(8,128)(2,1)S(1)} collective-permute-done((bf16[2,400,200]{2,1,0:T(8,128)(2,1)}, bf16[2,400,200]{2,1,0:T(8,128)(2,1)S(1)}, u32[]{:S(2)}, u32[]{:S(2)}) %collective-permute-start.18) | collective-permute-done | bytes 320032 | tf_op jit(solution)/shard_map/ppermute | solution.py:162
  170.7 6.9 %shard_map.176 = (f32[128,1600]{1,0:T(8,128)}, bf16[128,1600]{1,0:T(8,128)(2,1)}) custom-call(s32[2]{0:T(128)} %pad_add_fusion.where, bf16[8,128,256]{2,1,0:T(8,128)(2,1)} %copy-done.3, f32[8,1600]{1,0:T(8,128)} %copy-done.10, bf16[128,1600]{1,0:T(8,128)(2,1)} %copy.62.x_hbm, bf16[4,400,200]{2,1,0:T(8,128)(2,1)} %copy-done, ...), custom_call_target="tpu_custom_call" | custom-call | tf_op jit(solution)/shard_map/pallas_call | solution.py:974
  182.2 4.0 shard_map.177.wf
  186.2 10.0 %collective-permute-done.25.rest_1_ = bf16[208,1600]{1,0:T(8,128)(2,1)S(1)} collective-permute-done((bf16[208,1600]{1,0:T(8,128)(2,1)S(1)}, bf16[208,1600]{1,0:T(8,128)(2,1)S(1)}, u32[]{:S(2)}, u32[]{:S(2)}) %collective-permute-start.25) | collective-permute-done | bytes 665632 | tf_op jit(solution)/shard_map/ppermute | solution.py:90
  196.2 14.9 %collective-permute-done.27.rest_3_ = bf16[208,1600]{1,0:T(8,128)(2,1)S(1)} collective-permute-done((bf16[208,1600]{1,0:T(8,128)(2,1)S(1)}, bf16[208,1600]{1,0:T(8,128)(2,1)S(1)}, u32[]{:S(2)}, u32[]{:S(2)}) %collective-permute-start.27) | collective-permute-done | bytes 665632 | tf_op jit(solution)/shard_map/ppermute | solution.py:90
  212.0 3.9 shard_map.178.wp
  218.6 16.4 %shard_map.179 = (bf16[1024,800]{1,0:T(8,128)(2,1)}, bf16[1024,800]{1,0:T(8,128)(2,1)}, bf16[1024,1600]{1,0:T(8,128)(2,1)}, f32[1,800]{1,0:T(1,128)}) custom-call(bf16[1024,1600]{1,0:T(8,128)(2,1)} %all-gather.8.cloned.1.call-done.n2_ref.a_ref, bf16[1024,1600]{1,0:T(8,128)(2,1)} %all-gather.4.cloned.1.call-done.gm_ref, f32[1,800]{1,0:T(1,128)} %broadcast_in_dim.40.bias_ref, ...), custom_call_target="tpu_custom_call" | custom-call | tf_op jit(solution)/shard_map/pallas_call | solution.py:816
  235.5 7.7 %shard_map.181 = (bf16[208,1600]{1,0:T(8,128)(2,1)}, bf16[208,1600]{1,0:T(8,128)(2,1)}, bf16[208,1600]{1,0:T(8,128)(2,1)}, bf16[112,1600]{1,0:T(8,128)(2,1)}, bf16[96,1600]{1,0:T(8,128)(2,1)}) custom-call(s32[2]{0:T(128)} %pad_add_fusion.where, bf16[1024,1600]{1,0:T(8,128)(2,1)} %all-gather.4.cloned.1.call-done.gm_ref, ...), custom_call_target="tpu_custom_call" | custom-call | tf_op jit(solution)/shard_map/pallas_call | solution.py:851
  246.2 7.9 %shard_map.180 = (bf16[400,800]{1,0:T(8,128)(2,1)}, bf16[400,800]{1,0:T(8,128)(2,1)}, bf16[400,800]{1,0:T(8,128)(2,1)}, bf16[208,800]{1,0:T(8,128)(2,1)}, bf16[192,800]{1,0:T(8,128)(2,1)}) custom-call(s32[2]{0:T(128)} %pad_add_fusion.where, bf16[1024,1600]{1,0:T(8,128)(2,1)} %all-gather.8.cloned.1.call-done.n2_ref.a_ref, ...), custom_call_target="tpu_custom_call" | custom-call | tf_op jit(solution)/shard_map/pallas_call | solution.py:714
  260.7 7.6 %shard_map.182 = bf16[1024,1600]{1,0:T(8,128)(2,1)} custom-call(bf16[1024,800]{1,0:T(8,128)(2,1)} %get-tuple-element.235.e_ref, bf16[800,1600]{1,0:T(8,128)(2,1)} %shard_map.178.wp), custom_call_target="tpu_custom_call" | custom-call | tf_op jit(solution)/shard_map/pallas_call | solution.py:871
  268.3 6.8 %collective-permute-done.31.refs_1_ = bf16[208,1600]{1,0:T(8,128)(2,1)S(1)} collective-permute-done((bf16[208,1600]{1,0:T(8,128)(2,1)}, bf16[208,1600]{1,0:T(8,128)(2,1)S(1)}, u32[]{:S(2)}, u32[]{:S(2)}) %collective-permute-start.31) | collective-permute-done | bytes 665632 | tf_op jit(solution)/shard_map/ppermute | solution.py:131
  280.6 8.0 %shard_map.184 = (f32[128,1600]{1,0:T(8,128)}, bf16[128,1600]{1,0:T(8,128)(2,1)}, bf16[8,128,256]{2,1,0:T(8,128)(2,1)}, f32[4,1600]{1,0:T(4,128)}) custom-call(s32[2]{0:T(128)} %pad_add_fusion.where, bf16[128,1600]{1,0:T(8,128)(2,1)} %reduce-scatter.4.cloned.1.call-done.gn2_ref, f32[128,1600]{1,0:T(8,128)} %get-tuple-element.244.r_ref, ...), custom_call_target="tpu_custom_call" | custom-call | tf_op jit(solution)/shard_map/pallas_call | solution.py:1022
  301.0 5.4 %shard_map.185 = (bf16[4,400,200]{2,1,0:T(8,128)(2,1)}, bf16[4,400,200]{2,1,0:T(8,128)(2,1)}, bf16[4,400,200]{2,1,0:T(8,128)(2,1)}, bf16[4,400,200]{2,1,0:T(8,128)(2,1)}) custom-call(s32[2]{0:T(128)} %pad_add_fusion.where, bf16[8,128,256]{2,1,0:T(8,128)(2,1)} %copy-done.3, bf16[8,128,256]{2,1,0:T(8,128)(2,1)} %copy-done.29, ...), custom_call_target="tpu_custom_call" | custom-call | tf_op jit(solution)/shard_map/pallas_call | solution.py:1054
  307.6 6.3 %collective-permute-done.36 = bf16[400,800]{1,0:T(8,128)(2,1)S(1)} collective-permute-done((bf16[400,800]{1,0:T(8,128)(2,1)}, bf16[400,800]{1,0:T(8,128)(2,1)S(1)}, u32[]{:S(2)}, u32[]{:S(2)}) %collective-permute-start.36) | collective-permute-done | bytes 640032 | tf_op jit(solution)/shard_map/ppermute | solution.py:131
  323.1 16.9 %shard_map.188 = (bf16[1024,768]{1,0:T(8,128)(2,1)}, bf16[1024,1600]{1,0:T(8,128)(2,1)}, f32[1,768]{1,0:T(1,128)}, f32[2,1600]{1,0:T(2,128)}) custom-call(s32[2]{0:T(128)} %pad_add_fusion.where, bf16[1024,768]{1,0:T(8,128)(2,1)} %get-tuple-element.185.qkv_ref, bf16[8,128,256]{2,1,0:T(8,128)(2,1)} %copy-done.11, f32[4,1024]{1,0:T(4,128)} %get-tuple-element.267.lse_ref, ...), custom_call_target="tpu_custom_call" | custom-call | tf_op jit(solution)/shard_map/pallas_call | solution.py:669
  340.0 7.5 %all-to-all-done.4 = bf16[8,208,200]{1,2,0:T(8,128)(2,1)S(1)} async-done(((bf16[8,208,200]{1,2,0:T(8,128)(2,1)}), bf16[8,208,200]{1,2,0:T(8,128)(2,1)S(1)}, u32[]{:S(2)}, u32[]{:S(2)}) %all-to-all-start.4) | async-done | bytes 665632 | tf_op jit(solution)/shard_map/all_to_all | solution.py:172
  356.3 6.9 %shard_map.189 = (bf16[400,768]{1,0:T(8,128)(2,1)}, bf16[400,768]{1,0:T(8,128)(2,1)}, bf16[400,768]{1,0:T(8,128)(2,1)}, bf16[208,768]{1,0:T(8,128)(2,1)}, bf16[192,768]{1,0:T(8,128)(2,1)}) custom-call(s32[2]{0:T(128)} %pad_add_fusion.where, bf16[1024,1600]{1,0:T(8,128)(2,1)} %get-tuple-element.184.n1_hbm.a_ref, bf16[1024,768]{1,0:T(8,128)(2,1)} %get-tuple-element.277.g_ref), custom_call_target="tpu_custom_call" | custom-call | tf_op jit(solution)/shard_map/pallas_call | solution.py:714
  363.2 8.8 %collective-permute-done.40 = bf16[4,400,200]{2,1,0:T(8,128)(2,1)S(1)} collective-permute-done((bf16[4,400,200]{2,1,0:T(8,128)(2,1)}, bf16[4,400,200]{2,1,0:T(8,128)(2,1)S(1)}, u32[]{:S(2)}, u32[]{:S(2)}) %collective-permute-start.40) | collective-permute-done | bytes 640032 | tf_op jit(solution)/shard_map/ppermute | solution.py:131
  387.9 5.4 %collective-permute-start.47 = (bf16[400,200]{1,0:T(8,128)(2,1)S(1)}, bf16[400,200]{1,0:T(8,128)(2,1)S(1)}, u32[]{:S(2)}, u32[]{:S(2)}) collective-permute-start(bf16[400,200]{1,0:T(8,128)(2,1)S(1)} %get-tuple-element.341), channel_id=1, source_target_pairs={{0,2},{1,3},{2,4},{3,5},{4,6},{5,7},{6,0},{7,1},{8,10},{9,11},{10,... | collective-permute-start | bytes 480008 | tf_op jit(solution)/shard_map/ppermute | solution.py:176
  402.9 3.9 shard_map.193
  406.8 3.8 all-to-all-start.5
  415.4 4.6 %collective-permute-done.50.rest_1_ = bf16[2,208,200]{2,1,0:T(8,128)(2,1)S(1)} collective-permute-done((bf16[2,208,200]{2,1,0:T(8,128)(2,1)S(1)}, bf16[2,208,200]{2,1,0:T(8,128)(2,1)S(1)}, u32[]{:S(2)}, u32[]{:S(2)}) %collective-permute-start.50) | collective-permute-done | bytes 166432 | tf_op jit(solution)/shard_map/ppermute | solution.py:90
  419.9 5.4 %collective-permute-done.51.rest_2_ = bf16[2,208,200]{2,1,0:T(8,128)(2,1)S(1)} collective-permute-done((bf16[2,208,200]{2,1,0:T(8,128)(2,1)S(1)}, bf16[2,208,200]{2,1,0:T(8,128)(2,1)S(1)}, u32[]{:S(2)}, u32[]{:S(2)}) %collective-permute-start.51) | collective-permute-done | bytes 166432 | tf_op jit(solution)/shard_map/ppermute | solution.py:90
  (338 shorter events, 182.3 us)
Async XLA Ops:
  7.2 64.2 %all-gather.4.cloned.1.call-start = ((), (), s32[]{:S(2)}) async-start(), calls=%async_computation.9 | async-start | bytes 3833856 | tf_op jit(solution)/shard_map/all_gather | solution.py:1097
  23.9 46.3 %all-to-all-start = ((bf16[8,432,128]{2,1,0:T(8,128)(2,1)}), bf16[8,432,128]{2,1,0:T(8,128)(2,1)S(1)}, u32[]{:S(2)}, u32[]{:S(2)}) async-start(bf16[8,432,128]{2,1,0:T(8,128)(2,1)} %shard_map.170), calls=%async_computation | async-start | bytes 1769472 | tf_op jit(solution)/shard_map/all_to_all | solution.py:172
  28.9 89.7 %all-gather.6.cloned.1.call-start = ((), (), s32[]{:S(2)}) async-start(), calls=%async_computation.10 | async-start | bytes 3833856 | tf_op jit(solution)/shard_map/all_gather | solution.py:1109
  29.0 18.9 %collective-permute-start.3 = (bf16[400,800]{1,0:T(8,128)(2,1)S(1)}, bf16[400,800]{1,0:T(8,128)(2,1)S(1)}, u32[]{:S(2)}, u32[]{:S(2)}) collective-permute-start(bf16[400,800]{1,0:T(8,128)(2,1)S(1)} %copy-done.16), channel_id=1, source_target_pairs={{0,8},{8,0},{16,24},{24,16},{1,9},{9,1},{17,25},{25,17},{2,10},{10... | collective-permute-start | bytes 1920008 | tf_op jit(solution)/shard_map/ppermute | solution.py:90
  29.5 33.5 %collective-permute-start.4 = (bf16[400,800]{1,0:T(8,128)(2,1)S(1)}, bf16[400,800]{1,0:T(8,128)(2,1)S(1)}, u32[]{:S(2)}, u32[]{:S(2)}) collective-permute-start(bf16[400,800]{1,0:T(8,128)(2,1)S(1)} %copy-done.16), channel_id=1, source_target_pairs={{0,16},{8,24},{16,0},{24,8},{1,17},{9,25},{17,1},{25,9},{2,18},{10... | collective-permute-start | bytes 1920008 | tf_op jit(solution)/shard_map/ppermute | solution.py:90
  30.1 33.0 %collective-permute-start.5 = (bf16[400,800]{1,0:T(8,128)(2,1)S(1)}, bf16[400,800]{1,0:T(8,128)(2,1)}, u32[]{:S(2)}, u32[]{:S(2)}) collective-permute-start(bf16[400,800]{1,0:T(8,128)(2,1)S(1)} %copy-done.16), channel_id=1, source_target_pairs={{0,24},{8,16},{16,8},{24,0},{1,25},{9,17},{17,9},{25,1},{2,26},{10... | collective-permute-start | bytes 1920008 | tf_op jit(solution)/shard_map/ppermute | solution.py:90
  73.3 19.3 %collective-permute-start.9 = (bf16[400,200]{1,0:T(8,128)(2,1)}, bf16[400,200]{1,0:T(8,128)(2,1)}, u32[]{:S(2)}, u32[]{:S(2)}) collective-permute-start(bf16[400,200]{1,0:T(8,128)(2,1)} %param.13), channel_id=1, source_target_pairs={{2,0},{3,1},{4,2},{5,3},{6,4},{7,5},{0,6},{1,7},{10,8},{11,9},{12,... | collective-permute-start | bytes 480008 | tf_op jit(solution)/shard_map/ppermute | solution.py:176
  86.2 26.8 %collective-permute-start.6 = (bf16[400,768]{1,0:T(8,128)(2,1)}, bf16[400,768]{1,0:T(8,128)(2,1)}, u32[]{:S(2)}, u32[]{:S(2)}) collective-permute-start(bf16[400,768]{1,0:T(8,128)(2,1)} %shard_map.172.rest_0_), channel_id=1, source_target_pairs={{0,8},{8,0},{16,24},{24,16},{1,9},{9,1},{17,25},{25,17},{2,10},{10... | collective-permute-start | bytes 1843208 | tf_op jit(solution)/shard_map/ppermute | solution.py:90
  92.6 26.1 %collective-permute-start.7 = (bf16[400,768]{1,0:T(8,128)(2,1)}, bf16[400,768]{1,0:T(8,128)(2,1)}, u32[]{:S(2)}, u32[]{:S(2)}) collective-permute-start(bf16[400,768]{1,0:T(8,128)(2,1)} %shard_map.172.rest_0_), channel_id=1, source_target_pairs={{0,16},{8,24},{16,0},{24,8},{1,17},{9,25},{17,1},{25,9},{2,18},{10... | collective-permute-start | bytes 1843208 | tf_op jit(solution)/shard_map/ppermute | solution.py:90
  94.5 24.1 %collective-permute-start.8 = (bf16[400,768]{1,0:T(8,128)(2,1)}, bf16[400,768]{1,0:T(8,128)(2,1)}, u32[]{:S(2)}, u32[]{:S(2)}) collective-permute-start(bf16[400,768]{1,0:T(8,128)(2,1)} %shard_map.172.rest_0_), channel_id=1, source_target_pairs={{0,24},{8,16},{16,8},{24,0},{1,25},{9,17},{17,9},{25,1},{2,26},{10... | collective-permute-start | bytes 1843208 | tf_op jit(solution)/shard_map/ppermute | solution.py:90
  119.9 25.8 %all-to-all-start.1 = ((bf16[8,208,200]{1,2,0:T(8,128)(2,1)}), bf16[8,208,200]{1,2,0:T(8,128)(2,1)S(1)}, u32[]{:S(2)}, u32[]{:S(2)}) async-start(bf16[8,208,200]{1,2,0:T(8,128)(2,1)} %copy.65), calls=%async_computation.1 | async-start | bytes 1638400 | tf_op jit(solution)/shard_map/all_to_all | solution.py:172
  123.6 20.7 %collective-permute-start.16 = (bf16[4,400,200]{2,1,0:T(8,128)(2,1)S(1)}, bf16[4,400,200]{2,1,0:T(8,128)(2,1)S(1)}, u32[]{:S(2)}, u32[]{:S(2)}) collective-permute-start(bf16[4,400,200]{2,1,0:T(8,128)(2,1)S(1)} %pad_maximum_fusion.rest_0_), channel_id=1, source_target_pairs={{0,8},{8,0},{16,24},{24,16},{1,9},{9,1},{17,25},{25,17},{2,10},{10... | collective-permute-start | bytes 1920008 | tf_op jit(solution)/shard_map/ppermute | solution.py:90
  125.4 20.3 %collective-permute-start.17 = (bf16[4,400,200]{2,1,0:T(8,128)(2,1)S(1)}, bf16[4,400,200]{2,1,0:T(8,128)(2,1)S(1)}, u32[]{:S(2)}, u32[]{:S(2)}) collective-permute-start(bf16[4,400,200]{2,1,0:T(8,128)(2,1)S(1)} %pad_maximum_fusion.rest_0_), channel_id=1, source_target_pairs={{0,16},{8,24},{16,0},{24,8},{1,17},{9,25},{17,1},{25,9},{2,18},{10... | collective-permute-start | bytes 1920008 | tf_op jit(solution)/shard_map/ppermute | solution.py:90
  146.8 20.1 %all-to-all-start.2 = ((bf16[8,128,256]{2,1,0:T(8,128)(2,1)}), bf16[8,128,256]{2,1,0:T(8,128)(2,1)S(1)}, u32[]{:S(2)}, u32[]{:S(2)}) async-start(bf16[8,128,256]{2,1,0:T(8,128)(2,1)} %get-tuple-element.189), calls=%async_computation.2 | async-start | bytes 1048576 | tf_op jit(solution)/shard_map/all_to_all | solution.py:172
  151.5 67.0 %all-gather.8.cloned.1.call-start = ((), (), s32[]{:S(2)}) async-start(), calls=%async_computation.11 | async-start | bytes 3833856 | tf_op jit(solution)/shard_map/all_gather | solution.py:1145
  177.7 98.9 %reduce-scatter.4.cloned.1.call-start = ((), (), s32[]{:S(2)}) async-start(), calls=%async_computation.12 | async-start | bytes 3833856 | tf_op jit(solution)/shard_map/reduce_scatter | solution.py:1154
  177.7 18.4 %collective-permute-start.25 = (bf16[208,1600]{1,0:T(8,128)(2,1)S(1)}, bf16[208,1600]{1,0:T(8,128)(2,1)S(1)}, u32[]{:S(2)}, u32[]{:S(2)}) collective-permute-start(bf16[208,1600]{1,0:T(8,128)(2,1)S(1)} %copy-done.9), channel_id=1, source_target_pairs={{0,8},{8,0},{16,24},{24,16},{1,9},{9,1},{17,25},{25,17},{2,10},{10... | collective-permute-start | bytes 1996808 | tf_op jit(solution)/shard_map/ppermute | solution.py:90
  178.2 18.0 %collective-permute-start.26 = (bf16[208,1600]{1,0:T(8,128)(2,1)S(1)}, bf16[208,1600]{1,0:T(8,128)(2,1)S(1)}, u32[]{:S(2)}, u32[]{:S(2)}) collective-permute-start(bf16[208,1600]{1,0:T(8,128)(2,1)S(1)} %copy-done.9), channel_id=1, source_target_pairs={{0,16},{8,24},{16,0},{24,8},{1,17},{9,25},{17,1},{25,9},{2,18},{10... | collective-permute-start | bytes 1996808 | tf_op jit(solution)/shard_map/ppermute | solution.py:90
  179.7 31.4 %collective-permute-start.27 = (bf16[208,1600]{1,0:T(8,128)(2,1)S(1)}, bf16[208,1600]{1,0:T(8,128)(2,1)S(1)}, u32[]{:S(2)}, u32[]{:S(2)}) collective-permute-start(bf16[208,1600]{1,0:T(8,128)(2,1)S(1)} %copy-done.9), channel_id=1, source_target_pairs={{0,24},{8,16},{16,8},{24,0},{1,25},{9,17},{17,9},{25,1},{2,26},{10... | collective-permute-start | bytes 1996808 | tf_op jit(solution)/shard_map/ppermute | solution.py:90
  181.3 34.6 %collective-permute-start.28 = (bf16[8,128,256]{2,1,0:T(8,128)(2,1)}, bf16[8,128,256]{2,1,0:T(8,128)(2,1)S(1)}, u32[]{:S(2)}, u32[]{:S(2)}) collective-permute-start(bf16[8,128,256]{2,1,0:T(8,128)(2,1)} %copy-done.3), channel_id=1, source_target_pairs={{0,1},{1,0},{2,3},{3,2},{4,5},{5,4},{6,7},{7,6},{8,9},{9,8},{10,11... | collective-permute-start | bytes 1572872 | tf_op jit(solution)/shard_map/ppermute | solution.py:168
  235.0 112.5 %reduce-scatter.6.cloned.1.call-start = ((), (), s32[]{:S(2)}) async-start(), calls=%async_computation.13 | async-start | bytes 3833856 | tf_op jit(solution)/shard_map/reduce_scatter | solution.py:1163
  288.7 27.7 %all-to-all-start.3 = ((bf16[8,128,256]{2,1,0:T(8,128)(2,1)}), bf16[8,128,256]{2,1,0:T(8,128)(2,1)S(1)}, u32[]{:S(2)}, u32[]{:S(2)}) async-start(bf16[8,128,256]{2,1,0:T(8,128)(2,1)} %get-tuple-element.249), calls=%async_computation.4 | async-start | bytes 1048576 | tf_op jit(solution)/shard_map/all_to_all | solution.py:172
  295.6 18.2 %collective-permute-start.36 = (bf16[400,800]{1,0:T(8,128)(2,1)}, bf16[400,800]{1,0:T(8,128)(2,1)S(1)}, u32[]{:S(2)}, u32[]{:S(2)}) collective-permute-start(bf16[400,800]{1,0:T(8,128)(2,1)} %get-tuple-element.261), channel_id=1, source_target_pairs={{0,8},{8,0},{16,24},{24,16},{1,9},{9,1},{17,25},{25,17},{2,10},{10... | collective-permute-start | bytes 1920008 | tf_op jit(solution)/shard_map/ppermute | solution.py:131
  296.0 18.8 %collective-permute-start.37 = (bf16[400,800]{1,0:T(8,128)(2,1)}, bf16[400,800]{1,0:T(8,128)(2,1)}, u32[]{:S(2)}, u32[]{:S(2)}) collective-permute-start(bf16[400,800]{1,0:T(8,128)(2,1)} %get-tuple-element.262), channel_id=1, source_target_pairs={{0,16},{8,24},{16,0},{24,8},{1,17},{9,25},{17,1},{25,9},{2,18},{10... | collective-permute-start | bytes 1920008 | tf_op jit(solution)/shard_map/ppermute | solution.py:132
  317.7 29.9 %all-to-all-start.4 = ((bf16[8,208,200]{1,2,0:T(8,128)(2,1)}), bf16[8,208,200]{1,2,0:T(8,128)(2,1)S(1)}, u32[]{:S(2)}, u32[]{:S(2)}) async-start(bf16[8,208,200]{1,2,0:T(8,128)(2,1)} %copy.69), calls=%async_computation.6 | async-start | bytes 1638400 | tf_op jit(solution)/shard_map/all_to_all | solution.py:172
  321.2 109.2 %reduce-scatter.8.cloned.1.call-start = ((), (), s32[]{:S(2)}) async-start(), calls=%async_computation.14 | async-start | bytes 3833856 | tf_op jit(solution)/shard_map/reduce_scatter | solution.py:1181
  321.3 18.7 %collective-permute-start.38 = (bf16[2,400,200]{2,1,0:T(8,128)(2,1)S(1)}, bf16[2,400,200]{2,1,0:T(8,128)(2,1)S(1)}, u32[]{:S(2)}, u32[]{:S(2)}) collective-permute-start(bf16[2,400,200]{2,1,0:T(8,128)(2,1)S(1)} %get-tuple-element.275), channel_id=1, source_target_pairs={{0,8},{8,0},{16,24},{24,16},{1,9},{9,1},{17,25},{25,17},{2,10},{10... | collective-permute-start | bytes 960008 | tf_op jit(solution)/shard_map/ppermute | solution.py:119
  322.2 17.8 %collective-permute-start.39 = (bf16[2,400,200]{2,1,0:T(8,128)(2,1)S(1)}, bf16[2,400,200]{2,1,0:T(8,128)(2,1)S(1)}, u32[]{:S(2)}, u32[]{:S(2)}) collective-permute-start(bf16[2,400,200]{2,1,0:T(8,128)(2,1)S(1)} %get-tuple-element.276), channel_id=1, source_target_pairs={{0,16},{8,24},{16,0},{24,8},{1,17},{9,25},{17,1},{25,9},{2,18},{10... | collective-permute-start | bytes 960008 | tf_op jit(solution)/shard_map/ppermute | solution.py:120
  351.6 20.4 %collective-permute-start.40 = (bf16[4,400,200]{2,1,0:T(8,128)(2,1)}, bf16[4,400,200]{2,1,0:T(8,128)(2,1)S(1)}, u32[]{:S(2)}, u32[]{:S(2)}) collective-permute-start(bf16[4,400,200]{2,1,0:T(8,128)(2,1)} %get-tuple-element.288), channel_id=1, source_target_pairs={{0,8},{8,0},{16,24},{24,16},{1,9},{9,1},{17,25},{25,17},{2,10},{10... | collective-permute-start | bytes 1920008 | tf_op jit(solution)/shard_map/ppermute | solution.py:131
  353.0 20.1 %collective-permute-start.41 = (bf16[4,400,200]{2,1,0:T(8,128)(2,1)}, bf16[4,400,200]{2,1,0:T(8,128)(2,1)S(1)}, u32[]{:S(2)}, u32[]{:S(2)}) collective-permute-start(bf16[4,400,200]{2,1,0:T(8,128)(2,1)} %get-tuple-element.289), channel_id=1, source_target_pairs={{0,16},{8,24},{16,0},{24,8},{1,17},{9,25},{17,1},{25,9},{2,18},{10... | collective-permute-start | bytes 1920008 | tf_op jit(solution)/shard_map/ppermute | solution.py:132
  384.4 17.4 %collective-permute-start.44 = (bf16[400,768]{1,0:T(8,128)(2,1)}, bf16[400,768]{1,0:T(8,128)(2,1)S(1)}, u32[]{:S(2)}, u32[]{:S(2)}) collective-permute-start(bf16[400,768]{1,0:T(8,128)(2,1)} %get-tuple-element.295), channel_id=1, source_target_pairs={{0,8},{8,0},{16,24},{24,16},{1,9},{9,1},{17,25},{25,17},{2,10},{10... | collective-permute-start | bytes 1843208 | tf_op jit(solution)/shard_map/ppermute | solution.py:131
  406.8 27.4 %all-to-all-start.5 = ((bf16[8,432,128]{2,1,0:T(8,128)(2,1)}), bf16[8,432,128]{2,1,0:T(8,128)(2,1)S(1)}, u32[]{:S(2)}, u32[]{:S(2)}) async-start(bf16[8,432,128]{2,1,0:T(8,128)(2,1)} %shard_map.193), calls=%async_computation.7 | async-start | bytes 1769472 | tf_op jit(solution)/shard_map/all_to_all | solution.py:172
  (92 other events, 917.0 us)
Sparse Core Ops, SparseCore 0:
  9.6 61.7 all-gather.3
  73.1 45.4 all-gather.5
  177.8 40.7 all-gather.7
  235.1 41.4 reduce-scatter.3
  278.8 50.6 reduce-scatter.5
  347.7 49.8 reduce-scatter.7
